TPU v7x, 32 devices: a whole 2x2x4 slice. The times are simulated.
32 devices in a mesh: row: 4 (over x, core), col: 8 (over z, y).
Axes of the slice: x: 2, y: 2, z: 4, core: 2. Of those that a mesh axis runs over, the one named last changes fastest.
Arguments:
- amplitudes: bfloat16 [8192, 4096], P('row', 'col'), may hold values from -6 to 6
- integrals: bfloat16 [4096, 2048], P('col'), may hold values from -0.125 to 0.125
- pair_index: int32 [8192], P('row'), may hold values from 0 to 39999, as said below
- partner: int32 [8192], P('row'), may hold values from 0 to 8191, as said below
- occ_energy: float32 [200], replicated, may hold values from -1 to -0.3
- vir_energy: float32 [2000], replicated, may hold values from 0.05 to 1
Outputs:
- increment: bfloat16 [8192, 4096], P('row', 'col')
Inputs may be any that keep to these rules, and one draw needn't show every extreme that they name: `pair_index`: rows 0 and 1 hold the pairs (199, 199) and (0, 0); otherwise i and j are independent and uniform over 0 to 199. partner is an involution; partner[k] lies in row block (k // 2048) XOR (2), and pair_index[partner[k]] is pair_index[k] with i and j exchanged.
All inputs are finite; a program needn't handle non-finite values.
Results may differ from a plain program's by a relative error of at most 0.001.
Values may be sent and summed in bfloat16 or wider, within the bound.
No kernel may reach another device: no remote copies, remote signals or barrier semaphores. Data moves between devices by JAX's collectives and lax.ppermute only.
A program may use at most 128 MiB of HBM per device.

v0:
```python
import jax
import jax.numpy as jnp
from jax import lax
from jax.sharding import PartitionSpec as P

NOCC = 200
NV = 2000


def passed_along(value, axis, steps):
    count = lax.axis_size(axis)
    pairs = [(source, (source + steps) % count) for source in range(count)]
    return lax.ppermute(value, axis, pairs)


def partner_2(x, axis, apart):
    return lax.ppermute(x, axis, [(i, i ^ 1 << apart) for i in range(lax.axis_size(axis))])


def mirror_pairs(values):
    pair_width = values.shape[1]
    parity = jnp.arange(pair_width, dtype=jnp.int32) % 2 == 0
    return jnp.where(parity[None, :], jnp.roll(values, -1, axis=1), jnp.roll(values, 1, axis=1))


def table_lookup(table, positions):
    slots = jnp.arange(table.shape[0], dtype=jnp.int32)
    return jnp.sum(jnp.where(positions[:, None] == slots[None, :], table[None, :], 0.0), axis=1)


def contract_stops(amp_rows, integrals, pair_width):
    stop_count = integrals.shape[1] // pair_width
    running = jnp.dot(amp_rows, integrals[:, :pair_width], preferred_element_type=jnp.float32)
    slab_rest = integrals[:, pair_width:]
    moving = amp_rows
    for stop_index in range(1, stop_count):
        slab_rest, moving = passed_along((slab_rest, moving), "col", 1)
        running = running + jnp.dot(
            moving, slab_rest[:, :pair_width], preferred_element_type=jnp.float32
        )
        slab_rest = slab_rest[:, pair_width:]
    return running


def shards(amplitudes, integrals, pair_index, partner, occ_energy, vir_energy):
    row_count, pair_width = amplitudes.shape
    bit_number = lax.axis_size("row").bit_length() - 2
    local_partner = partner % row_count
    running = contract_stops(amplitudes, integrals, pair_width)
    partner_sums = partner_2(running, "row", bit_number)
    opposite = jnp.take(partner_sums, local_partner, axis=0)
    summed = running + mirror_pairs(opposite)
    occ_sum = table_lookup(occ_energy, pair_index // NOCC) + table_lookup(
        occ_energy, pair_index % NOCC
    )
    global_pair = lax.axis_index("col") * pair_width + jnp.arange(pair_width, dtype=jnp.int32)
    unordered = global_pair // 2
    vir_sum = table_lookup(vir_energy, unordered // NV) + table_lookup(vir_energy, unordered % NV)
    denom = vir_sum[None, :] - occ_sum[:, None]
    return (summed / denom).astype(jnp.bfloat16)


def solution(mesh):
    in_specs = (P("row", "col"), P("col", None), P("row"), P("row"), P(), P())
    out_specs = P("row", "col")
    return jax.shard_map(shards, mesh=mesh, in_specs=in_specs, out_specs=out_specs, check_vma=False)
```

profile of v0, /device:TPU:0, one launch (start us, length us, event | category | flops | bytes accessed | tf_op | source)
XLA Modules:
  0.0 332.5 jit_solution(10046414713768555589)
XLA Ops:
  0.0 3.0 collective-permute-start
  3.0 48.9 %collective-permute-done = bf16[2048,512]{1,0:T(8,128)(2,1)S(1)} collective-permute-done((bf16[2048,512]{1,0:T(8,128)(2,1)}, bf16[2048,512]{1,0:T(8,128)(2,1)S(1)}, u32[]{:S(2)}, u32[]{:S(2)}) %collective-permute-start) | collective-permute-done | bytes 2097184 | tf_op jit(solution)/shard_map/ppermute | solution.py:13
  51.9 0.0 collective-permute-start.2
  51.9 1.5 slice.35
  53.4 1.1 collective-permute-start.1
  54.5 48.6 %collective-permute-done.2 = bf16[2048,512]{1,0:T(8,128)(2,1)S(1)} collective-permute-done((bf16[2048,512]{1,0:T(8,128)(2,1)S(1)}, bf16[2048,512]{1,0:T(8,128)(2,1)S(1)}, u32[]{:S(2)}, u32[]{:S(2)}) %collective-permute-start.2) | collective-permute-done | bytes 2097184 | tf_op jit(solution)/shard_map/ppermute | solution.py:13
  103.2 0.0 collective-permute-start.4
  103.2 33.7 %collective-permute-done.1 = bf16[512,1536]{1,0:T(8,128)(2,1)S(1)} collective-permute-done((bf16[512,1536]{1,0:T(8,128)(2,1)S(1)}, bf16[512,1536]{1,0:T(8,128)(2,1)S(1)}, u32[]{:S(2)}, u32[]{:S(2)}) %collective-permute-start.1) | collective-permute-done | bytes 1572896 | tf_op jit(solution)/shard_map/ppermute | solution.py:13
  136.9 0.1 slice.47
  137.0 0.1 collective-permute-start.3
  137.1 0.0 copy-done
  137.1 2.3 fusion.7
  139.4 63.1 %collective-permute-done.3 = bf16[512,1024]{1,0:T(8,128)(2,1)S(1)} collective-permute-done((bf16[512,1024]{1,0:T(8,128)(2,1)S(1)}, bf16[512,1024]{1,0:T(8,128)(2,1)S(1)}, u32[]{:S(2)}, u32[]{:S(2)}) %collective-permute-start.3) | collective-permute-done | bytes 1048608 | tf_op jit(solution)/shard_map/ppermute | solution.py:13
  202.6 0.1 collective-permute-start.5
  202.7 1.2 fusion.5
  203.9 1.3 fusion.3
  205.2 0.0 copy-start.2
  205.2 0.0 copy-start.3
  205.2 0.0 copy-start.4
  205.2 0.0 copy-start.1
  205.2 12.3 %collective-permute-done.5 = bf16[512,512]{1,0:T(8,128)(2,1)S(1)} collective-permute-done((bf16[512,512]{1,0:T(8,128)(2,1)S(1)}, bf16[512,512]{1,0:T(8,128)(2,1)S(1)}, u32[]{:S(2)}, u32[]{:S(2)}) %collective-permute-start.5) | collective-permute-done | bytes 524320 | tf_op jit(solution)/shard_map/ppermute | solution.py:13
  217.5 0.0 collective-permute-done.4
  217.5 3.5 %add_add_fusion = f32[2048,512]{1,0:T(8,128)} fusion(f32[2048,512]{1,0:T(8,128)S(1)} %fusion.3, f32[2048,512]{1,0:T(8,128)S(1)} %fusion.7, f32[2048,512]{1,0:T(8,128)S(1)} %fusion.5, bf16[2048,512]{1,0:T(8,128)(2,1)S(1)} %collective-permute-done.4, bf16[512,512]{1,0:T(8,128)(2,1)S(1)} %collective-permute-done.5), kind=kOutput, calls=%fused_computation.4 | convolution fusion | flops 1076887552 | bytes 19398656 | tf_op jit(solution)/shard_map/dot_general | solution.py:38
  221.0 1.3 collective-permute-start.6
  222.3 0.6 select_reduce_fusion.2
  222.9 0.9 select_reduce_fusion
  223.9 87.3 %collective-permute-done.6 = f32[2048,512]{1,0:T(8,128)} collective-permute-done((f32[2048,512]{1,0:T(8,128)}, f32[2048,512]{1,0:T(8,128)}, u32[]{:S(2)}, u32[]{:S(2)}) %collective-permute-start.6) | collective-permute-done | bytes 4194336 | tf_op jit(solution)/shard_map/ppermute | solution.py:17
  311.2 11.7 %gather_fusion = f32[2048,512]{1,0:T(8,128)} fusion(f32[2048,512]{1,0:T(8,128)} %collective-permute-done.6, s32[2048]{0:T(1024)S(1)} %broadcast_clamp_fusion), kind=kCustom, calls=%fused_computation | custom fusion | bytes 8396800 | tf_op jit(solution)/shard_map/jit(_take)/gather | solution.py:51
  323.0 2.5 broadcast_select_fusion
  325.4 1.5 fusion.19
  326.9 0.4 fusion.20
  327.3 5.1 %fusion.2 = bf16[2048,512]{1,0:T(8,128)(2,1)} fusion(f32[2048,512]{1,0:T(8,128)} %add_add_fusion, f32[2048,511]{1,0:T(8,128)S(1)} %get-tuple-element.10, f32[2048,1]{1,0:T(8,128)S(1)} %get-tuple-element.12, f32[2048,1]{1,0:T(8,128)S(1)} %get-tuple-element.11, f32[2048,511]{1,0:T(8,128)S(1)} %get-tuple-element.9, f32[2048]{0:T(1024)S(1)} %add.99, ...), kind=kLoop, calls=%fused_computation.5 | loop fusion | flops 7340032 | bytes 14690816 | tf_op jit(solution)/shard_map/convert_element_type | solution.py:60
  (13 shorter events, 0.1 us)
Async XLA Ops:
  0.0 137.1 %copy-start = (bf16[2048,512]{1,0:T(8,128)(2,1)S(1)}, bf16[2048,512]{1,0:T(8,128)(2,1)}, u32[]{:S(2)}) copy-start(bf16[2048,512]{1,0:T(8,128)(2,1)} %param.6) | copy-start | bytes 6291460
  0.0 51.9 %collective-permute-start = (bf16[2048,512]{1,0:T(8,128)(2,1)}, bf16[2048,512]{1,0:T(8,128)(2,1)S(1)}, u32[]{:S(2)}, u32[]{:S(2)}) collective-permute-start(bf16[2048,512]{1,0:T(8,128)(2,1)} %param.6), channel_id=1, source_target_pairs={{0,1},{1,2},{2,3},{3,4},{4,5},{5,6},{6,7},{7,0},{8,9},{9,10},{10,1... | collective-permute-start | bytes 6291464 | tf_op jit(solution)/shard_map/ppermute | solution.py:13
  51.9 51.3 %collective-permute-start.2 = (bf16[2048,512]{1,0:T(8,128)(2,1)S(1)}, bf16[2048,512]{1,0:T(8,128)(2,1)S(1)}, u32[]{:S(2)}, u32[]{:S(2)}) collective-permute-start(bf16[2048,512]{1,0:T(8,128)(2,1)S(1)} %collective-permute-done), channel_id=1, source_target_pairs={{0,1},{1,2},{2,3},{3,4},{4,5},{5,6},{6,7},{7,0},{8,9},{9,10},{10,1... | collective-permute-start | bytes 6291464 | tf_op jit(solution)/shard_map/ppermute | solution.py:13
  53.4 83.5 %collective-permute-start.1 = (bf16[512,1536]{1,0:T(8,128)(2,1)S(1)}, bf16[512,1536]{1,0:T(8,128)(2,1)S(1)}, u32[]{:S(2)}, u32[]{:S(2)}) collective-permute-start(bf16[512,1536]{1,0:T(8,128)(2,1)S(1)} %slice.35), channel_id=1, source_target_pairs={{0,1},{1,2},{2,3},{3,4},{4,5},{5,6},{6,7},{7,0},{8,9},{9,10},{10,1... | collective-permute-start | bytes 4718600 | tf_op jit(solution)/shard_map/ppermute | solution.py:13
  103.2 114.3 %collective-permute-start.4 = (bf16[2048,512]{1,0:T(8,128)(2,1)S(1)}, bf16[2048,512]{1,0:T(8,128)(2,1)S(1)}, u32[]{:S(2)}, u32[]{:S(2)}) collective-permute-start(bf16[2048,512]{1,0:T(8,128)(2,1)S(1)} %collective-permute-done.2), channel_id=1, source_target_pairs={{0,1},{1,2},{2,3},{3,4},{4,5},{5,6},{6,7},{7,0},{8,9},{9,10},{10,1... | collective-permute-start | bytes 6291464 | tf_op jit(solution)/shard_map/ppermute | solution.py:13
  137.0 65.5 %collective-permute-start.3 = (bf16[512,1024]{1,0:T(8,128)(2,1)S(1)}, bf16[512,1024]{1,0:T(8,128)(2,1)S(1)}, u32[]{:S(2)}, u32[]{:S(2)}) collective-permute-start(bf16[512,1024]{1,0:T(8,128)(2,1)S(1)} %slice.47), channel_id=1, source_target_pairs={{0,1},{1,2},{2,3},{3,4},{4,5},{5,6},{6,7},{7,0},{8,9},{9,10},{10,1... | collective-permute-start | bytes 3145736 | tf_op jit(solution)/shard_map/ppermute | solution.py:13
  202.6 14.9 %collective-permute-start.5 = (bf16[512,512]{1,0:T(8,128)(2,1)S(1)}, bf16[512,512]{1,0:T(8,128)(2,1)S(1)}, u32[]{:S(2)}, u32[]{:S(2)}) collective-permute-start(bf16[512,512]{1,0:T(8,128)(2,1)S(1)} %slice.49), channel_id=1, source_target_pairs={{0,1},{1,2},{2,3},{3,4},{4,5},{5,6},{6,7},{7,0},{8,9},{9,10},{10,1... | collective-permute-start | bytes 1572872 | tf_op jit(solution)/shard_map/ppermute | solution.py:13
  205.2 17.1 %copy-start.2 = (s32[2048]{0:T(1024)S(1)}, s32[2048]{0:T(1024)}, u32[]{:S(2)}) copy-start(s32[2048]{0:T(1024)} %param.8) | copy-start | bytes 24580
  205.2 17.1 %copy-start.3 = (f32[200]{0:T(256)S(1)}, f32[200]{0:T(256)}, u32[]{:S(2)}) copy-start(f32[200]{0:T(256)} %param.10) | copy-start | bytes 2404
  205.2 17.7 %copy-start.4 = (f32[2000]{0:T(1024)S(1)}, f32[2000]{0:T(1024)}, u32[]{:S(2)}) copy-start(f32[2000]{0:T(1024)} %param.11) | copy-start | bytes 24004
  205.2 18.7 %copy-start.1 = (s32[2048]{0:T(1024)S(1)}, s32[2048]{0:T(1024)}, u32[]{:S(2)}) copy-start(s32[2048]{0:T(1024)} %param.9) | copy-start | bytes 24580
  221.0 90.2 %collective-permute-start.6 = (f32[2048,512]{1,0:T(8,128)}, f32[2048,512]{1,0:T(8,128)}, u32[]{:S(2)}, u32[]{:S(2)}) collective-permute-start(f32[2048,512]{1,0:T(8,128)} %add_add_fusion), channel_id=1, source_target_pairs={{0,16},{8,24},{16,0},{24,8},{1,17},{9,25},{17,1},{25,9},{2,18},{10... | collective-permute-start | bytes 12582920 | tf_op jit(solution)/shard_map/ppermute | solution.py:17
where the time goes:
time: 333 us; the launch traced here: 332 us
  waiting for transfers between devices  294 us (88%)
  local copies, waits for them, and re-layouts  15.3 us (5%)
  other arithmetic  9.18 us (3%)
  matrix products  8.25 us (2%)
  starting transfers between devices  5.48 us (2%)
    ppermute x6, waiting for transfers between devices, passed_along(): return lax.ppermute(value, axis, pairs)  207 us
    ppermute x1, waiting for transfers between devices, partner_2(): lax.ppermute(x, axis, [(i, i ^ 1 << apart) for i in range(lax.axis_size(a...  87.3 us
    gather x1, local copies, waits for them, and re-layouts, shards(): opposite = jnp.take(partner_sums, local_partner, axis=0)  11.7 us
  transfers between devices with their start and end apart: 7, of which 6 were waited for; matrix products, arithmetic and copies ran while one was open for 2% of the time, Pallas kernels for 0%

commit v1 on v0

v1 whole, which is shorter than its diff:
```python
import functools

import jax
import jax.numpy as jnp
from jax import lax
from jax.experimental import pallas as pl
from jax.experimental.pallas import tpu as pltpu
from jax.sharding import PartitionSpec as P

NOCC = 200
NV = 2000
CHUNKS = 4
SCALE_ROWS = 16
TOP = 32767.0
STEPS = 64.0
TINY = 1e-33

VMEM = pl.BlockSpec(memory_space=pltpu.VMEM)
SMEM = pl.BlockSpec(memory_space=pltpu.SMEM)


def call(body, out_shape, flops, moved, scratch=()):
    def run(*operands):
        return pl.pallas_call(
            body,
            out_shape=out_shape,
            in_specs=[SMEM] + [VMEM] * (len(operands) - 1),
            out_specs=jax.tree.map(lambda _: VMEM, out_shape),
            scratch_shapes=list(scratch),
            compiler_params=pltpu.CompilerParams(vmem_limit_bytes=48 * 1024 * 1024),
            cost_estimate=pl.CostEstimate(flops=flops, bytes_accessed=moved, transcendentals=0),
        )(*operands)

    return run


def swap_matrix(width):
    down = lax.broadcasted_iota(jnp.int32, (width, width), 0)
    across = lax.broadcasted_iota(jnp.int32, (width, width), 1)
    return jnp.where(down == (across ^ 1), 1.0, 0.0).astype(jnp.bfloat16)


def mirrored(values, swap):
    return jnp.dot(values, swap, preferred_element_type=jnp.float32).astype(jnp.bfloat16)


def mirror_kernel(flags, integrals, out):
    width = integrals.shape[0]
    swap = swap_matrix(width)
    for stop in range(integrals.shape[1] // width):
        cols = pl.ds(stop * width, width)
        out[:, cols] = mirrored(integrals[:, cols], swap)


def align_kernel(index, send, flags, slots, amplitudes, out):
    rows = amplitudes.shape[0]
    chunk = out.shape[0]
    upper = flags[0]
    side = 1 - upper if send else upper
    first = side * (rows // 2) + index * chunk

    @pl.when(upper == 0)
    def _():
        out[...] = amplitudes[pl.ds(pl.multiple_of(first, chunk), chunk), :]

    @pl.when(upper == 1)
    def _():
        wanted = first + lax.broadcasted_iota(jnp.int32, (chunk, rows), 0)
        pick = jnp.where(slots[...] == wanted, 1.0, 0.0).astype(jnp.bfloat16)
        out[...] = jnp.dot(pick, amplitudes[...], preferred_element_type=jnp.float32).astype(jnp.bfloat16)


def product(own, other, direct, swapped):
    return jnp.dot(own[...], direct[...], preferred_element_type=jnp.float32) + jnp.dot(
        other[...], swapped[...], preferred_element_type=jnp.float32
    )


def code(values, out):
    rows = values.shape[0]
    top = jnp.max(jnp.abs(values), axis=0, keepdims=True)
    level = jnp.ceil(STEPS * jnp.log2(jnp.maximum(top, TINY) * (1.0001 / TOP)))
    coded = jnp.round(values * jnp.exp2(level * (-1.0 / STEPS)))
    out[pl.ds(0, rows), :] = coded.astype(jnp.int32).astype(jnp.int16)
    spread = jnp.broadcast_to(level.astype(jnp.int32), (SCALE_ROWS, values.shape[1]))
    out[pl.ds(rows, SCALE_ROWS), :] = spread.astype(jnp.int16)


def decode(coded):
    rows = coded.shape[0] - SCALE_ROWS
    level = coded[pl.ds(rows, SCALE_ROWS), :].astype(jnp.int32).astype(jnp.float32)[0:1, :]
    return coded[pl.ds(0, rows), :].astype(jnp.int32).astype(jnp.float32) * jnp.exp2(level * (1.0 / STEPS))


def first_kernel(flags, own, other, direct, swapped, out):
    code(product(own, other, direct, swapped), out)


def second_kernel(flags, own, other, direct, swapped, arrived, out):
    code(product(own, other, direct, swapped) + decode(arrived), out)


def third_kernel(flags, own, other, direct, swapped, arrived, out):
    here = jnp.where(flags[1] == 0, 1.0, 0.0)
    code(product(own, other, direct, swapped) + decode(arrived) * here, out)


def last_kernel(flags, own, other, direct, swapped, crossed, arrived, occ_sum, vir_sum, out):
    here = jnp.where(flags[1] == 1, 1.0, 0.0)
    total = product(own, other, direct, swapped) + decode(arrived) + decode(crossed) * here
    out[...] = (total / (vir_sum[...] - occ_sum[...])).astype(jnp.bfloat16)


def place_kernel(count, flags, slots, *refs):
    own, other, out, whole = refs[:count], refs[count : 2 * count], refs[-2], refs[-1]
    upper = flags[0]
    rows, width = out.shape
    chunk = rows // (2 * count)
    swap = swap_matrix(width)
    for index in range(count):
        here = upper * (rows // 2) + index * chunk
        there = (1 - upper) * (rows // 2) + index * chunk
        whole[pl.ds(pl.multiple_of(here, chunk), chunk), :] = own[index][...]
        whole[pl.ds(pl.multiple_of(there, chunk), chunk), :] = mirrored(other[index][...], swap)

    @pl.when(upper == 0)
    def _():
        out[...] = whole[...]

    @pl.when(upper == 1)
    def _():
        block = 256

        @pl.loop(0, rows // block)
        def _(step):
            part = pl.ds(pl.multiple_of(step * block, block), block)
            source = lax.broadcasted_iota(jnp.int32, (block, rows), 1)
            pick = jnp.where(slots[part, :] == source, 1.0, 0.0).astype(jnp.bfloat16)
            out[part, :] = jnp.dot(pick, whole[...], preferred_element_type=jnp.float32).astype(jnp.bfloat16)


def table_lookup(table, positions):
    slots = jnp.arange(table.shape[0], dtype=jnp.int32)
    return jnp.sum(jnp.where(positions[:, None] == slots[None, :], table[None, :], 0.0), axis=1)


def across_rows(value):
    count = lax.axis_size("row")
    return lax.ppermute(value, "row", [(i, i ^ (count // 2)) for i in range(count)])


def across_pair(value):
    return lax.ppermute(value, "col", [(i, i ^ 1) for i in range(lax.axis_size("col"))])


def two_along(value):
    count = lax.axis_size("col")
    return lax.ppermute(value, "col", [(i, (i + 2) % count) for i in range(count)])


def shards(amplitudes, integrals, pair_index, partner, occ_energy, vir_energy):
    rows, width = amplitudes.shape
    chunk = rows // (2 * CHUNKS)
    upper = (lax.axis_index("row") // (lax.axis_size("row") // 2)).astype(jnp.int32)
    odd = (lax.axis_index("col") % 2).astype(jnp.int32)
    flags = jnp.stack([upper, odd])
    slots = partner % rows

    chunk_shape = jax.ShapeDtypeStruct((chunk, width), jnp.bfloat16)
    coded_shape = jax.ShapeDtypeStruct((chunk + SCALE_ROWS, width), jnp.int16)
    pair_bytes = 4 * chunk * width + 4 * width * width

    def align(index, send):
        return call(
            functools.partial(align_kernel, index, send), chunk_shape, 2 * chunk * rows * width, 2 * rows * width
        )(flags, slots[None, :], amplitudes)

    def stage(body, out_shape, *operands):
        return call(body, out_shape, 4 * chunk * width * width, pair_bytes + 2 * chunk * width)(flags, *operands)

    sent = [align(index, True) for index in range(CHUNKS)]
    other = [across_rows(value) for value in sent]
    own = [align(index, False) for index in range(CHUNKS)]

    swapped = call(
        mirror_kernel, jax.ShapeDtypeStruct(integrals.shape, jnp.bfloat16), 8 * width**3, 4 * integrals.size
    )(flags, integrals)
    direct = [integrals[:, s * width : (s + 1) * width] for s in range(4)]
    swapped = [swapped[:, s * width : (s + 1) * width] for s in range(4)]

    occ_sum = table_lookup(occ_energy, pair_index // NOCC) + table_lookup(occ_energy, pair_index % NOCC)
    occ_upper = across_rows(occ_sum[rows // 2 :])
    occ_sum = jnp.where(upper == 0, occ_sum[: rows // 2], occ_upper)[:, None]
    global_pair = lax.axis_index("col") * width + jnp.arange(width, dtype=jnp.int32)
    unordered = global_pair // 2
    vir_sum = table_lookup(vir_energy, unordered // NV) + table_lookup(vir_energy, unordered % NV)
    vir_sum = vir_sum[None, :]

    done = []
    for index in range(CHUNKS):
        pair = (own[index], other[index])
        moved = two_along(stage(first_kernel, coded_shape, *pair, direct[3], swapped[3]))
        crossed = across_pair(stage(second_kernel, coded_shape, *pair, direct[1], swapped[1], moved))
        arrived = two_along(stage(third_kernel, coded_shape, *pair, direct[2], swapped[2], crossed))
        done.append(
            stage(
                last_kernel,
                chunk_shape,
                *pair,
                direct[0],
                swapped[0],
                crossed,
                arrived,
                occ_sum[index * chunk : (index + 1) * chunk],
                vir_sum,
            )
        )
    theirs = [across_rows(value) for value in done]
    return call(
        functools.partial(place_kernel, CHUNKS),
        jax.ShapeDtypeStruct((rows, width), jnp.bfloat16),
        2 * rows * rows * width,
        4 * rows * width,
        [pltpu.VMEM((rows, width), jnp.bfloat16)],
    )(flags, slots[:, None], *done, *theirs)


def solution(mesh):
    in_specs = (P("row", "col"), P("col", None), P("row"), P("row"), P(), P())
    out_specs = P("row", "col")
    return jax.shard_map(shards, mesh=mesh, in_specs=in_specs, out_specs=out_specs, check_vma=False)
```

time: 333 us -> 109 us (0.33)
  the two profiles are of different devices: /device:TPU:0 before, /device:TPU:2 now
where the time goes in v1:
time: 109 us; the launch traced here: 108 us
  Pallas kernels  51.3 us (47%)
  waiting for transfers between devices  22 us (20%)
  starting transfers between devices  21.9 us (20%)
  local copies, waits for them, and re-layouts  9.9 us (9%)
  other arithmetic  2.35 us (2%)
    pallas_call x26, Pallas kernels, run(): pl.pallas_call(body, out_shape=out_shape, in_specs=[SMEM] + [VMEM] * (len...  51.3 us
    ppermute x8, waiting for transfers between devices, two_along(): lax.ppermute(value, 'col', [(i, (i + 2) % count) for i in range(count)])  12.4 us
    ppermute x8, starting transfers between devices, two_along(): lax.ppermute(value, 'col', [(i, (i + 2) % count) for i in range(count)])  10.2 us
    ppermute x9, waiting for transfers between devices, across_rows(): lax.ppermute(value, 'row', [(i, i ^ count // 2) for i in range(count)])  9.56 us
    ppermute x4, starting transfers between devices, across_pair(): lax.ppermute(value, 'col', [(i, i ^ 1) for i in range(lax.axis_size('col'...  6.34 us
    unnamed x44, local copies, waits for them, and re-layouts  5.96 us
    ppermute x9, starting transfers between devices, across_rows(): lax.ppermute(value, 'row', [(i, i ^ count // 2) for i in range(count)])  5.32 us
  transfers between devices with their start and end apart: 21, of which 10 were waited for; matrix products, arithmetic and copies ran while one was open for 5% of the time, Pallas kernels for 37%

profile of v1, /device:TPU:2, one launch (start us, length us, event | category | flops | bytes accessed | tf_op | source)
XLA Modules:
  0.0 107.8 jit_solution(7565179577797688672)
XLA Ops:
  0.8 1.6 %copy-done = bf16[2048,512]{1,0:T(8,128)(2,1)S(1)} copy-done((bf16[2048,512]{1,0:T(8,128)(2,1)S(1)}, bf16[2048,512]{1,0:T(8,128)(2,1)}, u32[]{:S(2)}) %copy-start) | copy-done | bytes 2097176
  2.4 2.0 %shard_map.84 = bf16[256,512]{1,0:T(8,128)(2,1)} custom-call(s32[2]{0:T(128)S(1)} %pad_add_fusion.flags, s32[1,2048]{1,0:T(1,128)S(1)} %bitcast.9, bf16[2048,512]{1,0:T(8,128)(2,1)S(1)} %copy-done), custom_call_target="tpu_custom_call" | custom-call | flops 536870912 | bytes 2097152 | tf_op jit(solution)/shard_map/pallas_call | solution.py:24
  5.0 2.1 %collective-permute-start.4 = (f32[1024]{0:T(1024)S(1)}, f32[1024]{0:T(1024)S(1)}, u32[]{:S(2)}, u32[]{:S(2)}) collective-permute-start(f32[1024]{0:T(1024)S(1)} %slice.77), channel_id=1, source_target_pairs={{0,16},{8,24},{16,0},{24,8},{1,17},{9,25},{17,1},{25,9},{2,18},{10... | collective-permute-start | bytes 12296 | tf_op jit(solution)/shard_map/ppermute | solution.py:149
  7.1 2.0 %shard_map.78 = bf16[256,512]{1,0:T(8,128)(2,1)} custom-call(s32[2]{0:T(128)S(1)} %pad_add_fusion.flags, s32[1,2048]{1,0:T(1,128)S(1)} %bitcast.10, bf16[2048,512]{1,0:T(8,128)(2,1)S(1)} %copy-done), custom_call_target="tpu_custom_call" | custom-call | flops 536870912 | bytes 2097152 | tf_op jit(solution)/shard_map/pallas_call | solution.py:24
  9.0 2.0 %shard_map.72 = bf16[256,512]{1,0:T(8,128)(2,1)} custom-call(s32[2]{0:T(128)S(1)} %pad_add_fusion.flags, s32[1,2048]{1,0:T(1,128)S(1)} %bitcast.11, bf16[2048,512]{1,0:T(8,128)(2,1)S(1)} %copy-done), custom_call_target="tpu_custom_call" | custom-call | flops 536870912 | bytes 2097152 | tf_op jit(solution)/shard_map/pallas_call | solution.py:24
  12.3 2.0 %shard_map.65 = bf16[256,512]{1,0:T(8,128)(2,1)} custom-call(s32[2]{0:T(128)S(1)} %pad_add_fusion.flags, s32[1,2048]{1,0:T(1,128)S(1)} %bitcast.12, bf16[2048,512]{1,0:T(8,128)(2,1)S(1)} %copy-done), custom_call_target="tpu_custom_call" | custom-call | flops 536870912 | bytes 2097152 | tf_op jit(solution)/shard_map/pallas_call | solution.py:24
  15.6 1.8 %shard_map.66 = bf16[512,2048]{1,0:T(8,128)(2,1)S(1)} custom-call(s32[2]{0:T(128)S(1)} %pad_add_fusion.flags, bf16[512,2048]{1,0:T(8,128)(2,1)S(1)} %copy-done.8), custom_call_target="tpu_custom_call" | custom-call | flops 1073741824 | bytes 4194304 | tf_op jit(solution)/shard_map/pallas_call | solution.py:24
  17.4 1.7 %fusion.6 = (bf16[512,512]{1,0:T(8,128)(2,1)}, bf16[512,512]{1,0:T(8,128)(2,1)}, bf16[512,512]{1,0:T(8,128)(2,1)}, bf16[512,512]{1,0:T(8,128)(2,1)S(1)}, bf16[51...) fusion(bf16[512,2048]{1,0:T(8,128)(2,1)S(1)} %shard_map.66, ...), kind=kLoop, calls=%fused_computation.33 | loop fusion | bytes 8388608 | tf_op jit(solution)/shard_map/slice | solution.py:189
  27.8 1.6 %collective-permute-start.14 = (s16[272,512]{1,0:T(8,128)(2,1)S(1)}, s16[272,512]{1,0:T(8,128)(2,1)S(1)}, u32[]{:S(2)}, u32[]{:S(2)}) collective-permute-start(s16[272,512]{1,0:T(8,128)(2,1)S(1)} %shard_map.85), channel_id=1, source_target_pairs={{0,2},{1,3},{2,4},{3,5},{4,6},{5,7},{6,0},{7,1},{8,10},{9,11},{10,... | collective-permute-start | bytes 835592 | tf_op jit(solution)/shard_map/ppermute | solution.py:158
  30.9 1.6 %collective-permute-start.10 = (s16[272,512]{1,0:T(8,128)(2,1)S(1)}, s16[272,512]{1,0:T(8,128)(2,1)S(1)}, u32[]{:S(2)}, u32[]{:S(2)}) collective-permute-start(s16[272,512]{1,0:T(8,128)(2,1)S(1)} %shard_map.79), channel_id=1, source_target_pairs={{0,2},{1,3},{2,4},{3,5},{4,6},{5,7},{6,0},{7,1},{8,10},{9,11},{10,... | collective-permute-start | bytes 835592 | tf_op jit(solution)/shard_map/ppermute | solution.py:158
  34.1 1.6 %collective-permute-start.6 = (s16[272,512]{1,0:T(8,128)(2,1)S(1)}, s16[272,512]{1,0:T(8,128)(2,1)S(1)}, u32[]{:S(2)}, u32[]{:S(2)}) collective-permute-start(s16[272,512]{1,0:T(8,128)(2,1)S(1)} %shard_map.73), channel_id=1, source_target_pairs={{0,2},{1,3},{2,4},{3,5},{4,6},{5,7},{6,0},{7,1},{8,10},{9,11},{10,... | collective-permute-start | bytes 835592 | tf_op jit(solution)/shard_map/ppermute | solution.py:158
  40.7 1.6 %collective-permute-start.15 = (s16[272,512]{1,0:T(8,128)(2,1)S(1)}, s16[272,512]{1,0:T(8,128)(2,1)S(1)}, u32[]{:S(2)}, u32[]{:S(2)}) collective-permute-start(s16[272,512]{1,0:T(8,128)(2,1)S(1)} %shard_map.86), channel_id=1, source_target_pairs={{0,1},{1,0},{2,3},{3,2},{4,5},{5,4},{6,7},{7,6},{8,9},{9,8},{10,11... | collective-permute-start | bytes 835592 | tf_op jit(solution)/shard_map/ppermute | solution.py:153
  42.3 2.9 %collective-permute-done.10.arrived = s16[272,512]{1,0:T(8,128)(2,1)S(1)} collective-permute-done((s16[272,512]{1,0:T(8,128)(2,1)S(1)}, s16[272,512]{1,0:T(8,128)(2,1)S(1)}, u32[]{:S(2)}, u32[]{:S(2)}) %collective-permute-start.10) | collective-permute-done | bytes 278560 | tf_op jit(solution)/shard_map/ppermute | solution.py:158
  46.7 1.6 %collective-permute-start.11 = (s16[272,512]{1,0:T(8,128)(2,1)S(1)}, s16[272,512]{1,0:T(8,128)(2,1)S(1)}, u32[]{:S(2)}, u32[]{:S(2)}) collective-permute-start(s16[272,512]{1,0:T(8,128)(2,1)S(1)} %shard_map.80), channel_id=1, source_target_pairs={{0,1},{1,0},{2,3},{3,2},{4,5},{5,4},{6,7},{7,6},{8,9},{9,8},{10,11... | collective-permute-start | bytes 835592 | tf_op jit(solution)/shard_map/ppermute | solution.py:153
  48.3 2.9 %collective-permute-done.6.arrived = s16[272,512]{1,0:T(8,128)(2,1)S(1)} collective-permute-done((s16[272,512]{1,0:T(8,128)(2,1)S(1)}, s16[272,512]{1,0:T(8,128)(2,1)S(1)}, u32[]{:S(2)}, u32[]{:S(2)}) %collective-permute-start.6) | collective-permute-done | bytes 278560 | tf_op jit(solution)/shard_map/ppermute | solution.py:158
  52.7 1.6 %collective-permute-start.7 = (s16[272,512]{1,0:T(8,128)(2,1)S(1)}, s16[272,512]{1,0:T(8,128)(2,1)S(1)}, u32[]{:S(2)}, u32[]{:S(2)}) collective-permute-start(s16[272,512]{1,0:T(8,128)(2,1)S(1)} %shard_map.74), channel_id=1, source_target_pairs={{0,1},{1,0},{2,3},{3,2},{4,5},{5,4},{6,7},{7,6},{8,9},{9,8},{10,11... | collective-permute-start | bytes 835592 | tf_op jit(solution)/shard_map/ppermute | solution.py:153
  56.4 1.6 %collective-permute-start.2 = (s16[272,512]{1,0:T(8,128)(2,1)S(1)}, s16[272,512]{1,0:T(8,128)(2,1)S(1)}, u32[]{:S(2)}, u32[]{:S(2)}) collective-permute-start(s16[272,512]{1,0:T(8,128)(2,1)S(1)} %shard_map.68), channel_id=1, source_target_pairs={{0,1},{1,0},{2,3},{3,2},{4,5},{5,4},{6,7},{7,6},{8,9},{9,8},{10,11... | collective-permute-start | bytes 835592 | tf_op jit(solution)/shard_map/ppermute | solution.py:153
  58.0 2.2 %shard_map.87 = s16[272,512]{1,0:T(8,128)(2,1)} custom-call(s32[2]{0:T(128)S(1)} %pad_add_fusion.flags, bf16[256,512]{1,0:T(8,128)(2,1)S(1)} %copy-done.16, bf16[256,512]{1,0:T(8,128)(2,1)} %collective-permute-done.13.other, bf16[512,512]{1,0:T(8,128)(2,1)S(1)} %copy-done.3, bf16[512,512]{1,0:T(8,128)(2,1)S(1)} %copy-done.2, ...), custom_call_target="tpu_custom_call" | custom-call | flops 268435456 | bytes 1835008 | tf_op jit(solution)/shard_map/pallas_call | solution.py:24
  60.2 2.2 %shard_map.81 = s16[272,512]{1,0:T(8,128)(2,1)} custom-call(s32[2]{0:T(128)S(1)} %pad_add_fusion.flags, bf16[256,512]{1,0:T(8,128)(2,1)S(1)} %copy-done.12, bf16[256,512]{1,0:T(8,128)(2,1)} %collective-permute-done.9.other, bf16[512,512]{1,0:T(8,128)(2,1)S(1)} %copy-done.3, bf16[512,512]{1,0:T(8,128)(2,1)S(1)} %copy-done.2, ...), custom_call_target="tpu_custom_call" | custom-call | flops 268435456 | bytes 1835008 | tf_op jit(solution)/shard_map/pallas_call | solution.py:24
  63.7 2.2 %shard_map.75 = s16[272,512]{1,0:T(8,128)(2,1)} custom-call(s32[2]{0:T(128)S(1)} %pad_add_fusion.flags, bf16[256,512]{1,0:T(8,128)(2,1)S(1)} %copy-done.10, bf16[256,512]{1,0:T(8,128)(2,1)} %collective-permute-done.5.other, bf16[512,512]{1,0:T(8,128)(2,1)S(1)} %copy-done.3, bf16[512,512]{1,0:T(8,128)(2,1)S(1)} %copy-done.2, ...), custom_call_target="tpu_custom_call" | custom-call | flops 268435456 | bytes 1835008 | tf_op jit(solution)/shard_map/pallas_call | solution.py:24
  65.9 1.6 %collective-permute-start.8 = (s16[272,512]{1,0:T(8,128)(2,1)}, s16[272,512]{1,0:T(8,128)(2,1)}, u32[]{:S(2)}, u32[]{:S(2)}) collective-permute-start(s16[272,512]{1,0:T(8,128)(2,1)} %shard_map.75), channel_id=1, source_target_pairs={{0,2},{1,3},{2,4},{3,5},{4,6},{5,7},{6,0},{7,1},{8,10},{9,11},{10,... | collective-permute-start | bytes 835592 | tf_op jit(solution)/shard_map/ppermute | solution.py:158
  67.4 2.2 %shard_map.69 = s16[272,512]{1,0:T(8,128)(2,1)} custom-call(s32[2]{0:T(128)S(1)} %pad_add_fusion.flags, bf16[256,512]{1,0:T(8,128)(2,1)S(1)} %shard_map.64.own, bf16[256,512]{1,0:T(8,128)(2,1)} %collective-permute-done.other, bf16[512,512]{1,0:T(8,128)(2,1)S(1)} %copy-done.3, bf16[512,512]{1,0:T(8,128)(2,1)S(1)} %copy-done.2, ...), custom_call_target="tpu_custom_call" | custom-call | flops 268435456 | bytes 1835008 | tf_op jit(solution)/shard_map/pallas_call | solution.py:24
  69.6 2.1 %collective-permute-start.3 = (s16[272,512]{1,0:T(8,128)(2,1)}, s16[272,512]{1,0:T(8,128)(2,1)}, u32[]{:S(2)}, u32[]{:S(2)}) collective-permute-start(s16[272,512]{1,0:T(8,128)(2,1)} %shard_map.69), channel_id=1, source_target_pairs={{0,2},{1,3},{2,4},{3,5},{4,6},{5,7},{6,0},{7,1},{8,10},{9,11},{10,... | collective-permute-start | bytes 835592 | tf_op jit(solution)/shard_map/ppermute | solution.py:158
  74.6 2.3 %shard_map.88.refs_3_ = bf16[256,512]{1,0:T(8,128)(2,1)} custom-call(s32[2]{0:T(128)S(1)} %pad_add_fusion.flags, bf16[256,512]{1,0:T(8,128)(2,1)S(1)} %copy-done.16, bf16[256,512]{1,0:T(8,128)(2,1)} %collective-permute-done.13.other, bf16[512,512]{1,0:T(8,128)(2,1)S(1)} %get-tuple-element.24.direct, bf16[512,512]{1,0:T(8,128)(2,1)S(1)} %get-tuple-element.12.swapped, ...), custom_call_target="tpu_custom_call" | custom-call | flops 268435456 | bytes 1835008 | tf_op jit(solution)/shard_map/pallas_call | solution.py:24
  77.8 1.6 %shard_map.82.refs_2_ = bf16[256,512]{1,0:T(8,128)(2,1)S(1)} custom-call(s32[2]{0:T(128)S(1)} %pad_add_fusion.flags, bf16[256,512]{1,0:T(8,128)(2,1)S(1)} %copy-done.13, bf16[256,512]{1,0:T(8,128)(2,1)} %collective-permute-done.9.other, bf16[512,512]{1,0:T(8,128)(2,1)S(1)} %get-tuple-element.24.direct, bf16[512,512]{1,0:T(8,128)(2,1)S(1)} %get-tuple-element.12.swapped, ...), custom_call_target="tpu_custom_call" | custom-call | flops 268435456 | bytes 1835008 | tf_op jit(solution)/shard_map/pallas_call | solution.py:24
  80.5 2.9 %collective-permute-done.8.arrived = s16[272,512]{1,0:T(8,128)(2,1)} collective-permute-done((s16[272,512]{1,0:T(8,128)(2,1)}, s16[272,512]{1,0:T(8,128)(2,1)}, u32[]{:S(2)}, u32[]{:S(2)}) %collective-permute-start.8) | collective-permute-done | bytes 278560 | tf_op jit(solution)/shard_map/ppermute | solution.py:158
  83.3 1.6 %shard_map.76.refs_1_ = bf16[256,512]{1,0:T(8,128)(2,1)S(1)} custom-call(s32[2]{0:T(128)S(1)} %pad_add_fusion.flags, bf16[256,512]{1,0:T(8,128)(2,1)S(1)} %copy-done.10, bf16[256,512]{1,0:T(8,128)(2,1)} %collective-permute-done.5.other, bf16[512,512]{1,0:T(8,128)(2,1)S(1)} %get-tuple-element.24.direct, bf16[512,512]{1,0:T(8,128)(2,1)S(1)} %get-tuple-element.12.swapped, ...), custom_call_target="tpu_custom_call" | custom-call | flops 268435456 | bytes 1835008 | tf_op jit(solution)/shard_map/pallas_call | solution.py:24
  86.3 1.6 %shard_map.70.refs_0_ = bf16[256,512]{1,0:T(8,128)(2,1)S(1)} custom-call(s32[2]{0:T(128)S(1)} %pad_add_fusion.flags, bf16[256,512]{1,0:T(8,128)(2,1)S(1)} %shard_map.64.own, bf16[256,512]{1,0:T(8,128)(2,1)} %collective-permute-done.other, bf16[512,512]{1,0:T(8,128)(2,1)S(1)} %get-tuple-element.24.direct, bf16[512,512]{1,0:T(8,128)(2,1)S(1)} %get-tuple-element.12.swapped, ...), custom_call_target="tpu_custom_call" | custom-call | flops 268435456 | bytes 1835008 | tf_op jit(solution)/shard_map/pallas_call | solution.py:24
  89.0 3.0 %collective-permute-done.19.refs_6_ = bf16[256,512]{1,0:T(8,128)(2,1)} collective-permute-done((bf16[256,512]{1,0:T(8,128)(2,1)S(1)}, bf16[256,512]{1,0:T(8,128)(2,1)}, u32[]{:S(2)}, u32[]{:S(2)}) %collective-permute-start.19) | collective-permute-done | bytes 262176 | tf_op jit(solution)/shard_map/ppermute | solution.py:149
  92.0 3.9 %collective-permute-done.18.refs_5_ = bf16[256,512]{1,0:T(8,128)(2,1)} collective-permute-done((bf16[256,512]{1,0:T(8,128)(2,1)S(1)}, bf16[256,512]{1,0:T(8,128)(2,1)}, u32[]{:S(2)}, u32[]{:S(2)}) %collective-permute-start.18) | collective-permute-done | bytes 262176 | tf_op jit(solution)/shard_map/ppermute | solution.py:149
  95.8 2.7 %collective-permute-done.17.refs_4_ = bf16[256,512]{1,0:T(8,128)(2,1)S(1)} collective-permute-done((bf16[256,512]{1,0:T(8,128)(2,1)S(1)}, bf16[256,512]{1,0:T(8,128)(2,1)S(1)}, u32[]{:S(2)}, u32[]{:S(2)}) %collective-permute-start.17) | collective-permute-done | bytes 262176 | tf_op jit(solution)/shard_map/ppermute | solution.py:149
  98.5 9.2 %shard_map.89 = bf16[2048,512]{1,0:T(8,128)(2,1)} custom-call(s32[2]{0:T(128)S(1)} %pad_add_fusion.flags, s32[2048,1]{1,0:T(8,128)S(1)} %copy.16.slots, bf16[256,512]{1,0:T(8,128)(2,1)S(1)} %shard_map.70.refs_0_, bf16[256,512]{1,0:T(8,128)(2,1)S(1)} %shard_map.76.refs_1_, bf16[256,512]{1,0:T(8,128)(2,1)S(1)} %shard_map.82.refs_2_, ...), custom_call_target="tpu_custom_call" | custom-call | flops 4294967296 | bytes 4194304 | tf_op jit(solution)/shard_map/pallas_call | solution.py:24
  (97 shorter events, 34.4 us)
Async XLA Ops:
  0.0 4.4 %copy-start.20 = (f32[200]{0:T(256)S(1)}, f32[200]{0:T(256)}, u32[]{:S(2)}) copy-start(f32[200]{0:T(256)} %param.10) | copy-start | bytes 2404
  4.4 20.9 %collective-permute-start.13 = (bf16[256,512]{1,0:T(8,128)(2,1)}, bf16[256,512]{1,0:T(8,128)(2,1)}, u32[]{:S(2)}, u32[]{:S(2)}) collective-permute-start(bf16[256,512]{1,0:T(8,128)(2,1)} %shard_map.84), channel_id=1, source_target_pairs={{0,16},{8,24},{16,0},{24,8},{1,17},{9,25},{17,1},{25,9},{2,18},{10... | collective-permute-start | bytes 786440 | tf_op jit(solution)/shard_map/ppermute | solution.py:149
  5.0 53.0 %collective-permute-start.4 = (f32[1024]{0:T(1024)S(1)}, f32[1024]{0:T(1024)S(1)}, u32[]{:S(2)}, u32[]{:S(2)}) collective-permute-start(f32[1024]{0:T(1024)S(1)} %slice.77), channel_id=1, source_target_pairs={{0,16},{8,24},{16,0},{24,8},{1,17},{9,25},{17,1},{25,9},{2,18},{10... | collective-permute-start | bytes 12296 | tf_op jit(solution)/shard_map/ppermute | solution.py:149
  9.0 20.4 %collective-permute-start.9 = (bf16[256,512]{1,0:T(8,128)(2,1)}, bf16[256,512]{1,0:T(8,128)(2,1)}, u32[]{:S(2)}, u32[]{:S(2)}) collective-permute-start(bf16[256,512]{1,0:T(8,128)(2,1)} %shard_map.78), channel_id=1, source_target_pairs={{0,16},{8,24},{16,0},{24,8},{1,17},{9,25},{17,1},{25,9},{2,18},{10... | collective-permute-start | bytes 786440 | tf_op jit(solution)/shard_map/ppermute | solution.py:149
  11.0 4.6 %copy-start.8 = (bf16[512,2048]{1,0:T(8,128)(2,1)S(1)}, bf16[512,2048]{1,0:T(8,128)(2,1)}, u32[]{:S(2)}) copy-start(bf16[512,2048]{1,0:T(8,128)(2,1)} %integrals.1) | copy-start | bytes 6291460
  11.0 21.6 %collective-permute-start.5 = (bf16[256,512]{1,0:T(8,128)(2,1)}, bf16[256,512]{1,0:T(8,128)(2,1)}, u32[]{:S(2)}, u32[]{:S(2)}) collective-permute-start(bf16[256,512]{1,0:T(8,128)(2,1)} %shard_map.72), channel_id=1, source_target_pairs={{0,16},{8,24},{16,0},{24,8},{1,17},{9,25},{17,1},{25,9},{2,18},{10... | collective-permute-start | bytes 786440 | tf_op jit(solution)/shard_map/ppermute | solution.py:149
  14.3 21.4 %collective-permute-start = (bf16[256,512]{1,0:T(8,128)(2,1)}, bf16[256,512]{1,0:T(8,128)(2,1)}, u32[]{:S(2)}, u32[]{:S(2)}) collective-permute-start(bf16[256,512]{1,0:T(8,128)(2,1)} %shard_map.65), channel_id=1, source_target_pairs={{0,16},{8,24},{16,0},{24,8},{1,17},{9,25},{17,1},{25,9},{2,18},{10... | collective-permute-start | bytes 786440 | tf_op jit(solution)/shard_map/ppermute | solution.py:149
  24.0 5.4 %copy-start.12 = (bf16[256,512]{1,0:T(8,128)(2,1)S(1)}, bf16[256,512]{1,0:T(8,128)(2,1)}, u32[]{:S(2)}) copy-start(bf16[256,512]{1,0:T(8,128)(2,1)} %copy-done.11) | copy-start | bytes 786436
  25.3 7.3 %copy-start.10 = (bf16[256,512]{1,0:T(8,128)(2,1)S(1)}, bf16[256,512]{1,0:T(8,128)(2,1)}, u32[]{:S(2)}) copy-start(bf16[256,512]{1,0:T(8,128)(2,1)} %copy-done.9) | copy-start | bytes 786436
  27.8 11.4 %collective-permute-start.14 = (s16[272,512]{1,0:T(8,128)(2,1)S(1)}, s16[272,512]{1,0:T(8,128)(2,1)S(1)}, u32[]{:S(2)}, u32[]{:S(2)}) collective-permute-start(s16[272,512]{1,0:T(8,128)(2,1)S(1)} %shard_map.85), channel_id=1, source_target_pairs={{0,2},{1,3},{2,4},{3,5},{4,6},{5,7},{6,0},{7,1},{8,10},{9,11},{10,... | collective-permute-start | bytes 835592 | tf_op jit(solution)/shard_map/ppermute | solution.py:158
  30.9 6.6 %copy-start.21 = (f32[2000]{0:T(1024)S(1)}, f32[2000]{0:T(1024)}, u32[]{:S(2)}) copy-start(f32[2000]{0:T(1024)} %param.11) | copy-start | bytes 24004
  30.9 8.3 %copy-start.4 = (bf16[512,512]{1,0:T(8,128)(2,1)S(1)}, bf16[512,512]{1,0:T(8,128)(2,1)}, u32[]{:S(2)}) copy-start(bf16[512,512]{1,0:T(8,128)(2,1)} %get-tuple-element.11.swapped) | copy-start | bytes 1572868
  30.9 8.3 %copy-start.5 = (bf16[512,512]{1,0:T(8,128)(2,1)S(1)}, bf16[512,512]{1,0:T(8,128)(2,1)}, u32[]{:S(2)}) copy-start(bf16[512,512]{1,0:T(8,128)(2,1)} %get-tuple-element.25.direct) | copy-start | bytes 1572868
  30.9 8.3 %copy-start.16 = (bf16[256,512]{1,0:T(8,128)(2,1)S(1)}, bf16[256,512]{1,0:T(8,128)(2,1)}, u32[]{:S(2)}) copy-start(bf16[256,512]{1,0:T(8,128)(2,1)} %copy-done.14) | copy-start | bytes 786436
  30.9 14.3 %collective-permute-start.10 = (s16[272,512]{1,0:T(8,128)(2,1)S(1)}, s16[272,512]{1,0:T(8,128)(2,1)S(1)}, u32[]{:S(2)}, u32[]{:S(2)}) collective-permute-start(s16[272,512]{1,0:T(8,128)(2,1)S(1)} %shard_map.79), channel_id=1, source_target_pairs={{0,2},{1,3},{2,4},{3,5},{4,6},{5,7},{6,0},{7,1},{8,10},{9,11},{10,... | collective-permute-start | bytes 835592 | tf_op jit(solution)/shard_map/ppermute | solution.py:158
  34.1 17.1 %collective-permute-start.6 = (s16[272,512]{1,0:T(8,128)(2,1)S(1)}, s16[272,512]{1,0:T(8,128)(2,1)S(1)}, u32[]{:S(2)}, u32[]{:S(2)}) collective-permute-start(s16[272,512]{1,0:T(8,128)(2,1)S(1)} %shard_map.73), channel_id=1, source_target_pairs={{0,2},{1,3},{2,4},{3,5},{4,6},{5,7},{6,0},{7,1},{8,10},{9,11},{10,... | collective-permute-start | bytes 835592 | tf_op jit(solution)/shard_map/ppermute | solution.py:158
  37.2 17.7 %collective-permute-start.1 = (s16[272,512]{1,0:T(8,128)(2,1)S(1)}, s16[272,512]{1,0:T(8,128)(2,1)S(1)}, u32[]{:S(2)}, u32[]{:S(2)}) collective-permute-start(s16[272,512]{1,0:T(8,128)(2,1)S(1)} %shard_map.67), channel_id=1, source_target_pairs={{0,2},{1,3},{2,4},{3,5},{4,6},{5,7},{6,0},{7,1},{8,10},{9,11},{10,... | collective-permute-start | bytes 835592 | tf_op jit(solution)/shard_map/ppermute | solution.py:158
  40.7 17.2 %collective-permute-start.15 = (s16[272,512]{1,0:T(8,128)(2,1)S(1)}, s16[272,512]{1,0:T(8,128)(2,1)S(1)}, u32[]{:S(2)}, u32[]{:S(2)}) collective-permute-start(s16[272,512]{1,0:T(8,128)(2,1)S(1)} %shard_map.86), channel_id=1, source_target_pairs={{0,1},{1,0},{2,3},{3,2},{4,5},{5,4},{6,7},{7,6},{8,9},{9,8},{10,11... | collective-permute-start | bytes 835592 | tf_op jit(solution)/shard_map/ppermute | solution.py:153
  46.7 11.3 %copy-start.2 = (bf16[512,512]{1,0:T(8,128)(2,1)S(1)}, bf16[512,512]{1,0:T(8,128)(2,1)}, u32[]{:S(2)}) copy-start(bf16[512,512]{1,0:T(8,128)(2,1)} %get-tuple-element.9.swapped) | copy-start | bytes 1572868
  46.7 11.3 %copy-start.3 = (bf16[512,512]{1,0:T(8,128)(2,1)S(1)}, bf16[512,512]{1,0:T(8,128)(2,1)}, u32[]{:S(2)}) copy-start(bf16[512,512]{1,0:T(8,128)(2,1)} %get-tuple-element.26.direct) | copy-start | bytes 1572868
  46.7 13.5 %collective-permute-start.11 = (s16[272,512]{1,0:T(8,128)(2,1)S(1)}, s16[272,512]{1,0:T(8,128)(2,1)S(1)}, u32[]{:S(2)}, u32[]{:S(2)}) collective-permute-start(s16[272,512]{1,0:T(8,128)(2,1)S(1)} %shard_map.80), channel_id=1, source_target_pairs={{0,1},{1,0},{2,3},{3,2},{4,5},{5,4},{6,7},{7,6},{8,9},{9,8},{10,11... | collective-permute-start | bytes 835592 | tf_op jit(solution)/shard_map/ppermute | solution.py:153
  52.7 11.0 %collective-permute-start.7 = (s16[272,512]{1,0:T(8,128)(2,1)S(1)}, s16[272,512]{1,0:T(8,128)(2,1)S(1)}, u32[]{:S(2)}, u32[]{:S(2)}) collective-permute-start(s16[272,512]{1,0:T(8,128)(2,1)S(1)} %shard_map.74), channel_id=1, source_target_pairs={{0,1},{1,0},{2,3},{3,2},{4,5},{5,4},{6,7},{7,6},{8,9},{9,8},{10,11... | collective-permute-start | bytes 835592 | tf_op jit(solution)/shard_map/ppermute | solution.py:153
  56.4 11.1 %collective-permute-start.2 = (s16[272,512]{1,0:T(8,128)(2,1)S(1)}, s16[272,512]{1,0:T(8,128)(2,1)S(1)}, u32[]{:S(2)}, u32[]{:S(2)}) collective-permute-start(s16[272,512]{1,0:T(8,128)(2,1)S(1)} %shard_map.68), channel_id=1, source_target_pairs={{0,1},{1,0},{2,3},{3,2},{4,5},{5,4},{6,7},{7,6},{8,9},{9,8},{10,11... | collective-permute-start | bytes 835592 | tf_op jit(solution)/shard_map/ppermute | solution.py:153
  60.2 13.4 %collective-permute-start.16 = (s16[272,512]{1,0:T(8,128)(2,1)}, s16[272,512]{1,0:T(8,128)(2,1)}, u32[]{:S(2)}, u32[]{:S(2)}) collective-permute-start(s16[272,512]{1,0:T(8,128)(2,1)} %shard_map.87), channel_id=1, source_target_pairs={{0,2},{1,3},{2,4},{3,5},{4,6},{5,7},{6,0},{7,1},{8,10},{9,11},{10,... | collective-permute-start | bytes 835592 | tf_op jit(solution)/shard_map/ppermute | solution.py:158
  62.4 15.5 %collective-permute-start.12 = (s16[272,512]{1,0:T(8,128)(2,1)}, s16[272,512]{1,0:T(8,128)(2,1)}, u32[]{:S(2)}, u32[]{:S(2)}) collective-permute-start(s16[272,512]{1,0:T(8,128)(2,1)} %shard_map.81), channel_id=1, source_target_pairs={{0,2},{1,3},{2,4},{3,5},{4,6},{5,7},{6,0},{7,1},{8,10},{9,11},{10,... | collective-permute-start | bytes 835592 | tf_op jit(solution)/shard_map/ppermute | solution.py:158
  65.9 12.0 %copy-start.13 = (bf16[256,512]{1,0:T(8,128)(2,1)S(1)}, bf16[256,512]{1,0:T(8,128)(2,1)}, u32[]{:S(2)}) copy-start(bf16[256,512]{1,0:T(8,128)(2,1)} %copy-done.11) | copy-start | bytes 786436
  65.9 17.5 %collective-permute-start.8 = (s16[272,512]{1,0:T(8,128)(2,1)}, s16[272,512]{1,0:T(8,128)(2,1)}, u32[]{:S(2)}, u32[]{:S(2)}) collective-permute-start(s16[272,512]{1,0:T(8,128)(2,1)} %shard_map.75), channel_id=1, source_target_pairs={{0,2},{1,3},{2,4},{3,5},{4,6},{5,7},{6,0},{7,1},{8,10},{9,11},{10,... | collective-permute-start | bytes 835592 | tf_op jit(solution)/shard_map/ppermute | solution.py:158
  69.6 16.7 %collective-permute-start.3 = (s16[272,512]{1,0:T(8,128)(2,1)}, s16[272,512]{1,0:T(8,128)(2,1)}, u32[]{:S(2)}, u32[]{:S(2)}) collective-permute-start(s16[272,512]{1,0:T(8,128)(2,1)} %shard_map.69), channel_id=1, source_target_pairs={{0,2},{1,3},{2,4},{3,5},{4,6},{5,7},{6,0},{7,1},{8,10},{9,11},{10,... | collective-permute-start | bytes 835592 | tf_op jit(solution)/shard_map/ppermute | solution.py:158
  76.8 12.2 %collective-permute-start.20 = (bf16[256,512]{1,0:T(8,128)(2,1)}, bf16[256,512]{1,0:T(8,128)(2,1)}, u32[]{:S(2)}, u32[]{:S(2)}) collective-permute-start(bf16[256,512]{1,0:T(8,128)(2,1)} %shard_map.88.refs_3_), channel_id=1, source_target_pairs={{0,16},{8,24},{16,0},{24,8},{1,17},{9,25},{17,1},{25,9},{2,18},{10... | collective-permute-start | bytes 786440 | tf_op jit(solution)/shard_map/ppermute | solution.py:149
  79.4 12.6 %collective-permute-start.19 = (bf16[256,512]{1,0:T(8,128)(2,1)S(1)}, bf16[256,512]{1,0:T(8,128)(2,1)}, u32[]{:S(2)}, u32[]{:S(2)}) collective-permute-start(bf16[256,512]{1,0:T(8,128)(2,1)S(1)} %shard_map.82.refs_2_), channel_id=1, source_target_pairs={{0,16},{8,24},{16,0},{24,8},{1,17},{9,25},{17,1},{25,9},{2,18},{10... | collective-permute-start | bytes 786440 | tf_op jit(solution)/shard_map/ppermute | solution.py:149
  84.9 10.9 %collective-permute-start.18 = (bf16[256,512]{1,0:T(8,128)(2,1)S(1)}, bf16[256,512]{1,0:T(8,128)(2,1)}, u32[]{:S(2)}, u32[]{:S(2)}) collective-permute-start(bf16[256,512]{1,0:T(8,128)(2,1)S(1)} %shard_map.76.refs_1_), channel_id=1, source_target_pairs={{0,16},{8,24},{16,0},{24,8},{1,17},{9,25},{17,1},{25,9},{2,18},{10... | collective-permute-start | bytes 786440 | tf_op jit(solution)/shard_map/ppermute | solution.py:149
  87.9 10.7 %collective-permute-start.17 = (bf16[256,512]{1,0:T(8,128)(2,1)S(1)}, bf16[256,512]{1,0:T(8,128)(2,1)S(1)}, u32[]{:S(2)}, u32[]{:S(2)}) collective-permute-start(bf16[256,512]{1,0:T(8,128)(2,1)S(1)} %shard_map.70.refs_0_), channel_id=1, source_target_pairs={{0,16},{8,24},{16,0},{24,8},{1,17},{9,25},{17,1},{25,9},{2,18},{10... | collective-permute-start | bytes 786440 | tf_op jit(solution)/shard_map/ppermute | solution.py:149
  (11 other events, 20.7 us)

commit v2 on v1

v2 whole, which is shorter than its diff:
```python
import functools

import jax
import jax.numpy as jnp
from jax import lax
from jax.experimental import pallas as pl
from jax.experimental.pallas import tpu as pltpu
from jax.sharding import PartitionSpec as P

NOCC = 200
NV = 2000
CHUNKS = 4
SCALE_ROWS = 16
TOP = 32767.0
STEPS = 64.0
TINY = 1e-33
VMEM_LIMIT = 16 * 1024 * 1024

VMEM = pl.BlockSpec(memory_space=pltpu.VMEM)
SMEM = pl.BlockSpec(memory_space=pltpu.SMEM)
ANY = pl.BlockSpec(memory_space=pl.ANY)


def call(body, out_shape, flops, moved, operands, after=()):
    count = len(operands)

    def kernel(*refs):
        body(*refs[:count], *refs[count + len(after) :])

    return pl.pallas_call(
        kernel,
        out_shape=out_shape,
        in_specs=[SMEM] + [VMEM] * (count - 1) + [ANY] * len(after),
        out_specs=jax.tree.map(lambda _: VMEM, out_shape),
        compiler_params=pltpu.CompilerParams(vmem_limit_bytes=VMEM_LIMIT),
        cost_estimate=pl.CostEstimate(flops=flops, bytes_accessed=moved, transcendentals=0),
    )(*operands, *after)


def swap_matrix(width):
    down = lax.broadcasted_iota(jnp.int32, (width, width), 0)
    across = lax.broadcasted_iota(jnp.int32, (width, width), 1)
    return jnp.where(down == (across ^ 1), 1.0, 0.0).astype(jnp.bfloat16)


def exact_dot(left, right):
    return jnp.dot(left, right, preferred_element_type=jnp.float32).astype(jnp.bfloat16)


def mirror_kernel(flags, integrals, out):
    width = integrals.shape[0]
    swap = swap_matrix(width)
    for stop in range(integrals.shape[1] // width):
        cols = pl.ds(stop * width, width)
        out[:, cols] = exact_dot(integrals[:, cols], swap)


def align_kernel(begin, send, flags, partner, amplitudes, *outs):
    rows = amplitudes.shape[0]
    chunk = outs[0].shape[0]
    upper = flags[0]
    side = 1 - upper if send else upper
    first = side * (rows // 2) + begin

    @pl.when(upper == 0)
    def _():
        for index, out in enumerate(outs):
            out[...] = amplitudes[pl.ds(pl.multiple_of(first + index * chunk, chunk), chunk), :]

    @pl.when(upper == 1)
    def _():
        for index, out in enumerate(outs):
            wanted = flags[2] + first + index * chunk + lax.broadcasted_iota(jnp.int32, (chunk, rows), 0)
            pick = jnp.where(partner[...] == wanted, 1.0, 0.0).astype(jnp.bfloat16)
            out[...] = exact_dot(pick, amplitudes[...])


def product(stop, own, other, integrals, mirrored):
    cols = pl.ds(stop * own.shape[1], own.shape[1])
    return jnp.dot(own[...], integrals[:, cols], preferred_element_type=jnp.float32) + jnp.dot(
        other[...], mirrored[:, cols], preferred_element_type=jnp.float32
    )


def code(values, out):
    rows = values.shape[0]
    top = jnp.max(jnp.abs(values), axis=0, keepdims=True)
    level = jnp.ceil(STEPS * jnp.log2(jnp.maximum(top, TINY) * (1.0001 / TOP)))
    coded = jnp.round(values * jnp.exp2(level * (-1.0 / STEPS)))
    out[pl.ds(0, rows), :] = coded.astype(jnp.int32).astype(jnp.int16)
    spread = jnp.broadcast_to(level.astype(jnp.int32), (SCALE_ROWS, values.shape[1]))
    out[pl.ds(rows, SCALE_ROWS), :] = spread.astype(jnp.int16)


def decode(coded):
    rows = coded.shape[0] - SCALE_ROWS
    level = coded[pl.ds(rows, SCALE_ROWS), :].astype(jnp.int32).astype(jnp.float32)[0:1, :]
    return coded[pl.ds(0, rows), :].astype(jnp.int32).astype(jnp.float32) * jnp.exp2(level * (1.0 / STEPS))


def first_kernel(flags, own, other, integrals, mirrored, out):
    code(product(3, own, other, integrals, mirrored), out)


def second_kernel(flags, own, other, integrals, mirrored, arrived, out):
    code(product(1, own, other, integrals, mirrored) + decode(arrived), out)


def third_kernel(flags, own, other, integrals, mirrored, crossed, out):
    here = jnp.where(flags[1] == 0, 1.0, 0.0)
    code(product(2, own, other, integrals, mirrored) + decode(crossed) * here, out)


def last_kernel(index, flags, own, other, integrals, mirrored, crossed, arrived, occ_sum, vir_sum, out):
    chunk, width = out.shape
    here = jnp.where(flags[1] == 1, 1.0, 0.0)
    total = product(0, own, other, integrals, mirrored) + decode(arrived) + decode(crossed) * here
    occ_rows = occ_sum[:, pl.ds(index * chunk, chunk)]
    occ_down = jnp.broadcast_to(occ_rows, (128, chunk)).T
    for lane in range(0, width, 128):
        denom = vir_sum[:, lane : lane + 128] - occ_down
        out[:, lane : lane + 128] = (total[:, lane : lane + 128] / denom).astype(jnp.bfloat16)


def place_kernel(index, flags, partner, own, other, *refs):
    out = refs[-1]
    rows, width = out.shape
    chunk = own.shape[0]
    upper = flags[0]
    here = upper * (rows // 2) + index * chunk
    there = (1 - upper) * (rows // 2) + index * chunk
    opposite = exact_dot(other[...], swap_matrix(width))

    @pl.when(upper == 0)
    def _():
        if index:
            out[...] = refs[0][...]
        out[pl.ds(pl.multiple_of(here, chunk), chunk), :] = own[...]
        out[pl.ds(pl.multiple_of(there, chunk), chunk), :] = opposite

    @pl.when(upper == 1)
    def _():
        block = 256
        lanes = lax.broadcasted_iota(jnp.int32, (block, chunk), 1) + flags[2]
        for begin in range(0, rows, block):
            part = pl.ds(begin, block)
            slots = partner[part, :]
            pick_here = jnp.where(slots == lanes + here, 1.0, 0.0).astype(jnp.bfloat16)
            pick_there = jnp.where(slots == lanes + there, 1.0, 0.0).astype(jnp.bfloat16)
            found = jnp.dot(pick_here, own[...], preferred_element_type=jnp.float32)
            found += jnp.dot(pick_there, opposite, preferred_element_type=jnp.float32)
            if index:
                found += refs[0][part, :].astype(jnp.float32)
            out[part, :] = found.astype(jnp.bfloat16)


def table_lookup(table, positions):
    slots = jnp.arange(table.shape[0], dtype=jnp.int32)
    return jnp.sum(jnp.where(positions[:, None] == slots[None, :], table[None, :], 0.0), axis=1)


def across_rows(value):
    count = lax.axis_size("row")
    return lax.ppermute(value, "row", [(i, i ^ (count // 2)) for i in range(count)])


def across_pair(value):
    return lax.ppermute(value, "col", [(i, i ^ 1) for i in range(lax.axis_size("col"))])


def two_along(value):
    count = lax.axis_size("col")
    return lax.ppermute(value, "col", [(i, (i + 2) % count) for i in range(count)])


def shards(amplitudes, integrals, pair_index, partner, occ_energy, vir_energy):
    rows, width = amplitudes.shape
    half = rows // 2
    chunk = half // CHUNKS
    row_count = lax.axis_size("row")
    row = lax.axis_index("row")
    upper = (row // (row_count // 2)).astype(jnp.int32)
    odd = (lax.axis_index("col") % 2).astype(jnp.int32)
    partner_base = ((row ^ (row_count // 2)) * rows).astype(jnp.int32)
    flags = jnp.stack([upper, odd, partner_base])

    chunk_shape = jax.ShapeDtypeStruct((chunk, width), jnp.bfloat16)
    coded_shape = jax.ShapeDtypeStruct((chunk + SCALE_ROWS, width), jnp.int16)
    whole_shape = jax.ShapeDtypeStruct((rows, width), jnp.bfloat16)

    def align(begin, count, send, after=()):
        return call(
            functools.partial(align_kernel, begin * chunk, send),
            [chunk_shape] * count,
            2 * count * chunk * rows * width,
            2 * rows * width,
            (flags, partner[None, :], amplitudes),
            after,
        )

    def stage(body, out_shape, *operands):
        return call(body, out_shape, 4 * chunk * width * width, 16 * chunk * width, (flags, *operands))

    sent = align(0, 1, True)
    mirrored = call(
        mirror_kernel,
        jax.ShapeDtypeStruct(integrals.shape, jnp.bfloat16),
        8 * width**3,
        4 * integrals.size,
        (flags, integrals),
        (sent[0],),
    )
    sent += align(1, 1, True, (mirrored,))
    own = align(0, CHUNKS, False, (sent[1],))
    sent += align(2, CHUNKS - 2, True, (own[0],))
    other = [across_rows(value) for value in sent]

    occ_sum = table_lookup(occ_energy, pair_index // NOCC) + table_lookup(occ_energy, pair_index % NOCC)
    occ_sum = jnp.where(upper == 0, occ_sum[:half], across_rows(occ_sum[half:]))[None, :]
    global_pair = lax.axis_index("col") * width + jnp.arange(width, dtype=jnp.int32)
    unordered = global_pair // 2
    vir_sum = table_lookup(vir_energy, unordered // NV) + table_lookup(vir_energy, unordered % NV)
    vir_sum = vir_sum[None, :]

    placed = ()
    for index in range(CHUNKS):
        inputs = (own[index], other[index], integrals, mirrored)
        moved = two_along(stage(first_kernel, coded_shape, *inputs))
        crossed = across_pair(stage(second_kernel, coded_shape, *inputs, moved))
        arrived = two_along(stage(third_kernel, coded_shape, *inputs, crossed))
        done = stage(
            functools.partial(last_kernel, index), chunk_shape, *inputs, crossed, arrived, occ_sum, vir_sum
        )
        placed = (
            call(
                functools.partial(place_kernel, index),
                whole_shape,
                4 * chunk * rows * width,
                4 * rows * width,
                (flags, partner[:, None], done, across_rows(done), *placed),
            ),
        )
    return placed[0]


def solution(mesh):
    in_specs = (P("row", "col"), P("col", None), P("row"), P("row"), P(), P())
    out_specs = P("row", "col")
    return jax.shard_map(shards, mesh=mesh, in_specs=in_specs, out_specs=out_specs, check_vma=False)
```

time: 109 us -> 106 us (0.972)
  Pallas kernels: 51.3 us -> 45.2 us
  starting transfers between devices: 21.9 us -> 24.8 us
  waiting for transfers between devices: 22 us -> 23.3 us
    ppermute x4, waiting for transfers between devices: 0.01 us -> 6.32 us  [across_pair(): lax.ppermute(value, 'col', [(i, i ^ 1) for i in range(lax.axis_size('col'...]
    pallas_call x26 -> x25, Pallas kernels: 51.3 us -> 45.2 us  [call(): pl.pallas_call(kernel, out_shape=out_shape, in_specs=[SMEM] + [VMEM] * (c...]
    ppermute x8, waiting for transfers between devices: 12.4 us -> 6.49 us  [two_along(): lax.ppermute(value, 'col', [(i, (i + 2) % count) for i in range(count)])]
    slice x7 -> x1, local copies, waits for them, and re-layouts: 3.57 us -> 0.01 us  [shards(): occ_sum[half:]]
    unnamed x44, local copies, waits for them, and re-layouts: 5.96 us -> 9.46 us
    ppermute x8, starting transfers between devices: 10.2 us -> 13 us  [two_along(): lax.ppermute(value, 'col', [(i, (i + 2) % count) for i in range(count)])]
    ppermute x9, starting transfers between devices: 5.32 us -> 7.56 us  [across_rows(): lax.ppermute(value, 'row', [(i, i ^ count // 2) for i in range(count)])]
    ppermute x4, starting transfers between devices: 6.34 us -> 4.31 us  [across_pair(): lax.ppermute(value, 'col', [(i, i ^ 1) for i in range(lax.axis_size('col'...]
  transfers between devices with their start and end apart: 21 -> 21, of which waited for: 10 -> 6; matrix products, arithmetic and copies ran while one was open for 5% -> 2% of each run, Pallas kernels for 37% -> 38%
where the time goes in v2:
time: 106 us; the launch traced here: 105 us
  Pallas kernels  45.2 us (43%)
  starting transfers between devices  24.8 us (23%)
  waiting for transfers between devices  23.3 us (22%)
  local copies, waits for them, and re-layouts  9.83 us (9%)
  other arithmetic  1.61 us (2%)
    pallas_call x25, Pallas kernels, call(): pl.pallas_call(kernel, out_shape=out_shape, in_specs=[SMEM] + [VMEM] * (c...  45.2 us
    ppermute x8, starting transfers between devices, two_along(): lax.ppermute(value, 'col', [(i, (i + 2) % count) for i in range(count)])  13 us
    ppermute x9, waiting for transfers between devices, across_rows(): lax.ppermute(value, 'row', [(i, i ^ count // 2) for i in range(count)])  10.4 us
    unnamed x44, local copies, waits for them, and re-layouts  9.46 us
    ppermute x9, starting transfers between devices, across_rows(): lax.ppermute(value, 'row', [(i, i ^ count // 2) for i in range(count)])  7.56 us
    ppermute x8, waiting for transfers between devices, two_along(): lax.ppermute(value, 'col', [(i, (i + 2) % count) for i in range(count)])  6.49 us
    ppermute x4, waiting for transfers between devices, across_pair(): lax.ppermute(value, 'col', [(i, i ^ 1) for i in range(lax.axis_size('col'...  6.32 us
    ppermute x4, starting transfers between devices, across_pair(): lax.ppermute(value, 'col', [(i, i ^ 1) for i in range(lax.axis_size('col'...  4.31 us
  transfers between devices with their start and end apart: 21, of which 6 were waited for; matrix products, arithmetic and copies ran while one was open for 2% of the time, Pallas kernels for 38%

profile of v2, /device:TPU:2, one launch (start us, length us, event | category | flops | bytes accessed | tf_op | source)
XLA Modules:
  0.0 105.1 jit_solution(17325627994637996419)
XLA Ops:
  0.1 1.7 %copy-done.3 = bf16[2048,512]{1,0:T(8,128)(2,1)S(1)} copy-done((bf16[2048,512]{1,0:T(8,128)(2,1)S(1)}, bf16[2048,512]{1,0:T(8,128)(2,1)}, u32[]{:S(2)}) %copy-start.3) | copy-done | bytes 2097176
  3.9 1.8 %shard_map.65.refs_3_.refs_4_ = bf16[512,2048]{1,0:T(8,128)(2,1)S(1)} custom-call(s32[3]{0:T(128)S(1)} %pad_add_fusion.refs_0_, bf16[512,2048]{1,0:T(8,128)(2,1)S(1)} %copy-done, bf16[256,512]{1,0:T(8,128)(2,1)S(1)} %shard_map.64.refs_2_), custom_call_target="tpu_custom_call" | custom-call | flops 1073741824 | bytes 4194304 | tf_op jit(solution)/shard_map/pallas_call | solution.py:30
  6.9 2.9 %shard_map.67 = (bf16[256,512]{1,0:T(8,128)(2,1)S(1)}, bf16[256,512]{1,0:T(8,128)(2,1)S(1)}, bf16[256,512]{1,0:T(8,128)(2,1)S(1)}, bf16[256,512]{1,0:T(8,128)(2,1)S(1)}) custom-call(s32[3]{0:T(128)S(1)} %pad_add_fusion.refs_0_, s32[1,2048]{1,0:T(1,128)S(1)} %bitcast.13, bf16[2048,512]{1,0:T(8,128)(2,1)S(1)} %copy-done.4, bf16[256,512]{1,0:T(8,128)(2,1)S(1)} %shard_map.66.refs_3_), custom_call_target="tpu_custom_call" | custom-call | flops 2147483648 | bytes 2097152 | tf_op jit(solution)/shard_map/pallas_call | solution.py:30
  9.8 1.8 %shard_map.68 = (bf16[256,512]{1,0:T(8,128)(2,1)S(1)}, bf16[256,512]{1,0:T(8,128)(2,1)S(1)}) custom-call(s32[3]{0:T(128)S(1)} %pad_add_fusion.refs_0_, s32[1,2048]{1,0:T(1,128)S(1)} %bitcast.14, bf16[2048,512]{1,0:T(8,128)(2,1)S(1)} %copy-done.4, bf16[256,512]{1,0:T(8,128)(2,1)S(1)} %get-tuple-element.12.refs_3_.refs_1_), custom_call_target="tpu_custom_call" | custom-call | flops 1073741824 | bytes 2097152 | tf_op jit(solution)/shard_map/pallas_call | solution.py:30
  11.7 2.0 %collective-permute-start.11 = (bf16[256,512]{1,0:T(8,128)(2,1)S(1)}, bf16[256,512]{1,0:T(8,128)(2,1)S(1)}, u32[]{:S(2)}, u32[]{:S(2)}) collective-permute-start(bf16[256,512]{1,0:T(8,128)(2,1)S(1)} %shard_map.66.refs_3_), channel_id=1, source_target_pairs={{0,16},{8,24},{16,0},{24,8},{1,17},{9,25},{17,1},{25,9},{2,18},{10... | collective-permute-start | bytes 786440 | tf_op jit(solution)/shard_map/ppermute | solution.py:164
  13.8 1.8 %shard_map.81 = s16[272,512]{1,0:T(8,128)(2,1)} custom-call(s32[3]{0:T(128)S(1)} %pad_add_fusion.refs_0_, bf16[256,512]{1,0:T(8,128)(2,1)S(1)} %get-tuple-element.12.refs_3_.refs_1_, bf16[256,512]{1,0:T(8,128)(2,1)S(1)} %collective-permute-done.16.refs_2_, bf16[512,2048]{1,0:T(8,128)(2,1)S(1)} %copy-done, bf16[512,2048]{1,0:T(8,128)(2,1)S(1)} %shard_map.65.refs_3_.refs_4_), custom_call_target="tpu_custom_call" | custom-call | flops 268435456 | bytes 2097152 | tf_op jit(solution)/shard_map/pallas_call | solution.py:30
  15.6 1.6 %collective-permute-start.17 = (s16[272,512]{1,0:T(8,128)(2,1)}, s16[272,512]{1,0:T(8,128)(2,1)}, u32[]{:S(2)}, u32[]{:S(2)}) collective-permute-start(s16[272,512]{1,0:T(8,128)(2,1)} %shard_map.81), channel_id=1, source_target_pairs={{0,2},{1,3},{2,4},{3,5},{4,6},{5,7},{6,0},{7,1},{8,10},{9,11},{10,... | collective-permute-start | bytes 835592 | tf_op jit(solution)/shard_map/ppermute | solution.py:173
  17.2 3.7 %collective-permute-done.refs_2_ = bf16[256,512]{1,0:T(8,128)(2,1)S(1)} collective-permute-done((bf16[256,512]{1,0:T(8,128)(2,1)S(1)}, bf16[256,512]{1,0:T(8,128)(2,1)S(1)}, u32[]{:S(2)}, u32[]{:S(2)}) %collective-permute-start) | collective-permute-done | bytes 262176 | tf_op jit(solution)/shard_map/ppermute | solution.py:164
  20.9 1.8 %shard_map.69 = s16[272,512]{1,0:T(8,128)(2,1)} custom-call(s32[3]{0:T(128)S(1)} %pad_add_fusion.refs_0_, bf16[256,512]{1,0:T(8,128)(2,1)S(1)} %get-tuple-element.11.refs_1_, bf16[256,512]{1,0:T(8,128)(2,1)S(1)} %collective-permute-done.refs_2_, bf16[512,2048]{1,0:T(8,128)(2,1)S(1)} %copy-done, bf16[512,2048]{1,0:T(8,128)(2,1)S(1)} %shard_map.65.refs_3_.refs_4_), custom_call_target="tpu_custom_call" | custom-call | flops 268435456 | bytes 2097152 | tf_op jit(solution)/shard_map/pallas_call | solution.py:30
  24.2 6.7 %collective-permute-done.6.refs_2_ = bf16[256,512]{1,0:T(8,128)(2,1)S(1)} collective-permute-done((bf16[256,512]{1,0:T(8,128)(2,1)S(1)}, bf16[256,512]{1,0:T(8,128)(2,1)S(1)}, u32[]{:S(2)}, u32[]{:S(2)}) %collective-permute-start.6) | collective-permute-done | bytes 262176 | tf_op jit(solution)/shard_map/ppermute | solution.py:164
  31.0 1.8 %shard_map.73 = s16[272,512]{1,0:T(8,128)(2,1)} custom-call(s32[3]{0:T(128)S(1)} %pad_add_fusion.refs_0_, bf16[256,512]{1,0:T(8,128)(2,1)S(1)} %get-tuple-element.14.refs_1_, bf16[256,512]{1,0:T(8,128)(2,1)S(1)} %collective-permute-done.6.refs_2_, bf16[512,2048]{1,0:T(8,128)(2,1)S(1)} %copy-done, bf16[512,2048]{1,0:T(8,128)(2,1)S(1)} %shard_map.65.refs_3_.refs_4_), custom_call_target="tpu_custom_call" | custom-call | flops 268435456 | bytes 2097152 | tf_op jit(solution)/shard_map/pallas_call | solution.py:30
  34.3 1.8 %shard_map.77 = s16[272,512]{1,0:T(8,128)(2,1)} custom-call(s32[3]{0:T(128)S(1)} %pad_add_fusion.refs_0_, bf16[256,512]{1,0:T(8,128)(2,1)S(1)} %get-tuple-element.16.refs_1_, bf16[256,512]{1,0:T(8,128)(2,1)S(1)} %collective-permute-done.11.refs_2_, bf16[512,2048]{1,0:T(8,128)(2,1)S(1)} %copy-done, bf16[512,2048]{1,0:T(8,128)(2,1)S(1)} %shard_map.65.refs_3_.refs_4_), custom_call_target="tpu_custom_call" | custom-call | flops 268435456 | bytes 2097152 | tf_op jit(solution)/shard_map/pallas_call | solution.py:30
  36.1 1.6 %collective-permute-start.12 = (s16[272,512]{1,0:T(8,128)(2,1)}, s16[272,512]{1,0:T(8,128)(2,1)}, u32[]{:S(2)}, u32[]{:S(2)}) collective-permute-start(s16[272,512]{1,0:T(8,128)(2,1)} %shard_map.77), channel_id=1, source_target_pairs={{0,2},{1,3},{2,4},{3,5},{4,6},{5,7},{6,0},{7,1},{8,10},{9,11},{10,... | collective-permute-start | bytes 835592 | tf_op jit(solution)/shard_map/ppermute | solution.py:173
  38.6 1.6 %copy-done.1 = bf16[512,2048]{1,0:T(8,128)(2,1)S(1)} copy-done((bf16[512,2048]{1,0:T(8,128)(2,1)S(1)}, bf16[512,2048]{1,0:T(8,128)(2,1)}, u32[]{:S(2)}) %copy-start.1) | copy-done | bytes 2097176
  43.6 1.6 %collective-permute-start.18 = (s16[272,512]{1,0:T(8,128)(2,1)S(1)}, s16[272,512]{1,0:T(8,128)(2,1)S(1)}, u32[]{:S(2)}, u32[]{:S(2)}) collective-permute-start(s16[272,512]{1,0:T(8,128)(2,1)S(1)} %shard_map.82), channel_id=1, source_target_pairs={{0,1},{1,0},{2,3},{3,2},{4,5},{5,4},{6,7},{7,6},{8,9},{9,8},{10,11... | collective-permute-start | bytes 835592 | tf_op jit(solution)/shard_map/ppermute | solution.py:168
  48.8 1.6 %collective-permute-start.8 = (s16[272,512]{1,0:T(8,128)(2,1)S(1)}, s16[272,512]{1,0:T(8,128)(2,1)S(1)}, u32[]{:S(2)}, u32[]{:S(2)}) collective-permute-start(s16[272,512]{1,0:T(8,128)(2,1)S(1)} %shard_map.74), channel_id=1, source_target_pairs={{0,1},{1,0},{2,3},{3,2},{4,5},{5,4},{6,7},{7,6},{8,9},{9,8},{10,11... | collective-permute-start | bytes 835592 | tf_op jit(solution)/shard_map/ppermute | solution.py:168
  54.5 1.6 %collective-permute-start.19 = (s16[272,512]{1,0:T(8,128)(2,1)S(1)}, s16[272,512]{1,0:T(8,128)(2,1)S(1)}, u32[]{:S(2)}, u32[]{:S(2)}) collective-permute-start(s16[272,512]{1,0:T(8,128)(2,1)S(1)} %shard_map.83), channel_id=1, source_target_pairs={{0,2},{1,3},{2,4},{3,5},{4,6},{5,7},{6,0},{7,1},{8,10},{9,11},{10,... | collective-permute-start | bytes 835592 | tf_op jit(solution)/shard_map/ppermute | solution.py:173
  56.1 3.1 %collective-permute-done.2.refs_5_ = s16[272,512]{1,0:T(8,128)(2,1)S(1)} collective-permute-done((s16[272,512]{1,0:T(8,128)(2,1)S(1)}, s16[272,512]{1,0:T(8,128)(2,1)S(1)}, u32[]{:S(2)}, u32[]{:S(2)}) %collective-permute-start.2) | collective-permute-done | bytes 278560 | tf_op jit(solution)/shard_map/ppermute | solution.py:168
  59.2 1.8 %shard_map.71 = s16[272,512]{1,0:T(8,128)(2,1)} custom-call(s32[3]{0:T(128)S(1)} %pad_add_fusion.refs_0_, bf16[256,512]{1,0:T(8,128)(2,1)S(1)} %get-tuple-element.11.refs_1_, bf16[256,512]{1,0:T(8,128)(2,1)S(1)} %collective-permute-done.refs_2_, bf16[512,2048]{1,0:T(8,128)(2,1)S(1)} %copy-done.1, bf16[512,2048]{1,0:T(8,128)(2,1)S(1)} %shard_map.65.refs_3_.refs_4_, ...), custom_call_target="tpu_custom_call" | custom-call | flops 268435456 | bytes 2097152 | tf_op jit(solution)/shard_map/pallas_call | solution.py:30
  62.6 2.6 %collective-permute-done.8.refs_5_ = s16[272,512]{1,0:T(8,128)(2,1)S(1)} collective-permute-done((s16[272,512]{1,0:T(8,128)(2,1)S(1)}, s16[272,512]{1,0:T(8,128)(2,1)S(1)}, u32[]{:S(2)}, u32[]{:S(2)}) %collective-permute-start.8) | collective-permute-done | bytes 278560 | tf_op jit(solution)/shard_map/ppermute | solution.py:168
  66.3 1.8 %collective-permute-start.9 = (s16[272,512]{1,0:T(8,128)(2,1)S(1)}, s16[272,512]{1,0:T(8,128)(2,1)S(1)}, u32[]{:S(2)}, u32[]{:S(2)}) collective-permute-start(s16[272,512]{1,0:T(8,128)(2,1)S(1)} %shard_map.75), channel_id=1, source_target_pairs={{0,2},{1,3},{2,4},{3,5},{4,6},{5,7},{6,0},{7,1},{8,10},{9,11},{10,... | collective-permute-start | bytes 835592 | tf_op jit(solution)/shard_map/ppermute | solution.py:173
  69.7 1.6 %collective-permute-start.14 = (s16[272,512]{1,0:T(8,128)(2,1)S(1)}, s16[272,512]{1,0:T(8,128)(2,1)S(1)}, u32[]{:S(2)}, u32[]{:S(2)}) collective-permute-start(s16[272,512]{1,0:T(8,128)(2,1)S(1)} %shard_map.79), channel_id=1, source_target_pairs={{0,2},{1,3},{2,4},{3,5},{4,6},{5,7},{6,0},{7,1},{8,10},{9,11},{10,... | collective-permute-start | bytes 835592 | tf_op jit(solution)/shard_map/ppermute | solution.py:173
  71.4 1.8 %shard_map.84.refs_2_ = bf16[256,512]{1,0:T(8,128)(2,1)} custom-call(s32[3]{0:T(128)S(1)} %pad_add_fusion.refs_0_, bf16[256,512]{1,0:T(8,128)(2,1)S(1)} %copy-done.12, bf16[256,512]{1,0:T(8,128)(2,1)S(1)} %copy-done.9, bf16[512,2048]{1,0:T(8,128)(2,1)S(1)} %copy-done.1, bf16[512,2048]{1,0:T(8,128)(2,1)S(1)} %shard_map.65.refs_3_.refs_4_, ...), custom_call_target="tpu_custom_call" | custom-call | flops 268435456 | bytes 2097152 | tf_op jit(solution)/shard_map/pallas_call | solution.py:30
  74.5 6.5 %collective-permute-done.14.refs_6_ = s16[272,512]{1,0:T(8,128)(2,1)S(1)} collective-permute-done((s16[272,512]{1,0:T(8,128)(2,1)S(1)}, s16[272,512]{1,0:T(8,128)(2,1)S(1)}, u32[]{:S(2)}, u32[]{:S(2)}) %collective-permute-start.14) | collective-permute-done | bytes 278560 | tf_op jit(solution)/shard_map/ppermute | solution.py:173
  81.0 1.8 %shard_map.80.refs_2_ = bf16[256,512]{1,0:T(8,128)(2,1)} custom-call(s32[3]{0:T(128)S(1)} %pad_add_fusion.refs_0_, bf16[256,512]{1,0:T(8,128)(2,1)S(1)} %get-tuple-element.16.refs_1_, bf16[256,512]{1,0:T(8,128)(2,1)S(1)} %copy-done.14, bf16[512,2048]{1,0:T(8,128)(2,1)S(1)} %copy-done.1, bf16[512,2048]{1,0:T(8,128)(2,1)S(1)} %shard_map.65.refs_3_.refs_4_, ...), custom_call_target="tpu_custom_call" | custom-call | flops 268435456 | bytes 2097152 | tf_op jit(solution)/shard_map/pallas_call | solution.py:30
  84.3 1.8 %shard_map.76.refs_2_ = bf16[256,512]{1,0:T(8,128)(2,1)} custom-call(s32[3]{0:T(128)S(1)} %pad_add_fusion.refs_0_, bf16[256,512]{1,0:T(8,128)(2,1)S(1)} %get-tuple-element.14.refs_1_, bf16[256,512]{1,0:T(8,128)(2,1)S(1)} %collective-permute-done.6.refs_2_, bf16[512,2048]{1,0:T(8,128)(2,1)S(1)} %copy-done.1, bf16[512,2048]{1,0:T(8,128)(2,1)S(1)} %shard_map.65.refs_3_.refs_4_, ...), custom_call_target="tpu_custom_call" | custom-call | flops 268435456 | bytes 2097152 | tf_op jit(solution)/shard_map/pallas_call | solution.py:30
  86.9 1.6 %copy-done.2 = bf16[512,2048]{1,0:T(8,128)(2,1)S(1)} copy-done((bf16[512,2048]{1,0:T(8,128)(2,1)S(1)}, bf16[512,2048]{1,0:T(8,128)(2,1)}, u32[]{:S(2)}) %copy-start.2) | copy-done | bytes 2097176
  91.9 1.6 %collective-permute-start.5 = (bf16[256,512]{1,0:T(8,128)(2,1)S(1)}, bf16[256,512]{1,0:T(8,128)(2,1)S(1)}, u32[]{:S(2)}, u32[]{:S(2)}) collective-permute-start(bf16[256,512]{1,0:T(8,128)(2,1)S(1)} %shard_map.72.refs_2_), channel_id=1, source_target_pairs={{0,16},{8,24},{16,0},{24,8},{1,17},{9,25},{17,1},{25,9},{2,18},{10... | collective-permute-start | bytes 786440 | tf_op jit(solution)/shard_map/ppermute | solution.py:164
  93.6 2.6 %shard_map.85.refs_4_ = bf16[2048,512]{1,0:T(8,128)(2,1)S(1)} custom-call(s32[3]{0:T(128)S(1)} %pad_add_fusion.refs_0_, s32[2048,1]{1,0:T(8,128)S(1)} %copy.14.refs_1_, bf16[256,512]{1,0:T(8,128)(2,1)} %shard_map.84.refs_2_, bf16[256,512]{1,0:T(8,128)(2,1)} %collective-permute-done.20.refs_3_), custom_call_target="tpu_custom_call" | custom-call | flops 1073741824 | bytes 4194304 | tf_op jit(solution)/shard_map/pallas_call | solution.py:30
  96.2 2.7 %shard_map.86.refs_4_ = bf16[2048,512]{1,0:T(8,128)(2,1)S(1)} custom-call(s32[3]{0:T(128)S(1)} %pad_add_fusion.refs_0_, s32[2048,1]{1,0:T(8,128)S(1)} %copy.14.refs_1_, bf16[256,512]{1,0:T(8,128)(2,1)} %shard_map.80.refs_2_, bf16[256,512]{1,0:T(8,128)(2,1)} %collective-permute-done.15.refs_3_, bf16[2048,512]{1,0:T(8,128)(2,1)S(1)} %shard_map.85.refs_4_), custom_call_target="tpu_custom_call" | custom-call | flops 1073741824 | bytes 4194304 | tf_op jit(solution)/shard_map/pallas_call | solution.py:30
  98.9 2.7 %shard_map.87.refs_4_ = bf16[2048,512]{1,0:T(8,128)(2,1)S(1)} custom-call(s32[3]{0:T(128)S(1)} %pad_add_fusion.refs_0_, s32[2048,1]{1,0:T(8,128)S(1)} %copy.14.refs_1_, bf16[256,512]{1,0:T(8,128)(2,1)} %shard_map.76.refs_2_, bf16[256,512]{1,0:T(8,128)(2,1)} %collective-permute-done.10.refs_3_, bf16[2048,512]{1,0:T(8,128)(2,1)S(1)} %shard_map.86.refs_4_), custom_call_target="tpu_custom_call" | custom-call | flops 1073741824 | bytes 4194304 | tf_op jit(solution)/shard_map/pallas_call | solution.py:30
  101.6 3.5 %shard_map.88 = bf16[2048,512]{1,0:T(8,128)(2,1)} custom-call(s32[3]{0:T(128)S(1)} %pad_add_fusion.refs_0_, s32[2048,1]{1,0:T(8,128)S(1)} %copy.14.refs_1_, bf16[256,512]{1,0:T(8,128)(2,1)S(1)} %shard_map.72.refs_2_, bf16[256,512]{1,0:T(8,128)(2,1)S(1)} %collective-permute-done.5.refs_3_, bf16[2048,512]{1,0:T(8,128)(2,1)S(1)} %shard_map.87.refs_4_), custom_call_target="tpu_custom_call" | custom-call | flops 1073741824 | bytes 4194304 | tf_op jit(solution)/shard_map/pallas_call | solution.py:30
  (89 shorter events, 30.1 us)
Async XLA Ops:
  0.0 3.9 %copy-start = (bf16[512,2048]{1,0:T(8,128)(2,1)S(1)}, bf16[512,2048]{1,0:T(8,128)(2,1)}, u32[]{:S(2)}) copy-start(bf16[512,2048]{1,0:T(8,128)(2,1)} %refs_3_.31) | copy-start | bytes 6291460
  3.8 1.9 %copy-start.4 = (bf16[2048,512]{1,0:T(8,128)(2,1)S(1)}, bf16[2048,512]{1,0:T(8,128)(2,1)}, u32[]{:S(2)}) copy-start(bf16[2048,512]{1,0:T(8,128)(2,1)} %refs_2_.7) | copy-start | bytes 6291460
  3.8 10.0 %collective-permute-start.16 = (bf16[256,512]{1,0:T(8,128)(2,1)S(1)}, bf16[256,512]{1,0:T(8,128)(2,1)S(1)}, u32[]{:S(2)}, u32[]{:S(2)}) collective-permute-start(bf16[256,512]{1,0:T(8,128)(2,1)S(1)} %shard_map.64.refs_2_), channel_id=1, source_target_pairs={{0,16},{8,24},{16,0},{24,8},{1,17},{9,25},{17,1},{25,9},{2,18},{10... | collective-permute-start | bytes 786440 | tf_op jit(solution)/shard_map/ppermute | solution.py:164
  9.8 5.8 %copy-start.10 = (bf16[256,512]{1,0:T(8,128)(2,1)}, bf16[256,512]{1,0:T(8,128)(2,1)S(1)}, u32[]{:S(2)}) copy-start(bf16[256,512]{1,0:T(8,128)(2,1)S(1)} %get-tuple-element.12.refs_3_.refs_1_) | copy-start | bytes 786436
  9.8 4.0 %copy-start.19 = (s32[2048]{0:T(1024)S(1)}, s32[2048]{0:T(1024)}, u32[]{:S(2)}) copy-start(s32[2048]{0:T(1024)} %param.8) | copy-start | bytes 24580
  11.6 9.3 %collective-permute-start = (bf16[256,512]{1,0:T(8,128)(2,1)S(1)}, bf16[256,512]{1,0:T(8,128)(2,1)S(1)}, u32[]{:S(2)}, u32[]{:S(2)}) collective-permute-start(bf16[256,512]{1,0:T(8,128)(2,1)S(1)} %get-tuple-element.13), channel_id=1, source_target_pairs={{0,16},{8,24},{16,0},{24,8},{1,17},{9,25},{17,1},{25,9},{2,18},{10... | collective-permute-start | bytes 786440 | tf_op jit(solution)/shard_map/ppermute | solution.py:164
  11.7 22.6 %collective-permute-start.11 = (bf16[256,512]{1,0:T(8,128)(2,1)S(1)}, bf16[256,512]{1,0:T(8,128)(2,1)S(1)}, u32[]{:S(2)}, u32[]{:S(2)}) collective-permute-start(bf16[256,512]{1,0:T(8,128)(2,1)S(1)} %shard_map.66.refs_3_), channel_id=1, source_target_pairs={{0,16},{8,24},{16,0},{24,8},{1,17},{9,25},{17,1},{25,9},{2,18},{10... | collective-permute-start | bytes 786440 | tf_op jit(solution)/shard_map/ppermute | solution.py:164
  13.7 17.3 %collective-permute-start.6 = (bf16[256,512]{1,0:T(8,128)(2,1)S(1)}, bf16[256,512]{1,0:T(8,128)(2,1)S(1)}, u32[]{:S(2)}, u32[]{:S(2)}) collective-permute-start(bf16[256,512]{1,0:T(8,128)(2,1)S(1)} %get-tuple-element.15), channel_id=1, source_target_pairs={{0,16},{8,24},{16,0},{24,8},{1,17},{9,25},{17,1},{25,9},{2,18},{10... | collective-permute-start | bytes 786440 | tf_op jit(solution)/shard_map/ppermute | solution.py:164
  15.6 23.0 %collective-permute-start.17 = (s16[272,512]{1,0:T(8,128)(2,1)}, s16[272,512]{1,0:T(8,128)(2,1)}, u32[]{:S(2)}, u32[]{:S(2)}) collective-permute-start(s16[272,512]{1,0:T(8,128)(2,1)} %shard_map.81), channel_id=1, source_target_pairs={{0,2},{1,3},{2,4},{3,5},{4,6},{5,7},{6,0},{7,1},{8,10},{9,11},{10,... | collective-permute-start | bytes 835592 | tf_op jit(solution)/shard_map/ppermute | solution.py:173
  20.9 38.4 %copy-start.5 = (bf16[256,512]{1,0:T(8,128)(2,1)}, bf16[256,512]{1,0:T(8,128)(2,1)S(1)}, u32[]{:S(2)}) copy-start(bf16[256,512]{1,0:T(8,128)(2,1)S(1)} %collective-permute-done.refs_2_) | copy-start | bytes 786436
  22.6 22.5 %collective-permute-start.1 = (s16[272,512]{1,0:T(8,128)(2,1)}, s16[272,512]{1,0:T(8,128)(2,1)}, u32[]{:S(2)}, u32[]{:S(2)}) collective-permute-start(s16[272,512]{1,0:T(8,128)(2,1)} %shard_map.69), channel_id=1, source_target_pairs={{0,2},{1,3},{2,4},{3,5},{4,6},{5,7},{6,0},{7,1},{8,10},{9,11},{10,... | collective-permute-start | bytes 835592 | tf_op jit(solution)/shard_map/ppermute | solution.py:173
  32.7 14.5 %collective-permute-start.7 = (s16[272,512]{1,0:T(8,128)(2,1)}, s16[272,512]{1,0:T(8,128)(2,1)}, u32[]{:S(2)}, u32[]{:S(2)}) collective-permute-start(s16[272,512]{1,0:T(8,128)(2,1)} %shard_map.73), channel_id=1, source_target_pairs={{0,2},{1,3},{2,4},{3,5},{4,6},{5,7},{6,0},{7,1},{8,10},{9,11},{10,... | collective-permute-start | bytes 835592 | tf_op jit(solution)/shard_map/ppermute | solution.py:173
  34.3 3.3 %copy-start.20 = (f32[200]{0:T(256)S(1)}, f32[200]{0:T(256)}, u32[]{:S(2)}) copy-start(f32[200]{0:T(256)} %param.10) | copy-start | bytes 2404
  36.1 14.3 %collective-permute-start.12 = (s16[272,512]{1,0:T(8,128)(2,1)}, s16[272,512]{1,0:T(8,128)(2,1)}, u32[]{:S(2)}, u32[]{:S(2)}) collective-permute-start(s16[272,512]{1,0:T(8,128)(2,1)} %shard_map.77), channel_id=1, source_target_pairs={{0,2},{1,3},{2,4},{3,5},{4,6},{5,7},{6,0},{7,1},{8,10},{9,11},{10,... | collective-permute-start | bytes 835592 | tf_op jit(solution)/shard_map/ppermute | solution.py:173
  38.2 33.1 %collective-permute-start.4 = (f32[1024]{0:T(1024)S(1)}, f32[1024]{0:T(1024)S(1)}, u32[]{:S(2)}, u32[]{:S(2)}) collective-permute-start(f32[1024]{0:T(1024)S(1)} %slice.9), channel_id=1, source_target_pairs={{0,16},{8,24},{16,0},{24,8},{1,17},{9,25},{17,1},{25,9},{2,18},{10... | collective-permute-start | bytes 12296 | tf_op jit(solution)/shard_map/ppermute | solution.py:164
  43.6 9.8 %collective-permute-start.18 = (s16[272,512]{1,0:T(8,128)(2,1)S(1)}, s16[272,512]{1,0:T(8,128)(2,1)S(1)}, u32[]{:S(2)}, u32[]{:S(2)}) collective-permute-start(s16[272,512]{1,0:T(8,128)(2,1)S(1)} %shard_map.82), channel_id=1, source_target_pairs={{0,1},{1,0},{2,3},{3,2},{4,5},{5,4},{6,7},{7,6},{8,9},{9,8},{10,11... | collective-permute-start | bytes 835592 | tf_op jit(solution)/shard_map/ppermute | solution.py:168
  46.7 3.7 %copy-start.14 = (bf16[256,512]{1,0:T(8,128)(2,1)S(1)}, bf16[256,512]{1,0:T(8,128)(2,1)}, u32[]{:S(2)}) copy-start(bf16[256,512]{1,0:T(8,128)(2,1)} %copy-done.13) | copy-start | bytes 786436
  46.7 12.5 %collective-permute-start.2 = (s16[272,512]{1,0:T(8,128)(2,1)S(1)}, s16[272,512]{1,0:T(8,128)(2,1)S(1)}, u32[]{:S(2)}, u32[]{:S(2)}) collective-permute-start(s16[272,512]{1,0:T(8,128)(2,1)S(1)} %shard_map.70), channel_id=1, source_target_pairs={{0,1},{1,0},{2,3},{3,2},{4,5},{5,4},{6,7},{7,6},{8,9},{9,8},{10,11... | collective-permute-start | bytes 835592 | tf_op jit(solution)/shard_map/ppermute | solution.py:168
  48.8 3.7 %copy-start.21 = (f32[2000]{0:T(1024)S(1)}, f32[2000]{0:T(1024)}, u32[]{:S(2)}) copy-start(f32[2000]{0:T(1024)} %param.11) | copy-start | bytes 24004
  48.8 4.6 %copy-start.9 = (bf16[256,512]{1,0:T(8,128)(2,1)S(1)}, bf16[256,512]{1,0:T(8,128)(2,1)}, u32[]{:S(2)}) copy-start(bf16[256,512]{1,0:T(8,128)(2,1)} %copy-done.7) | copy-start | bytes 786436
  48.8 4.6 %copy-start.12 = (bf16[256,512]{1,0:T(8,128)(2,1)S(1)}, bf16[256,512]{1,0:T(8,128)(2,1)}, u32[]{:S(2)}) copy-start(bf16[256,512]{1,0:T(8,128)(2,1)} %copy-done.10) | copy-start | bytes 786436
  48.8 16.4 %collective-permute-start.8 = (s16[272,512]{1,0:T(8,128)(2,1)S(1)}, s16[272,512]{1,0:T(8,128)(2,1)S(1)}, u32[]{:S(2)}, u32[]{:S(2)}) collective-permute-start(s16[272,512]{1,0:T(8,128)(2,1)S(1)} %shard_map.74), channel_id=1, source_target_pairs={{0,1},{1,0},{2,3},{3,2},{4,5},{5,4},{6,7},{7,6},{8,9},{9,8},{10,11... | collective-permute-start | bytes 835592 | tf_op jit(solution)/shard_map/ppermute | solution.py:168
  51.9 16.8 %collective-permute-start.13 = (s16[272,512]{1,0:T(8,128)(2,1)S(1)}, s16[272,512]{1,0:T(8,128)(2,1)S(1)}, u32[]{:S(2)}, u32[]{:S(2)}) collective-permute-start(s16[272,512]{1,0:T(8,128)(2,1)S(1)} %shard_map.78), channel_id=1, source_target_pairs={{0,1},{1,0},{2,3},{3,2},{4,5},{5,4},{6,7},{7,6},{8,9},{9,8},{10,11... | collective-permute-start | bytes 835592 | tf_op jit(solution)/shard_map/ppermute | solution.py:168
  54.5 16.9 %collective-permute-start.19 = (s16[272,512]{1,0:T(8,128)(2,1)S(1)}, s16[272,512]{1,0:T(8,128)(2,1)S(1)}, u32[]{:S(2)}, u32[]{:S(2)}) collective-permute-start(s16[272,512]{1,0:T(8,128)(2,1)S(1)} %shard_map.83), channel_id=1, source_target_pairs={{0,2},{1,3},{2,4},{3,5},{4,6},{5,7},{6,0},{7,1},{8,10},{9,11},{10,... | collective-permute-start | bytes 835592 | tf_op jit(solution)/shard_map/ppermute | solution.py:173
  61.0 25.9 %collective-permute-start.3 = (s16[272,512]{1,0:T(8,128)(2,1)}, s16[272,512]{1,0:T(8,128)(2,1)}, u32[]{:S(2)}, u32[]{:S(2)}) collective-permute-start(s16[272,512]{1,0:T(8,128)(2,1)} %shard_map.71), channel_id=1, source_target_pairs={{0,2},{1,3},{2,4},{3,5},{4,6},{5,7},{6,0},{7,1},{8,10},{9,11},{10,... | collective-permute-start | bytes 835592 | tf_op jit(solution)/shard_map/ppermute | solution.py:173
  66.3 18.0 %collective-permute-start.9 = (s16[272,512]{1,0:T(8,128)(2,1)S(1)}, s16[272,512]{1,0:T(8,128)(2,1)S(1)}, u32[]{:S(2)}, u32[]{:S(2)}) collective-permute-start(s16[272,512]{1,0:T(8,128)(2,1)S(1)} %shard_map.75), channel_id=1, source_target_pairs={{0,2},{1,3},{2,4},{3,5},{4,6},{5,7},{6,0},{7,1},{8,10},{9,11},{10,... | collective-permute-start | bytes 835592 | tf_op jit(solution)/shard_map/ppermute | solution.py:173
  69.7 11.2 %collective-permute-start.14 = (s16[272,512]{1,0:T(8,128)(2,1)S(1)}, s16[272,512]{1,0:T(8,128)(2,1)S(1)}, u32[]{:S(2)}, u32[]{:S(2)}) collective-permute-start(s16[272,512]{1,0:T(8,128)(2,1)S(1)} %shard_map.79), channel_id=1, source_target_pairs={{0,2},{1,3},{2,4},{3,5},{4,6},{5,7},{6,0},{7,1},{8,10},{9,11},{10,... | collective-permute-start | bytes 835592 | tf_op jit(solution)/shard_map/ppermute | solution.py:173
  73.2 20.4 %collective-permute-start.20 = (bf16[256,512]{1,0:T(8,128)(2,1)}, bf16[256,512]{1,0:T(8,128)(2,1)}, u32[]{:S(2)}, u32[]{:S(2)}) collective-permute-start(bf16[256,512]{1,0:T(8,128)(2,1)} %shard_map.84.refs_2_), channel_id=1, source_target_pairs={{0,16},{8,24},{16,0},{24,8},{1,17},{9,25},{17,1},{25,9},{2,18},{10... | collective-permute-start | bytes 786440 | tf_op jit(solution)/shard_map/ppermute | solution.py:164
  82.7 3.8 %copy-start.18 = (s32[2048]{0:T(1024)S(1)}, s32[2048]{0:T(1024)}, u32[]{:S(2)}) copy-start(s32[2048]{0:T(1024)} %param.9) | copy-start | bytes 24580
  82.7 13.5 %collective-permute-start.15 = (bf16[256,512]{1,0:T(8,128)(2,1)}, bf16[256,512]{1,0:T(8,128)(2,1)}, u32[]{:S(2)}, u32[]{:S(2)}) collective-permute-start(bf16[256,512]{1,0:T(8,128)(2,1)} %shard_map.80.refs_2_), channel_id=1, source_target_pairs={{0,16},{8,24},{16,0},{24,8},{1,17},{9,25},{17,1},{25,9},{2,18},{10... | collective-permute-start | bytes 786440 | tf_op jit(solution)/shard_map/ppermute | solution.py:164
  86.1 12.8 %collective-permute-start.10 = (bf16[256,512]{1,0:T(8,128)(2,1)}, bf16[256,512]{1,0:T(8,128)(2,1)}, u32[]{:S(2)}, u32[]{:S(2)}) collective-permute-start(bf16[256,512]{1,0:T(8,128)(2,1)} %shard_map.76.refs_2_), channel_id=1, source_target_pairs={{0,16},{8,24},{16,0},{24,8},{1,17},{9,25},{17,1},{25,9},{2,18},{10... | collective-permute-start | bytes 786440 | tf_op jit(solution)/shard_map/ppermute | solution.py:164
  91.9 9.6 %collective-permute-start.5 = (bf16[256,512]{1,0:T(8,128)(2,1)S(1)}, bf16[256,512]{1,0:T(8,128)(2,1)S(1)}, u32[]{:S(2)}, u32[]{:S(2)}) collective-permute-start(bf16[256,512]{1,0:T(8,128)(2,1)S(1)} %shard_map.72.refs_2_), channel_id=1, source_target_pairs={{0,16},{8,24},{16,0},{24,8},{1,17},{9,25},{17,1},{25,9},{2,18},{10... | collective-permute-start | bytes 786440 | tf_op jit(solution)/shard_map/ppermute | solution.py:164
  (11 other events, 14.7 us)

commit v3 on v2

--- a/solution.py
+++ b/solution.py
@@ -14,14 +14,18 @@
 TOP = 32767.0
 STEPS = 64.0
 TINY = 1e-33
-VMEM_LIMIT = 16 * 1024 * 1024
+VMEM_LIMIT = 8 * 1024 * 1024
+ORDER = (
+    ((1, 0), (1, 1), (2, 0), (1, 2), (2, 1), (1, 3), (3, 0), (2, 2), (3, 1), (2, 3))
+    + ((3, 2), (4, 0), (3, 3), (4, 1), (5, 0), (4, 2), (5, 1), (4, 3), (5, 2), (5, 3))
+)
 
 VMEM = pl.BlockSpec(memory_space=pltpu.VMEM)
 SMEM = pl.BlockSpec(memory_space=pltpu.SMEM)
 ANY = pl.BlockSpec(memory_space=pl.ANY)
 
 
-def call(body, out_shape, flops, moved, operands, after=()):
+def call(body, out_shape, operands, after=()):
     count = len(operands)
 
     def kernel(*refs):
@@ -33,7 +37,7 @@
         in_specs=[SMEM] + [VMEM] * (count - 1) + [ANY] * len(after),
         out_specs=jax.tree.map(lambda _: VMEM, out_shape),
         compiler_params=pltpu.CompilerParams(vmem_limit_bytes=VMEM_LIMIT),
-        cost_estimate=pl.CostEstimate(flops=flops, bytes_accessed=moved, transcendentals=0),
+        cost_estimate=pl.CostEstimate(flops=1, bytes_accessed=1, transcendentals=0),
     )(*operands, *after)
 
 
@@ -47,12 +51,13 @@
     return jnp.dot(left, right, preferred_element_type=jnp.float32).astype(jnp.bfloat16)
 
 
-def mirror_kernel(flags, integrals, out):
+def mirror_kernel(flags, integrals, *outs):
     width = integrals.shape[0]
     swap = swap_matrix(width)
-    for stop in range(integrals.shape[1] // width):
-        cols = pl.ds(stop * width, width)
-        out[:, cols] = exact_dot(integrals[:, cols], swap)
+    for stop, out in enumerate(outs):
+        block = integrals[:, pl.ds(stop * width, width)]
+        out[pl.ds(0, width), :] = block
+        out[pl.ds(width, width), :] = exact_dot(block, swap)
 
 
 def align_kernel(begin, send, flags, partner, amplitudes, *outs):
@@ -75,10 +80,10 @@
             out[...] = exact_dot(pick, amplitudes[...])
 
 
-def product(stop, own, other, integrals, mirrored):
-    cols = pl.ds(stop * own.shape[1], own.shape[1])
-    return jnp.dot(own[...], integrals[:, cols], preferred_element_type=jnp.float32) + jnp.dot(
-        other[...], mirrored[:, cols], preferred_element_type=jnp.float32
+def product(own, other, factor):
+    width = own.shape[1]
+    return jnp.dot(own[...], factor[pl.ds(0, width), :], preferred_element_type=jnp.float32) + jnp.dot(
+        other[...], factor[pl.ds(width, width), :], preferred_element_type=jnp.float32
     )
 
 
@@ -98,23 +103,23 @@
     return coded[pl.ds(0, rows), :].astype(jnp.int32).astype(jnp.float32) * jnp.exp2(level * (1.0 / STEPS))
 
 
-def first_kernel(flags, own, other, integrals, mirrored, out):
-    code(product(3, own, other, integrals, mirrored), out)
-
-
-def second_kernel(flags, own, other, integrals, mirrored, arrived, out):
-    code(product(1, own, other, integrals, mirrored) + decode(arrived), out)
-
-
-def third_kernel(flags, own, other, integrals, mirrored, crossed, out):
+def first_kernel(flags, own, other, factor, out):
+    code(product(own, other, factor), out)
+
+
+def second_kernel(flags, own, other, factor, arrived, out):
+    code(product(own, other, factor) + decode(arrived), out)
+
+
+def third_kernel(flags, own, other, factor, crossed, out):
     here = jnp.where(flags[1] == 0, 1.0, 0.0)
-    code(product(2, own, other, integrals, mirrored) + decode(crossed) * here, out)
-
-
-def last_kernel(index, flags, own, other, integrals, mirrored, crossed, arrived, occ_sum, vir_sum, out):
+    code(product(own, other, factor) + decode(crossed) * here, out)
+
+
+def last_kernel(index, flags, own, other, factor, crossed, arrived, occ_sum, vir_sum, out):
     chunk, width = out.shape
     here = jnp.where(flags[1] == 1, 1.0, 0.0)
-    total = product(0, own, other, integrals, mirrored) + decode(arrived) + decode(crossed) * here
+    total = product(own, other, factor) + decode(arrived) + decode(crossed) * here
     occ_rows = occ_sum[:, pl.ds(index * chunk, chunk)]
     occ_down = jnp.broadcast_to(occ_rows, (128, chunk)).T
     for lane in range(0, width, 128):
@@ -192,27 +197,17 @@
         return call(
             functools.partial(align_kernel, begin * chunk, send),
             [chunk_shape] * count,
-            2 * count * chunk * rows * width,
-            2 * rows * width,
             (flags, partner[None, :], amplitudes),
             after,
         )
 
-    def stage(body, out_shape, *operands):
-        return call(body, out_shape, 4 * chunk * width * width, 16 * chunk * width, (flags, *operands))
-
     sent = align(0, 1, True)
-    mirrored = call(
-        mirror_kernel,
-        jax.ShapeDtypeStruct(integrals.shape, jnp.bfloat16),
-        8 * width**3,
-        4 * integrals.size,
-        (flags, integrals),
-        (sent[0],),
+    factors = call(
+        mirror_kernel, [jax.ShapeDtypeStruct((2 * width, width), jnp.bfloat16)] * 4, (flags, integrals), sent[:1]
     )
-    sent += align(1, 1, True, (mirrored,))
-    own = align(0, CHUNKS, False, (sent[1],))
-    sent += align(2, CHUNKS - 2, True, (own[0],))
+    sent += align(1, 1, True, factors[:1])
+    own = align(0, CHUNKS, False, sent[1:2])
+    sent += align(2, CHUNKS - 2, True, own[:1])
     other = [across_rows(value) for value in sent]
 
     occ_sum = table_lookup(occ_energy, pair_index // NOCC) + table_lookup(occ_energy, pair_index % NOCC)
@@ -222,25 +217,36 @@
     vir_sum = table_lookup(vir_energy, unordered // NV) + table_lookup(vir_energy, unordered % NV)
     vir_sum = vir_sum[None, :]
 
-    placed = ()
-    for index in range(CHUNKS):
-        inputs = (own[index], other[index], integrals, mirrored)
-        moved = two_along(stage(first_kernel, coded_shape, *inputs))
-        crossed = across_pair(stage(second_kernel, coded_shape, *inputs, moved))
-        arrived = two_along(stage(third_kernel, coded_shape, *inputs, crossed))
-        done = stage(
-            functools.partial(last_kernel, index), chunk_shape, *inputs, crossed, arrived, occ_sum, vir_sum
-        )
-        placed = (
-            call(
+    moved, crossed, arrived, done, placed = {}, {}, {}, {}, ()
+    last = sent[CHUNKS - 1]
+    for step, index in ORDER:
+        pair = (flags, own[index], other[index])
+        if step == 1:
+            last = call(first_kernel, coded_shape, (*pair, factors[3]), (last,))
+            moved[index] = two_along(last)
+        elif step == 2:
+            last = call(second_kernel, coded_shape, (*pair, factors[1], moved[index]), (last,))
+            crossed[index] = across_pair(last)
+        elif step == 3:
+            last = call(third_kernel, coded_shape, (*pair, factors[2], crossed[index]), (last,))
+            arrived[index] = two_along(last)
+        elif step == 4:
+            last = call(
+                functools.partial(last_kernel, index),
+                chunk_shape,
+                (*pair, factors[0], crossed[index], arrived[index], occ_sum, vir_sum),
+                (last,),
+            )
+            done[index] = (last, across_rows(last))
+        else:
+            last = call(
                 functools.partial(place_kernel, index),
                 whole_shape,
-                4 * chunk * rows * width,
-                4 * rows * width,
-                (flags, partner[:, None], done, across_rows(done), *placed),
-            ),
-        )
-    return placed[0]
+                (flags, partner[:, None], *done[index], *placed),
+                (last,),
+            )
+            placed = (last,)
+    return last
 
 
 def solution(mesh):

time: 106 us -> 97.5 us (0.920)
  the two profiles are of different devices: /device:TPU:2 before, /device:TPU:0 now
where the time goes in v3:
time: 97.5 us; the launch traced here: 97 us
  Pallas kernels  39.3 us (40%)
  starting transfers between devices  29 us (30%)
  waiting for transfers between devices  18.5 us (19%)
  local copies, waits for them, and re-layouts  8.21 us (8%)
  other arithmetic  1.62 us (2%)
    pallas_call x25, Pallas kernels, call(): pl.pallas_call(kernel, out_shape=out_shape, in_specs=[SMEM] + [VMEM] * (c...  39.3 us
    ppermute x9, waiting for transfers between devices, across_rows(): lax.ppermute(value, 'row', [(i, i ^ count // 2) for i in range(count)])  17.2 us
    ppermute x8, starting transfers between devices, two_along(): lax.ppermute(value, 'col', [(i, (i + 2) % count) for i in range(count)])  12.3 us
    ppermute x9, starting transfers between devices, across_rows(): lax.ppermute(value, 'row', [(i, i ^ count // 2) for i in range(count)])  12.1 us
    unnamed x60, local copies, waits for them, and re-layouts  7.84 us
    ppermute x4, starting transfers between devices, across_pair(): lax.ppermute(value, 'col', [(i, i ^ 1) for i in range(lax.axis_size('col'...  4.62 us
  transfers between devices with their start and end apart: 21, of which 8 were waited for; matrix products, arithmetic and copies ran while one was open for 2% of the time, Pallas kernels for 38%

profile of v3, /device:TPU:0, one launch (start us, length us, event | category | flops | bytes accessed | tf_op | source)
XLA Modules:
  0.0 97.0 jit_solution(13234495265826199665)
XLA Ops:
  0.1 1.6 %copy-done = bf16[2048,512]{1,0:T(8,128)(2,1)S(1)} copy-done((bf16[2048,512]{1,0:T(8,128)(2,1)S(1)}, bf16[2048,512]{1,0:T(8,128)(2,1)}, u32[]{:S(2)}) %copy-start) | copy-done | bytes 2097176
  2.9 3.7 %collective-permute-start.2 = (bf16[256,512]{1,0:T(8,128)(2,1)S(1)}, bf16[256,512]{1,0:T(8,128)(2,1)S(1)}, u32[]{:S(2)}, u32[]{:S(2)}) collective-permute-start(bf16[256,512]{1,0:T(8,128)(2,1)S(1)} %shard_map.64.refs_2_), channel_id=1, source_target_pairs={{0,16},{8,24},{16,0},{24,8},{1,17},{9,25},{17,1},{25,9},{2,18},{10... | collective-permute-start | bytes 786440 | tf_op jit(solution)/shard_map/ppermute | solution.py:169
  6.6 1.6 %copy-done.24 = bf16[512,2048]{1,0:T(8,128)(2,1)S(1)} copy-done((bf16[512,2048]{1,0:T(8,128)(2,1)S(1)}, bf16[512,2048]{1,0:T(8,128)(2,1)}, u32[]{:S(2)}) %copy-start.24) | copy-done | bytes 2097176
  8.2 1.8 %shard_map.65 = (bf16[1024,512]{1,0:T(8,128)(2,1)S(1)}, bf16[1024,512]{1,0:T(8,128)(2,1)S(1)}, bf16[1024,512]{1,0:T(8,128)(2,1)S(1)}, bf16[1024,512]{1,0:T(8,128)(2,1)S(1)}) custom-call(s32[3]{0:T(128)S(1)} %pad_add_fusion.refs_0_, bf16[512,2048]{1,0:T(8,128)(2,1)S(1)} %copy-done.24, bf16[256,512]{1,0:T(8,128)(2,1)S(1)} %shard_map.64.refs_2_), custom_call_target="tpu_custom_call" | custom-call | flops 1 | bytes 1 | tf_op jit(solution)/shard_map/pallas_call | solution.py:34
  14.1 1.6 %collective-permute-start.5 = (s16[272,512]{1,0:T(8,128)(2,1)S(1)}, s16[272,512]{1,0:T(8,128)(2,1)S(1)}, u32[]{:S(2)}, u32[]{:S(2)}) collective-permute-start(s16[272,512]{1,0:T(8,128)(2,1)S(1)} %shard_map.69.refs_4_), channel_id=1, source_target_pairs={{0,2},{1,3},{2,4},{3,5},{4,6},{5,7},{6,0},{7,1},{8,10},{9,11},{10,... | collective-permute-start | bytes 835592 | tf_op jit(solution)/shard_map/ppermute | solution.py:178
  15.7 2.8 %collective-permute-done.1.refs_2_ = bf16[256,512]{1,0:T(8,128)(2,1)S(1)} collective-permute-done((bf16[256,512]{1,0:T(8,128)(2,1)S(1)}, bf16[256,512]{1,0:T(8,128)(2,1)S(1)}, u32[]{:S(2)}, u32[]{:S(2)}) %collective-permute-start.1) | collective-permute-done | bytes 262176 | tf_op jit(solution)/shard_map/ppermute | solution.py:169
  19.6 1.6 %collective-permute-start.3 = (s16[272,512]{1,0:T(8,128)(2,1)S(1)}, s16[272,512]{1,0:T(8,128)(2,1)S(1)}, u32[]{:S(2)}, u32[]{:S(2)}) collective-permute-start(s16[272,512]{1,0:T(8,128)(2,1)S(1)} %shard_map.70.refs_5_), channel_id=1, source_target_pairs={{0,2},{1,3},{2,4},{3,5},{4,6},{5,7},{6,0},{7,1},{8,10},{9,11},{10,... | collective-permute-start | bytes 835592 | tf_op jit(solution)/shard_map/ppermute | solution.py:178
  21.2 1.7 %collective-permute-start.4 = (bf16[256,512]{1,0:T(8,128)(2,1)S(1)}, bf16[256,512]{1,0:T(8,128)(2,1)S(1)}, u32[]{:S(2)}, u32[]{:S(2)}) collective-permute-start(bf16[256,512]{1,0:T(8,128)(2,1)S(1)} %get-tuple-element.23), channel_id=1, source_target_pairs={{0,16},{8,24},{16,0},{24,8},{1,17},{9,25},{17,1},{25,9},{2,18},{10... | collective-permute-start | bytes 786440 | tf_op jit(solution)/shard_map/ppermute | solution.py:169
  24.5 1.8 %shard_map.71.refs_4_ = s16[272,512]{1,0:T(8,128)(2,1)} custom-call(s32[3]{0:T(128)S(1)} %pad_add_fusion.refs_0_, bf16[256,512]{1,0:T(8,128)(2,1)S(1)} %get-tuple-element.17.refs_3_.refs_1_, bf16[256,512]{1,0:T(8,128)(2,1)S(1)} %collective-permute-done.2.refs_2_, bf16[1024,512]{1,0:T(8,128)(2,1)S(1)} %get-tuple-element.19.refs_3_, ...), custom_call_target="tpu_custom_call" | custom-call | flops 1 | bytes 1 | tf_op jit(solution)/shard_map/pallas_call | solution.py:34
  27.8 2.6 %collective-permute-done.4.refs_2_ = bf16[256,512]{1,0:T(8,128)(2,1)S(1)} collective-permute-done((bf16[256,512]{1,0:T(8,128)(2,1)S(1)}, bf16[256,512]{1,0:T(8,128)(2,1)S(1)}, u32[]{:S(2)}, u32[]{:S(2)}) %collective-permute-start.4) | collective-permute-done | bytes 262176 | tf_op jit(solution)/shard_map/ppermute | solution.py:169
  30.5 1.8 %shard_map.72.refs_5_ = s16[272,512]{1,0:T(8,128)(2,1)} custom-call(s32[3]{0:T(128)S(1)} %pad_add_fusion.refs_0_, bf16[256,512]{1,0:T(8,128)(2,1)S(1)} %get-tuple-element.22.refs_1_, bf16[256,512]{1,0:T(8,128)(2,1)S(1)} %collective-permute-done.4.refs_2_, bf16[1024,512]{1,0:T(8,128)(2,1)S(1)} %get-tuple-element.20.refs_3_, s16[272,512]{1,0:T(8,128)(2,1)} %shard_map.71.refs_4_), custom_call_target="tpu_custom_call" | custom-call | flops 1 | bytes 1 | tf_op jit(solution)/shard_map/pallas_call | solution.py:34
  32.3 1.6 %collective-permute-start.8 = (s16[272,512]{1,0:T(8,128)(2,1)}, s16[272,512]{1,0:T(8,128)(2,1)}, u32[]{:S(2)}, u32[]{:S(2)}) collective-permute-start(s16[272,512]{1,0:T(8,128)(2,1)} %shard_map.72.refs_5_), channel_id=1, source_target_pairs={{0,2},{1,3},{2,4},{3,5},{4,6},{5,7},{6,0},{7,1},{8,10},{9,11},{10,... | collective-permute-start | bytes 835592 | tf_op jit(solution)/shard_map/ppermute | solution.py:178
  33.9 1.8 %shard_map.73.refs_4_ = s16[272,512]{1,0:T(8,128)(2,1)} custom-call(s32[3]{0:T(128)S(1)} %pad_add_fusion.refs_0_, bf16[256,512]{1,0:T(8,128)(2,1)S(1)} %get-tuple-element.21.refs_1_, bf16[256,512]{1,0:T(8,128)(2,1)S(1)} %collective-permute-done.1.refs_2_, bf16[1024,512]{1,0:T(8,128)(2,1)S(1)} %get-tuple-element.19.refs_3_, ...), custom_call_target="tpu_custom_call" | custom-call | flops 1 | bytes 1 | tf_op jit(solution)/shard_map/pallas_call | solution.py:34
  37.2 1.8 %shard_map.74.refs_5_ = s16[272,512]{1,0:T(8,128)(2,1)} custom-call(s32[3]{0:T(128)S(1)} %pad_add_fusion.refs_0_, bf16[256,512]{1,0:T(8,128)(2,1)S(1)} %get-tuple-element.16.refs_1_, bf16[256,512]{1,0:T(8,128)(2,1)S(1)} %collective-permute-done.refs_2_, bf16[1024,512]{1,0:T(8,128)(2,1)S(1)} %get-tuple-element.20.refs_3_, s16[272,512]{1,0:T(8,128)(2,1)} %shard_map.73.refs_4_), custom_call_target="tpu_custom_call" | custom-call | flops 1 | bytes 1 | tf_op jit(solution)/shard_map/pallas_call | solution.py:34
  38.9 1.6 %collective-permute-start.6 = (s16[272,512]{1,0:T(8,128)(2,1)}, s16[272,512]{1,0:T(8,128)(2,1)}, u32[]{:S(2)}, u32[]{:S(2)}) collective-permute-start(s16[272,512]{1,0:T(8,128)(2,1)} %shard_map.74.refs_5_), channel_id=1, source_target_pairs={{0,2},{1,3},{2,4},{3,5},{4,6},{5,7},{6,0},{7,1},{8,10},{9,11},{10,... | collective-permute-start | bytes 835592 | tf_op jit(solution)/shard_map/ppermute | solution.py:178
  41.1 1.8 %collective-permute-start.12 = (f32[1024]{0:T(1024)S(1)}, f32[1024]{0:T(1024)S(1)}, u32[]{:S(2)}, u32[]{:S(2)}) collective-permute-start(f32[1024]{0:T(1024)S(1)} %slice.9), channel_id=1, source_target_pairs={{0,16},{8,24},{16,0},{24,8},{1,17},{9,25},{17,1},{25,9},{2,18},{10... | collective-permute-start | bytes 12296 | tf_op jit(solution)/shard_map/ppermute | solution.py:169
  44.0 2.2 %shard_map.75.refs_5_ = s16[272,512]{1,0:T(8,128)(2,1)} custom-call(s32[3]{0:T(128)S(1)} %pad_add_fusion.refs_0_, bf16[256,512]{1,0:T(8,128)(2,1)S(1)} %get-tuple-element.17.refs_3_.refs_1_, bf16[256,512]{1,0:T(8,128)(2,1)S(1)} %copy-done.22, bf16[1024,512]{1,0:T(8,128)(2,1)S(1)} %get-tuple-element.24.refs_3_, ...), custom_call_target="tpu_custom_call" | custom-call | flops 1 | bytes 1 | tf_op jit(solution)/shard_map/pallas_call | solution.py:34
  46.4 2.2 %shard_map.76.refs_5_ = s16[272,512]{1,0:T(8,128)(2,1)} custom-call(s32[3]{0:T(128)S(1)} %pad_add_fusion.refs_0_, bf16[256,512]{1,0:T(8,128)(2,1)S(1)} %copy-done.6, bf16[256,512]{1,0:T(8,128)(2,1)S(1)} %copy-done.18, bf16[1024,512]{1,0:T(8,128)(2,1)S(1)} %get-tuple-element.19.refs_3_, s16[272,512]{1,0:T(8,128)(2,1)} %collective-permute-done.8.refs_4_, ...), custom_call_target="tpu_custom_call" | custom-call | flops 1 | bytes 1 | tf_op jit(solution)/shard_map/pallas_call | solution.py:34
  49.7 2.2 %shard_map.77.refs_5_ = s16[272,512]{1,0:T(8,128)(2,1)} custom-call(s32[3]{0:T(128)S(1)} %pad_add_fusion.refs_0_, bf16[256,512]{1,0:T(8,128)(2,1)S(1)} %copy-done.15, bf16[256,512]{1,0:T(8,128)(2,1)S(1)} %copy-done.12, bf16[1024,512]{1,0:T(8,128)(2,1)S(1)} %get-tuple-element.24.refs_3_, s16[272,512]{1,0:T(8,128)(2,1)} %collective-permute-done.7.refs_4_, ...), custom_call_target="tpu_custom_call" | custom-call | flops 1 | bytes 1 | tf_op jit(solution)/shard_map/pallas_call | solution.py:34
  51.9 2.0 %collective-permute-start.15 = (s16[272,512]{1,0:T(8,128)(2,1)}, s16[272,512]{1,0:T(8,128)(2,1)}, u32[]{:S(2)}, u32[]{:S(2)}) collective-permute-start(s16[272,512]{1,0:T(8,128)(2,1)} %shard_map.77.refs_5_), channel_id=1, source_target_pairs={{0,2},{1,3},{2,4},{3,5},{4,6},{5,7},{6,0},{7,1},{8,10},{9,11},{10,... | collective-permute-start | bytes 835592 | tf_op jit(solution)/shard_map/ppermute | solution.py:178
  53.9 2.2 %shard_map.78.refs_5_ = s16[272,512]{1,0:T(8,128)(2,1)} custom-call(s32[3]{0:T(128)S(1)} %pad_add_fusion.refs_0_, bf16[256,512]{1,0:T(8,128)(2,1)S(1)} %copy-done.3, bf16[256,512]{1,0:T(8,128)(2,1)S(1)} %copy-done.9, bf16[1024,512]{1,0:T(8,128)(2,1)S(1)} %get-tuple-element.19.refs_3_, s16[272,512]{1,0:T(8,128)(2,1)} %collective-permute-done.6.refs_4_, ...), custom_call_target="tpu_custom_call" | custom-call | flops 1 | bytes 1 | tf_op jit(solution)/shard_map/pallas_call | solution.py:34
  59.6 2.2 %shard_map.79.refs_8_ = s16[272,512]{1,0:T(8,128)(2,1)} custom-call(s32[3]{0:T(128)S(1)} %pad_add_fusion.refs_0_, bf16[256,512]{1,0:T(8,128)(2,1)S(1)} %copy-done.7, bf16[256,512]{1,0:T(8,128)(2,1)S(1)} %copy-done.19, bf16[1024,512]{1,0:T(8,128)(2,1)S(1)} %get-tuple-element.24.refs_3_, s16[272,512]{1,0:T(8,128)(2,1)} %collective-permute-done.13.refs_4_, ...), custom_call_target="tpu_custom_call" | custom-call | flops 1 | bytes 1 | tf_op jit(solution)/shard_map/pallas_call | solution.py:34
  64.4 2.4 %shard_map.80.refs_5_.refs_2_ = bf16[256,512]{1,0:T(8,128)(2,1)} custom-call(s32[3]{0:T(128)S(1)} %pad_add_fusion.refs_0_, bf16[256,512]{1,0:T(8,128)(2,1)S(1)} %get-tuple-element.17.refs_3_.refs_1_, bf16[256,512]{1,0:T(8,128)(2,1)S(1)} %copy-done.23, bf16[1024,512]{1,0:T(8,128)(2,1)S(1)} %get-tuple-element.15.refs_3_, ...), custom_call_target="tpu_custom_call" | custom-call | flops 1 | bytes 1 | tf_op jit(solution)/shard_map/pallas_call | solution.py:34
  66.8 2.2 %shard_map.81.refs_8_ = s16[272,512]{1,0:T(8,128)(2,1)} custom-call(s32[3]{0:T(128)S(1)} %pad_add_fusion.refs_0_, bf16[256,512]{1,0:T(8,128)(2,1)S(1)} %copy-done.4, bf16[256,512]{1,0:T(8,128)(2,1)S(1)} %copy-done.10, bf16[1024,512]{1,0:T(8,128)(2,1)S(1)} %get-tuple-element.24.refs_3_, s16[272,512]{1,0:T(8,128)(2,1)} %collective-permute-done.10.refs_4_, ...), custom_call_target="tpu_custom_call" | custom-call | flops 1 | bytes 1 | tf_op jit(solution)/shard_map/pallas_call | solution.py:34
  69.0 2.1 %collective-permute-start.14 = (s16[272,512]{1,0:T(8,128)(2,1)}, s16[272,512]{1,0:T(8,128)(2,1)}, u32[]{:S(2)}, u32[]{:S(2)}) collective-permute-start(s16[272,512]{1,0:T(8,128)(2,1)} %shard_map.81.refs_8_), channel_id=1, source_target_pairs={{0,2},{1,3},{2,4},{3,5},{4,6},{5,7},{6,0},{7,1},{8,10},{9,11},{10,... | collective-permute-start | bytes 835592 | tf_op jit(solution)/shard_map/ppermute | solution.py:178
  71.3 1.6 %shard_map.82.refs_4_.refs_2_ = bf16[256,512]{1,0:T(8,128)(2,1)S(1)} custom-call(s32[3]{0:T(128)S(1)} %pad_add_fusion.refs_0_, bf16[256,512]{1,0:T(8,128)(2,1)S(1)} %copy-done.16, bf16[256,512]{1,0:T(8,128)(2,1)S(1)} %copy-done.13, bf16[1024,512]{1,0:T(8,128)(2,1)S(1)} %get-tuple-element.15.refs_3_, s16[272,512]{1,0:T(8,128)(2,1)} %collective-permute-done.7.refs_4_, ...), custom_call_target="tpu_custom_call" | custom-call | flops 1 | bytes 1 | tf_op jit(solution)/shard_map/pallas_call | solution.py:34
  72.9 1.8 %collective-permute-start.16 = (bf16[256,512]{1,0:T(8,128)(2,1)S(1)}, bf16[256,512]{1,0:T(8,128)(2,1)S(1)}, u32[]{:S(2)}, u32[]{:S(2)}) collective-permute-start(bf16[256,512]{1,0:T(8,128)(2,1)S(1)} %shard_map.82.refs_4_.refs_2_), channel_id=1, source_target_pairs={{0,16},{8,24},{16,0},{24,8},{1,17},{9,25},{17,1},{25,9},{2,18},{10... | collective-permute-start | bytes 786440 | tf_op jit(solution)/shard_map/ppermute | solution.py:169
  75.1 5.0 %collective-permute-done.17.refs_3_ = bf16[256,512]{1,0:T(8,128)(2,1)} collective-permute-done((bf16[256,512]{1,0:T(8,128)(2,1)}, bf16[256,512]{1,0:T(8,128)(2,1)}, u32[]{:S(2)}, u32[]{:S(2)}) %collective-permute-start.17) | collective-permute-done | bytes 262176 | tf_op jit(solution)/shard_map/ppermute | solution.py:169
  81.5 1.6 %shard_map.84.refs_5_.refs_2_ = bf16[256,512]{1,0:T(8,128)(2,1)S(1)} custom-call(s32[3]{0:T(128)S(1)} %pad_add_fusion.refs_0_, bf16[256,512]{1,0:T(8,128)(2,1)S(1)} %copy-done.7, bf16[256,512]{1,0:T(8,128)(2,1)S(1)} %copy-done.20, bf16[1024,512]{1,0:T(8,128)(2,1)S(1)} %get-tuple-element.15.refs_3_, s16[272,512]{1,0:T(8,128)(2,1)} %collective-permute-done.13.refs_4_, ...), custom_call_target="tpu_custom_call" | custom-call | flops 1 | bytes 1 | tf_op jit(solution)/shard_map/pallas_call | solution.py:34
  84.0 1.7 %collective-permute-done.16.refs_3_ = bf16[256,512]{1,0:T(8,128)(2,1)S(1)} collective-permute-done((bf16[256,512]{1,0:T(8,128)(2,1)S(1)}, bf16[256,512]{1,0:T(8,128)(2,1)S(1)}, u32[]{:S(2)}, u32[]{:S(2)}) %collective-permute-start.16) | collective-permute-done | bytes 262176 | tf_op jit(solution)/shard_map/ppermute | solution.py:169
  90.5 4.1 %collective-permute-done.19.refs_3_ = bf16[256,512]{1,0:T(8,128)(2,1)S(1)} collective-permute-done((bf16[256,512]{1,0:T(8,128)(2,1)S(1)}, bf16[256,512]{1,0:T(8,128)(2,1)S(1)}, u32[]{:S(2)}, u32[]{:S(2)}) %collective-permute-start.19) | collective-permute-done | bytes 262176 | tf_op jit(solution)/shard_map/ppermute | solution.py:169
  94.6 2.3 %shard_map.88 = bf16[2048,512]{1,0:T(8,128)(2,1)} custom-call(s32[3]{0:T(128)S(1)} %pad_add_fusion.refs_0_, s32[2048,1]{1,0:T(8,128)S(1)} %copy.14.refs_1_, bf16[256,512]{1,0:T(8,128)(2,1)S(1)} %shard_map.86.refs_5_.refs_2_, bf16[256,512]{1,0:T(8,128)(2,1)S(1)} %collective-permute-done.19.refs_3_, bf16[2048,512]{1,0:T(8,128)(2,1)S(1)} %shard_map.87.refs_4_.refs_5_, ...), custom_call_target="tpu_custom_call" | custom-call | flops 1 | bytes 1 | tf_op jit(solution)/shard_map/pallas_call | solution.py:34
  (105 shorter events, 27.6 us)
Async XLA Ops:
  2.9 10.1 %collective-permute-start.2 = (bf16[256,512]{1,0:T(8,128)(2,1)S(1)}, bf16[256,512]{1,0:T(8,128)(2,1)S(1)}, u32[]{:S(2)}, u32[]{:S(2)}) collective-permute-start(bf16[256,512]{1,0:T(8,128)(2,1)S(1)} %shard_map.64.refs_2_), channel_id=1, source_target_pairs={{0,16},{8,24},{16,0},{24,8},{1,17},{9,25},{17,1},{25,9},{2,18},{10... | collective-permute-start | bytes 786440 | tf_op jit(solution)/shard_map/ppermute | solution.py:169
  10.6 8.0 %collective-permute-start.1 = (bf16[256,512]{1,0:T(8,128)(2,1)S(1)}, bf16[256,512]{1,0:T(8,128)(2,1)S(1)}, u32[]{:S(2)}, u32[]{:S(2)}) collective-permute-start(bf16[256,512]{1,0:T(8,128)(2,1)S(1)} %shard_map.66.refs_3_), channel_id=1, source_target_pairs={{0,16},{8,24},{16,0},{24,8},{1,17},{9,25},{17,1},{25,9},{2,18},{10... | collective-permute-start | bytes 786440 | tf_op jit(solution)/shard_map/ppermute | solution.py:169
  12.0 18.5 %copy-start.5 = (bf16[256,512]{1,0:T(8,128)(2,1)}, bf16[256,512]{1,0:T(8,128)(2,1)S(1)}, u32[]{:S(2)}) copy-start(bf16[256,512]{1,0:T(8,128)(2,1)S(1)} %get-tuple-element.22.refs_1_) | copy-start | bytes 786436
  12.0 21.9 %copy-start.14 = (bf16[256,512]{1,0:T(8,128)(2,1)}, bf16[256,512]{1,0:T(8,128)(2,1)S(1)}, u32[]{:S(2)}) copy-start(bf16[256,512]{1,0:T(8,128)(2,1)S(1)} %get-tuple-element.21.refs_1_) | copy-start | bytes 786436
  12.0 25.2 %copy-start.2 = (bf16[256,512]{1,0:T(8,128)(2,1)}, bf16[256,512]{1,0:T(8,128)(2,1)S(1)}, u32[]{:S(2)}) copy-start(bf16[256,512]{1,0:T(8,128)(2,1)S(1)} %get-tuple-element.16.refs_1_) | copy-start | bytes 786436
  13.0 11.5 %copy-start.21 = (bf16[256,512]{1,0:T(8,128)(2,1)}, bf16[256,512]{1,0:T(8,128)(2,1)S(1)}, u32[]{:S(2)}) copy-start(bf16[256,512]{1,0:T(8,128)(2,1)S(1)} %collective-permute-done.2.refs_2_) | copy-start | bytes 786436
  13.0 10.2 %copy-start.27 = (s32[2048]{0:T(1024)S(1)}, s32[2048]{0:T(1024)}, u32[]{:S(2)}) copy-start(s32[2048]{0:T(1024)} %param.8) | copy-start | bytes 24580
  14.1 10.5 %collective-permute-start.5 = (s16[272,512]{1,0:T(8,128)(2,1)S(1)}, s16[272,512]{1,0:T(8,128)(2,1)S(1)}, u32[]{:S(2)}, u32[]{:S(2)}) collective-permute-start(s16[272,512]{1,0:T(8,128)(2,1)S(1)} %shard_map.69.refs_4_), channel_id=1, source_target_pairs={{0,2},{1,3},{2,4},{3,5},{4,6},{5,7},{6,0},{7,1},{8,10},{9,11},{10,... | collective-permute-start | bytes 835592 | tf_op jit(solution)/shard_map/ppermute | solution.py:178
  18.6 15.3 %copy-start.11 = (bf16[256,512]{1,0:T(8,128)(2,1)}, bf16[256,512]{1,0:T(8,128)(2,1)S(1)}, u32[]{:S(2)}) copy-start(bf16[256,512]{1,0:T(8,128)(2,1)S(1)} %collective-permute-done.1.refs_2_) | copy-start | bytes 786436
  19.6 14.2 %collective-permute-start.3 = (s16[272,512]{1,0:T(8,128)(2,1)S(1)}, s16[272,512]{1,0:T(8,128)(2,1)S(1)}, u32[]{:S(2)}, u32[]{:S(2)}) collective-permute-start(s16[272,512]{1,0:T(8,128)(2,1)S(1)} %shard_map.70.refs_5_), channel_id=1, source_target_pairs={{0,2},{1,3},{2,4},{3,5},{4,6},{5,7},{6,0},{7,1},{8,10},{9,11},{10,... | collective-permute-start | bytes 835592 | tf_op jit(solution)/shard_map/ppermute | solution.py:178
  21.2 9.2 %collective-permute-start.4 = (bf16[256,512]{1,0:T(8,128)(2,1)S(1)}, bf16[256,512]{1,0:T(8,128)(2,1)S(1)}, u32[]{:S(2)}, u32[]{:S(2)}) collective-permute-start(bf16[256,512]{1,0:T(8,128)(2,1)S(1)} %get-tuple-element.23), channel_id=1, source_target_pairs={{0,16},{8,24},{16,0},{24,8},{1,17},{9,25},{17,1},{25,9},{2,18},{10... | collective-permute-start | bytes 786440 | tf_op jit(solution)/shard_map/ppermute | solution.py:169
  23.0 14.2 %collective-permute-start = (bf16[256,512]{1,0:T(8,128)(2,1)S(1)}, bf16[256,512]{1,0:T(8,128)(2,1)S(1)}, u32[]{:S(2)}, u32[]{:S(2)}) collective-permute-start(bf16[256,512]{1,0:T(8,128)(2,1)S(1)} %get-tuple-element.18.refs_4_), channel_id=1, source_target_pairs={{0,16},{8,24},{16,0},{24,8},{1,17},{9,25},{17,1},{25,9},{2,18},{10... | collective-permute-start | bytes 786440 | tf_op jit(solution)/shard_map/ppermute | solution.py:169
  26.3 16.6 %collective-permute-start.9 = (s16[272,512]{1,0:T(8,128)(2,1)}, s16[272,512]{1,0:T(8,128)(2,1)}, u32[]{:S(2)}, u32[]{:S(2)}) collective-permute-start(s16[272,512]{1,0:T(8,128)(2,1)} %shard_map.71.refs_4_), channel_id=1, source_target_pairs={{0,1},{1,0},{2,3},{3,2},{4,5},{5,4},{6,7},{7,6},{8,9},{9,8},{10,11... | collective-permute-start | bytes 835592 | tf_op jit(solution)/shard_map/ppermute | solution.py:173
  32.3 8.3 %copy-start.28 = (f32[200]{0:T(256)S(1)}, f32[200]{0:T(256)}, u32[]{:S(2)}) copy-start(f32[200]{0:T(256)} %param.10) | copy-start | bytes 2404
  32.3 14.2 %collective-permute-start.8 = (s16[272,512]{1,0:T(8,128)(2,1)}, s16[272,512]{1,0:T(8,128)(2,1)}, u32[]{:S(2)}, u32[]{:S(2)}) collective-permute-start(s16[272,512]{1,0:T(8,128)(2,1)} %shard_map.72.refs_5_), channel_id=1, source_target_pairs={{0,2},{1,3},{2,4},{3,5},{4,6},{5,7},{6,0},{7,1},{8,10},{9,11},{10,... | collective-permute-start | bytes 835592 | tf_op jit(solution)/shard_map/ppermute | solution.py:178
  35.6 14.1 %collective-permute-start.7 = (s16[272,512]{1,0:T(8,128)(2,1)}, s16[272,512]{1,0:T(8,128)(2,1)}, u32[]{:S(2)}, u32[]{:S(2)}) collective-permute-start(s16[272,512]{1,0:T(8,128)(2,1)} %shard_map.73.refs_4_), channel_id=1, source_target_pairs={{0,1},{1,0},{2,3},{3,2},{4,5},{5,4},{6,7},{7,6},{8,9},{9,8},{10,11... | collective-permute-start | bytes 835592 | tf_op jit(solution)/shard_map/ppermute | solution.py:173
  38.9 15.0 %collective-permute-start.6 = (s16[272,512]{1,0:T(8,128)(2,1)}, s16[272,512]{1,0:T(8,128)(2,1)}, u32[]{:S(2)}, u32[]{:S(2)}) collective-permute-start(s16[272,512]{1,0:T(8,128)(2,1)} %shard_map.74.refs_5_), channel_id=1, source_target_pairs={{0,2},{1,3},{2,4},{3,5},{4,6},{5,7},{6,0},{7,1},{8,10},{9,11},{10,... | collective-permute-start | bytes 835592 | tf_op jit(solution)/shard_map/ppermute | solution.py:178
  41.1 16.5 %collective-permute-start.12 = (f32[1024]{0:T(1024)S(1)}, f32[1024]{0:T(1024)S(1)}, u32[]{:S(2)}, u32[]{:S(2)}) collective-permute-start(f32[1024]{0:T(1024)S(1)} %slice.9), channel_id=1, source_target_pairs={{0,16},{8,24},{16,0},{24,8},{1,17},{9,25},{17,1},{25,9},{2,18},{10... | collective-permute-start | bytes 12296 | tf_op jit(solution)/shard_map/ppermute | solution.py:169
  46.2 7.7 %copy-start.9 = (bf16[256,512]{1,0:T(8,128)(2,1)S(1)}, bf16[256,512]{1,0:T(8,128)(2,1)}, u32[]{:S(2)}) copy-start(bf16[256,512]{1,0:T(8,128)(2,1)} %copy-done.8) | copy-start | bytes 786436
  46.2 17.2 %collective-permute-start.11 = (s16[272,512]{1,0:T(8,128)(2,1)}, s16[272,512]{1,0:T(8,128)(2,1)}, u32[]{:S(2)}, u32[]{:S(2)}) collective-permute-start(s16[272,512]{1,0:T(8,128)(2,1)} %shard_map.75.refs_5_), channel_id=1, source_target_pairs={{0,2},{1,3},{2,4},{3,5},{4,6},{5,7},{6,0},{7,1},{8,10},{9,11},{10,... | collective-permute-start | bytes 835592 | tf_op jit(solution)/shard_map/ppermute | solution.py:178
  48.6 8.0 %copy-start.29 = (f32[2000]{0:T(1024)S(1)}, f32[2000]{0:T(1024)}, u32[]{:S(2)}) copy-start(f32[2000]{0:T(1024)} %param.11) | copy-start | bytes 24004
  48.6 9.0 %collective-permute-start.13 = (s16[272,512]{1,0:T(8,128)(2,1)}, s16[272,512]{1,0:T(8,128)(2,1)}, u32[]{:S(2)}, u32[]{:S(2)}) collective-permute-start(s16[272,512]{1,0:T(8,128)(2,1)} %shard_map.76.refs_5_), channel_id=1, source_target_pairs={{0,1},{1,0},{2,3},{3,2},{4,5},{5,4},{6,7},{7,6},{8,9},{9,8},{10,11... | collective-permute-start | bytes 835592 | tf_op jit(solution)/shard_map/ppermute | solution.py:173
  51.9 19.4 %collective-permute-start.15 = (s16[272,512]{1,0:T(8,128)(2,1)}, s16[272,512]{1,0:T(8,128)(2,1)}, u32[]{:S(2)}, u32[]{:S(2)}) collective-permute-start(s16[272,512]{1,0:T(8,128)(2,1)} %shard_map.77.refs_5_), channel_id=1, source_target_pairs={{0,2},{1,3},{2,4},{3,5},{4,6},{5,7},{6,0},{7,1},{8,10},{9,11},{10,... | collective-permute-start | bytes 835592 | tf_op jit(solution)/shard_map/ppermute | solution.py:178
  56.1 10.6 %collective-permute-start.10 = (s16[272,512]{1,0:T(8,128)(2,1)}, s16[272,512]{1,0:T(8,128)(2,1)}, u32[]{:S(2)}, u32[]{:S(2)}) collective-permute-start(s16[272,512]{1,0:T(8,128)(2,1)} %shard_map.78.refs_5_), channel_id=1, source_target_pairs={{0,1},{1,0},{2,3},{3,2},{4,5},{5,4},{6,7},{7,6},{8,9},{9,8},{10,11... | collective-permute-start | bytes 835592 | tf_op jit(solution)/shard_map/ppermute | solution.py:173
  57.6 9.1 %copy-start.4 = (bf16[256,512]{1,0:T(8,128)(2,1)S(1)}, bf16[256,512]{1,0:T(8,128)(2,1)}, u32[]{:S(2)}) copy-start(bf16[256,512]{1,0:T(8,128)(2,1)} %copy-done.2) | copy-start | bytes 786436
  61.9 19.6 %collective-permute-start.18 = (s16[272,512]{1,0:T(8,128)(2,1)}, s16[272,512]{1,0:T(8,128)(2,1)}, u32[]{:S(2)}, u32[]{:S(2)}) collective-permute-start(s16[272,512]{1,0:T(8,128)(2,1)} %shard_map.79.refs_8_), channel_id=1, source_target_pairs={{0,2},{1,3},{2,4},{3,5},{4,6},{5,7},{6,0},{7,1},{8,10},{9,11},{10,... | collective-permute-start | bytes 835592 | tf_op jit(solution)/shard_map/ppermute | solution.py:178
  66.7 8.0 %copy-start.26 = (s32[2048]{0:T(1024)S(1)}, s32[2048]{0:T(1024)}, u32[]{:S(2)}) copy-start(s32[2048]{0:T(1024)} %param.9) | copy-start | bytes 24580
  69.0 17.7 %collective-permute-start.14 = (s16[272,512]{1,0:T(8,128)(2,1)}, s16[272,512]{1,0:T(8,128)(2,1)}, u32[]{:S(2)}, u32[]{:S(2)}) collective-permute-start(s16[272,512]{1,0:T(8,128)(2,1)} %shard_map.81.refs_8_), channel_id=1, source_target_pairs={{0,2},{1,3},{2,4},{3,5},{4,6},{5,7},{6,0},{7,1},{8,10},{9,11},{10,... | collective-permute-start | bytes 835592 | tf_op jit(solution)/shard_map/ppermute | solution.py:178
  71.0 9.1 %collective-permute-start.17 = (bf16[256,512]{1,0:T(8,128)(2,1)}, bf16[256,512]{1,0:T(8,128)(2,1)}, u32[]{:S(2)}, u32[]{:S(2)}) collective-permute-start(bf16[256,512]{1,0:T(8,128)(2,1)} %shard_map.80.refs_5_.refs_2_), channel_id=1, source_target_pairs={{0,16},{8,24},{16,0},{24,8},{1,17},{9,25},{17,1},{25,9},{2,18},{10... | collective-permute-start | bytes 786440 | tf_op jit(solution)/shard_map/ppermute | solution.py:169
  72.9 12.7 %collective-permute-start.16 = (bf16[256,512]{1,0:T(8,128)(2,1)S(1)}, bf16[256,512]{1,0:T(8,128)(2,1)S(1)}, u32[]{:S(2)}, u32[]{:S(2)}) collective-permute-start(bf16[256,512]{1,0:T(8,128)(2,1)S(1)} %shard_map.82.refs_4_.refs_2_), channel_id=1, source_target_pairs={{0,16},{8,24},{16,0},{24,8},{1,17},{9,25},{17,1},{25,9},{2,18},{10... | collective-permute-start | bytes 786440 | tf_op jit(solution)/shard_map/ppermute | solution.py:169
  83.1 6.4 %collective-permute-start.20 = (bf16[256,512]{1,0:T(8,128)(2,1)S(1)}, bf16[256,512]{1,0:T(8,128)(2,1)S(1)}, u32[]{:S(2)}, u32[]{:S(2)}) collective-permute-start(bf16[256,512]{1,0:T(8,128)(2,1)S(1)} %shard_map.84.refs_5_.refs_2_), channel_id=1, source_target_pairs={{0,16},{8,24},{16,0},{24,8},{1,17},{9,25},{17,1},{25,9},{2,18},{10... | collective-permute-start | bytes 786440 | tf_op jit(solution)/shard_map/ppermute | solution.py:169
  88.2 6.4 %collective-permute-start.19 = (bf16[256,512]{1,0:T(8,128)(2,1)S(1)}, bf16[256,512]{1,0:T(8,128)(2,1)S(1)}, u32[]{:S(2)}, u32[]{:S(2)}) collective-permute-start(bf16[256,512]{1,0:T(8,128)(2,1)S(1)} %shard_map.86.refs_5_.refs_2_), channel_id=1, source_target_pairs={{0,16},{8,24},{16,0},{24,8},{1,17},{9,25},{17,1},{25,9},{2,18},{10... | collective-permute-start | bytes 786440 | tf_op jit(solution)/shard_map/ppermute | solution.py:169
  (19 other events, 75.9 us)

commit v4 on v3

v4 whole, which is shorter than its diff:
```python
import functools

import jax
import jax.numpy as jnp
from jax import lax
from jax.experimental import pallas as pl
from jax.experimental.pallas import tpu as pltpu
from jax.sharding import PartitionSpec as P

NOCC = 200
NV = 2000
CHUNKS = 4
SCALE_ROWS = 16
TOP = 32767.0
STEPS = 64.0
TINY = 1e-33
LANES = 128
VMEM_LIMIT = 8 * 1024 * 1024
KERNEL_BYTES = 300 * 1024
ORDER = (
    (("align", 0), ("align", 1), ("energy", 0), ("first", 0), ("align", 2), ("first", 1))
    + (("align", 3), ("first", 2), ("second", 0), ("second", 1), ("first", 3), ("third", 0))
    + (("second", 2), ("third", 1), ("second", 3), ("third", 2), ("last", 0), ("third", 3))
    + (("last", 1), ("last", 2), ("place", 0), ("last", 3), ("place", 1), ("place", 2))
    + (("place", 3),)
)
ALIGNED = (
    ((0, True),),
    ((1, True), (0, False)),
    ((2, True), (1, False)),
    ((3, True), (2, False), (3, False)),
)

VMEM = pl.BlockSpec(memory_space=pltpu.VMEM)
SMEM = pl.BlockSpec(memory_space=pltpu.SMEM)
ANY = pl.BlockSpec(memory_space=pl.ANY)


def call(body, out_shape, operands, after=()):
    count = len(operands)

    def kernel(*refs):
        body(*refs[:count], *refs[count + len(after) :])

    return pl.pallas_call(
        kernel,
        out_shape=out_shape,
        in_specs=[SMEM] + [VMEM] * (count - 1) + [ANY] * len(after),
        out_specs=jax.tree.map(lambda _: VMEM, out_shape),
        compiler_params=pltpu.CompilerParams(vmem_limit_bytes=VMEM_LIMIT),
        cost_estimate=pl.CostEstimate(flops=1, bytes_accessed=KERNEL_BYTES, transcendentals=0),
    )(*operands, *after)


def exchanged(values):
    even = lax.broadcasted_iota(jnp.int32, (values.shape[0], LANES), 1) % 2 == 0
    parts = []
    for lane in range(0, values.shape[1], LANES):
        part = values[:, lane : lane + LANES]
        parts.append(jnp.where(even, pltpu.roll(part, LANES - 1, 1), pltpu.roll(part, 1, 1)))
    return jnp.concatenate(parts, axis=1)


def align_kernel(wanted, flags, partner, amplitudes, *outs):
    rows = amplitudes.shape[0]
    chunk = outs[0].shape[0]
    upper = flags[0]

    def first(index):
        begin, send = wanted[index]
        return (1 - upper if send else upper) * (rows // 2) + begin

    @pl.when(upper == 0)
    def _():
        for index, out in enumerate(outs):
            out[...] = amplitudes[pl.ds(pl.multiple_of(first(index), chunk), chunk), :]

    @pl.when(upper == 1)
    def _():
        for index, out in enumerate(outs):
            target = flags[2] + first(index) + lax.broadcasted_iota(jnp.int32, (chunk, rows), 0)
            pick = jnp.where(partner[...] == target, 1.0, 0.0).astype(jnp.bfloat16)
            out[...] = jnp.dot(pick, amplitudes[...], preferred_element_type=jnp.float32).astype(jnp.bfloat16)


def product(stop, own, other, integrals):
    factor = integrals[:, pl.ds(stop * own.shape[1], own.shape[1])]
    direct = jnp.dot(own[...], factor, preferred_element_type=jnp.float32)
    return direct + exchanged(jnp.dot(other[...], factor, preferred_element_type=jnp.float32))


def code(values, out):
    rows = values.shape[0]
    top = jnp.max(jnp.abs(values), axis=0, keepdims=True)
    level = jnp.ceil(STEPS * jnp.log2(jnp.maximum(top, TINY) * (1.0001 / TOP)))
    coded = jnp.round(values * jnp.exp2(level * (-1.0 / STEPS)))
    out[pl.ds(0, rows), :] = coded.astype(jnp.int32).astype(jnp.int16)
    spread = jnp.broadcast_to(level.astype(jnp.int32), (SCALE_ROWS, values.shape[1]))
    out[pl.ds(rows, SCALE_ROWS), :] = spread.astype(jnp.int16)


def decode(coded):
    rows = coded.shape[0] - SCALE_ROWS
    level = coded[pl.ds(rows, SCALE_ROWS), :].astype(jnp.int32).astype(jnp.float32)[0:1, :]
    return coded[pl.ds(0, rows), :].astype(jnp.int32).astype(jnp.float32) * jnp.exp2(level * (1.0 / STEPS))


def first_kernel(flags, own, other, integrals, out):
    code(product(3, own, other, integrals), out)


def second_kernel(flags, own, other, integrals, arrived, out):
    code(product(1, own, other, integrals) + decode(arrived), out)


def third_kernel(flags, own, other, integrals, crossed, out):
    here = jnp.where(flags[1] == 0, 1.0, 0.0)
    code(product(2, own, other, integrals) + decode(crossed) * here, out)


def last_kernel(index, flags, own, other, integrals, crossed, arrived, occ_here, occ_there, vir_sum, out):
    chunk, width = out.shape
    here = jnp.where(flags[1] == 1, 1.0, 0.0)
    total = product(0, own, other, integrals) + decode(arrived) + decode(crossed) * here
    part = pl.ds(index * chunk, chunk)
    occ_rows = jnp.where(flags[0] == 0, occ_here[:, part], occ_there[:, part])
    occ_down = jnp.broadcast_to(occ_rows, (LANES, chunk)).T
    for lane in range(0, width, LANES):
        denom = vir_sum[:, lane : lane + LANES] - occ_down
        out[:, lane : lane + LANES] = (total[:, lane : lane + LANES] / denom).astype(jnp.bfloat16)


def place_kernel(index, flags, partner, own, other, *refs):
    out = refs[-1]
    rows, width = out.shape
    chunk = own.shape[0]
    upper = flags[0]
    here = upper * (rows // 2) + index * chunk
    there = (1 - upper) * (rows // 2) + index * chunk
    opposite = exchanged(other[...].astype(jnp.float32)).astype(jnp.bfloat16)

    @pl.when(upper == 0)
    def _():
        if index:
            out[...] = refs[0][...]
        out[pl.ds(pl.multiple_of(here, chunk), chunk), :] = own[...]
        out[pl.ds(pl.multiple_of(there, chunk), chunk), :] = opposite

    @pl.when(upper == 1)
    def _():
        block = 256
        lanes = lax.broadcasted_iota(jnp.int32, (block, LANES), 1) + flags[2]

        def pick(slots, begin):
            parts = [jnp.where(slots == lanes + (begin + lane), 1.0, 0.0) for lane in range(0, chunk, LANES)]
            return jnp.concatenate(parts, axis=1).astype(jnp.bfloat16)

        for begin in range(0, rows, block):
            part = pl.ds(begin, block)
            slots = jnp.broadcast_to(partner[:, part], (LANES, block)).T
            found = jnp.dot(pick(slots, here), own[...], preferred_element_type=jnp.float32)
            found += jnp.dot(pick(slots, there), opposite, preferred_element_type=jnp.float32)
            if index:
                found += refs[0][part, :].astype(jnp.float32)
            out[part, :] = found.astype(jnp.bfloat16)


def split_index(values, count):
    high = jnp.floor((values.astype(jnp.float32) + 0.5) * (1.0 / count)).astype(jnp.int32)
    return high, values - high * count


def lookup(table, positions):
    found = jnp.zeros(positions.shape, jnp.float32)
    for begin in range(0, table.shape[1], LANES):
        size = min(LANES, table.shape[1] - begin)
        part = jnp.broadcast_to(table[:, begin : begin + size], (size, size))
        down = lax.broadcasted_iota(jnp.int32, (size, size), 0)
        across = lax.broadcasted_iota(jnp.int32, (size, size), 1)
        column = jnp.sum(jnp.where(down == across, part, 0.0), axis=1, keepdims=True)
        entry = begin + lax.broadcasted_iota(jnp.int32, (size, positions.shape[1]), 0)
        found += jnp.sum(jnp.where(entry == positions, column, 0.0), axis=0, keepdims=True)
    return found


def energy_kernel(flags, pair_index, occ_energy, vir_energy, occ_lower, occ_upper, vir_sum):
    half = occ_lower.shape[1]
    for out, begin in ((occ_lower, 0), (occ_upper, half)):
        first, second = split_index(pair_index[:, pl.ds(begin, half)], NOCC)
        out[...] = lookup(occ_energy[...], first) + lookup(occ_energy[...], second)
    width = vir_sum.shape[1]
    unordered = flags[3] * (width // 2) + lax.broadcasted_iota(jnp.int32, (1, width), 1) // 2
    first, second = split_index(unordered, NV)
    vir_sum[...] = lookup(vir_energy[...], first) + lookup(vir_energy[...], second)


def across_rows(value):
    count = lax.axis_size("row")
    return lax.ppermute(value, "row", [(i, i ^ (count // 2)) for i in range(count)])


def across_pair(value):
    return lax.ppermute(value, "col", [(i, i ^ 1) for i in range(lax.axis_size("col"))])


def two_along(value):
    count = lax.axis_size("col")
    return lax.ppermute(value, "col", [(i, (i + 2) % count) for i in range(count)])


def shards(amplitudes, integrals, pair_index, partner, occ_energy, vir_energy):
    rows, width = amplitudes.shape
    half = rows // 2
    chunk = half // CHUNKS
    row_count = lax.axis_size("row")
    row = lax.axis_index("row")
    upper = (row // (row_count // 2)).astype(jnp.int32)
    col = lax.axis_index("col").astype(jnp.int32)
    odd = col % 2
    partner_base = ((row ^ (row_count // 2)) * rows).astype(jnp.int32)
    flags = jnp.stack([upper, odd, partner_base, col])

    chunk_shape = jax.ShapeDtypeStruct((chunk, width), jnp.bfloat16)
    coded_shape = jax.ShapeDtypeStruct((chunk + SCALE_ROWS, width), jnp.int16)
    whole_shape = jax.ShapeDtypeStruct((rows, width), jnp.bfloat16)

    def align(wanted, after=()):
        return call(
            functools.partial(align_kernel, wanted),
            [chunk_shape] * len(wanted),
            (flags, partner[None, :], amplitudes),
            after,
        )

    half_shape = jax.ShapeDtypeStruct((1, half), jnp.float32)
    energy_shapes = [half_shape, half_shape, jax.ShapeDtypeStruct((1, width), jnp.float32)]

    own, other, moved, crossed, arrived, done, placed = {}, {}, {}, {}, {}, {}, ()
    last = ()
    for step, index in ORDER:
        if step == "align":
            wanted = [(begin * chunk, send) for begin, send in ALIGNED[index]]
            result = align(wanted, last)
            for (begin, send), picked in zip(ALIGNED[index], result):
                if send:
                    other[begin] = across_rows(picked)
                else:
                    own[begin] = picked
            last = result[:1]
            continue
        if step == "energy":
            occ_lower, occ_upper, vir_sum = call(
                energy_kernel,
                energy_shapes,
                (flags, pair_index[None, :], occ_energy[None, :], vir_energy[None, :]),
                last,
            )
            occ_there = across_rows(occ_upper)
            last = (vir_sum,)
            continue
        inputs = (flags, own[index], other[index], integrals)
        if step == "first":
            result = call(first_kernel, coded_shape, inputs, last)
            moved[index] = two_along(result)
        elif step == "second":
            result = call(second_kernel, coded_shape, (*inputs, moved[index]), last)
            crossed[index] = across_pair(result)
        elif step == "third":
            result = call(third_kernel, coded_shape, (*inputs, crossed[index]), last)
            arrived[index] = two_along(result)
        elif step == "last":
            sums = (crossed[index], arrived[index], occ_lower, occ_there, vir_sum)
            result = call(functools.partial(last_kernel, index), chunk_shape, (*inputs, *sums), last)
            done[index] = (result, across_rows(result))
        else:
            ready = (flags, partner[None, :], *done[index], *placed)
            result = call(functools.partial(place_kernel, index), whole_shape, ready, last)
            placed = (result,)
        last = (result,)
    return result


def solution(mesh):
    in_specs = (P("row", "col"), P("col", None), P("row"), P("row"), P(), P())
    out_specs = P("row", "col")
    return jax.shard_map(shards, mesh=mesh, in_specs=in_specs, out_specs=out_specs, check_vma=False)
```

time: 97.5 us -> 84.6 us (0.87)
  Pallas kernels: 39.3 us -> 28.2 us
  local copies, waits for them, and re-layouts: 8.21 us -> 2.32 us
  waiting for transfers between devices: 18.5 us -> 23.3 us
  other arithmetic: 1.62 us -> 0.08 us
  starting transfers between devices: 29 us -> 30 us
    pallas_call x25, Pallas kernels: 39.3 us -> 28.2 us  [call(): pl.pallas_call(kernel, out_shape=out_shape, in_specs=[SMEM] + [VMEM] * (c...]
    ppermute x8, waiting for transfers between devices: 1.28 us -> 9.24 us  [two_along(): lax.ppermute(value, 'col', [(i, (i + 2) % count) for i in range(count)])]
    unnamed x60 -> x16, local copies, waits for them, and re-layouts: 7.84 us -> 2.32 us
    ppermute x9, starting transfers between devices: 12.1 us -> 16.3 us  [across_rows(): lax.ppermute(value, 'row', [(i, i ^ count // 2) for i in range(count)])]
    ppermute x9, waiting for transfers between devices: 17.2 us -> 13.3 us  [across_rows(): lax.ppermute(value, 'row', [(i, i ^ count // 2) for i in range(count)])]
    ppermute x8, starting transfers between devices: 12.3 us -> 8.98 us  [two_along(): lax.ppermute(value, 'col', [(i, (i + 2) % count) for i in range(count)])]
    reduce_sum x2 -> x0, other arithmetic: 1.49 us -> none  [table_lookup(): jnp.sum(jnp.where(positions[:, None] == slots[None, :], table[None, :], 0...]
  transfers between devices with their start and end apart: 21 -> 21, of which waited for: 8 -> 11; matrix products, arithmetic and copies ran while one was open for 2% -> 0% of each run, Pallas kernels for 38% -> 30%
where the time goes in v4:
time: 84.6 us; the launch traced here: 84.2 us
  starting transfers between devices  30 us (35%)
  Pallas kernels  28.2 us (33%)
  waiting for transfers between devices  23.3 us (28%)
  local copies, waits for them, and re-layouts  2.32 us (3%)
    pallas_call x25, Pallas kernels, call(): pl.pallas_call(kernel, out_shape=out_shape, in_specs=[SMEM] + [VMEM] * (c...  28.2 us
    ppermute x9, starting transfers between devices, across_rows(): lax.ppermute(value, 'row', [(i, i ^ count // 2) for i in range(count)])  16.3 us
    ppermute x9, waiting for transfers between devices, across_rows(): lax.ppermute(value, 'row', [(i, i ^ count // 2) for i in range(count)])  13.3 us
    ppermute x8, waiting for transfers between devices, two_along(): lax.ppermute(value, 'col', [(i, (i + 2) % count) for i in range(count)])  9.24 us
    ppermute x8, starting transfers between devices, two_along(): lax.ppermute(value, 'col', [(i, (i + 2) % count) for i in range(count)])  8.98 us
    ppermute x4, starting transfers between devices, across_pair(): lax.ppermute(value, 'col', [(i, i ^ 1) for i in range(lax.axis_size('col'...  4.77 us
    unnamed x16, local copies, waits for them, and re-layouts  2.32 us
  transfers between devices with their start and end apart: 21, of which 11 were waited for; matrix products, arithmetic and copies ran while one was open for 0% of the time, Pallas kernels for 30%

profile of v4, /device:TPU:0, one launch (start us, length us, event | category | flops | bytes accessed | tf_op | source)
XLA Modules:
  0.0 84.2 jit_solution(10149061066359440529)
XLA Ops:
  0.1 1.6 %copy-done.1 = bf16[2048,512]{1,0:T(8,128)(2,1)S(1)} copy-done((bf16[2048,512]{1,0:T(8,128)(2,1)S(1)}, bf16[2048,512]{1,0:T(8,128)(2,1)}, u32[]{:S(2)}) %copy-start.1) | copy-done | bytes 2097176
  3.0 3.7 %collective-permute-start = (bf16[256,512]{1,0:T(8,128)(2,1)S(1)}, bf16[256,512]{1,0:T(8,128)(2,1)S(1)}, u32[]{:S(2)}, u32[]{:S(2)}) collective-permute-start(bf16[256,512]{1,0:T(8,128)(2,1)S(1)} %shard_map.64.refs_3_), channel_id=1, source_target_pairs={{0,16},{8,24},{16,0},{24,8},{1,17},{9,25},{17,1},{25,9},{2,18},{10... | collective-permute-start | bytes 786440 | tf_op jit(solution)/shard_map/ppermute | solution.py:199
  7.3 1.3 %collective-permute-start.1 = (bf16[256,512]{1,0:T(8,128)(2,1)S(1)}, bf16[256,512]{1,0:T(8,128)(2,1)S(1)}, u32[]{:S(2)}, u32[]{:S(2)}) collective-permute-start(bf16[256,512]{1,0:T(8,128)(2,1)S(1)} %get-tuple-element.16.refs_4_), channel_id=1, source_target_pairs={{0,16},{8,24},{16,0},{24,8},{1,17},{9,25},{17,1},{25,9},{2,18},{10... | collective-permute-start | bytes 786440 | tf_op jit(solution)/shard_map/ppermute | solution.py:199
  8.6 2.2 %shard_map.66 = (f32[1,1024]{1,0:T(1,128)S(1)}, f32[1,1024]{1,0:T(1,128)S(1)}, f32[1,512]{1,0:T(1,128)S(1)}) custom-call(s32[4]{0:T(128)S(1)} %pad_add_fusion.refs_0_, s32[1,2048]{1,0:T(1,128)S(1)} %bitcast.16, f32[1,200]{1,0:T(1,128)S(1)} %bitcast.18, f32[1,2000]{1,0:T(1,128)S(1)} %bitcast.17, bf16[256,512]{1,0:T(8,128)(2,1)S(1)} %get-tuple-element.16.refs_4_), custom_call_target="tpu_custom_call" | custom-call | flops 1 | bytes 307200 | tf_op jit(solution)/shard_map/pallas_call | solution.py:45
  10.7 3.1 %collective-permute-done.refs_2_ = bf16[256,512]{1,0:T(8,128)(2,1)S(1)} collective-permute-done((bf16[256,512]{1,0:T(8,128)(2,1)S(1)}, bf16[256,512]{1,0:T(8,128)(2,1)S(1)}, u32[]{:S(2)}, u32[]{:S(2)}) %collective-permute-start) | collective-permute-done | bytes 262176 | tf_op jit(solution)/shard_map/ppermute | solution.py:199
  15.0 1.6 %collective-permute-start.4 = (s16[272,512]{1,0:T(8,128)(2,1)S(1)}, s16[272,512]{1,0:T(8,128)(2,1)S(1)}, u32[]{:S(2)}, u32[]{:S(2)}) collective-permute-start(s16[272,512]{1,0:T(8,128)(2,1)S(1)} %shard_map.67.refs_3_), channel_id=1, source_target_pairs={{0,2},{1,3},{2,4},{3,5},{4,6},{5,7},{6,0},{7,1},{8,10},{9,11},{10,... | collective-permute-start | bytes 835592 | tf_op jit(solution)/shard_map/ppermute | solution.py:208
  17.2 1.4 %collective-permute-done.1.refs_2_ = bf16[256,512]{1,0:T(8,128)(2,1)S(1)} collective-permute-done((bf16[256,512]{1,0:T(8,128)(2,1)S(1)}, bf16[256,512]{1,0:T(8,128)(2,1)S(1)}, u32[]{:S(2)}, u32[]{:S(2)}) %collective-permute-start.1) | collective-permute-done | bytes 262176 | tf_op jit(solution)/shard_map/ppermute | solution.py:199
  19.8 1.6 %collective-permute-start.3 = (s16[272,512]{1,0:T(8,128)(2,1)S(1)}, s16[272,512]{1,0:T(8,128)(2,1)S(1)}, u32[]{:S(2)}, u32[]{:S(2)}) collective-permute-start(s16[272,512]{1,0:T(8,128)(2,1)S(1)} %shard_map.69.refs_3_), channel_id=1, source_target_pairs={{0,2},{1,3},{2,4},{3,5},{4,6},{5,7},{6,0},{7,1},{8,10},{9,11},{10,... | collective-permute-start | bytes 835592 | tf_op jit(solution)/shard_map/ppermute | solution.py:208
  21.4 1.9 %collective-permute-start.5 = (bf16[256,512]{1,0:T(8,128)(2,1)S(1)}, bf16[256,512]{1,0:T(8,128)(2,1)S(1)}, u32[]{:S(2)}, u32[]{:S(2)}) collective-permute-start(bf16[256,512]{1,0:T(8,128)(2,1)S(1)} %get-tuple-element.19.refs_4_), channel_id=1, source_target_pairs={{0,16},{8,24},{16,0},{24,8},{1,17},{9,25},{17,1},{25,9},{2,18},{10... | collective-permute-start | bytes 786440 | tf_op jit(solution)/shard_map/ppermute | solution.py:199
  23.9 1.9 %collective-permute-start.2 = (bf16[256,512]{1,0:T(8,128)(2,1)S(1)}, bf16[256,512]{1,0:T(8,128)(2,1)S(1)}, u32[]{:S(2)}, u32[]{:S(2)}) collective-permute-start(bf16[256,512]{1,0:T(8,128)(2,1)S(1)} %get-tuple-element.21.refs_4_), channel_id=1, source_target_pairs={{0,16},{8,24},{16,0},{24,8},{1,17},{9,25},{17,1},{25,9},{2,18},{10... | collective-permute-start | bytes 786440 | tf_op jit(solution)/shard_map/ppermute | solution.py:199
  25.8 4.8 %collective-permute-done.5.refs_2_ = bf16[256,512]{1,0:T(8,128)(2,1)S(1)} collective-permute-done((bf16[256,512]{1,0:T(8,128)(2,1)S(1)}, bf16[256,512]{1,0:T(8,128)(2,1)S(1)}, u32[]{:S(2)}, u32[]{:S(2)}) %collective-permute-start.5) | collective-permute-done | bytes 262176 | tf_op jit(solution)/shard_map/ppermute | solution.py:199
  33.0 1.6 %collective-permute-start.9 = (s16[272,512]{1,0:T(8,128)(2,1)S(1)}, s16[272,512]{1,0:T(8,128)(2,1)S(1)}, u32[]{:S(2)}, u32[]{:S(2)}) collective-permute-start(s16[272,512]{1,0:T(8,128)(2,1)S(1)} %shard_map.72.refs_5_), channel_id=1, source_target_pairs={{0,1},{1,0},{2,3},{3,2},{4,5},{5,4},{6,7},{7,6},{8,9},{9,8},{10,11... | collective-permute-start | bytes 835592 | tf_op jit(solution)/shard_map/ppermute | solution.py:203
  34.6 1.6 %collective-permute-start.8 = (s16[272,512]{1,0:T(8,128)(2,1)S(1)}, s16[272,512]{1,0:T(8,128)(2,1)S(1)}, u32[]{:S(2)}, u32[]{:S(2)}) collective-permute-start(s16[272,512]{1,0:T(8,128)(2,1)S(1)} %shard_map.71.refs_5_), channel_id=1, source_target_pairs={{0,2},{1,3},{2,4},{3,5},{4,6},{5,7},{6,0},{7,1},{8,10},{9,11},{10,... | collective-permute-start | bytes 835592 | tf_op jit(solution)/shard_map/ppermute | solution.py:208
  36.2 1.2 %shard_map.73.refs_4_ = s16[272,512]{1,0:T(8,128)(2,1)S(1)} custom-call(s32[4]{0:T(128)S(1)} %pad_add_fusion.refs_0_, bf16[256,512]{1,0:T(8,128)(2,1)S(1)} %get-tuple-element.18.refs_1_, bf16[256,512]{1,0:T(8,128)(2,1)S(1)} %collective-permute-done.1.refs_2_, bf16[512,2048]{1,0:T(8,128)(2,1)S(1)} %copy-done, ...), custom_call_target="tpu_custom_call" | custom-call | flops 1 | bytes 307200 | tf_op jit(solution)/shard_map/pallas_call | solution.py:45
  39.1 1.6 %collective-permute-start.6 = (s16[272,512]{1,0:T(8,128)(2,1)S(1)}, s16[272,512]{1,0:T(8,128)(2,1)S(1)}, u32[]{:S(2)}, u32[]{:S(2)}) collective-permute-start(s16[272,512]{1,0:T(8,128)(2,1)S(1)} %shard_map.74.refs_5_), channel_id=1, source_target_pairs={{0,2},{1,3},{2,4},{3,5},{4,6},{5,7},{6,0},{7,1},{8,10},{9,11},{10,... | collective-permute-start | bytes 835592 | tf_op jit(solution)/shard_map/ppermute | solution.py:208
  42.7 3.0 %collective-permute-done.8.refs_4_ = s16[272,512]{1,0:T(8,128)(2,1)S(1)} collective-permute-done((s16[272,512]{1,0:T(8,128)(2,1)S(1)}, s16[272,512]{1,0:T(8,128)(2,1)S(1)}, u32[]{:S(2)}, u32[]{:S(2)}) %collective-permute-start.8) | collective-permute-done | bytes 278560 | tf_op jit(solution)/shard_map/ppermute | solution.py:208
  45.7 1.2 %shard_map.76.refs_5_ = s16[272,512]{1,0:T(8,128)(2,1)S(1)} custom-call(s32[4]{0:T(128)S(1)} %pad_add_fusion.refs_0_, bf16[256,512]{1,0:T(8,128)(2,1)S(1)} %get-tuple-element.22.refs_1_, bf16[256,512]{1,0:T(8,128)(2,1)S(1)} %collective-permute-done.5.refs_2_, bf16[512,2048]{1,0:T(8,128)(2,1)S(1)} %copy-done, ...), custom_call_target="tpu_custom_call" | custom-call | flops 1 | bytes 307200 | tf_op jit(solution)/shard_map/pallas_call | solution.py:45
  47.7 1.2 %shard_map.77.refs_5_ = s16[272,512]{1,0:T(8,128)(2,1)S(1)} custom-call(s32[4]{0:T(128)S(1)} %pad_add_fusion.refs_0_, bf16[256,512]{1,0:T(8,128)(2,1)S(1)} %get-tuple-element.18.refs_1_, bf16[256,512]{1,0:T(8,128)(2,1)S(1)} %collective-permute-done.1.refs_2_, bf16[512,2048]{1,0:T(8,128)(2,1)S(1)} %copy-done, ...), custom_call_target="tpu_custom_call" | custom-call | flops 1 | bytes 307200 | tf_op jit(solution)/shard_map/pallas_call | solution.py:45
  48.9 1.8 %collective-permute-done.6.refs_4_ = s16[272,512]{1,0:T(8,128)(2,1)S(1)} collective-permute-done((s16[272,512]{1,0:T(8,128)(2,1)S(1)}, s16[272,512]{1,0:T(8,128)(2,1)S(1)}, u32[]{:S(2)}, u32[]{:S(2)}) %collective-permute-start.6) | collective-permute-done | bytes 278560 | tf_op jit(solution)/shard_map/ppermute | solution.py:208
  50.7 1.2 %shard_map.78.refs_5_ = s16[272,512]{1,0:T(8,128)(2,1)S(1)} custom-call(s32[4]{0:T(128)S(1)} %pad_add_fusion.refs_0_, bf16[256,512]{1,0:T(8,128)(2,1)S(1)} %get-tuple-element.20.refs_1_, bf16[256,512]{1,0:T(8,128)(2,1)S(1)} %collective-permute-done.2.refs_2_, bf16[512,2048]{1,0:T(8,128)(2,1)S(1)} %copy-done, ...), custom_call_target="tpu_custom_call" | custom-call | flops 1 | bytes 307200 | tf_op jit(solution)/shard_map/pallas_call | solution.py:45
  51.9 1.8 %collective-permute-start.10 = (s16[272,512]{1,0:T(8,128)(2,1)S(1)}, s16[272,512]{1,0:T(8,128)(2,1)S(1)}, u32[]{:S(2)}, u32[]{:S(2)}) collective-permute-start(s16[272,512]{1,0:T(8,128)(2,1)S(1)} %shard_map.78.refs_5_), channel_id=1, source_target_pairs={{0,1},{1,0},{2,3},{3,2},{4,5},{5,4},{6,7},{7,6},{8,9},{9,8},{10,11... | collective-permute-start | bytes 835592 | tf_op jit(solution)/shard_map/ppermute | solution.py:203
  55.2 1.2 %shard_map.79.refs_9_ = s16[272,512]{1,0:T(8,128)(2,1)S(1)} custom-call(s32[4]{0:T(128)S(1)} %pad_add_fusion.refs_0_, bf16[256,512]{1,0:T(8,128)(2,1)S(1)} %get-tuple-element.22.refs_1_, bf16[256,512]{1,0:T(8,128)(2,1)S(1)} %collective-permute-done.5.refs_2_, bf16[512,2048]{1,0:T(8,128)(2,1)S(1)} %copy-done, ...), custom_call_target="tpu_custom_call" | custom-call | flops 1 | bytes 307200 | tf_op jit(solution)/shard_map/pallas_call | solution.py:45
  56.4 1.6 %collective-permute-start.16 = (s16[272,512]{1,0:T(8,128)(2,1)S(1)}, s16[272,512]{1,0:T(8,128)(2,1)S(1)}, u32[]{:S(2)}, u32[]{:S(2)}) collective-permute-start(s16[272,512]{1,0:T(8,128)(2,1)S(1)} %shard_map.79.refs_9_), channel_id=1, source_target_pairs={{0,2},{1,3},{2,4},{3,5},{4,6},{5,7},{6,0},{7,1},{8,10},{9,11},{10,... | collective-permute-start | bytes 835592 | tf_op jit(solution)/shard_map/ppermute | solution.py:208
  60.3 1.2 %shard_map.81.refs_9_ = s16[272,512]{1,0:T(8,128)(2,1)S(1)} custom-call(s32[4]{0:T(128)S(1)} %pad_add_fusion.refs_0_, bf16[256,512]{1,0:T(8,128)(2,1)S(1)} %get-tuple-element.20.refs_1_, bf16[256,512]{1,0:T(8,128)(2,1)S(1)} %collective-permute-done.2.refs_2_, bf16[512,2048]{1,0:T(8,128)(2,1)S(1)} %copy-done, ...), custom_call_target="tpu_custom_call" | custom-call | flops 1 | bytes 307200 | tf_op jit(solution)/shard_map/pallas_call | solution.py:45
  61.5 2.0 %collective-permute-start.15 = (bf16[256,512]{1,0:T(8,128)(2,1)S(1)}, bf16[256,512]{1,0:T(8,128)(2,1)S(1)}, u32[]{:S(2)}, u32[]{:S(2)}) collective-permute-start(bf16[256,512]{1,0:T(8,128)(2,1)S(1)} %shard_map.80.refs_5_.refs_2_), channel_id=1, source_target_pairs={{0,16},{8,24},{16,0},{24,8},{1,17},{9,25},{17,1},{25,9},{2,18},{10... | collective-permute-start | bytes 786440 | tf_op jit(solution)/shard_map/ppermute | solution.py:199
  63.5 2.3 %collective-permute-done.17.refs_5_ = s16[272,512]{1,0:T(8,128)(2,1)S(1)} collective-permute-done((s16[272,512]{1,0:T(8,128)(2,1)S(1)}, s16[272,512]{1,0:T(8,128)(2,1)S(1)}, u32[]{:S(2)}, u32[]{:S(2)}) %collective-permute-start.17) | collective-permute-done | bytes 278560 | tf_op jit(solution)/shard_map/ppermute | solution.py:208
  67.0 1.3 %collective-permute-start.20 = (bf16[256,512]{1,0:T(8,128)(2,1)S(1)}, bf16[256,512]{1,0:T(8,128)(2,1)S(1)}, u32[]{:S(2)}, u32[]{:S(2)}) collective-permute-start(bf16[256,512]{1,0:T(8,128)(2,1)S(1)} %shard_map.82.refs_9_.refs_2_), channel_id=1, source_target_pairs={{0,16},{8,24},{16,0},{24,8},{1,17},{9,25},{17,1},{25,9},{2,18},{10... | collective-permute-start | bytes 786440 | tf_op jit(solution)/shard_map/ppermute | solution.py:199
  70.7 1.8 %collective-permute-start.19 = (bf16[256,512]{1,0:T(8,128)(2,1)S(1)}, bf16[256,512]{1,0:T(8,128)(2,1)S(1)}, u32[]{:S(2)}, u32[]{:S(2)}) collective-permute-start(bf16[256,512]{1,0:T(8,128)(2,1)S(1)} %shard_map.83.refs_4_.refs_2_), channel_id=1, source_target_pairs={{0,16},{8,24},{16,0},{24,8},{1,17},{9,25},{17,1},{25,9},{2,18},{10... | collective-permute-start | bytes 786440 | tf_op jit(solution)/shard_map/ppermute | solution.py:199
  74.5 1.6 %collective-permute-start.18 = (bf16[256,512]{1,0:T(8,128)(2,1)S(1)}, bf16[256,512]{1,0:T(8,128)(2,1)S(1)}, u32[]{:S(2)}, u32[]{:S(2)}) collective-permute-start(bf16[256,512]{1,0:T(8,128)(2,1)S(1)} %shard_map.85.refs_5_.refs_2_), channel_id=1, source_target_pairs={{0,16},{8,24},{16,0},{24,8},{1,17},{9,25},{17,1},{25,9},{2,18},{10... | collective-permute-start | bytes 786440 | tf_op jit(solution)/shard_map/ppermute | solution.py:199
  77.0 2.2 %collective-permute-done.19.refs_3_ = bf16[256,512]{1,0:T(8,128)(2,1)S(1)} collective-permute-done((bf16[256,512]{1,0:T(8,128)(2,1)S(1)}, bf16[256,512]{1,0:T(8,128)(2,1)S(1)}, u32[]{:S(2)}, u32[]{:S(2)}) %collective-permute-start.19) | collective-permute-done | bytes 262176 | tf_op jit(solution)/shard_map/ppermute | solution.py:199
  80.1 1.9 %collective-permute-done.18.refs_3_ = bf16[256,512]{1,0:T(8,128)(2,1)S(1)} collective-permute-done((bf16[256,512]{1,0:T(8,128)(2,1)S(1)}, bf16[256,512]{1,0:T(8,128)(2,1)S(1)}, u32[]{:S(2)}, u32[]{:S(2)}) %collective-permute-start.18) | collective-permute-done | bytes 262176 | tf_op jit(solution)/shard_map/ppermute | solution.py:199
  82.0 2.2 %shard_map.88 = bf16[2048,512]{1,0:T(8,128)(2,1)} custom-call(s32[4]{0:T(128)S(1)} %pad_add_fusion.refs_0_, s32[1,2048]{1,0:T(1,128)S(1)} %bitcast.15, bf16[256,512]{1,0:T(8,128)(2,1)S(1)} %shard_map.85.refs_5_.refs_2_, bf16[256,512]{1,0:T(8,128)(2,1)S(1)} %collective-permute-done.18.refs_3_, bf16[2048,512]{1,0:T(8,128)(2,1)S(1)} %shard_map.87.refs_4_.refs_5_, ...), custom_call_target="tpu_custom_call" | custom-call | flops 1 | bytes 307200 | tf_op jit(solution)/shard_map/pallas_call | solution.py:45
  (52 shorter events, 23.5 us)
Async XLA Ops:
  0.1 1.6 %copy-start.1 = (bf16[2048,512]{1,0:T(8,128)(2,1)S(1)}, bf16[2048,512]{1,0:T(8,128)(2,1)}, u32[]{:S(2)}) copy-start(bf16[2048,512]{1,0:T(8,128)(2,1)} %refs_2_.7) | copy-start | bytes 6291460
  1.7 0.7 copy-start.3
  2.4 6.2 %copy-start.5 = (s32[2048]{0:T(1024)S(1)}, s32[2048]{0:T(1024)}, u32[]{:S(2)}) copy-start(s32[2048]{0:T(1024)} %param.8) | copy-start | bytes 24580
  2.4 6.2 %copy-start.6 = (f32[2000]{0:T(1024)S(1)}, f32[2000]{0:T(1024)}, u32[]{:S(2)}) copy-start(f32[2000]{0:T(1024)} %param.11) | copy-start | bytes 24004
  2.4 6.2 %copy-start.7 = (f32[200]{0:T(256)S(1)}, f32[200]{0:T(256)}, u32[]{:S(2)}) copy-start(f32[200]{0:T(256)} %param.10) | copy-start | bytes 2404
  2.4 11.4 %copy-start = (bf16[512,2048]{1,0:T(8,128)(2,1)S(1)}, bf16[512,2048]{1,0:T(8,128)(2,1)}, u32[]{:S(2)}) copy-start(bf16[512,2048]{1,0:T(8,128)(2,1)} %refs_3_.31) | copy-start | bytes 6291460
  3.0 10.8 %collective-permute-start = (bf16[256,512]{1,0:T(8,128)(2,1)S(1)}, bf16[256,512]{1,0:T(8,128)(2,1)S(1)}, u32[]{:S(2)}, u32[]{:S(2)}) collective-permute-start(bf16[256,512]{1,0:T(8,128)(2,1)S(1)} %shard_map.64.refs_3_), channel_id=1, source_target_pairs={{0,16},{8,24},{16,0},{24,8},{1,17},{9,25},{17,1},{25,9},{2,18},{10... | collective-permute-start | bytes 786440 | tf_op jit(solution)/shard_map/ppermute | solution.py:199
  7.2 9.4 %copy-start.2 = (bf16[2048,512]{1,0:T(8,128)(2,1)S(1)}, bf16[2048,512]{1,0:T(8,128)(2,1)}, u32[]{:S(2)}) copy-start(bf16[2048,512]{1,0:T(8,128)(2,1)} %refs_2_.7) | copy-start | bytes 6291460
  7.2 9.4 %copy-start.4 = (s32[2048]{0:T(1024)S(1)}, s32[2048]{0:T(1024)}, u32[]{:S(2)}) copy-start(s32[2048]{0:T(1024)} %param.9) | copy-start | bytes 24580
  7.3 11.3 %collective-permute-start.1 = (bf16[256,512]{1,0:T(8,128)(2,1)S(1)}, bf16[256,512]{1,0:T(8,128)(2,1)S(1)}, u32[]{:S(2)}, u32[]{:S(2)}) collective-permute-start(bf16[256,512]{1,0:T(8,128)(2,1)S(1)} %get-tuple-element.16.refs_4_), channel_id=1, source_target_pairs={{0,16},{8,24},{16,0},{24,8},{1,17},{9,25},{17,1},{25,9},{2,18},{10... | collective-permute-start | bytes 786440 | tf_op jit(solution)/shard_map/ppermute | solution.py:199
  15.0 16.8 %collective-permute-start.4 = (s16[272,512]{1,0:T(8,128)(2,1)S(1)}, s16[272,512]{1,0:T(8,128)(2,1)S(1)}, u32[]{:S(2)}, u32[]{:S(2)}) collective-permute-start(s16[272,512]{1,0:T(8,128)(2,1)S(1)} %shard_map.67.refs_3_), channel_id=1, source_target_pairs={{0,2},{1,3},{2,4},{3,5},{4,6},{5,7},{6,0},{7,1},{8,10},{9,11},{10,... | collective-permute-start | bytes 835592 | tf_op jit(solution)/shard_map/ppermute | solution.py:208
  19.8 16.4 %collective-permute-start.3 = (s16[272,512]{1,0:T(8,128)(2,1)S(1)}, s16[272,512]{1,0:T(8,128)(2,1)S(1)}, u32[]{:S(2)}, u32[]{:S(2)}) collective-permute-start(s16[272,512]{1,0:T(8,128)(2,1)S(1)} %shard_map.69.refs_3_), channel_id=1, source_target_pairs={{0,2},{1,3},{2,4},{3,5},{4,6},{5,7},{6,0},{7,1},{8,10},{9,11},{10,... | collective-permute-start | bytes 835592 | tf_op jit(solution)/shard_map/ppermute | solution.py:208
  21.4 9.2 %collective-permute-start.5 = (bf16[256,512]{1,0:T(8,128)(2,1)S(1)}, bf16[256,512]{1,0:T(8,128)(2,1)S(1)}, u32[]{:S(2)}, u32[]{:S(2)}) collective-permute-start(bf16[256,512]{1,0:T(8,128)(2,1)S(1)} %get-tuple-element.19.refs_4_), channel_id=1, source_target_pairs={{0,16},{8,24},{16,0},{24,8},{1,17},{9,25},{17,1},{25,9},{2,18},{10... | collective-permute-start | bytes 786440 | tf_op jit(solution)/shard_map/ppermute | solution.py:199
  23.9 14.1 %collective-permute-start.2 = (bf16[256,512]{1,0:T(8,128)(2,1)S(1)}, bf16[256,512]{1,0:T(8,128)(2,1)S(1)}, u32[]{:S(2)}, u32[]{:S(2)}) collective-permute-start(bf16[256,512]{1,0:T(8,128)(2,1)S(1)} %get-tuple-element.21.refs_4_), channel_id=1, source_target_pairs={{0,16},{8,24},{16,0},{24,8},{1,17},{9,25},{17,1},{25,9},{2,18},{10... | collective-permute-start | bytes 786440 | tf_op jit(solution)/shard_map/ppermute | solution.py:199
  33.0 8.5 %collective-permute-start.9 = (s16[272,512]{1,0:T(8,128)(2,1)S(1)}, s16[272,512]{1,0:T(8,128)(2,1)S(1)}, u32[]{:S(2)}, u32[]{:S(2)}) collective-permute-start(s16[272,512]{1,0:T(8,128)(2,1)S(1)} %shard_map.72.refs_5_), channel_id=1, source_target_pairs={{0,1},{1,0},{2,3},{3,2},{4,5},{5,4},{6,7},{7,6},{8,9},{9,8},{10,11... | collective-permute-start | bytes 835592 | tf_op jit(solution)/shard_map/ppermute | solution.py:203
  34.6 11.0 %collective-permute-start.8 = (s16[272,512]{1,0:T(8,128)(2,1)S(1)}, s16[272,512]{1,0:T(8,128)(2,1)S(1)}, u32[]{:S(2)}, u32[]{:S(2)}) collective-permute-start(s16[272,512]{1,0:T(8,128)(2,1)S(1)} %shard_map.71.refs_5_), channel_id=1, source_target_pairs={{0,2},{1,3},{2,4},{3,5},{4,6},{5,7},{6,0},{7,1},{8,10},{9,11},{10,... | collective-permute-start | bytes 835592 | tf_op jit(solution)/shard_map/ppermute | solution.py:208
  37.4 10.3 %collective-permute-start.7 = (s16[272,512]{1,0:T(8,128)(2,1)S(1)}, s16[272,512]{1,0:T(8,128)(2,1)S(1)}, u32[]{:S(2)}, u32[]{:S(2)}) collective-permute-start(s16[272,512]{1,0:T(8,128)(2,1)S(1)} %shard_map.73.refs_4_), channel_id=1, source_target_pairs={{0,1},{1,0},{2,3},{3,2},{4,5},{5,4},{6,7},{7,6},{8,9},{9,8},{10,11... | collective-permute-start | bytes 835592 | tf_op jit(solution)/shard_map/ppermute | solution.py:203
  39.1 11.6 %collective-permute-start.6 = (s16[272,512]{1,0:T(8,128)(2,1)S(1)}, s16[272,512]{1,0:T(8,128)(2,1)S(1)}, u32[]{:S(2)}, u32[]{:S(2)}) collective-permute-start(s16[272,512]{1,0:T(8,128)(2,1)S(1)} %shard_map.74.refs_5_), channel_id=1, source_target_pairs={{0,2},{1,3},{2,4},{3,5},{4,6},{5,7},{6,0},{7,1},{8,10},{9,11},{10,... | collective-permute-start | bytes 835592 | tf_op jit(solution)/shard_map/ppermute | solution.py:208
  46.8 8.4 %collective-permute-start.13 = (s16[272,512]{1,0:T(8,128)(2,1)S(1)}, s16[272,512]{1,0:T(8,128)(2,1)S(1)}, u32[]{:S(2)}, u32[]{:S(2)}) collective-permute-start(s16[272,512]{1,0:T(8,128)(2,1)S(1)} %shard_map.76.refs_5_), channel_id=1, source_target_pairs={{0,1},{1,0},{2,3},{3,2},{4,5},{5,4},{6,7},{7,6},{8,9},{9,8},{10,11... | collective-permute-start | bytes 835592 | tf_op jit(solution)/shard_map/ppermute | solution.py:203
  47.7 11.4 %collective-permute-start.11 = (s16[272,512]{1,0:T(8,128)(2,1)S(1)}, s16[272,512]{1,0:T(8,128)(2,1)S(1)}, u32[]{:S(2)}, u32[]{:S(2)}) collective-permute-start(s16[272,512]{1,0:T(8,128)(2,1)S(1)} %shard_map.75.refs_5_), channel_id=1, source_target_pairs={{0,2},{1,3},{2,4},{3,5},{4,6},{5,7},{6,0},{7,1},{8,10},{9,11},{10,... | collective-permute-start | bytes 835592 | tf_op jit(solution)/shard_map/ppermute | solution.py:208
  51.9 8.3 %collective-permute-start.10 = (s16[272,512]{1,0:T(8,128)(2,1)S(1)}, s16[272,512]{1,0:T(8,128)(2,1)S(1)}, u32[]{:S(2)}, u32[]{:S(2)}) collective-permute-start(s16[272,512]{1,0:T(8,128)(2,1)S(1)} %shard_map.78.refs_5_), channel_id=1, source_target_pairs={{0,1},{1,0},{2,3},{3,2},{4,5},{5,4},{6,7},{7,6},{8,9},{9,8},{10,11... | collective-permute-start | bytes 835592 | tf_op jit(solution)/shard_map/ppermute | solution.py:203
  53.7 4.4 %collective-permute-start.12 = (f32[1,1024]{1,0:T(1,128)S(1)}, f32[1,1024]{1,0:T(1,128)S(1)}, u32[]{:S(2)}, u32[]{:S(2)}) collective-permute-start(f32[1,1024]{1,0:T(1,128)S(1)} %get-tuple-element.24), channel_id=1, source_target_pairs={{0,16},{8,24},{16,0},{24,8},{1,17},{9,25},{17,1},{25,9},{2,18},{10... | collective-permute-start | bytes 12296 | tf_op jit(solution)/shard_map/ppermute | solution.py:199
  54.4 11.4 %collective-permute-start.17 = (s16[272,512]{1,0:T(8,128)(2,1)S(1)}, s16[272,512]{1,0:T(8,128)(2,1)S(1)}, u32[]{:S(2)}, u32[]{:S(2)}) collective-permute-start(s16[272,512]{1,0:T(8,128)(2,1)S(1)} %shard_map.77.refs_5_), channel_id=1, source_target_pairs={{0,2},{1,3},{2,4},{3,5},{4,6},{5,7},{6,0},{7,1},{8,10},{9,11},{10,... | collective-permute-start | bytes 835592 | tf_op jit(solution)/shard_map/ppermute | solution.py:208
  56.4 13.1 %collective-permute-start.16 = (s16[272,512]{1,0:T(8,128)(2,1)S(1)}, s16[272,512]{1,0:T(8,128)(2,1)S(1)}, u32[]{:S(2)}, u32[]{:S(2)}) collective-permute-start(s16[272,512]{1,0:T(8,128)(2,1)S(1)} %shard_map.79.refs_9_), channel_id=1, source_target_pairs={{0,2},{1,3},{2,4},{3,5},{4,6},{5,7},{6,0},{7,1},{8,10},{9,11},{10,... | collective-permute-start | bytes 835592 | tf_op jit(solution)/shard_map/ppermute | solution.py:208
  61.5 11.8 %collective-permute-start.14 = (s16[272,512]{1,0:T(8,128)(2,1)S(1)}, s16[272,512]{1,0:T(8,128)(2,1)S(1)}, u32[]{:S(2)}, u32[]{:S(2)}) collective-permute-start(s16[272,512]{1,0:T(8,128)(2,1)S(1)} %shard_map.81.refs_9_), channel_id=1, source_target_pairs={{0,2},{1,3},{2,4},{3,5},{4,6},{5,7},{6,0},{7,1},{8,10},{9,11},{10,... | collective-permute-start | bytes 835592 | tf_op jit(solution)/shard_map/ppermute | solution.py:208
  61.5 11.0 %collective-permute-start.15 = (bf16[256,512]{1,0:T(8,128)(2,1)S(1)}, bf16[256,512]{1,0:T(8,128)(2,1)S(1)}, u32[]{:S(2)}, u32[]{:S(2)}) collective-permute-start(bf16[256,512]{1,0:T(8,128)(2,1)S(1)} %shard_map.80.refs_5_.refs_2_), channel_id=1, source_target_pairs={{0,16},{8,24},{16,0},{24,8},{1,17},{9,25},{17,1},{25,9},{2,18},{10... | collective-permute-start | bytes 786440 | tf_op jit(solution)/shard_map/ppermute | solution.py:199
  67.0 9.1 %collective-permute-start.20 = (bf16[256,512]{1,0:T(8,128)(2,1)S(1)}, bf16[256,512]{1,0:T(8,128)(2,1)S(1)}, u32[]{:S(2)}, u32[]{:S(2)}) collective-permute-start(bf16[256,512]{1,0:T(8,128)(2,1)S(1)} %shard_map.82.refs_9_.refs_2_), channel_id=1, source_target_pairs={{0,16},{8,24},{16,0},{24,8},{1,17},{9,25},{17,1},{25,9},{2,18},{10... | collective-permute-start | bytes 786440 | tf_op jit(solution)/shard_map/ppermute | solution.py:199
  70.7 8.5 %collective-permute-start.19 = (bf16[256,512]{1,0:T(8,128)(2,1)S(1)}, bf16[256,512]{1,0:T(8,128)(2,1)S(1)}, u32[]{:S(2)}, u32[]{:S(2)}) collective-permute-start(bf16[256,512]{1,0:T(8,128)(2,1)S(1)} %shard_map.83.refs_4_.refs_2_), channel_id=1, source_target_pairs={{0,16},{8,24},{16,0},{24,8},{1,17},{9,25},{17,1},{25,9},{2,18},{10... | collective-permute-start | bytes 786440 | tf_op jit(solution)/shard_map/ppermute | solution.py:199
  74.5 7.5 %collective-permute-start.18 = (bf16[256,512]{1,0:T(8,128)(2,1)S(1)}, bf16[256,512]{1,0:T(8,128)(2,1)S(1)}, u32[]{:S(2)}, u32[]{:S(2)}) collective-permute-start(bf16[256,512]{1,0:T(8,128)(2,1)S(1)} %shard_map.85.refs_5_.refs_2_), channel_id=1, source_target_pairs={{0,16},{8,24},{16,0},{24,8},{1,17},{9,25},{17,1},{25,9},{2,18},{10... | collective-permute-start | bytes 786440 | tf_op jit(solution)/shard_map/ppermute | solution.py:199

commit v5 on v4

--- a/solution.py
+++ b/solution.py
@@ -16,7 +16,7 @@
 TINY = 1e-33
 LANES = 128
 VMEM_LIMIT = 8 * 1024 * 1024
-KERNEL_BYTES = 300 * 1024
+KERNEL_FLOPS = 4 * 10**9
 ORDER = (
     (("align", 0), ("align", 1), ("energy", 0), ("first", 0), ("align", 2), ("first", 1))
     + (("align", 3), ("first", 2), ("second", 0), ("second", 1), ("first", 3), ("third", 0))
@@ -48,7 +48,7 @@
         in_specs=[SMEM] + [VMEM] * (count - 1) + [ANY] * len(after),
         out_specs=jax.tree.map(lambda _: VMEM, out_shape),
         compiler_params=pltpu.CompilerParams(vmem_limit_bytes=VMEM_LIMIT),
-        cost_estimate=pl.CostEstimate(flops=1, bytes_accessed=KERNEL_BYTES, transcendentals=0),
+        cost_estimate=pl.CostEstimate(flops=KERNEL_FLOPS, bytes_accessed=1, transcendentals=0),
     )(*operands, *after)
 
 

time: 84.6 us -> 79.1 us (0.935)
  waiting for transfers between devices: 23.3 us -> 13.7 us
  starting transfers between devices: 30 us -> 34.3 us
    ppermute x8, waiting for transfers between devices: 9.24 us -> 2.27 us  [two_along(): lax.ppermute(value, 'col', [(i, (i + 2) % count) for i in range(count)])]
    ppermute x9, waiting for transfers between devices: 13.3 us -> 7.49 us  [across_rows(): lax.ppermute(value, 'row', [(i, i ^ count // 2) for i in range(count)])]
    ppermute x8, starting transfers between devices: 8.98 us -> 12.3 us  [two_along(): lax.ppermute(value, 'col', [(i, (i + 2) % count) for i in range(count)])]
    ppermute x4, waiting for transfers between devices: 0.73 us -> 3.95 us  [across_pair(): lax.ppermute(value, 'col', [(i, i ^ 1) for i in range(lax.axis_size('col'...]
  transfers between devices with their start and end apart: 21 -> 21, of which waited for: 11 -> 8; matrix products, arithmetic and copies ran while one was open for 0% -> 0% of each run, Pallas kernels for 30% -> 32%
where the time goes in v5:
time: 79.1 us; the launch traced here: 78.9 us
  starting transfers between devices  34.3 us (43%)
  Pallas kernels  28.2 us (36%)
  waiting for transfers between devices  13.7 us (17%)
  local copies, waits for them, and re-layouts  2.32 us (3%)
    pallas_call x25, Pallas kernels, call(): pl.pallas_call(kernel, out_shape=out_shape, in_specs=[SMEM] + [VMEM] * (c...  28.2 us
    ppermute x9, starting transfers between devices, across_rows(): lax.ppermute(value, 'row', [(i, i ^ count // 2) for i in range(count)])  16.4 us
    ppermute x8, starting transfers between devices, two_along(): lax.ppermute(value, 'col', [(i, (i + 2) % count) for i in range(count)])  12.3 us
    ppermute x9, waiting for transfers between devices, across_rows(): lax.ppermute(value, 'row', [(i, i ^ count // 2) for i in range(count)])  7.49 us
    ppermute x4, starting transfers between devices, across_pair(): lax.ppermute(value, 'col', [(i, i ^ 1) for i in range(lax.axis_size('col'...  5.56 us
    ppermute x4, waiting for transfers between devices, across_pair(): lax.ppermute(value, 'col', [(i, i ^ 1) for i in range(lax.axis_size('col'...  3.95 us
    unnamed x16, local copies, waits for them, and re-layouts  2.32 us
    ppermute x8, waiting for transfers between devices, two_along(): lax.ppermute(value, 'col', [(i, (i + 2) % count) for i in range(count)])  2.27 us
  transfers between devices with their start and end apart: 21, of which 8 were waited for; matrix products, arithmetic and copies ran while one was open for 0% of the time, Pallas kernels for 32%

profile of v5, /device:TPU:0, one launch (start us, length us, event | category | flops | bytes accessed | tf_op | source)
XLA Modules:
  0.0 78.9 jit_solution(8216189829574688279)
XLA Ops:
  0.1 1.6 %copy-done = bf16[2048,512]{1,0:T(8,128)(2,1)S(1)} copy-done((bf16[2048,512]{1,0:T(8,128)(2,1)S(1)}, bf16[2048,512]{1,0:T(8,128)(2,1)}, u32[]{:S(2)}) %copy-start) | copy-done | bytes 2097176
  3.0 3.7 %collective-permute-start = (bf16[256,512]{1,0:T(8,128)(2,1)S(1)}, bf16[256,512]{1,0:T(8,128)(2,1)S(1)}, u32[]{:S(2)}, u32[]{:S(2)}) collective-permute-start(bf16[256,512]{1,0:T(8,128)(2,1)S(1)} %shard_map.64.refs_3_), channel_id=1, source_target_pairs={{0,16},{8,24},{16,0},{24,8},{1,17},{9,25},{17,1},{25,9},{2,18},{10... | collective-permute-start | bytes 786440 | tf_op jit(solution)/shard_map/ppermute | solution.py:199
  7.3 1.3 %collective-permute-start.1 = (bf16[256,512]{1,0:T(8,128)(2,1)S(1)}, bf16[256,512]{1,0:T(8,128)(2,1)S(1)}, u32[]{:S(2)}, u32[]{:S(2)}) collective-permute-start(bf16[256,512]{1,0:T(8,128)(2,1)S(1)} %get-tuple-element.16.refs_4_), channel_id=1, source_target_pairs={{0,16},{8,24},{16,0},{24,8},{1,17},{9,25},{17,1},{25,9},{2,18},{10... | collective-permute-start | bytes 786440 | tf_op jit(solution)/shard_map/ppermute | solution.py:199
  8.6 2.2 %shard_map.66 = (f32[1,1024]{1,0:T(1,128)S(1)}, f32[1,1024]{1,0:T(1,128)S(1)}, f32[1,512]{1,0:T(1,128)S(1)}) custom-call(s32[4]{0:T(128)S(1)} %pad_add_fusion.refs_0_, s32[1,2048]{1,0:T(1,128)S(1)} %bitcast.8, f32[1,200]{1,0:T(1,128)S(1)} %bitcast.18, f32[1,2000]{1,0:T(1,128)S(1)} %bitcast.9, bf16[256,512]{1,0:T(8,128)(2,1)S(1)} %get-tuple-element.16.refs_4_), custom_call_target="tpu_custom_call" | custom-call | flops 4000000000 | bytes 1 | tf_op jit(solution)/shard_map/pallas_call | solution.py:45
  11.6 2.2 %collective-permute-done.refs_2_ = bf16[256,512]{1,0:T(8,128)(2,1)S(1)} collective-permute-done((bf16[256,512]{1,0:T(8,128)(2,1)S(1)}, bf16[256,512]{1,0:T(8,128)(2,1)S(1)}, u32[]{:S(2)}, u32[]{:S(2)}) %collective-permute-start) | collective-permute-done | bytes 262176 | tf_op jit(solution)/shard_map/ppermute | solution.py:199
  15.0 1.6 %collective-permute-start.4 = (s16[272,512]{1,0:T(8,128)(2,1)S(1)}, s16[272,512]{1,0:T(8,128)(2,1)S(1)}, u32[]{:S(2)}, u32[]{:S(2)}) collective-permute-start(s16[272,512]{1,0:T(8,128)(2,1)S(1)} %shard_map.67.refs_3_), channel_id=1, source_target_pairs={{0,2},{1,3},{2,4},{3,5},{4,6},{5,7},{6,0},{7,1},{8,10},{9,11},{10,... | collective-permute-start | bytes 835592 | tf_op jit(solution)/shard_map/ppermute | solution.py:208
  17.2 3.3 %collective-permute-start.5 = (bf16[256,512]{1,0:T(8,128)(2,1)S(1)}, bf16[256,512]{1,0:T(8,128)(2,1)S(1)}, u32[]{:S(2)}, u32[]{:S(2)}) collective-permute-start(bf16[256,512]{1,0:T(8,128)(2,1)S(1)} %get-tuple-element.19.refs_4_), channel_id=1, source_target_pairs={{0,16},{8,24},{16,0},{24,8},{1,17},{9,25},{17,1},{25,9},{2,18},{10... | collective-permute-start | bytes 786440 | tf_op jit(solution)/shard_map/ppermute | solution.py:199
  21.8 1.6 %collective-permute-start.3 = (s16[272,512]{1,0:T(8,128)(2,1)S(1)}, s16[272,512]{1,0:T(8,128)(2,1)S(1)}, u32[]{:S(2)}, u32[]{:S(2)}) collective-permute-start(s16[272,512]{1,0:T(8,128)(2,1)S(1)} %shard_map.69.refs_3_), channel_id=1, source_target_pairs={{0,2},{1,3},{2,4},{3,5},{4,6},{5,7},{6,0},{7,1},{8,10},{9,11},{10,... | collective-permute-start | bytes 835592 | tf_op jit(solution)/shard_map/ppermute | solution.py:208
  24.0 1.8 %collective-permute-start.2 = (bf16[256,512]{1,0:T(8,128)(2,1)S(1)}, bf16[256,512]{1,0:T(8,128)(2,1)S(1)}, u32[]{:S(2)}, u32[]{:S(2)}) collective-permute-start(bf16[256,512]{1,0:T(8,128)(2,1)S(1)} %get-tuple-element.21.refs_4_), channel_id=1, source_target_pairs={{0,16},{8,24},{16,0},{24,8},{1,17},{9,25},{17,1},{25,9},{2,18},{10... | collective-permute-start | bytes 786440 | tf_op jit(solution)/shard_map/ppermute | solution.py:199
  27.0 1.6 %collective-permute-start.8 = (s16[272,512]{1,0:T(8,128)(2,1)S(1)}, s16[272,512]{1,0:T(8,128)(2,1)S(1)}, u32[]{:S(2)}, u32[]{:S(2)}) collective-permute-start(s16[272,512]{1,0:T(8,128)(2,1)S(1)} %shard_map.71.refs_5_), channel_id=1, source_target_pairs={{0,2},{1,3},{2,4},{3,5},{4,6},{5,7},{6,0},{7,1},{8,10},{9,11},{10,... | collective-permute-start | bytes 835592 | tf_op jit(solution)/shard_map/ppermute | solution.py:208
  28.6 1.2 %shard_map.72.refs_5_ = s16[272,512]{1,0:T(8,128)(2,1)S(1)} custom-call(s32[4]{0:T(128)S(1)} %pad_add_fusion.refs_0_, bf16[256,512]{1,0:T(8,128)(2,1)S(1)} %get-tuple-element.15.refs_1_, bf16[256,512]{1,0:T(8,128)(2,1)S(1)} %collective-permute-done.refs_2_, bf16[512,2048]{1,0:T(8,128)(2,1)S(1)} %copy-done.2, ...), custom_call_target="tpu_custom_call" | custom-call | flops 4000000000 | bytes 1 | tf_op jit(solution)/shard_map/pallas_call | solution.py:45
  29.8 1.6 %collective-permute-start.9 = (s16[272,512]{1,0:T(8,128)(2,1)S(1)}, s16[272,512]{1,0:T(8,128)(2,1)S(1)}, u32[]{:S(2)}, u32[]{:S(2)}) collective-permute-start(s16[272,512]{1,0:T(8,128)(2,1)S(1)} %shard_map.72.refs_5_), channel_id=1, source_target_pairs={{0,1},{1,0},{2,3},{3,2},{4,5},{5,4},{6,7},{7,6},{8,9},{9,8},{10,11... | collective-permute-start | bytes 835592 | tf_op jit(solution)/shard_map/ppermute | solution.py:203
  31.4 1.2 %shard_map.73.refs_4_ = s16[272,512]{1,0:T(8,128)(2,1)S(1)} custom-call(s32[4]{0:T(128)S(1)} %pad_add_fusion.refs_0_, bf16[256,512]{1,0:T(8,128)(2,1)S(1)} %get-tuple-element.18.refs_1_, bf16[256,512]{1,0:T(8,128)(2,1)S(1)} %collective-permute-done.1.refs_2_, bf16[512,2048]{1,0:T(8,128)(2,1)S(1)} %copy-done.2, ...), custom_call_target="tpu_custom_call" | custom-call | flops 4000000000 | bytes 1 | tf_op jit(solution)/shard_map/pallas_call | solution.py:45
  34.6 1.8 %collective-permute-start.6 = (s16[272,512]{1,0:T(8,128)(2,1)S(1)}, s16[272,512]{1,0:T(8,128)(2,1)S(1)}, u32[]{:S(2)}, u32[]{:S(2)}) collective-permute-start(s16[272,512]{1,0:T(8,128)(2,1)S(1)} %shard_map.74.refs_5_), channel_id=1, source_target_pairs={{0,2},{1,3},{2,4},{3,5},{4,6},{5,7},{6,0},{7,1},{8,10},{9,11},{10,... | collective-permute-start | bytes 835592 | tf_op jit(solution)/shard_map/ppermute | solution.py:208
  36.4 2.9 %collective-permute-done.9.refs_4_ = s16[272,512]{1,0:T(8,128)(2,1)S(1)} collective-permute-done((s16[272,512]{1,0:T(8,128)(2,1)S(1)}, s16[272,512]{1,0:T(8,128)(2,1)S(1)}, u32[]{:S(2)}, u32[]{:S(2)}) %collective-permute-start.9) | collective-permute-done | bytes 278560 | tf_op jit(solution)/shard_map/ppermute | solution.py:203
  39.3 1.2 %shard_map.75.refs_5_ = s16[272,512]{1,0:T(8,128)(2,1)S(1)} custom-call(s32[4]{0:T(128)S(1)} %pad_add_fusion.refs_0_, bf16[256,512]{1,0:T(8,128)(2,1)S(1)} %get-tuple-element.15.refs_1_, bf16[256,512]{1,0:T(8,128)(2,1)S(1)} %collective-permute-done.refs_2_, bf16[512,2048]{1,0:T(8,128)(2,1)S(1)} %copy-done.2, ...), custom_call_target="tpu_custom_call" | custom-call | flops 4000000000 | bytes 1 | tf_op jit(solution)/shard_map/pallas_call | solution.py:45
  40.5 2.2 %collective-permute-start.11 = (s16[272,512]{1,0:T(8,128)(2,1)S(1)}, s16[272,512]{1,0:T(8,128)(2,1)S(1)}, u32[]{:S(2)}, u32[]{:S(2)}) collective-permute-start(s16[272,512]{1,0:T(8,128)(2,1)S(1)} %shard_map.75.refs_5_), channel_id=1, source_target_pairs={{0,2},{1,3},{2,4},{3,5},{4,6},{5,7},{6,0},{7,1},{8,10},{9,11},{10,... | collective-permute-start | bytes 835592 | tf_op jit(solution)/shard_map/ppermute | solution.py:208
  42.7 1.2 %shard_map.76.refs_5_ = s16[272,512]{1,0:T(8,128)(2,1)S(1)} custom-call(s32[4]{0:T(128)S(1)} %pad_add_fusion.refs_0_, bf16[256,512]{1,0:T(8,128)(2,1)S(1)} %get-tuple-element.22.refs_1_, bf16[256,512]{1,0:T(8,128)(2,1)S(1)} %collective-permute-done.5.refs_2_, bf16[512,2048]{1,0:T(8,128)(2,1)S(1)} %copy-done.2, ...), custom_call_target="tpu_custom_call" | custom-call | flops 4000000000 | bytes 1 | tf_op jit(solution)/shard_map/pallas_call | solution.py:45
  43.9 1.6 %collective-permute-start.13 = (s16[272,512]{1,0:T(8,128)(2,1)S(1)}, s16[272,512]{1,0:T(8,128)(2,1)S(1)}, u32[]{:S(2)}, u32[]{:S(2)}) collective-permute-start(s16[272,512]{1,0:T(8,128)(2,1)S(1)} %shard_map.76.refs_5_), channel_id=1, source_target_pairs={{0,1},{1,0},{2,3},{3,2},{4,5},{5,4},{6,7},{7,6},{8,9},{9,8},{10,11... | collective-permute-start | bytes 835592 | tf_op jit(solution)/shard_map/ppermute | solution.py:203
  45.5 1.2 %shard_map.77.refs_5_ = s16[272,512]{1,0:T(8,128)(2,1)S(1)} custom-call(s32[4]{0:T(128)S(1)} %pad_add_fusion.refs_0_, bf16[256,512]{1,0:T(8,128)(2,1)S(1)} %get-tuple-element.18.refs_1_, bf16[256,512]{1,0:T(8,128)(2,1)S(1)} %collective-permute-done.1.refs_2_, bf16[512,2048]{1,0:T(8,128)(2,1)S(1)} %copy-done.2, ...), custom_call_target="tpu_custom_call" | custom-call | flops 4000000000 | bytes 1 | tf_op jit(solution)/shard_map/pallas_call | solution.py:45
  46.7 2.2 %collective-permute-start.17 = (s16[272,512]{1,0:T(8,128)(2,1)S(1)}, s16[272,512]{1,0:T(8,128)(2,1)S(1)}, u32[]{:S(2)}, u32[]{:S(2)}) collective-permute-start(s16[272,512]{1,0:T(8,128)(2,1)S(1)} %shard_map.77.refs_5_), channel_id=1, source_target_pairs={{0,2},{1,3},{2,4},{3,5},{4,6},{5,7},{6,0},{7,1},{8,10},{9,11},{10,... | collective-permute-start | bytes 835592 | tf_op jit(solution)/shard_map/ppermute | solution.py:208
  50.0 1.6 %collective-permute-start.10 = (s16[272,512]{1,0:T(8,128)(2,1)S(1)}, s16[272,512]{1,0:T(8,128)(2,1)S(1)}, u32[]{:S(2)}, u32[]{:S(2)}) collective-permute-start(s16[272,512]{1,0:T(8,128)(2,1)S(1)} %shard_map.78.refs_5_), channel_id=1, source_target_pairs={{0,1},{1,0},{2,3},{3,2},{4,5},{5,4},{6,7},{7,6},{8,9},{9,8},{10,11... | collective-permute-start | bytes 835592 | tf_op jit(solution)/shard_map/ppermute | solution.py:203
  51.6 1.2 %shard_map.79.refs_9_ = s16[272,512]{1,0:T(8,128)(2,1)S(1)} custom-call(s32[4]{0:T(128)S(1)} %pad_add_fusion.refs_0_, bf16[256,512]{1,0:T(8,128)(2,1)S(1)} %get-tuple-element.22.refs_1_, bf16[256,512]{1,0:T(8,128)(2,1)S(1)} %collective-permute-done.5.refs_2_, bf16[512,2048]{1,0:T(8,128)(2,1)S(1)} %copy-done.2, ...), custom_call_target="tpu_custom_call" | custom-call | flops 4000000000 | bytes 1 | tf_op jit(solution)/shard_map/pallas_call | solution.py:45
  52.8 1.3 %collective-permute-start.16 = (s16[272,512]{1,0:T(8,128)(2,1)S(1)}, s16[272,512]{1,0:T(8,128)(2,1)S(1)}, u32[]{:S(2)}, u32[]{:S(2)}) collective-permute-start(s16[272,512]{1,0:T(8,128)(2,1)S(1)} %shard_map.79.refs_9_), channel_id=1, source_target_pairs={{0,2},{1,3},{2,4},{3,5},{4,6},{5,7},{6,0},{7,1},{8,10},{9,11},{10,... | collective-permute-start | bytes 835592 | tf_op jit(solution)/shard_map/ppermute | solution.py:208
  56.6 1.2 %shard_map.81.refs_9_ = s16[272,512]{1,0:T(8,128)(2,1)S(1)} custom-call(s32[4]{0:T(128)S(1)} %pad_add_fusion.refs_0_, bf16[256,512]{1,0:T(8,128)(2,1)S(1)} %get-tuple-element.20.refs_1_, bf16[256,512]{1,0:T(8,128)(2,1)S(1)} %collective-permute-done.2.refs_2_, bf16[512,2048]{1,0:T(8,128)(2,1)S(1)} %copy-done.2, ...), custom_call_target="tpu_custom_call" | custom-call | flops 4000000000 | bytes 1 | tf_op jit(solution)/shard_map/pallas_call | solution.py:45
  59.4 1.7 %collective-permute-start.20 = (bf16[256,512]{1,0:T(8,128)(2,1)S(1)}, bf16[256,512]{1,0:T(8,128)(2,1)S(1)}, u32[]{:S(2)}, u32[]{:S(2)}) collective-permute-start(bf16[256,512]{1,0:T(8,128)(2,1)S(1)} %shard_map.82.refs_9_.refs_2_), channel_id=1, source_target_pairs={{0,16},{8,24},{16,0},{24,8},{1,17},{9,25},{17,1},{25,9},{2,18},{10... | collective-permute-start | bytes 786440 | tf_op jit(solution)/shard_map/ppermute | solution.py:199
  61.1 1.9 %collective-permute-done.16.refs_5_ = s16[272,512]{1,0:T(8,128)(2,1)S(1)} collective-permute-done((s16[272,512]{1,0:T(8,128)(2,1)S(1)}, s16[272,512]{1,0:T(8,128)(2,1)S(1)}, u32[]{:S(2)}, u32[]{:S(2)}) %collective-permute-start.16) | collective-permute-done | bytes 278560 | tf_op jit(solution)/shard_map/ppermute | solution.py:208
  64.2 1.7 %collective-permute-start.19 = (bf16[256,512]{1,0:T(8,128)(2,1)S(1)}, bf16[256,512]{1,0:T(8,128)(2,1)S(1)}, u32[]{:S(2)}, u32[]{:S(2)}) collective-permute-start(bf16[256,512]{1,0:T(8,128)(2,1)S(1)} %shard_map.83.refs_4_.refs_2_), channel_id=1, source_target_pairs={{0,16},{8,24},{16,0},{24,8},{1,17},{9,25},{17,1},{25,9},{2,18},{10... | collective-permute-start | bytes 786440 | tf_op jit(solution)/shard_map/ppermute | solution.py:199
  67.8 1.8 %collective-permute-start.18 = (bf16[256,512]{1,0:T(8,128)(2,1)S(1)}, bf16[256,512]{1,0:T(8,128)(2,1)S(1)}, u32[]{:S(2)}, u32[]{:S(2)}) collective-permute-start(bf16[256,512]{1,0:T(8,128)(2,1)S(1)} %shard_map.85.refs_5_.refs_2_), channel_id=1, source_target_pairs={{0,16},{8,24},{16,0},{24,8},{1,17},{9,25},{17,1},{25,9},{2,18},{10... | collective-permute-start | bytes 786440 | tf_op jit(solution)/shard_map/ppermute | solution.py:199
  71.1 2.8 %collective-permute-done.19.refs_3_ = bf16[256,512]{1,0:T(8,128)(2,1)S(1)} collective-permute-done((bf16[256,512]{1,0:T(8,128)(2,1)S(1)}, bf16[256,512]{1,0:T(8,128)(2,1)S(1)}, u32[]{:S(2)}, u32[]{:S(2)}) %collective-permute-start.19) | collective-permute-done | bytes 262176 | tf_op jit(solution)/shard_map/ppermute | solution.py:199
  74.8 1.9 %collective-permute-done.18.refs_3_ = bf16[256,512]{1,0:T(8,128)(2,1)S(1)} collective-permute-done((bf16[256,512]{1,0:T(8,128)(2,1)S(1)}, bf16[256,512]{1,0:T(8,128)(2,1)S(1)}, u32[]{:S(2)}, u32[]{:S(2)}) %collective-permute-start.18) | collective-permute-done | bytes 262176 | tf_op jit(solution)/shard_map/ppermute | solution.py:199
  76.7 2.2 %shard_map.88 = bf16[2048,512]{1,0:T(8,128)(2,1)} custom-call(s32[4]{0:T(128)S(1)} %pad_add_fusion.refs_0_, s32[1,2048]{1,0:T(1,128)S(1)} %bitcast.17, bf16[256,512]{1,0:T(8,128)(2,1)S(1)} %shard_map.85.refs_5_.refs_2_, bf16[256,512]{1,0:T(8,128)(2,1)S(1)} %collective-permute-done.18.refs_3_, bf16[2048,512]{1,0:T(8,128)(2,1)S(1)} %shard_map.87.refs_4_.refs_5_, ...), custom_call_target="tpu_custom_call" | custom-call | flops 4000000000 | bytes 1 | tf_op jit(solution)/shard_map/pallas_call | solution.py:45
  (52 shorter events, 20.5 us)
Async XLA Ops:
  0.1 1.6 %copy-start = (bf16[2048,512]{1,0:T(8,128)(2,1)S(1)}, bf16[2048,512]{1,0:T(8,128)(2,1)}, u32[]{:S(2)}) copy-start(bf16[2048,512]{1,0:T(8,128)(2,1)} %refs_2_.7) | copy-start | bytes 6291460
  1.7 0.7 copy-start.5
  2.9 5.6 %copy-start.3 = (s32[2048]{0:T(1024)S(1)}, s32[2048]{0:T(1024)}, u32[]{:S(2)}) copy-start(s32[2048]{0:T(1024)} %param.8) | copy-start | bytes 24580
  3.0 5.6 %copy-start.4 = (f32[2000]{0:T(1024)S(1)}, f32[2000]{0:T(1024)}, u32[]{:S(2)}) copy-start(f32[2000]{0:T(1024)} %param.11) | copy-start | bytes 24004
  3.0 5.6 %copy-start.7 = (f32[200]{0:T(256)S(1)}, f32[200]{0:T(256)}, u32[]{:S(2)}) copy-start(f32[200]{0:T(256)} %param.10) | copy-start | bytes 2404
  3.0 10.8 %collective-permute-start = (bf16[256,512]{1,0:T(8,128)(2,1)S(1)}, bf16[256,512]{1,0:T(8,128)(2,1)S(1)}, u32[]{:S(2)}, u32[]{:S(2)}) collective-permute-start(bf16[256,512]{1,0:T(8,128)(2,1)S(1)} %shard_map.64.refs_3_), channel_id=1, source_target_pairs={{0,16},{8,24},{16,0},{24,8},{1,17},{9,25},{17,1},{25,9},{2,18},{10... | collective-permute-start | bytes 786440 | tf_op jit(solution)/shard_map/ppermute | solution.py:199
  7.3 13.3 %collective-permute-start.1 = (bf16[256,512]{1,0:T(8,128)(2,1)S(1)}, bf16[256,512]{1,0:T(8,128)(2,1)S(1)}, u32[]{:S(2)}, u32[]{:S(2)}) collective-permute-start(bf16[256,512]{1,0:T(8,128)(2,1)S(1)} %get-tuple-element.16.refs_4_), channel_id=1, source_target_pairs={{0,16},{8,24},{16,0},{24,8},{1,17},{9,25},{17,1},{25,9},{2,18},{10... | collective-permute-start | bytes 786440 | tf_op jit(solution)/shard_map/ppermute | solution.py:199
  8.6 5.2 %copy-start.2 = (bf16[512,2048]{1,0:T(8,128)(2,1)S(1)}, bf16[512,2048]{1,0:T(8,128)(2,1)}, u32[]{:S(2)}) copy-start(bf16[512,2048]{1,0:T(8,128)(2,1)} %refs_3_.31) | copy-start | bytes 6291460
  10.7 43.3 %collective-permute-start.12 = (f32[1,1024]{1,0:T(1,128)S(1)}, f32[1,1024]{1,0:T(1,128)S(1)}, u32[]{:S(2)}, u32[]{:S(2)}) collective-permute-start(f32[1,1024]{1,0:T(1,128)S(1)} %get-tuple-element.24), channel_id=1, source_target_pairs={{0,16},{8,24},{16,0},{24,8},{1,17},{9,25},{17,1},{25,9},{2,18},{10... | collective-permute-start | bytes 12296 | tf_op jit(solution)/shard_map/ppermute | solution.py:199
  13.8 2.8 %copy-start.1 = (bf16[2048,512]{1,0:T(8,128)(2,1)S(1)}, bf16[2048,512]{1,0:T(8,128)(2,1)}, u32[]{:S(2)}) copy-start(bf16[2048,512]{1,0:T(8,128)(2,1)} %refs_2_.7) | copy-start | bytes 6291460
  13.8 2.8 %copy-start.6 = (s32[2048]{0:T(1024)S(1)}, s32[2048]{0:T(1024)}, u32[]{:S(2)}) copy-start(s32[2048]{0:T(1024)} %param.9) | copy-start | bytes 24580
  15.0 13.6 %collective-permute-start.4 = (s16[272,512]{1,0:T(8,128)(2,1)S(1)}, s16[272,512]{1,0:T(8,128)(2,1)S(1)}, u32[]{:S(2)}, u32[]{:S(2)}) collective-permute-start(s16[272,512]{1,0:T(8,128)(2,1)S(1)} %shard_map.67.refs_3_), channel_id=1, source_target_pairs={{0,2},{1,3},{2,4},{3,5},{4,6},{5,7},{6,0},{7,1},{8,10},{9,11},{10,... | collective-permute-start | bytes 835592 | tf_op jit(solution)/shard_map/ppermute | solution.py:208
  17.2 8.6 %collective-permute-start.5 = (bf16[256,512]{1,0:T(8,128)(2,1)S(1)}, bf16[256,512]{1,0:T(8,128)(2,1)S(1)}, u32[]{:S(2)}, u32[]{:S(2)}) collective-permute-start(bf16[256,512]{1,0:T(8,128)(2,1)S(1)} %get-tuple-element.19.refs_4_), channel_id=1, source_target_pairs={{0,16},{8,24},{16,0},{24,8},{1,17},{9,25},{17,1},{25,9},{2,18},{10... | collective-permute-start | bytes 786440 | tf_op jit(solution)/shard_map/ppermute | solution.py:199
  21.8 9.7 %collective-permute-start.3 = (s16[272,512]{1,0:T(8,128)(2,1)S(1)}, s16[272,512]{1,0:T(8,128)(2,1)S(1)}, u32[]{:S(2)}, u32[]{:S(2)}) collective-permute-start(s16[272,512]{1,0:T(8,128)(2,1)S(1)} %shard_map.69.refs_3_), channel_id=1, source_target_pairs={{0,2},{1,3},{2,4},{3,5},{4,6},{5,7},{6,0},{7,1},{8,10},{9,11},{10,... | collective-permute-start | bytes 835592 | tf_op jit(solution)/shard_map/ppermute | solution.py:208
  24.0 9.4 %collective-permute-start.2 = (bf16[256,512]{1,0:T(8,128)(2,1)S(1)}, bf16[256,512]{1,0:T(8,128)(2,1)S(1)}, u32[]{:S(2)}, u32[]{:S(2)}) collective-permute-start(bf16[256,512]{1,0:T(8,128)(2,1)S(1)} %get-tuple-element.21.refs_4_), channel_id=1, source_target_pairs={{0,16},{8,24},{16,0},{24,8},{1,17},{9,25},{17,1},{25,9},{2,18},{10... | collective-permute-start | bytes 786440 | tf_op jit(solution)/shard_map/ppermute | solution.py:199
  27.0 15.7 %collective-permute-start.8 = (s16[272,512]{1,0:T(8,128)(2,1)S(1)}, s16[272,512]{1,0:T(8,128)(2,1)S(1)}, u32[]{:S(2)}, u32[]{:S(2)}) collective-permute-start(s16[272,512]{1,0:T(8,128)(2,1)S(1)} %shard_map.71.refs_5_), channel_id=1, source_target_pairs={{0,2},{1,3},{2,4},{3,5},{4,6},{5,7},{6,0},{7,1},{8,10},{9,11},{10,... | collective-permute-start | bytes 835592 | tf_op jit(solution)/shard_map/ppermute | solution.py:208
  29.8 9.5 %collective-permute-start.9 = (s16[272,512]{1,0:T(8,128)(2,1)S(1)}, s16[272,512]{1,0:T(8,128)(2,1)S(1)}, u32[]{:S(2)}, u32[]{:S(2)}) collective-permute-start(s16[272,512]{1,0:T(8,128)(2,1)S(1)} %shard_map.72.refs_5_), channel_id=1, source_target_pairs={{0,1},{1,0},{2,3},{3,2},{4,5},{5,4},{6,7},{7,6},{8,9},{9,8},{10,11... | collective-permute-start | bytes 835592 | tf_op jit(solution)/shard_map/ppermute | solution.py:203
  32.6 12.8 %collective-permute-start.7 = (s16[272,512]{1,0:T(8,128)(2,1)S(1)}, s16[272,512]{1,0:T(8,128)(2,1)S(1)}, u32[]{:S(2)}, u32[]{:S(2)}) collective-permute-start(s16[272,512]{1,0:T(8,128)(2,1)S(1)} %shard_map.73.refs_4_), channel_id=1, source_target_pairs={{0,1},{1,0},{2,3},{3,2},{4,5},{5,4},{6,7},{7,6},{8,9},{9,8},{10,11... | collective-permute-start | bytes 835592 | tf_op jit(solution)/shard_map/ppermute | solution.py:203
  34.6 14.2 %collective-permute-start.6 = (s16[272,512]{1,0:T(8,128)(2,1)S(1)}, s16[272,512]{1,0:T(8,128)(2,1)S(1)}, u32[]{:S(2)}, u32[]{:S(2)}) collective-permute-start(s16[272,512]{1,0:T(8,128)(2,1)S(1)} %shard_map.74.refs_5_), channel_id=1, source_target_pairs={{0,2},{1,3},{2,4},{3,5},{4,6},{5,7},{6,0},{7,1},{8,10},{9,11},{10,... | collective-permute-start | bytes 835592 | tf_op jit(solution)/shard_map/ppermute | solution.py:208
  40.5 13.6 %collective-permute-start.11 = (s16[272,512]{1,0:T(8,128)(2,1)S(1)}, s16[272,512]{1,0:T(8,128)(2,1)S(1)}, u32[]{:S(2)}, u32[]{:S(2)}) collective-permute-start(s16[272,512]{1,0:T(8,128)(2,1)S(1)} %shard_map.75.refs_5_), channel_id=1, source_target_pairs={{0,2},{1,3},{2,4},{3,5},{4,6},{5,7},{6,0},{7,1},{8,10},{9,11},{10,... | collective-permute-start | bytes 835592 | tf_op jit(solution)/shard_map/ppermute | solution.py:208
  43.9 7.7 %collective-permute-start.13 = (s16[272,512]{1,0:T(8,128)(2,1)S(1)}, s16[272,512]{1,0:T(8,128)(2,1)S(1)}, u32[]{:S(2)}, u32[]{:S(2)}) collective-permute-start(s16[272,512]{1,0:T(8,128)(2,1)S(1)} %shard_map.76.refs_5_), channel_id=1, source_target_pairs={{0,1},{1,0},{2,3},{3,2},{4,5},{5,4},{6,7},{7,6},{8,9},{9,8},{10,11... | collective-permute-start | bytes 835592 | tf_op jit(solution)/shard_map/ppermute | solution.py:203
  46.7 11.6 %collective-permute-start.17 = (s16[272,512]{1,0:T(8,128)(2,1)S(1)}, s16[272,512]{1,0:T(8,128)(2,1)S(1)}, u32[]{:S(2)}, u32[]{:S(2)}) collective-permute-start(s16[272,512]{1,0:T(8,128)(2,1)S(1)} %shard_map.77.refs_5_), channel_id=1, source_target_pairs={{0,2},{1,3},{2,4},{3,5},{4,6},{5,7},{6,0},{7,1},{8,10},{9,11},{10,... | collective-permute-start | bytes 835592 | tf_op jit(solution)/shard_map/ppermute | solution.py:208
  50.0 6.6 %collective-permute-start.10 = (s16[272,512]{1,0:T(8,128)(2,1)S(1)}, s16[272,512]{1,0:T(8,128)(2,1)S(1)}, u32[]{:S(2)}, u32[]{:S(2)}) collective-permute-start(s16[272,512]{1,0:T(8,128)(2,1)S(1)} %shard_map.78.refs_5_), channel_id=1, source_target_pairs={{0,1},{1,0},{2,3},{3,2},{4,5},{5,4},{6,7},{7,6},{8,9},{9,8},{10,11... | collective-permute-start | bytes 835592 | tf_op jit(solution)/shard_map/ppermute | solution.py:203
  52.8 10.2 %collective-permute-start.16 = (s16[272,512]{1,0:T(8,128)(2,1)S(1)}, s16[272,512]{1,0:T(8,128)(2,1)S(1)}, u32[]{:S(2)}, u32[]{:S(2)}) collective-permute-start(s16[272,512]{1,0:T(8,128)(2,1)S(1)} %shard_map.79.refs_9_), channel_id=1, source_target_pairs={{0,2},{1,3},{2,4},{3,5},{4,6},{5,7},{6,0},{7,1},{8,10},{9,11},{10,... | collective-permute-start | bytes 835592 | tf_op jit(solution)/shard_map/ppermute | solution.py:208
  55.3 10.6 %collective-permute-start.15 = (bf16[256,512]{1,0:T(8,128)(2,1)S(1)}, bf16[256,512]{1,0:T(8,128)(2,1)S(1)}, u32[]{:S(2)}, u32[]{:S(2)}) collective-permute-start(bf16[256,512]{1,0:T(8,128)(2,1)S(1)} %shard_map.80.refs_5_.refs_2_), channel_id=1, source_target_pairs={{0,16},{8,24},{16,0},{24,8},{1,17},{9,25},{17,1},{25,9},{2,18},{10... | collective-permute-start | bytes 786440 | tf_op jit(solution)/shard_map/ppermute | solution.py:199
  57.8 8.8 %collective-permute-start.14 = (s16[272,512]{1,0:T(8,128)(2,1)S(1)}, s16[272,512]{1,0:T(8,128)(2,1)S(1)}, u32[]{:S(2)}, u32[]{:S(2)}) collective-permute-start(s16[272,512]{1,0:T(8,128)(2,1)S(1)} %shard_map.81.refs_9_), channel_id=1, source_target_pairs={{0,2},{1,3},{2,4},{3,5},{4,6},{5,7},{6,0},{7,1},{8,10},{9,11},{10,... | collective-permute-start | bytes 835592 | tf_op jit(solution)/shard_map/ppermute | solution.py:208
  59.4 10.7 %collective-permute-start.20 = (bf16[256,512]{1,0:T(8,128)(2,1)S(1)}, bf16[256,512]{1,0:T(8,128)(2,1)S(1)}, u32[]{:S(2)}, u32[]{:S(2)}) collective-permute-start(bf16[256,512]{1,0:T(8,128)(2,1)S(1)} %shard_map.82.refs_9_.refs_2_), channel_id=1, source_target_pairs={{0,16},{8,24},{16,0},{24,8},{1,17},{9,25},{17,1},{25,9},{2,18},{10... | collective-permute-start | bytes 786440 | tf_op jit(solution)/shard_map/ppermute | solution.py:199
  64.2 9.7 %collective-permute-start.19 = (bf16[256,512]{1,0:T(8,128)(2,1)S(1)}, bf16[256,512]{1,0:T(8,128)(2,1)S(1)}, u32[]{:S(2)}, u32[]{:S(2)}) collective-permute-start(bf16[256,512]{1,0:T(8,128)(2,1)S(1)} %shard_map.83.refs_4_.refs_2_), channel_id=1, source_target_pairs={{0,16},{8,24},{16,0},{24,8},{1,17},{9,25},{17,1},{25,9},{2,18},{10... | collective-permute-start | bytes 786440 | tf_op jit(solution)/shard_map/ppermute | solution.py:199
  67.8 8.9 %collective-permute-start.18 = (bf16[256,512]{1,0:T(8,128)(2,1)S(1)}, bf16[256,512]{1,0:T(8,128)(2,1)S(1)}, u32[]{:S(2)}, u32[]{:S(2)}) collective-permute-start(bf16[256,512]{1,0:T(8,128)(2,1)S(1)} %shard_map.85.refs_5_.refs_2_), channel_id=1, source_target_pairs={{0,16},{8,24},{16,0},{24,8},{1,17},{9,25},{17,1},{25,9},{2,18},{10... | collective-permute-start | bytes 786440 | tf_op jit(solution)/shard_map/ppermute | solution.py:199

commit v6 on v5

v6 whole, which is shorter than its diff:
```python
import functools

import jax
import jax.numpy as jnp
from jax import lax
from jax.experimental import pallas as pl
from jax.experimental.pallas import tpu as pltpu
from jax.sharding import PartitionSpec as P

NOCC = 200
NV = 2000
SHARES = (2, 2, 2, 2)
SCALE_ROWS = 16
TOP = 32767.0
STEPS = 64.0
TINY = 1e-33
LANES = 128
PLACE_ROWS = 256
VMEM_LIMIT = 16 * 1024 * 1024
KERNEL_FLOPS = 4 * 10**9
ORDER = (
    (("align", 0), ("align", 1), ("factor", 0), ("energy", 0), ("first", 0), ("align", 2))
    + (("first", 1), ("align", 3), ("first", 2), ("second", 0), ("second", 1), ("first", 3))
    + (("third", 0), ("second", 2), ("third", 1), ("second", 3), ("third", 2), ("last", 0))
    + (("third", 3), ("last", 1), ("last", 2), ("place", 0), ("last", 3), ("place", 1))
    + (("place", 2), ("place", 3))
)
ALIGNED = (
    ((0, True),),
    ((1, True), (0, False)),
    ((2, True), (1, False)),
    ((3, True), (2, False), (3, False)),
)

VMEM = pl.BlockSpec(memory_space=pltpu.VMEM)
ANY = pl.BlockSpec(memory_space=pl.ANY)


def call(body, out_shape, operands, after=(), out_spec=None, scratch=()):
    count = len(operands)

    def kernel(*refs):
        body(*refs[:count], *refs[count + len(after) :])

    return pl.pallas_call(
        kernel,
        out_shape=out_shape,
        in_specs=[VMEM] * count + [ANY] * len(after),
        out_specs=jax.tree.map(lambda _: out_spec or VMEM, out_shape),
        scratch_shapes=list(scratch),
        compiler_params=pltpu.CompilerParams(vmem_limit_bytes=VMEM_LIMIT),
        cost_estimate=pl.CostEstimate(flops=KERNEL_FLOPS, bytes_accessed=1, transcendentals=0),
    )(*operands, *after)


def upper_side():
    return lax.axis_index("row") // (lax.axis_size("row") // 2)


def partner_base(rows):
    return (lax.axis_index("row") ^ (lax.axis_size("row") // 2)) * rows


def exchanged(values):
    even = lax.broadcasted_iota(jnp.int32, (values.shape[0], LANES), 1) % 2 == 0
    parts = []
    for lane in range(0, values.shape[1], LANES):
        part = values[:, lane : lane + LANES]
        parts.append(jnp.where(even, pltpu.roll(part, LANES - 1, 1), pltpu.roll(part, 1, 1)))
    return jnp.concatenate(parts, axis=1)


def align_kernel(wanted, partner, amplitudes, *outs):
    rows = amplitudes.shape[0]
    upper = upper_side()

    def first(index):
        begin, send = wanted[index]
        return (1 - upper if send else upper) * (rows // 2) + begin

    @pl.when(upper == 0)
    def _():
        for index, out in enumerate(outs):
            out[...] = amplitudes[pl.ds(pl.multiple_of(first(index), LANES), out.shape[0]), :]

    @pl.when(upper == 1)
    def _():
        for index, out in enumerate(outs):
            target = partner_base(rows) + first(index) + lax.broadcasted_iota(jnp.int32, (out.shape[0], rows), 0)
            pick = jnp.where(partner[...] == target, 1.0, 0.0).astype(jnp.bfloat16)
            out[...] = jnp.dot(pick, amplitudes[...], preferred_element_type=jnp.float32).astype(jnp.bfloat16)


def factor_kernel(integrals, *outs):
    width = integrals.shape[0]
    for stop, out in enumerate(outs):
        block = integrals[:, pl.ds(stop * width, width)]
        out[pl.ds(0, width), :] = block
        out[pl.ds(width, width), :] = exchanged(block.astype(jnp.float32)).astype(jnp.bfloat16)


def product(own, other, factor):
    both = jnp.concatenate([own[...], other[...]], axis=1)
    return jnp.dot(both, factor[...], preferred_element_type=jnp.float32)


def code(values, out):
    rows = values.shape[0]
    top = jnp.max(jnp.abs(values), axis=0, keepdims=True)
    level = jnp.ceil(STEPS * jnp.log2(jnp.maximum(top, TINY) * (1.0001 / TOP)))
    coded = jnp.round(values * jnp.exp2(level * (-1.0 / STEPS)))
    out[pl.ds(0, rows), :] = coded.astype(jnp.int32).astype(jnp.int16)
    spread = jnp.broadcast_to(level.astype(jnp.int32), (SCALE_ROWS, values.shape[1]))
    out[pl.ds(rows, SCALE_ROWS), :] = spread.astype(jnp.int16)


def decode(coded):
    rows = coded.shape[0] - SCALE_ROWS
    level = coded[pl.ds(rows, SCALE_ROWS), :].astype(jnp.int32).astype(jnp.float32)[0:1, :]
    return coded[pl.ds(0, rows), :].astype(jnp.int32).astype(jnp.float32) * jnp.exp2(level * (1.0 / STEPS))


def first_kernel(own, other, factor, out):
    code(product(own, other, factor), out)


def second_kernel(own, other, factor, arrived, out):
    code(product(own, other, factor) + decode(arrived), out)


def third_kernel(own, other, factor, crossed, out):
    here = jnp.where(lax.axis_index("col") % 2 == 0, 1.0, 0.0)
    code(product(own, other, factor) + decode(crossed) * here, out)


def last_kernel(begin, own, other, factor, crossed, arrived, occ_here, occ_there, vir_sum, out):
    chunk, width = out.shape
    here = jnp.where(lax.axis_index("col") % 2 == 1, 1.0, 0.0)
    total = product(own, other, factor) + decode(arrived) + decode(crossed) * here
    part = pl.ds(begin, chunk)
    occ_rows = jnp.where(upper_side() == 0, occ_here[:, part], occ_there[:, part])
    occ_down = jnp.broadcast_to(occ_rows, (LANES, chunk)).T
    for lane in range(0, width, LANES):
        denom = vir_sum[:, lane : lane + LANES] - occ_down
        out[:, lane : lane + LANES] = (total[:, lane : lane + LANES] / denom).astype(jnp.bfloat16)


def place_kernel(begin, partner, own, other, *refs):
    held, arrivals = refs[-2:] if len(refs) > 2 else (refs[-1], None)
    earlier = refs[0] if len(refs) != 1 else None
    rows, width = held.shape
    chunk = own.shape[0]
    upper = upper_side()
    here = upper * (rows // 2) + begin
    there = (1 - upper) * (rows // 2) + begin
    opposite = exchanged(other[...].astype(jnp.float32)).astype(jnp.bfloat16)

    def leave(block):
        part = pl.ds(block * PLACE_ROWS, PLACE_ROWS)
        return pltpu.make_async_copy(held.at[part, :], refs[-3].at[part, :], arrivals.at[block])

    @pl.when(upper == 0)
    def _():
        if earlier is not None:
            held[...] = earlier[...]
        held[pl.ds(pl.multiple_of(here, LANES), chunk), :] = own[...]
        held[pl.ds(pl.multiple_of(there, LANES), chunk), :] = opposite
        if arrivals is not None:
            for block in range(rows // PLACE_ROWS):
                leave(block).start()

    @pl.when(upper == 1)
    def _():
        lanes = lax.broadcasted_iota(jnp.int32, (PLACE_ROWS, LANES), 1) + partner_base(rows)

        def pick(slots, begin):
            parts = [jnp.where(slots == lanes + (begin + lane), 1.0, 0.0) for lane in range(0, chunk, LANES)]
            return jnp.concatenate(parts, axis=1).astype(jnp.bfloat16)

        for block in range(rows // PLACE_ROWS):
            part = pl.ds(block * PLACE_ROWS, PLACE_ROWS)
            slots = jnp.broadcast_to(partner[:, part], (LANES, PLACE_ROWS)).T
            found = jnp.dot(pick(slots, here), own[...], preferred_element_type=jnp.float32)
            found += jnp.dot(pick(slots, there), opposite, preferred_element_type=jnp.float32)
            if earlier is not None:
                found += earlier[part, :].astype(jnp.float32)
            held[part, :] = found.astype(jnp.bfloat16)
            if arrivals is not None:
                leave(block).start()

    if arrivals is not None:
        for block in range(rows // PLACE_ROWS):
            leave(block).wait()


def split_index(values, count):
    high = jnp.floor((values.astype(jnp.float32) + 0.5) * (1.0 / count)).astype(jnp.int32)
    return high, values - high * count


def lookup(table, positions):
    found = jnp.zeros(positions.shape, jnp.float32)
    for begin in range(0, table.shape[1], LANES):
        size = min(LANES, table.shape[1] - begin)
        part = jnp.broadcast_to(table[:, begin : begin + size], (size, size))
        down = lax.broadcasted_iota(jnp.int32, (size, size), 0)
        across = lax.broadcasted_iota(jnp.int32, (size, size), 1)
        column = jnp.sum(jnp.where(down == across, part, 0.0), axis=1, keepdims=True)
        entry = begin + lax.broadcasted_iota(jnp.int32, (size, positions.shape[1]), 0)
        found += jnp.sum(jnp.where(entry == positions, column, 0.0), axis=0, keepdims=True)
    return found


def energy_kernel(pair_index, occ_energy, vir_energy, occ_lower, occ_upper, vir_sum):
    half = occ_lower.shape[1]
    for out, begin in ((occ_lower, 0), (occ_upper, half)):
        first, second = split_index(pair_index[:, pl.ds(begin, half)], NOCC)
        out[...] = lookup(occ_energy[...], first) + lookup(occ_energy[...], second)
    width = vir_sum.shape[1]
    unordered = lax.axis_index("col") * (width // 2) + lax.broadcasted_iota(jnp.int32, (1, width), 1) // 2
    first, second = split_index(unordered, NV)
    vir_sum[...] = lookup(vir_energy[...], first) + lookup(vir_energy[...], second)


def across_rows(value):
    count = lax.axis_size("row")
    return lax.ppermute(value, "row", [(i, i ^ (count // 2)) for i in range(count)])


def across_pair(value):
    return lax.ppermute(value, "col", [(i, i ^ 1) for i in range(lax.axis_size("col"))])


def two_along(value):
    count = lax.axis_size("col")
    return lax.ppermute(value, "col", [(i, (i + 2) % count) for i in range(count)])


def shards(amplitudes, integrals, pair_index, partner, occ_energy, vir_energy):
    rows, width = amplitudes.shape
    half = rows // 2
    chunks = [half * share // sum(SHARES) for share in SHARES]
    begins = [sum(chunks[:index]) for index in range(len(chunks))]
    whole_shape = jax.ShapeDtypeStruct((rows, width), jnp.bfloat16)

    def chunk_shape(index):
        return jax.ShapeDtypeStruct((chunks[index], width), jnp.bfloat16)

    def coded_shape(index):
        return jax.ShapeDtypeStruct((chunks[index] + SCALE_ROWS, width), jnp.int16)

    half_shape = jax.ShapeDtypeStruct((1, half), jnp.float32)
    energy_shapes = [half_shape, half_shape, jax.ShapeDtypeStruct((1, width), jnp.float32)]

    own, other, moved, crossed, arrived, done, placed = {}, {}, {}, {}, {}, {}, ()
    last = ()
    for step, index in ORDER:
        if step == "align":
            wanted = tuple((begins[chunk], send) for chunk, send in ALIGNED[index])
            shapes = [chunk_shape(chunk) for chunk, _ in ALIGNED[index]]
            result = call(functools.partial(align_kernel, wanted), shapes, (partner[None, :], amplitudes), last)
            for (chunk, send), picked in zip(ALIGNED[index], result):
                if send:
                    other[chunk] = across_rows(picked)
                else:
                    own[chunk] = picked
            last = result[:1]
            continue
        if step == "factor":
            shapes = [jax.ShapeDtypeStruct((2 * width, width), jnp.bfloat16)] * 4
            factors = call(factor_kernel, shapes, (integrals,), last)
            last = factors[:1]
            continue
        if step == "energy":
            occ_lower, occ_upper, vir_sum = call(
                energy_kernel,
                energy_shapes,
                (pair_index[None, :], occ_energy[None, :], vir_energy[None, :]),
                last,
            )
            occ_there = across_rows(occ_upper)
            last = (vir_sum,)
            continue
        inputs = (own[index], other[index])
        if step == "first":
            result = call(first_kernel, coded_shape(index), (*inputs, factors[3]), last)
            moved[index] = two_along(result)
        elif step == "second":
            result = call(second_kernel, coded_shape(index), (*inputs, factors[1], moved[index]), last)
            crossed[index] = across_pair(result)
        elif step == "third":
            result = call(third_kernel, coded_shape(index), (*inputs, factors[2], crossed[index]), last)
            arrived[index] = two_along(result)
        elif step == "last":
            sums = (crossed[index], arrived[index], occ_lower, occ_there, vir_sum)
            result = call(functools.partial(last_kernel, begins[index]), chunk_shape(index), (*inputs, factors[0], *sums), last)
            done[index] = (result, across_rows(result))
        else:
            ready = (partner[None, :], *done[index], *placed)
            final = {}
            if (step, index) == ORDER[-1]:
                blocks = pltpu.SemaphoreType.DMA((rows // PLACE_ROWS,))
                final = {"out_spec": ANY, "scratch": (pltpu.VMEM((rows, width), jnp.bfloat16), blocks)}
            result = call(functools.partial(place_kernel, begins[index]), whole_shape, ready, last, **final)
            placed = (result,)
        last = (result,)
    return result


def solution(mesh):
    in_specs = (P("row", "col"), P("col", None), P("row"), P("row"), P(), P())
    out_specs = P("row", "col")
    return jax.shard_map(shards, mesh=mesh, in_specs=in_specs, out_specs=out_specs, check_vma=False)
```

time: 79.1 us -> 74.8 us (0.946)
  Pallas kernels: 28.2 us -> 14.2 us
  waiting for transfers between devices: 13.7 us -> 19.8 us
  starting transfers between devices: 34.3 us -> 37.7 us
    pallas_call x25 -> x26, Pallas kernels: 28.2 us -> 14.2 us  [call(): pl.pallas_call(kernel, out_shape=out_shape, in_specs=[VMEM] * count + [AN...]
    ppermute x8, waiting for transfers between devices: 2.27 us -> 5.96 us  [two_along(): lax.ppermute(value, 'col', [(i, (i + 2) % count) for i in range(count)])]
    ppermute x9, starting transfers between devices: 16.4 us -> 19.2 us  [across_rows(): lax.ppermute(value, 'row', [(i, i ^ count // 2) for i in range(count)])]
    ppermute x4, waiting for transfers between devices: 3.95 us -> 6.63 us  [across_pair(): lax.ppermute(value, 'col', [(i, i ^ 1) for i in range(lax.axis_size('col'...]
    ppermute x4, starting transfers between devices: 5.56 us -> 6.35 us  [across_pair(): lax.ppermute(value, 'col', [(i, i ^ 1) for i in range(lax.axis_size('col'...]
  transfers between devices with their start and end apart: 21 -> 21, of which waited for: 8 -> 11; matrix products, arithmetic and copies ran while one was open for 0% -> 0% of each run, Pallas kernels for 32% -> 17%
where the time goes in v6:
time: 74.8 us; the launch traced here: 74.4 us
  starting transfers between devices  37.7 us (50%)
  waiting for transfers between devices  19.8 us (26%)
  Pallas kernels  14.2 us (19%)
  local copies, waits for them, and re-layouts  2.32 us (3%)
    ppermute x9, starting transfers between devices, across_rows(): lax.ppermute(value, 'row', [(i, i ^ count // 2) for i in range(count)])  19.2 us
    pallas_call x26, Pallas kernels, call(): pl.pallas_call(kernel, out_shape=out_shape, in_specs=[VMEM] * count + [AN...  14.2 us
    ppermute x8, starting transfers between devices, two_along(): lax.ppermute(value, 'col', [(i, (i + 2) % count) for i in range(count)])  12.2 us
    ppermute x9, waiting for transfers between devices, across_rows(): lax.ppermute(value, 'row', [(i, i ^ count // 2) for i in range(count)])  7.2 us
    ppermute x4, waiting for transfers between devices, across_pair(): lax.ppermute(value, 'col', [(i, i ^ 1) for i in range(lax.axis_size('col'...  6.63 us
    ppermute x4, starting transfers between devices, across_pair(): lax.ppermute(value, 'col', [(i, i ^ 1) for i in range(lax.axis_size('col'...  6.35 us
    ppermute x8, waiting for transfers between devices, two_along(): lax.ppermute(value, 'col', [(i, (i + 2) % count) for i in range(count)])  5.96 us
    unnamed x16, local copies, waits for them, and re-layouts  2.32 us
  transfers between devices with their start and end apart: 21, of which 11 were waited for; matrix products, arithmetic and copies ran while one was open for 0% of the time, Pallas kernels for 17%

profile of v6, /device:TPU:0, one launch (start us, length us, event | category | flops | bytes accessed | tf_op | source)
XLA Modules:
  0.0 74.4 jit_solution(6101244243792261108)
XLA Ops:
  0.0 1.6 %copy-done.1 = bf16[2048,512]{1,0:T(8,128)(2,1)S(1)} copy-done((bf16[2048,512]{1,0:T(8,128)(2,1)S(1)}, bf16[2048,512]{1,0:T(8,128)(2,1)}, u32[]{:S(2)}) %copy-start.1) | copy-done | bytes 2097176
  2.3 3.7 %collective-permute-start = (bf16[256,512]{1,0:T(8,128)(2,1)S(1)}, bf16[256,512]{1,0:T(8,128)(2,1)S(1)}, u32[]{:S(2)}, u32[]{:S(2)}) collective-permute-start(bf16[256,512]{1,0:T(8,128)(2,1)S(1)} %shard_map.64.refs_2_), channel_id=1, source_target_pairs={{0,16},{8,24},{16,0},{24,8},{1,17},{9,25},{17,1},{25,9},{2,18},{10... | collective-permute-start | bytes 786440 | tf_op jit(solution)/shard_map/ppermute | solution.py:227
  6.1 1.3 %collective-permute-start.1 = (bf16[256,512]{1,0:T(8,128)(2,1)S(1)}, bf16[256,512]{1,0:T(8,128)(2,1)S(1)}, u32[]{:S(2)}, u32[]{:S(2)}) collective-permute-start(bf16[256,512]{1,0:T(8,128)(2,1)S(1)} %get-tuple-element.20.refs_1_), channel_id=1, source_target_pairs={{0,16},{8,24},{16,0},{24,8},{1,17},{9,25},{17,1},{25,9},{2,18},{10... | collective-permute-start | bytes 786440 | tf_op jit(solution)/shard_map/ppermute | solution.py:227
  7.4 1.4 %shard_map.66 = (bf16[1024,512]{1,0:T(8,128)(2,1)S(1)}, bf16[1024,512]{1,0:T(8,128)(2,1)S(1)}, bf16[1024,512]{1,0:T(8,128)(2,1)S(1)}, bf16[1024,512]{1,0:T(8,128)(2,1)S(1)}) custom-call(bf16[512,2048]{1,0:T(8,128)(2,1)S(1)} %copy-done, bf16[256,512]{1,0:T(8,128)(2,1)S(1)} %get-tuple-element.20.refs_1_), custom_call_target="tpu_custom_call" | custom-call | flops 4000000000 | bytes 1 | tf_op jit(solution)/shard_map/pallas_call | solution.py:45
  8.9 1.6 %shard_map.67 = (f32[1,1024]{1,0:T(1,128)S(1)}, f32[1,1024]{1,0:T(1,128)S(1)}, f32[1,512]{1,0:T(1,128)S(1)}) custom-call(s32[1,2048]{1,0:T(1,128)S(1)} %bitcast.4, f32[1,200]{1,0:T(1,128)S(1)} %bitcast.14, f32[1,2000]{1,0:T(1,128)S(1)} %bitcast.5, bf16[1024,512]{1,0:T(8,128)(2,1)S(1)} %get-tuple-element.22.refs_3_.refs_2_), custom_call_target="tpu_custom_call" | custom-call | flops 4000000000 | bytes 1 | tf_op jit(solution)/shard_map/pallas_call | solution.py:45
  11.3 1.8 %collective-permute-done.refs_1_ = bf16[256,512]{1,0:T(8,128)(2,1)S(1)} collective-permute-done((bf16[256,512]{1,0:T(8,128)(2,1)S(1)}, bf16[256,512]{1,0:T(8,128)(2,1)S(1)}, u32[]{:S(2)}, u32[]{:S(2)}) %collective-permute-start) | collective-permute-done | bytes 262176 | tf_op jit(solution)/shard_map/ppermute | solution.py:227
  13.7 1.6 %collective-permute-start.4 = (s16[272,512]{1,0:T(8,128)(2,1)S(1)}, s16[272,512]{1,0:T(8,128)(2,1)S(1)}, u32[]{:S(2)}, u32[]{:S(2)}) collective-permute-start(s16[272,512]{1,0:T(8,128)(2,1)S(1)} %shard_map.68.refs_2_), channel_id=1, source_target_pairs={{0,2},{1,3},{2,4},{3,5},{4,6},{5,7},{6,0},{7,1},{8,10},{9,11},{10,... | collective-permute-start | bytes 835592 | tf_op jit(solution)/shard_map/ppermute | solution.py:236
  15.3 3.3 %collective-permute-start.5 = (bf16[256,512]{1,0:T(8,128)(2,1)S(1)}, bf16[256,512]{1,0:T(8,128)(2,1)S(1)}, u32[]{:S(2)}, u32[]{:S(2)}) collective-permute-start(bf16[256,512]{1,0:T(8,128)(2,1)S(1)} %get-tuple-element.25.refs_3_), channel_id=1, source_target_pairs={{0,16},{8,24},{16,0},{24,8},{1,17},{9,25},{17,1},{25,9},{2,18},{10... | collective-permute-start | bytes 786440 | tf_op jit(solution)/shard_map/ppermute | solution.py:227
  19.3 1.6 %collective-permute-start.3 = (s16[272,512]{1,0:T(8,128)(2,1)S(1)}, s16[272,512]{1,0:T(8,128)(2,1)S(1)}, u32[]{:S(2)}, u32[]{:S(2)}) collective-permute-start(s16[272,512]{1,0:T(8,128)(2,1)S(1)} %shard_map.70.refs_2_), channel_id=1, source_target_pairs={{0,2},{1,3},{2,4},{3,5},{4,6},{5,7},{6,0},{7,1},{8,10},{9,11},{10,... | collective-permute-start | bytes 835592 | tf_op jit(solution)/shard_map/ppermute | solution.py:236
  21.0 3.6 %collective-permute-start.2 = (bf16[256,512]{1,0:T(8,128)(2,1)S(1)}, bf16[256,512]{1,0:T(8,128)(2,1)S(1)}, u32[]{:S(2)}, u32[]{:S(2)}) collective-permute-start(bf16[256,512]{1,0:T(8,128)(2,1)S(1)} %get-tuple-element.27.refs_3_), channel_id=1, source_target_pairs={{0,16},{8,24},{16,0},{24,8},{1,17},{9,25},{17,1},{25,9},{2,18},{10... | collective-permute-start | bytes 786440 | tf_op jit(solution)/shard_map/ppermute | solution.py:227
  25.1 1.6 %collective-permute-start.8 = (s16[272,512]{1,0:T(8,128)(2,1)S(1)}, s16[272,512]{1,0:T(8,128)(2,1)S(1)}, u32[]{:S(2)}, u32[]{:S(2)}) collective-permute-start(s16[272,512]{1,0:T(8,128)(2,1)S(1)} %shard_map.72.refs_4_), channel_id=1, source_target_pairs={{0,2},{1,3},{2,4},{3,5},{4,6},{5,7},{6,0},{7,1},{8,10},{9,11},{10,... | collective-permute-start | bytes 835592 | tf_op jit(solution)/shard_map/ppermute | solution.py:236
  27.2 1.6 %collective-permute-start.9 = (s16[272,512]{1,0:T(8,128)(2,1)S(1)}, s16[272,512]{1,0:T(8,128)(2,1)S(1)}, u32[]{:S(2)}, u32[]{:S(2)}) collective-permute-start(s16[272,512]{1,0:T(8,128)(2,1)S(1)} %shard_map.73.refs_4_), channel_id=1, source_target_pairs={{0,1},{1,0},{2,3},{3,2},{4,5},{5,4},{6,7},{7,6},{8,9},{9,8},{10,11... | collective-permute-start | bytes 835592 | tf_op jit(solution)/shard_map/ppermute | solution.py:231
  28.8 1.2 %collective-permute-done.3.refs_3_ = s16[272,512]{1,0:T(8,128)(2,1)S(1)} collective-permute-done((s16[272,512]{1,0:T(8,128)(2,1)S(1)}, s16[272,512]{1,0:T(8,128)(2,1)S(1)}, u32[]{:S(2)}, u32[]{:S(2)}) %collective-permute-start.3) | collective-permute-done | bytes 278560 | tf_op jit(solution)/shard_map/ppermute | solution.py:236
  30.5 1.6 %collective-permute-start.7 = (s16[272,512]{1,0:T(8,128)(2,1)S(1)}, s16[272,512]{1,0:T(8,128)(2,1)S(1)}, u32[]{:S(2)}, u32[]{:S(2)}) collective-permute-start(s16[272,512]{1,0:T(8,128)(2,1)S(1)} %shard_map.74.refs_3_), channel_id=1, source_target_pairs={{0,1},{1,0},{2,3},{3,2},{4,5},{5,4},{6,7},{7,6},{8,9},{9,8},{10,11... | collective-permute-start | bytes 835592 | tf_op jit(solution)/shard_map/ppermute | solution.py:231
  32.7 4.1 %collective-permute-done.9.refs_3_ = s16[272,512]{1,0:T(8,128)(2,1)S(1)} collective-permute-done((s16[272,512]{1,0:T(8,128)(2,1)S(1)}, s16[272,512]{1,0:T(8,128)(2,1)S(1)}, u32[]{:S(2)}, u32[]{:S(2)}) %collective-permute-start.9) | collective-permute-done | bytes 278560 | tf_op jit(solution)/shard_map/ppermute | solution.py:231
  37.3 1.7 %collective-permute-start.11 = (s16[272,512]{1,0:T(8,128)(2,1)S(1)}, s16[272,512]{1,0:T(8,128)(2,1)S(1)}, u32[]{:S(2)}, u32[]{:S(2)}) collective-permute-start(s16[272,512]{1,0:T(8,128)(2,1)S(1)} %shard_map.76.refs_4_), channel_id=1, source_target_pairs={{0,2},{1,3},{2,4},{3,5},{4,6},{5,7},{6,0},{7,1},{8,10},{9,11},{10,... | collective-permute-start | bytes 835592 | tf_op jit(solution)/shard_map/ppermute | solution.py:236
  39.5 1.6 %collective-permute-start.13 = (s16[272,512]{1,0:T(8,128)(2,1)S(1)}, s16[272,512]{1,0:T(8,128)(2,1)S(1)}, u32[]{:S(2)}, u32[]{:S(2)}) collective-permute-start(s16[272,512]{1,0:T(8,128)(2,1)S(1)} %shard_map.77.refs_4_), channel_id=1, source_target_pairs={{0,1},{1,0},{2,3},{3,2},{4,5},{5,4},{6,7},{7,6},{8,9},{9,8},{10,11... | collective-permute-start | bytes 835592 | tf_op jit(solution)/shard_map/ppermute | solution.py:231
  41.1 1.6 %collective-permute-done.7.refs_3_ = s16[272,512]{1,0:T(8,128)(2,1)S(1)} collective-permute-done((s16[272,512]{1,0:T(8,128)(2,1)S(1)}, s16[272,512]{1,0:T(8,128)(2,1)S(1)}, u32[]{:S(2)}, u32[]{:S(2)}) %collective-permute-start.7) | collective-permute-done | bytes 278560 | tf_op jit(solution)/shard_map/ppermute | solution.py:231
  43.2 1.7 %collective-permute-start.17 = (s16[272,512]{1,0:T(8,128)(2,1)S(1)}, s16[272,512]{1,0:T(8,128)(2,1)S(1)}, u32[]{:S(2)}, u32[]{:S(2)}) collective-permute-start(s16[272,512]{1,0:T(8,128)(2,1)S(1)} %shard_map.78.refs_4_), channel_id=1, source_target_pairs={{0,2},{1,3},{2,4},{3,5},{4,6},{5,7},{6,0},{7,1},{8,10},{9,11},{10,... | collective-permute-start | bytes 835592 | tf_op jit(solution)/shard_map/ppermute | solution.py:236
  45.5 1.6 %collective-permute-start.10 = (s16[272,512]{1,0:T(8,128)(2,1)S(1)}, s16[272,512]{1,0:T(8,128)(2,1)S(1)}, u32[]{:S(2)}, u32[]{:S(2)}) collective-permute-start(s16[272,512]{1,0:T(8,128)(2,1)S(1)} %shard_map.79.refs_4_), channel_id=1, source_target_pairs={{0,1},{1,0},{2,3},{3,2},{4,5},{5,4},{6,7},{7,6},{8,9},{9,8},{10,11... | collective-permute-start | bytes 835592 | tf_op jit(solution)/shard_map/ppermute | solution.py:231
  47.1 0.9 %collective-permute-done.13.refs_3_ = s16[272,512]{1,0:T(8,128)(2,1)S(1)} collective-permute-done((s16[272,512]{1,0:T(8,128)(2,1)S(1)}, s16[272,512]{1,0:T(8,128)(2,1)S(1)}, u32[]{:S(2)}, u32[]{:S(2)}) %collective-permute-start.13) | collective-permute-done | bytes 278560 | tf_op jit(solution)/shard_map/ppermute | solution.py:231
  48.5 1.8 %collective-permute-start.16 = (s16[272,512]{1,0:T(8,128)(2,1)S(1)}, s16[272,512]{1,0:T(8,128)(2,1)S(1)}, u32[]{:S(2)}, u32[]{:S(2)}) collective-permute-start(s16[272,512]{1,0:T(8,128)(2,1)S(1)} %shard_map.80.refs_8_), channel_id=1, source_target_pairs={{0,2},{1,3},{2,4},{3,5},{4,6},{5,7},{6,0},{7,1},{8,10},{9,11},{10,... | collective-permute-start | bytes 835592 | tf_op jit(solution)/shard_map/ppermute | solution.py:236
  50.9 1.6 %collective-permute-start.15 = (bf16[256,512]{1,0:T(8,128)(2,1)S(1)}, bf16[256,512]{1,0:T(8,128)(2,1)S(1)}, u32[]{:S(2)}, u32[]{:S(2)}) collective-permute-start(bf16[256,512]{1,0:T(8,128)(2,1)S(1)} %shard_map.81.refs_4_.refs_1_), channel_id=1, source_target_pairs={{0,16},{8,24},{16,0},{24,8},{1,17},{9,25},{17,1},{25,9},{2,18},{10... | collective-permute-start | bytes 786440 | tf_op jit(solution)/shard_map/ppermute | solution.py:227
  53.0 2.0 %collective-permute-start.14 = (s16[272,512]{1,0:T(8,128)(2,1)S(1)}, s16[272,512]{1,0:T(8,128)(2,1)S(1)}, u32[]{:S(2)}, u32[]{:S(2)}) collective-permute-start(s16[272,512]{1,0:T(8,128)(2,1)S(1)} %shard_map.82.refs_8_), channel_id=1, source_target_pairs={{0,2},{1,3},{2,4},{3,5},{4,6},{5,7},{6,0},{7,1},{8,10},{9,11},{10,... | collective-permute-start | bytes 835592 | tf_op jit(solution)/shard_map/ppermute | solution.py:236
  55.0 1.0 %collective-permute-done.17.refs_4_ = s16[272,512]{1,0:T(8,128)(2,1)S(1)} collective-permute-done((s16[272,512]{1,0:T(8,128)(2,1)S(1)}, s16[272,512]{1,0:T(8,128)(2,1)S(1)}, u32[]{:S(2)}, u32[]{:S(2)}) %collective-permute-start.17) | collective-permute-done | bytes 278560 | tf_op jit(solution)/shard_map/ppermute | solution.py:236
  56.5 1.7 %collective-permute-start.20 = (bf16[256,512]{1,0:T(8,128)(2,1)S(1)}, bf16[256,512]{1,0:T(8,128)(2,1)S(1)}, u32[]{:S(2)}, u32[]{:S(2)}) collective-permute-start(bf16[256,512]{1,0:T(8,128)(2,1)S(1)} %shard_map.83.refs_8_.refs_1_), channel_id=1, source_target_pairs={{0,16},{8,24},{16,0},{24,8},{1,17},{9,25},{17,1},{25,9},{2,18},{10... | collective-permute-start | bytes 786440 | tf_op jit(solution)/shard_map/ppermute | solution.py:227
  58.2 3.2 %collective-permute-done.16.refs_4_ = s16[272,512]{1,0:T(8,128)(2,1)S(1)} collective-permute-done((s16[272,512]{1,0:T(8,128)(2,1)S(1)}, s16[272,512]{1,0:T(8,128)(2,1)S(1)}, u32[]{:S(2)}, u32[]{:S(2)}) %collective-permute-start.16) | collective-permute-done | bytes 278560 | tf_op jit(solution)/shard_map/ppermute | solution.py:236
  61.9 1.6 %collective-permute-start.19 = (bf16[256,512]{1,0:T(8,128)(2,1)S(1)}, bf16[256,512]{1,0:T(8,128)(2,1)S(1)}, u32[]{:S(2)}, u32[]{:S(2)}) collective-permute-start(bf16[256,512]{1,0:T(8,128)(2,1)S(1)} %shard_map.84.refs_3_.refs_1_), channel_id=1, source_target_pairs={{0,16},{8,24},{16,0},{24,8},{1,17},{9,25},{17,1},{25,9},{2,18},{10... | collective-permute-start | bytes 786440 | tf_op jit(solution)/shard_map/ppermute | solution.py:227
  64.9 1.6 %collective-permute-start.18 = (bf16[256,512]{1,0:T(8,128)(2,1)S(1)}, bf16[256,512]{1,0:T(8,128)(2,1)S(1)}, u32[]{:S(2)}, u32[]{:S(2)}) collective-permute-start(bf16[256,512]{1,0:T(8,128)(2,1)S(1)} %shard_map.86.refs_4_.refs_1_), channel_id=1, source_target_pairs={{0,16},{8,24},{16,0},{24,8},{1,17},{9,25},{17,1},{25,9},{2,18},{10... | collective-permute-start | bytes 786440 | tf_op jit(solution)/shard_map/ppermute | solution.py:227
  66.9 2.9 %collective-permute-done.19.refs_2_ = bf16[256,512]{1,0:T(8,128)(2,1)S(1)} collective-permute-done((bf16[256,512]{1,0:T(8,128)(2,1)S(1)}, bf16[256,512]{1,0:T(8,128)(2,1)S(1)}, u32[]{:S(2)}, u32[]{:S(2)}) %collective-permute-start.19) | collective-permute-done | bytes 262176 | tf_op jit(solution)/shard_map/ppermute | solution.py:227
  70.1 2.4 %collective-permute-done.18.refs_2_ = bf16[256,512]{1,0:T(8,128)(2,1)S(1)} collective-permute-done((bf16[256,512]{1,0:T(8,128)(2,1)S(1)}, bf16[256,512]{1,0:T(8,128)(2,1)S(1)}, u32[]{:S(2)}, u32[]{:S(2)}) %collective-permute-start.18) | collective-permute-done | bytes 262176 | tf_op jit(solution)/shard_map/ppermute | solution.py:227
  72.5 1.7 %shard_map.89 = bf16[2048,512]{1,0:T(8,128)(2,1)} custom-call(s32[1,2048]{1,0:T(1,128)S(1)} %bitcast.13, bf16[256,512]{1,0:T(8,128)(2,1)S(1)} %shard_map.86.refs_4_.refs_1_, bf16[256,512]{1,0:T(8,128)(2,1)S(1)} %collective-permute-done.18.refs_2_, bf16[2048,512]{1,0:T(8,128)(2,1)S(1)} %shard_map.88.refs_3_.refs_4_, ...), custom_call_target="tpu_custom_call" | custom-call | flops 4000000000 | bytes 1 | tf_op jit(solution)/shard_map/pallas_call | solution.py:45
  (52 shorter events, 11.7 us)
Async XLA Ops:
  0.0 1.6 %copy-start.1 = (bf16[2048,512]{1,0:T(8,128)(2,1)S(1)}, bf16[2048,512]{1,0:T(8,128)(2,1)}, u32[]{:S(2)}) copy-start(bf16[2048,512]{1,0:T(8,128)(2,1)} %refs_1_.7) | copy-start | bytes 6291460
  1.6 0.7 copy-start.5
  2.3 5.1 %copy-start = (bf16[512,2048]{1,0:T(8,128)(2,1)S(1)}, bf16[512,2048]{1,0:T(8,128)(2,1)}, u32[]{:S(2)}) copy-start(bf16[512,2048]{1,0:T(8,128)(2,1)} %refs_0_.1) | copy-start | bytes 6291460
  2.3 10.8 %collective-permute-start = (bf16[256,512]{1,0:T(8,128)(2,1)S(1)}, bf16[256,512]{1,0:T(8,128)(2,1)S(1)}, u32[]{:S(2)}, u32[]{:S(2)}) collective-permute-start(bf16[256,512]{1,0:T(8,128)(2,1)S(1)} %shard_map.64.refs_2_), channel_id=1, source_target_pairs={{0,16},{8,24},{16,0},{24,8},{1,17},{9,25},{17,1},{25,9},{2,18},{10... | collective-permute-start | bytes 786440 | tf_op jit(solution)/shard_map/ppermute | solution.py:227
  6.1 2.8 %copy-start.3 = (s32[2048]{0:T(1024)S(1)}, s32[2048]{0:T(1024)}, u32[]{:S(2)}) copy-start(s32[2048]{0:T(1024)} %param.8) | copy-start | bytes 24580
  6.1 2.8 %copy-start.4 = (f32[2000]{0:T(1024)S(1)}, f32[2000]{0:T(1024)}, u32[]{:S(2)}) copy-start(f32[2000]{0:T(1024)} %param.11) | copy-start | bytes 24004
  6.1 2.8 %copy-start.7 = (f32[200]{0:T(256)S(1)}, f32[200]{0:T(256)}, u32[]{:S(2)}) copy-start(f32[200]{0:T(256)} %param.10) | copy-start | bytes 2404
  6.1 12.7 %collective-permute-start.1 = (bf16[256,512]{1,0:T(8,128)(2,1)S(1)}, bf16[256,512]{1,0:T(8,128)(2,1)S(1)}, u32[]{:S(2)}, u32[]{:S(2)}) collective-permute-start(bf16[256,512]{1,0:T(8,128)(2,1)S(1)} %get-tuple-element.20.refs_1_), channel_id=1, source_target_pairs={{0,16},{8,24},{16,0},{24,8},{1,17},{9,25},{17,1},{25,9},{2,18},{10... | collective-permute-start | bytes 786440 | tf_op jit(solution)/shard_map/ppermute | solution.py:227
  10.5 39.9 %collective-permute-start.12 = (f32[1,1024]{1,0:T(1,128)S(1)}, f32[1,1024]{1,0:T(1,128)S(1)}, u32[]{:S(2)}, u32[]{:S(2)}) collective-permute-start(f32[1,1024]{1,0:T(1,128)S(1)} %get-tuple-element.32), channel_id=1, source_target_pairs={{0,16},{8,24},{16,0},{24,8},{1,17},{9,25},{17,1},{25,9},{2,18},{10... | collective-permute-start | bytes 12296 | tf_op jit(solution)/shard_map/ppermute | solution.py:227
  13.1 2.2 %copy-start.2 = (bf16[2048,512]{1,0:T(8,128)(2,1)S(1)}, bf16[2048,512]{1,0:T(8,128)(2,1)}, u32[]{:S(2)}) copy-start(bf16[2048,512]{1,0:T(8,128)(2,1)} %refs_1_.7) | copy-start | bytes 6291460
  13.2 2.2 %copy-start.6 = (s32[2048]{0:T(1024)S(1)}, s32[2048]{0:T(1024)}, u32[]{:S(2)}) copy-start(s32[2048]{0:T(1024)} %param.9) | copy-start | bytes 24580
  13.7 13.1 %collective-permute-start.4 = (s16[272,512]{1,0:T(8,128)(2,1)S(1)}, s16[272,512]{1,0:T(8,128)(2,1)S(1)}, u32[]{:S(2)}, u32[]{:S(2)}) collective-permute-start(s16[272,512]{1,0:T(8,128)(2,1)S(1)} %shard_map.68.refs_2_), channel_id=1, source_target_pairs={{0,2},{1,3},{2,4},{3,5},{4,6},{5,7},{6,0},{7,1},{8,10},{9,11},{10,... | collective-permute-start | bytes 835592 | tf_op jit(solution)/shard_map/ppermute | solution.py:236
  15.3 9.2 %collective-permute-start.5 = (bf16[256,512]{1,0:T(8,128)(2,1)S(1)}, bf16[256,512]{1,0:T(8,128)(2,1)S(1)}, u32[]{:S(2)}, u32[]{:S(2)}) collective-permute-start(bf16[256,512]{1,0:T(8,128)(2,1)S(1)} %get-tuple-element.25.refs_3_), channel_id=1, source_target_pairs={{0,16},{8,24},{16,0},{24,8},{1,17},{9,25},{17,1},{25,9},{2,18},{10... | collective-permute-start | bytes 786440 | tf_op jit(solution)/shard_map/ppermute | solution.py:227
  19.3 10.7 %collective-permute-start.3 = (s16[272,512]{1,0:T(8,128)(2,1)S(1)}, s16[272,512]{1,0:T(8,128)(2,1)S(1)}, u32[]{:S(2)}, u32[]{:S(2)}) collective-permute-start(s16[272,512]{1,0:T(8,128)(2,1)S(1)} %shard_map.70.refs_2_), channel_id=1, source_target_pairs={{0,2},{1,3},{2,4},{3,5},{4,6},{5,7},{6,0},{7,1},{8,10},{9,11},{10,... | collective-permute-start | bytes 835592 | tf_op jit(solution)/shard_map/ppermute | solution.py:236
  21.0 11.1 %collective-permute-start.2 = (bf16[256,512]{1,0:T(8,128)(2,1)S(1)}, bf16[256,512]{1,0:T(8,128)(2,1)S(1)}, u32[]{:S(2)}, u32[]{:S(2)}) collective-permute-start(bf16[256,512]{1,0:T(8,128)(2,1)S(1)} %get-tuple-element.27.refs_3_), channel_id=1, source_target_pairs={{0,16},{8,24},{16,0},{24,8},{1,17},{9,25},{17,1},{25,9},{2,18},{10... | collective-permute-start | bytes 786440 | tf_op jit(solution)/shard_map/ppermute | solution.py:227
  25.1 13.9 %collective-permute-start.8 = (s16[272,512]{1,0:T(8,128)(2,1)S(1)}, s16[272,512]{1,0:T(8,128)(2,1)S(1)}, u32[]{:S(2)}, u32[]{:S(2)}) collective-permute-start(s16[272,512]{1,0:T(8,128)(2,1)S(1)} %shard_map.72.refs_4_), channel_id=1, source_target_pairs={{0,2},{1,3},{2,4},{3,5},{4,6},{5,7},{6,0},{7,1},{8,10},{9,11},{10,... | collective-permute-start | bytes 835592 | tf_op jit(solution)/shard_map/ppermute | solution.py:236
  27.2 9.5 %collective-permute-start.9 = (s16[272,512]{1,0:T(8,128)(2,1)S(1)}, s16[272,512]{1,0:T(8,128)(2,1)S(1)}, u32[]{:S(2)}, u32[]{:S(2)}) collective-permute-start(s16[272,512]{1,0:T(8,128)(2,1)S(1)} %shard_map.73.refs_4_), channel_id=1, source_target_pairs={{0,1},{1,0},{2,3},{3,2},{4,5},{5,4},{6,7},{7,6},{8,9},{9,8},{10,11... | collective-permute-start | bytes 835592 | tf_op jit(solution)/shard_map/ppermute | solution.py:231
  30.5 12.2 %collective-permute-start.7 = (s16[272,512]{1,0:T(8,128)(2,1)S(1)}, s16[272,512]{1,0:T(8,128)(2,1)S(1)}, u32[]{:S(2)}, u32[]{:S(2)}) collective-permute-start(s16[272,512]{1,0:T(8,128)(2,1)S(1)} %shard_map.74.refs_3_), channel_id=1, source_target_pairs={{0,1},{1,0},{2,3},{3,2},{4,5},{5,4},{6,7},{7,6},{8,9},{9,8},{10,11... | collective-permute-start | bytes 835592 | tf_op jit(solution)/shard_map/ppermute | solution.py:231
  32.6 12.3 %collective-permute-start.6 = (s16[272,512]{1,0:T(8,128)(2,1)S(1)}, s16[272,512]{1,0:T(8,128)(2,1)S(1)}, u32[]{:S(2)}, u32[]{:S(2)}) collective-permute-start(s16[272,512]{1,0:T(8,128)(2,1)S(1)} %shard_map.75.refs_4_), channel_id=1, source_target_pairs={{0,2},{1,3},{2,4},{3,5},{4,6},{5,7},{6,0},{7,1},{8,10},{9,11},{10,... | collective-permute-start | bytes 835592 | tf_op jit(solution)/shard_map/ppermute | solution.py:236
  37.3 13.1 %collective-permute-start.11 = (s16[272,512]{1,0:T(8,128)(2,1)S(1)}, s16[272,512]{1,0:T(8,128)(2,1)S(1)}, u32[]{:S(2)}, u32[]{:S(2)}) collective-permute-start(s16[272,512]{1,0:T(8,128)(2,1)S(1)} %shard_map.76.refs_4_), channel_id=1, source_target_pairs={{0,2},{1,3},{2,4},{3,5},{4,6},{5,7},{6,0},{7,1},{8,10},{9,11},{10,... | collective-permute-start | bytes 835592 | tf_op jit(solution)/shard_map/ppermute | solution.py:236
  39.5 8.5 %collective-permute-start.13 = (s16[272,512]{1,0:T(8,128)(2,1)S(1)}, s16[272,512]{1,0:T(8,128)(2,1)S(1)}, u32[]{:S(2)}, u32[]{:S(2)}) collective-permute-start(s16[272,512]{1,0:T(8,128)(2,1)S(1)} %shard_map.77.refs_4_), channel_id=1, source_target_pairs={{0,1},{1,0},{2,3},{3,2},{4,5},{5,4},{6,7},{7,6},{8,9},{9,8},{10,11... | collective-permute-start | bytes 835592 | tf_op jit(solution)/shard_map/ppermute | solution.py:231
  43.2 12.8 %collective-permute-start.17 = (s16[272,512]{1,0:T(8,128)(2,1)S(1)}, s16[272,512]{1,0:T(8,128)(2,1)S(1)}, u32[]{:S(2)}, u32[]{:S(2)}) collective-permute-start(s16[272,512]{1,0:T(8,128)(2,1)S(1)} %shard_map.78.refs_4_), channel_id=1, source_target_pairs={{0,2},{1,3},{2,4},{3,5},{4,6},{5,7},{6,0},{7,1},{8,10},{9,11},{10,... | collective-permute-start | bytes 835592 | tf_op jit(solution)/shard_map/ppermute | solution.py:236
  45.5 7.0 %collective-permute-start.10 = (s16[272,512]{1,0:T(8,128)(2,1)S(1)}, s16[272,512]{1,0:T(8,128)(2,1)S(1)}, u32[]{:S(2)}, u32[]{:S(2)}) collective-permute-start(s16[272,512]{1,0:T(8,128)(2,1)S(1)} %shard_map.79.refs_4_), channel_id=1, source_target_pairs={{0,1},{1,0},{2,3},{3,2},{4,5},{5,4},{6,7},{7,6},{8,9},{9,8},{10,11... | collective-permute-start | bytes 835592 | tf_op jit(solution)/shard_map/ppermute | solution.py:231
  48.5 12.8 %collective-permute-start.16 = (s16[272,512]{1,0:T(8,128)(2,1)S(1)}, s16[272,512]{1,0:T(8,128)(2,1)S(1)}, u32[]{:S(2)}, u32[]{:S(2)}) collective-permute-start(s16[272,512]{1,0:T(8,128)(2,1)S(1)} %shard_map.80.refs_8_), channel_id=1, source_target_pairs={{0,2},{1,3},{2,4},{3,5},{4,6},{5,7},{6,0},{7,1},{8,10},{9,11},{10,... | collective-permute-start | bytes 835592 | tf_op jit(solution)/shard_map/ppermute | solution.py:236
  50.9 12.6 %collective-permute-start.15 = (bf16[256,512]{1,0:T(8,128)(2,1)S(1)}, bf16[256,512]{1,0:T(8,128)(2,1)S(1)}, u32[]{:S(2)}, u32[]{:S(2)}) collective-permute-start(bf16[256,512]{1,0:T(8,128)(2,1)S(1)} %shard_map.81.refs_4_.refs_1_), channel_id=1, source_target_pairs={{0,16},{8,24},{16,0},{24,8},{1,17},{9,25},{17,1},{25,9},{2,18},{10... | collective-permute-start | bytes 786440 | tf_op jit(solution)/shard_map/ppermute | solution.py:227
  53.0 11.3 %collective-permute-start.14 = (s16[272,512]{1,0:T(8,128)(2,1)S(1)}, s16[272,512]{1,0:T(8,128)(2,1)S(1)}, u32[]{:S(2)}, u32[]{:S(2)}) collective-permute-start(s16[272,512]{1,0:T(8,128)(2,1)S(1)} %shard_map.82.refs_8_), channel_id=1, source_target_pairs={{0,2},{1,3},{2,4},{3,5},{4,6},{5,7},{6,0},{7,1},{8,10},{9,11},{10,... | collective-permute-start | bytes 835592 | tf_op jit(solution)/shard_map/ppermute | solution.py:236
  56.5 10.0 %collective-permute-start.20 = (bf16[256,512]{1,0:T(8,128)(2,1)S(1)}, bf16[256,512]{1,0:T(8,128)(2,1)S(1)}, u32[]{:S(2)}, u32[]{:S(2)}) collective-permute-start(bf16[256,512]{1,0:T(8,128)(2,1)S(1)} %shard_map.83.refs_8_.refs_1_), channel_id=1, source_target_pairs={{0,16},{8,24},{16,0},{24,8},{1,17},{9,25},{17,1},{25,9},{2,18},{10... | collective-permute-start | bytes 786440 | tf_op jit(solution)/shard_map/ppermute | solution.py:227
  61.9 7.8 %collective-permute-start.19 = (bf16[256,512]{1,0:T(8,128)(2,1)S(1)}, bf16[256,512]{1,0:T(8,128)(2,1)S(1)}, u32[]{:S(2)}, u32[]{:S(2)}) collective-permute-start(bf16[256,512]{1,0:T(8,128)(2,1)S(1)} %shard_map.84.refs_3_.refs_1_), channel_id=1, source_target_pairs={{0,16},{8,24},{16,0},{24,8},{1,17},{9,25},{17,1},{25,9},{2,18},{10... | collective-permute-start | bytes 786440 | tf_op jit(solution)/shard_map/ppermute | solution.py:227
  64.9 7.6 %collective-permute-start.18 = (bf16[256,512]{1,0:T(8,128)(2,1)S(1)}, bf16[256,512]{1,0:T(8,128)(2,1)S(1)}, u32[]{:S(2)}, u32[]{:S(2)}) collective-permute-start(bf16[256,512]{1,0:T(8,128)(2,1)S(1)} %shard_map.86.refs_4_.refs_1_), channel_id=1, source_target_pairs={{0,16},{8,24},{16,0},{24,8},{1,17},{9,25},{17,1},{25,9},{2,18},{10... | collective-permute-start | bytes 786440 | tf_op jit(solution)/shard_map/ppermute | solution.py:227

commit v7 on v6

--- a/solution.py
+++ b/solution.py
@@ -19,24 +19,24 @@
 VMEM_LIMIT = 16 * 1024 * 1024
 KERNEL_FLOPS = 4 * 10**9
 ORDER = (
-    (("align", 0), ("align", 1), ("factor", 0), ("energy", 0), ("first", 0), ("align", 2))
-    + (("first", 1), ("align", 3), ("first", 2), ("second", 0), ("second", 1), ("first", 3))
-    + (("third", 0), ("second", 2), ("third", 1), ("second", 3), ("third", 2), ("last", 0))
-    + (("third", 3), ("last", 1), ("last", 2), ("place", 0), ("last", 3), ("place", 1))
-    + (("place", 2), ("place", 3))
+    (("align", 1), ("factor", 0), ("energy", 0), ("first", 0), ("align", 2), ("first", 1))
+    + (("align", 3), ("first", 2), ("second", 0), ("second", 1), ("first", 3), ("third", 0))
+    + (("second", 2), ("second", 3), ("third", 1), ("third", 2), ("last", 0), ("third", 3))
+    + (("last", 1), ("last", 2), ("last", 3), ("place", 0), ("place", 1), ("place", 2))
 )
 ALIGNED = (
-    ((0, True),),
+    (),
     ((1, True), (0, False)),
     ((2, True), (1, False)),
     ((3, True), (2, False), (3, False)),
 )
 
 VMEM = pl.BlockSpec(memory_space=pltpu.VMEM)
+HBM = pl.BlockSpec(memory_space=pltpu.HBM)
 ANY = pl.BlockSpec(memory_space=pl.ANY)
 
 
-def call(body, out_shape, operands, after=(), out_spec=None, scratch=()):
+def call(body, out_shape, operands, after=(), in_spec=None, out_spec=None, scratch=()):
     count = len(operands)
 
     def kernel(*refs):
@@ -45,7 +45,7 @@
     return pl.pallas_call(
         kernel,
         out_shape=out_shape,
-        in_specs=[VMEM] * count + [ANY] * len(after),
+        in_specs=[in_spec or VMEM] * count + [ANY] * len(after),
         out_specs=jax.tree.map(lambda _: out_spec or VMEM, out_shape),
         scratch_shapes=list(scratch),
         compiler_params=pltpu.CompilerParams(vmem_limit_bytes=VMEM_LIMIT),
@@ -89,6 +89,40 @@
             target = partner_base(rows) + first(index) + lax.broadcasted_iota(jnp.int32, (out.shape[0], rows), 0)
             pick = jnp.where(partner[...] == target, 1.0, 0.0).astype(jnp.bfloat16)
             out[...] = jnp.dot(pick, amplitudes[...], preferred_element_type=jnp.float32).astype(jnp.bfloat16)
+
+
+def align_first_kernel(partner, amplitudes, out, held, slots, arrivals):
+    rows, chunk = amplitudes.shape[0], out.shape[0]
+    upper = upper_side()
+    first = (1 - upper) * (rows // 2)
+    blocks = rows // chunk
+
+    def fetch(block):
+        part = pl.ds(block * chunk, chunk)
+        return pltpu.make_async_copy(amplitudes.at[part, :], held.at[part, :], arrivals.at[block])
+
+    @pl.when(upper == 0)
+    def _():
+        part = pl.ds(pl.multiple_of(first, LANES), chunk)
+        straight = pltpu.make_async_copy(amplitudes.at[part, :], out, arrivals.at[0])
+        straight.start()
+        straight.wait()
+
+    @pl.when(upper == 1)
+    def _():
+        slots_copy = pltpu.make_async_copy(partner, slots, arrivals.at[blocks])
+        slots_copy.start()
+        for block in range(blocks):
+            fetch(block).start()
+        slots_copy.wait()
+        target = partner_base(rows) + first + lax.broadcasted_iota(jnp.int32, (chunk, chunk), 0)
+        total = jnp.zeros(out.shape, jnp.float32)
+        for block in range(blocks):
+            part = pl.ds(block * chunk, chunk)
+            pick = jnp.where(slots[:, part] == target, 1.0, 0.0).astype(jnp.bfloat16)
+            fetch(block).wait()
+            total += jnp.dot(pick, held[part, :], preferred_element_type=jnp.float32)
+        out[...] = total.astype(jnp.bfloat16)
 
 
 def factor_kernel(integrals, *outs):
@@ -145,52 +179,89 @@
         out[:, lane : lane + LANES] = (total[:, lane : lane + LANES] / denom).astype(jnp.bfloat16)
 
 
+def pick_rows(partner, block, size, begin, count):
+    slots = jnp.broadcast_to(partner[:, pl.ds(block * size, size)], (LANES, size)).T
+    lanes = lax.broadcasted_iota(jnp.int32, (size, LANES), 1) + (partner_base(partner.shape[1]) + begin)
+    parts = [jnp.where(slots == lanes + lane, 1.0, 0.0) for lane in range(0, count, LANES)]
+    return jnp.concatenate(parts, axis=1).astype(jnp.bfloat16)
+
+
 def place_kernel(begin, partner, own, other, *refs):
-    held, arrivals = refs[-2:] if len(refs) > 2 else (refs[-1], None)
-    earlier = refs[0] if len(refs) != 1 else None
-    rows, width = held.shape
-    chunk = own.shape[0]
+    earlier, out = refs[:-1], refs[-1]
+    rows, chunk = out.shape[0], own.shape[0]
     upper = upper_side()
     here = upper * (rows // 2) + begin
     there = (1 - upper) * (rows // 2) + begin
     opposite = exchanged(other[...].astype(jnp.float32)).astype(jnp.bfloat16)
 
-    def leave(block):
-        part = pl.ds(block * PLACE_ROWS, PLACE_ROWS)
-        return pltpu.make_async_copy(held.at[part, :], refs[-3].at[part, :], arrivals.at[block])
-
-    @pl.when(upper == 0)
-    def _():
-        if earlier is not None:
-            held[...] = earlier[...]
-        held[pl.ds(pl.multiple_of(here, LANES), chunk), :] = own[...]
-        held[pl.ds(pl.multiple_of(there, LANES), chunk), :] = opposite
-        if arrivals is not None:
-            for block in range(rows // PLACE_ROWS):
-                leave(block).start()
-
-    @pl.when(upper == 1)
-    def _():
-        lanes = lax.broadcasted_iota(jnp.int32, (PLACE_ROWS, LANES), 1) + partner_base(rows)
-
-        def pick(slots, begin):
-            parts = [jnp.where(slots == lanes + (begin + lane), 1.0, 0.0) for lane in range(0, chunk, LANES)]
-            return jnp.concatenate(parts, axis=1).astype(jnp.bfloat16)
-
+    @pl.when(upper == 0)
+    def _():
+        if earlier:
+            out[...] = earlier[0][...]
+        out[pl.ds(pl.multiple_of(here, LANES), chunk), :] = own[...]
+        out[pl.ds(pl.multiple_of(there, LANES), chunk), :] = opposite
+
+    @pl.when(upper == 1)
+    def _():
         for block in range(rows // PLACE_ROWS):
             part = pl.ds(block * PLACE_ROWS, PLACE_ROWS)
-            slots = jnp.broadcast_to(partner[:, part], (LANES, PLACE_ROWS)).T
-            found = jnp.dot(pick(slots, here), own[...], preferred_element_type=jnp.float32)
-            found += jnp.dot(pick(slots, there), opposite, preferred_element_type=jnp.float32)
-            if earlier is not None:
-                found += earlier[part, :].astype(jnp.float32)
-            held[part, :] = found.astype(jnp.bfloat16)
-            if arrivals is not None:
-                leave(block).start()
-
-    if arrivals is not None:
+            pick = pick_rows(partner, block, PLACE_ROWS, here, chunk)
+            found = jnp.dot(pick, own[...], preferred_element_type=jnp.float32)
+            pick = pick_rows(partner, block, PLACE_ROWS, there, chunk)
+            found += jnp.dot(pick, opposite, preferred_element_type=jnp.float32)
+            if earlier:
+                found += earlier[0][part, :].astype(jnp.float32)
+            out[part, :] = found.astype(jnp.bfloat16)
+
+
+def place_own_kernel(begin, partner, own, earlier, out, picks):
+    rows, chunk = out.shape[0], own.shape[0]
+    upper = upper_side()
+    here = upper * (rows // 2) + begin
+    there = (1 - upper) * (rows // 2) + begin
+
+    @pl.when(upper == 0)
+    def _():
+        out[...] = earlier[...]
+        out[pl.ds(pl.multiple_of(here, LANES), chunk), :] = own[...]
+
+    @pl.when(upper == 1)
+    def _():
         for block in range(rows // PLACE_ROWS):
-            leave(block).wait()
+            part = pl.ds(block * PLACE_ROWS, PLACE_ROWS)
+            pick = pick_rows(partner, block, PLACE_ROWS, here, chunk)
+            found = jnp.dot(pick, own[...], preferred_element_type=jnp.float32)
+            out[part, :] = (found + earlier[part, :].astype(jnp.float32)).astype(jnp.bfloat16)
+            picks[part, :] = pick_rows(partner, block, PLACE_ROWS, there, chunk)
+
+
+def place_other_kernel(begin, earlier, picks, other, out, held, arrivals):
+    rows, chunk = held.shape[0], other.shape[0]
+    upper = upper_side()
+    there = (1 - upper) * (rows // 2) + begin
+    opposite = exchanged(other[...].astype(jnp.float32)).astype(jnp.bfloat16)
+
+    def leave(block):
+        part = pl.ds(block * chunk, chunk)
+        return pltpu.make_async_copy(held.at[part, :], out.at[part, :], arrivals.at[block])
+
+    @pl.when(upper == 0)
+    def _():
+        for block in range(rows // chunk):
+            part = pl.ds(block * chunk, chunk)
+            held[part, :] = jnp.where(there == block * chunk, opposite, earlier[part, :])
+            leave(block).start()
+
+    @pl.when(upper == 1)
+    def _():
+        for block in range(rows // chunk):
+            part = pl.ds(block * chunk, chunk)
+            found = jnp.dot(picks[part, :], opposite, preferred_element_type=jnp.float32)
+            held[part, :] = (found + earlier[part, :].astype(jnp.float32)).astype(jnp.bfloat16)
+            leave(block).start()
+
+    for block in range(rows // chunk):
+        leave(block).wait()
 
 
 def split_index(values, count):
@@ -253,7 +324,12 @@
     energy_shapes = [half_shape, half_shape, jax.ShapeDtypeStruct((1, width), jnp.float32)]
 
     own, other, moved, crossed, arrived, done, placed = {}, {}, {}, {}, {}, {}, ()
-    last = ()
+    operands = [pltpu.with_memory_space_constraint(value, pltpu.HBM) for value in (partner[None, :], amplitudes)]
+    room = (pltpu.VMEM((rows, width), jnp.bfloat16), pltpu.VMEM((1, rows), jnp.int32))
+    room += (pltpu.SemaphoreType.DMA((rows // chunks[0] + 1,)),)
+    result = call(align_first_kernel, chunk_shape(0), operands, in_spec=HBM, scratch=room)
+    other[0] = across_rows(result)
+    last = (result,)
     for step, index in ORDER:
         if step == "align":
             wanted = tuple((begins[chunk], send) for chunk, send in ALIGNED[index])
@@ -297,14 +373,19 @@
             done[index] = (result, across_rows(result))
         else:
             ready = (partner[None, :], *done[index], *placed)
-            final = {}
-            if (step, index) == ORDER[-1]:
-                blocks = pltpu.SemaphoreType.DMA((rows // PLACE_ROWS,))
-                final = {"out_spec": ANY, "scratch": (pltpu.VMEM((rows, width), jnp.bfloat16), blocks)}
-            result = call(functools.partial(place_kernel, begins[index]), whole_shape, ready, last, **final)
+            result = call(functools.partial(place_kernel, begins[index]), whole_shape, ready, last)
             placed = (result,)
         last = (result,)
-    return result
+
+    index = len(SHARES) - 1
+    mine, theirs = done[index]
+    picks_shape = jax.ShapeDtypeStruct((rows, chunks[index]), jnp.bfloat16)
+    kernel = functools.partial(place_own_kernel, begins[index])
+    most, picks = call(kernel, [whole_shape, picks_shape], (partner[None, :], mine, *placed), last)
+    held = pltpu.VMEM((rows, width), jnp.bfloat16)
+    arrivals = pltpu.SemaphoreType.DMA((rows // chunks[index],))
+    kernel = functools.partial(place_other_kernel, begins[index])
+    return call(kernel, whole_shape, (most, picks, theirs), out_spec=ANY, scratch=(held, arrivals))
 
 
 def solution(mesh):

time: 74.8 us -> 73.7 us (0.985)
  local copies, waits for them, and re-layouts: 2.32 us -> 0.03 us
  starting transfers between devices: 37.7 us -> 36.3 us
  waiting for transfers between devices: 19.8 us -> 21.2 us
  Pallas kernels: 14.2 us -> 15.4 us
    unnamed x16 -> x12, local copies, waits for them, and re-layouts: 2.32 us -> 0.03 us
    ppermute x8, waiting for transfers between devices: 5.96 us -> 7.8 us  [two_along(): lax.ppermute(value, 'col', [(i, (i + 2) % count) for i in range(count)])]
    pallas_call x26 -> x27, Pallas kernels: 14.2 us -> 15.4 us  [call(): pl.pallas_call(kernel, out_shape=out_shape, in_specs=[in_spec or VMEM] *...]
    ppermute x4, starting transfers between devices: 6.35 us -> 5.33 us  [across_pair(): lax.ppermute(value, 'col', [(i, i ^ 1) for i in range(lax.axis_size('col'...]
    ppermute x9, waiting for transfers between devices: 7.2 us -> 6.41 us  [across_rows(): lax.ppermute(value, 'row', [(i, i ^ count // 2) for i in range(count)])]
where the time goes in v7:
time: 73.7 us; the launch traced here: 73.4 us
  starting transfers between devices  36.3 us (49%)
  waiting for transfers between devices  21.2 us (29%)
  Pallas kernels  15.4 us (21%)
    ppermute x9, starting transfers between devices, across_rows(): lax.ppermute(value, 'row', [(i, i ^ count // 2) for i in range(count)])  19.1 us
    pallas_call x27, Pallas kernels, call(): pl.pallas_call(kernel, out_shape=out_shape, in_specs=[in_spec or VMEM] *...  15.4 us
    ppermute x8, starting transfers between devices, two_along(): lax.ppermute(value, 'col', [(i, (i + 2) % count) for i in range(count)])  11.9 us
    ppermute x8, waiting for transfers between devices, two_along(): lax.ppermute(value, 'col', [(i, (i + 2) % count) for i in range(count)])  7.8 us
    ppermute x4, waiting for transfers between devices, across_pair(): lax.ppermute(value, 'col', [(i, i ^ 1) for i in range(lax.axis_size('col'...  7.02 us
    ppermute x9, waiting for transfers between devices, across_rows(): lax.ppermute(value, 'row', [(i, i ^ count // 2) for i in range(count)])  6.41 us
    ppermute x4, starting transfers between devices, across_pair(): lax.ppermute(value, 'col', [(i, i ^ 1) for i in range(lax.axis_size('col'...  5.33 us
  transfers between devices with their start and end apart: 21, of which 11 were waited for; matrix products, arithmetic and copies ran while one was open for 0% of the time, Pallas kernels for 17%

profile of v7, /device:TPU:0, one launch (start us, length us, event | category | flops | bytes accessed | tf_op | source)
XLA Modules:
  0.0 73.4 jit_solution(6974410639728268362)
XLA Ops:
  0.0 1.2 %shard_map.64.refs_2_ = bf16[256,512]{1,0:T(8,128)(2,1)S(1)} custom-call(s32[1,2048]{1,0:T(1,128)} %bitcast.6, bf16[2048,512]{1,0:T(8,128)(2,1)} %refs_1_.7), custom_call_target="tpu_custom_call" | custom-call | flops 4000000000 | bytes 1 | tf_op jit(solution)/shard_map/pallas_call | solution.py:45
  1.2 4.2 %collective-permute-start = (bf16[256,512]{1,0:T(8,128)(2,1)S(1)}, bf16[256,512]{1,0:T(8,128)(2,1)S(1)}, u32[]{:S(2)}, u32[]{:S(2)}) collective-permute-start(bf16[256,512]{1,0:T(8,128)(2,1)S(1)} %shard_map.64.refs_2_), channel_id=1, source_target_pairs={{0,16},{8,24},{16,0},{24,8},{1,17},{9,25},{17,1},{25,9},{2,18},{10... | collective-permute-start | bytes 786440 | tf_op jit(solution)/shard_map/ppermute | solution.py:298
  5.5 1.3 %collective-permute-start.1 = (bf16[256,512]{1,0:T(8,128)(2,1)S(1)}, bf16[256,512]{1,0:T(8,128)(2,1)S(1)}, u32[]{:S(2)}, u32[]{:S(2)}) collective-permute-start(bf16[256,512]{1,0:T(8,128)(2,1)S(1)} %get-tuple-element.22.refs_1_), channel_id=1, source_target_pairs={{0,16},{8,24},{16,0},{24,8},{1,17},{9,25},{17,1},{25,9},{2,18},{10... | collective-permute-start | bytes 786440 | tf_op jit(solution)/shard_map/ppermute | solution.py:298
  6.8 1.4 %shard_map.66 = (bf16[1024,512]{1,0:T(8,128)(2,1)S(1)}, bf16[1024,512]{1,0:T(8,128)(2,1)S(1)}, bf16[1024,512]{1,0:T(8,128)(2,1)S(1)}, bf16[1024,512]{1,0:T(8,128)(2,1)S(1)}) custom-call(bf16[512,2048]{1,0:T(8,128)(2,1)S(1)} %copy-done, bf16[256,512]{1,0:T(8,128)(2,1)S(1)} %get-tuple-element.22.refs_1_), custom_call_target="tpu_custom_call" | custom-call | flops 4000000000 | bytes 1 | tf_op jit(solution)/shard_map/pallas_call | solution.py:45
  8.3 1.6 %shard_map.67 = (f32[1,1024]{1,0:T(1,128)S(1)}, f32[1,1024]{1,0:T(1,128)S(1)}, f32[1,512]{1,0:T(1,128)S(1)}) custom-call(s32[1,2048]{1,0:T(1,128)S(1)} %bitcast.4, f32[1,200]{1,0:T(1,128)S(1)} %bitcast.14, f32[1,2000]{1,0:T(1,128)S(1)} %bitcast.5, bf16[1024,512]{1,0:T(8,128)(2,1)S(1)} %get-tuple-element.24.refs_3_.refs_2_), custom_call_target="tpu_custom_call" | custom-call | flops 4000000000 | bytes 1 | tf_op jit(solution)/shard_map/pallas_call | solution.py:45
  9.9 0.8 %collective-permute-start.11 = (f32[1,1024]{1,0:T(1,128)S(1)}, f32[1,1024]{1,0:T(1,128)S(1)}, u32[]{:S(2)}, u32[]{:S(2)}) collective-permute-start(f32[1,1024]{1,0:T(1,128)S(1)} %get-tuple-element.34), channel_id=1, source_target_pairs={{0,16},{8,24},{16,0},{24,8},{1,17},{9,25},{17,1},{25,9},{2,18},{10... | collective-permute-start | bytes 12296 | tf_op jit(solution)/shard_map/ppermute | solution.py:298
  10.7 1.8 %collective-permute-done.refs_1_ = bf16[256,512]{1,0:T(8,128)(2,1)S(1)} collective-permute-done((bf16[256,512]{1,0:T(8,128)(2,1)S(1)}, bf16[256,512]{1,0:T(8,128)(2,1)S(1)}, u32[]{:S(2)}, u32[]{:S(2)}) %collective-permute-start) | collective-permute-done | bytes 262176 | tf_op jit(solution)/shard_map/ppermute | solution.py:298
  13.0 1.6 %collective-permute-start.4 = (s16[272,512]{1,0:T(8,128)(2,1)S(1)}, s16[272,512]{1,0:T(8,128)(2,1)S(1)}, u32[]{:S(2)}, u32[]{:S(2)}) collective-permute-start(s16[272,512]{1,0:T(8,128)(2,1)S(1)} %shard_map.68.refs_2_), channel_id=1, source_target_pairs={{0,2},{1,3},{2,4},{3,5},{4,6},{5,7},{6,0},{7,1},{8,10},{9,11},{10,... | collective-permute-start | bytes 835592 | tf_op jit(solution)/shard_map/ppermute | solution.py:307
  14.7 3.3 %collective-permute-start.5 = (bf16[256,512]{1,0:T(8,128)(2,1)S(1)}, bf16[256,512]{1,0:T(8,128)(2,1)S(1)}, u32[]{:S(2)}, u32[]{:S(2)}) collective-permute-start(bf16[256,512]{1,0:T(8,128)(2,1)S(1)} %get-tuple-element.27.refs_3_), channel_id=1, source_target_pairs={{0,16},{8,24},{16,0},{24,8},{1,17},{9,25},{17,1},{25,9},{2,18},{10... | collective-permute-start | bytes 786440 | tf_op jit(solution)/shard_map/ppermute | solution.py:298
  18.7 1.6 %collective-permute-start.3 = (s16[272,512]{1,0:T(8,128)(2,1)S(1)}, s16[272,512]{1,0:T(8,128)(2,1)S(1)}, u32[]{:S(2)}, u32[]{:S(2)}) collective-permute-start(s16[272,512]{1,0:T(8,128)(2,1)S(1)} %shard_map.70.refs_2_), channel_id=1, source_target_pairs={{0,2},{1,3},{2,4},{3,5},{4,6},{5,7},{6,0},{7,1},{8,10},{9,11},{10,... | collective-permute-start | bytes 835592 | tf_op jit(solution)/shard_map/ppermute | solution.py:307
  20.4 3.6 %collective-permute-start.2 = (bf16[256,512]{1,0:T(8,128)(2,1)S(1)}, bf16[256,512]{1,0:T(8,128)(2,1)S(1)}, u32[]{:S(2)}, u32[]{:S(2)}) collective-permute-start(bf16[256,512]{1,0:T(8,128)(2,1)S(1)} %get-tuple-element.29.refs_3_), channel_id=1, source_target_pairs={{0,16},{8,24},{16,0},{24,8},{1,17},{9,25},{17,1},{25,9},{2,18},{10... | collective-permute-start | bytes 786440 | tf_op jit(solution)/shard_map/ppermute | solution.py:298
  24.5 1.6 %collective-permute-start.7 = (s16[272,512]{1,0:T(8,128)(2,1)S(1)}, s16[272,512]{1,0:T(8,128)(2,1)S(1)}, u32[]{:S(2)}, u32[]{:S(2)}) collective-permute-start(s16[272,512]{1,0:T(8,128)(2,1)S(1)} %shard_map.72.refs_4_), channel_id=1, source_target_pairs={{0,2},{1,3},{2,4},{3,5},{4,6},{5,7},{6,0},{7,1},{8,10},{9,11},{10,... | collective-permute-start | bytes 835592 | tf_op jit(solution)/shard_map/ppermute | solution.py:307
  26.6 1.6 %collective-permute-start.8 = (s16[272,512]{1,0:T(8,128)(2,1)S(1)}, s16[272,512]{1,0:T(8,128)(2,1)S(1)}, u32[]{:S(2)}, u32[]{:S(2)}) collective-permute-start(s16[272,512]{1,0:T(8,128)(2,1)S(1)} %shard_map.73.refs_4_), channel_id=1, source_target_pairs={{0,1},{1,0},{2,3},{3,2},{4,5},{5,4},{6,7},{7,6},{8,9},{9,8},{10,11... | collective-permute-start | bytes 835592 | tf_op jit(solution)/shard_map/ppermute | solution.py:302
  29.1 1.5 %collective-permute-start.13 = (s16[272,512]{1,0:T(8,128)(2,1)S(1)}, s16[272,512]{1,0:T(8,128)(2,1)S(1)}, u32[]{:S(2)}, u32[]{:S(2)}) collective-permute-start(s16[272,512]{1,0:T(8,128)(2,1)S(1)} %shard_map.74.refs_3_), channel_id=1, source_target_pairs={{0,1},{1,0},{2,3},{3,2},{4,5},{5,4},{6,7},{7,6},{8,9},{9,8},{10,11... | collective-permute-start | bytes 835592 | tf_op jit(solution)/shard_map/ppermute | solution.py:302
  31.1 0.6 collective-permute-start.6
  31.8 4.0 %collective-permute-done.8.refs_3_ = s16[272,512]{1,0:T(8,128)(2,1)S(1)} collective-permute-done((s16[272,512]{1,0:T(8,128)(2,1)S(1)}, s16[272,512]{1,0:T(8,128)(2,1)S(1)}, u32[]{:S(2)}, u32[]{:S(2)}) %collective-permute-start.8) | collective-permute-done | bytes 278560 | tf_op jit(solution)/shard_map/ppermute | solution.py:302
  36.2 1.4 %collective-permute-start.10 = (s16[272,512]{1,0:T(8,128)(2,1)S(1)}, s16[272,512]{1,0:T(8,128)(2,1)S(1)}, u32[]{:S(2)}, u32[]{:S(2)}) collective-permute-start(s16[272,512]{1,0:T(8,128)(2,1)S(1)} %shard_map.76.refs_4_), channel_id=1, source_target_pairs={{0,2},{1,3},{2,4},{3,5},{4,6},{5,7},{6,0},{7,1},{8,10},{9,11},{10,... | collective-permute-start | bytes 835592 | tf_op jit(solution)/shard_map/ppermute | solution.py:307
  38.1 1.6 %collective-permute-start.12 = (s16[272,512]{1,0:T(8,128)(2,1)S(1)}, s16[272,512]{1,0:T(8,128)(2,1)S(1)}, u32[]{:S(2)}, u32[]{:S(2)}) collective-permute-start(s16[272,512]{1,0:T(8,128)(2,1)S(1)} %shard_map.77.refs_4_), channel_id=1, source_target_pairs={{0,1},{1,0},{2,3},{3,2},{4,5},{5,4},{6,7},{7,6},{8,9},{9,8},{10,11... | collective-permute-start | bytes 835592 | tf_op jit(solution)/shard_map/ppermute | solution.py:302
  39.7 2.8 %collective-permute-done.6.refs_3_ = s16[272,512]{1,0:T(8,128)(2,1)S(1)} collective-permute-done((s16[272,512]{1,0:T(8,128)(2,1)S(1)}, s16[272,512]{1,0:T(8,128)(2,1)S(1)}, u32[]{:S(2)}, u32[]{:S(2)}) %collective-permute-start.6) | collective-permute-done | bytes 278560 | tf_op jit(solution)/shard_map/ppermute | solution.py:307
  44.4 3.1 %collective-permute-done.12.refs_3_ = s16[272,512]{1,0:T(8,128)(2,1)S(1)} collective-permute-done((s16[272,512]{1,0:T(8,128)(2,1)S(1)}, s16[272,512]{1,0:T(8,128)(2,1)S(1)}, u32[]{:S(2)}, u32[]{:S(2)}) %collective-permute-start.12) | collective-permute-done | bytes 278560 | tf_op jit(solution)/shard_map/ppermute | solution.py:302
  47.9 1.8 %collective-permute-start.15 = (s16[272,512]{1,0:T(8,128)(2,1)S(1)}, s16[272,512]{1,0:T(8,128)(2,1)S(1)}, u32[]{:S(2)}, u32[]{:S(2)}) collective-permute-start(s16[272,512]{1,0:T(8,128)(2,1)S(1)} %shard_map.80.refs_8_), channel_id=1, source_target_pairs={{0,2},{1,3},{2,4},{3,5},{4,6},{5,7},{6,0},{7,1},{8,10},{9,11},{10,... | collective-permute-start | bytes 835592 | tf_op jit(solution)/shard_map/ppermute | solution.py:307
  50.3 0.9 %collective-permute-start.19 = (bf16[256,512]{1,0:T(8,128)(2,1)S(1)}, bf16[256,512]{1,0:T(8,128)(2,1)S(1)}, u32[]{:S(2)}, u32[]{:S(2)}) collective-permute-start(bf16[256,512]{1,0:T(8,128)(2,1)S(1)} %shard_map.81.refs_4_.refs_1_), channel_id=1, source_target_pairs={{0,16},{8,24},{16,0},{24,8},{1,17},{9,25},{17,1},{25,9},{2,18},{10... | collective-permute-start | bytes 786440 | tf_op jit(solution)/shard_map/ppermute | solution.py:298
  51.7 3.0 %collective-permute-start.14 = (s16[272,512]{1,0:T(8,128)(2,1)S(1)}, s16[272,512]{1,0:T(8,128)(2,1)S(1)}, u32[]{:S(2)}, u32[]{:S(2)}) collective-permute-start(s16[272,512]{1,0:T(8,128)(2,1)S(1)} %shard_map.82.refs_8_), channel_id=1, source_target_pairs={{0,2},{1,3},{2,4},{3,5},{4,6},{5,7},{6,0},{7,1},{8,10},{9,11},{10,... | collective-permute-start | bytes 835592 | tf_op jit(solution)/shard_map/ppermute | solution.py:307
  54.8 0.9 %collective-permute-done.16.refs_4_ = s16[272,512]{1,0:T(8,128)(2,1)S(1)} collective-permute-done((s16[272,512]{1,0:T(8,128)(2,1)S(1)}, s16[272,512]{1,0:T(8,128)(2,1)S(1)}, u32[]{:S(2)}, u32[]{:S(2)}) %collective-permute-start.16) | collective-permute-done | bytes 278560 | tf_op jit(solution)/shard_map/ppermute | solution.py:307
  56.2 1.7 %collective-permute-start.18 = (bf16[256,512]{1,0:T(8,128)(2,1)S(1)}, bf16[256,512]{1,0:T(8,128)(2,1)S(1)}, u32[]{:S(2)}, u32[]{:S(2)}) collective-permute-start(bf16[256,512]{1,0:T(8,128)(2,1)S(1)} %shard_map.83.refs_8_.refs_1_), channel_id=1, source_target_pairs={{0,16},{8,24},{16,0},{24,8},{1,17},{9,25},{17,1},{25,9},{2,18},{10... | collective-permute-start | bytes 786440 | tf_op jit(solution)/shard_map/ppermute | solution.py:298
  57.9 2.9 %collective-permute-done.15.refs_4_ = s16[272,512]{1,0:T(8,128)(2,1)S(1)} collective-permute-done((s16[272,512]{1,0:T(8,128)(2,1)S(1)}, s16[272,512]{1,0:T(8,128)(2,1)S(1)}, u32[]{:S(2)}, u32[]{:S(2)}) %collective-permute-start.15) | collective-permute-done | bytes 278560 | tf_op jit(solution)/shard_map/ppermute | solution.py:307
  61.3 1.6 %collective-permute-start.17 = (bf16[256,512]{1,0:T(8,128)(2,1)S(1)}, bf16[256,512]{1,0:T(8,128)(2,1)S(1)}, u32[]{:S(2)}, u32[]{:S(2)}) collective-permute-start(bf16[256,512]{1,0:T(8,128)(2,1)S(1)} %shard_map.84.refs_8_.refs_1_), channel_id=1, source_target_pairs={{0,16},{8,24},{16,0},{24,8},{1,17},{9,25},{17,1},{25,9},{2,18},{10... | collective-permute-start | bytes 786440 | tf_op jit(solution)/shard_map/ppermute | solution.py:298
  62.9 0.8 %collective-permute-done.14.refs_4_ = s16[272,512]{1,0:T(8,128)(2,1)S(1)} collective-permute-done((s16[272,512]{1,0:T(8,128)(2,1)S(1)}, s16[272,512]{1,0:T(8,128)(2,1)S(1)}, u32[]{:S(2)}, u32[]{:S(2)}) %collective-permute-start.14) | collective-permute-done | bytes 278560 | tf_op jit(solution)/shard_map/ppermute | solution.py:307
  64.3 1.6 %collective-permute-start.20 = (bf16[256,512]{1,0:T(8,128)(2,1)S(1)}, bf16[256,512]{1,0:T(8,128)(2,1)S(1)}, u32[]{:S(2)}, u32[]{:S(2)}) collective-permute-start(bf16[256,512]{1,0:T(8,128)(2,1)S(1)} %shard_map.85.refs_3_.refs_1_), channel_id=1, source_target_pairs={{0,16},{8,24},{16,0},{24,8},{1,17},{9,25},{17,1},{25,9},{2,18},{10... | collective-permute-start | bytes 786440 | tf_op jit(solution)/shard_map/ppermute | solution.py:298
  66.5 2.3 %collective-permute-done.17.refs_2_ = bf16[256,512]{1,0:T(8,128)(2,1)S(1)} collective-permute-done((bf16[256,512]{1,0:T(8,128)(2,1)S(1)}, bf16[256,512]{1,0:T(8,128)(2,1)S(1)}, u32[]{:S(2)}, u32[]{:S(2)}) %collective-permute-start.17) | collective-permute-done | bytes 262176 | tf_op jit(solution)/shard_map/ppermute | solution.py:298
  69.3 2.3 %collective-permute-done.20.refs_2_ = bf16[256,512]{1,0:T(8,128)(2,1)S(1)} collective-permute-done((bf16[256,512]{1,0:T(8,128)(2,1)S(1)}, bf16[256,512]{1,0:T(8,128)(2,1)S(1)}, u32[]{:S(2)}, u32[]{:S(2)}) %collective-permute-start.20) | collective-permute-done | bytes 262176 | tf_op jit(solution)/shard_map/ppermute | solution.py:298
  71.6 1.6 %shard_map.90 = bf16[2048,512]{1,0:T(8,128)(2,1)} custom-call(bf16[2048,512]{1,0:T(8,128)(2,1)S(1)} %get-tuple-element.35.refs_0_, bf16[2048,256]{1,0:T(8,128)(2,1)S(1)} %get-tuple-element.36.refs_1_, bf16[256,512]{1,0:T(8,128)(2,1)S(1)} %collective-permute-done.20.refs_2_), custom_call_target="tpu_custom_call" | custom-call | flops 4000000000 | bytes 1 | tf_op jit(solution)/shard_map/pallas_call | solution.py:45
  (49 shorter events, 10.8 us)
Async XLA Ops:
  0.0 5.4 %copy-start.1 = (bf16[2048,512]{1,0:T(8,128)(2,1)S(1)}, bf16[2048,512]{1,0:T(8,128)(2,1)}, u32[]{:S(2)}) copy-start(bf16[2048,512]{1,0:T(8,128)(2,1)} %refs_1_.7) | copy-start | bytes 6291460
  0.0 5.4 %copy-start.4 = (s32[2048]{0:T(1024)S(1)}, s32[2048]{0:T(1024)}, u32[]{:S(2)}) copy-start(s32[2048]{0:T(1024)} %param.9) | copy-start | bytes 24580
  1.2 5.6 %copy-start = (bf16[512,2048]{1,0:T(8,128)(2,1)S(1)}, bf16[512,2048]{1,0:T(8,128)(2,1)}, u32[]{:S(2)}) copy-start(bf16[512,2048]{1,0:T(8,128)(2,1)} %refs_0_.1) | copy-start | bytes 6291460
  1.2 11.3 %collective-permute-start = (bf16[256,512]{1,0:T(8,128)(2,1)S(1)}, bf16[256,512]{1,0:T(8,128)(2,1)S(1)}, u32[]{:S(2)}, u32[]{:S(2)}) collective-permute-start(bf16[256,512]{1,0:T(8,128)(2,1)S(1)} %shard_map.64.refs_2_), channel_id=1, source_target_pairs={{0,16},{8,24},{16,0},{24,8},{1,17},{9,25},{17,1},{25,9},{2,18},{10... | collective-permute-start | bytes 786440 | tf_op jit(solution)/shard_map/ppermute | solution.py:298
  5.4 2.8 %copy-start.2 = (s32[2048]{0:T(1024)S(1)}, s32[2048]{0:T(1024)}, u32[]{:S(2)}) copy-start(s32[2048]{0:T(1024)} %param.8) | copy-start | bytes 24580
  5.4 2.8 %copy-start.3 = (f32[2000]{0:T(1024)S(1)}, f32[2000]{0:T(1024)}, u32[]{:S(2)}) copy-start(f32[2000]{0:T(1024)} %param.11) | copy-start | bytes 24004
  5.5 2.8 %copy-start.5 = (f32[200]{0:T(256)S(1)}, f32[200]{0:T(256)}, u32[]{:S(2)}) copy-start(f32[200]{0:T(256)} %param.10) | copy-start | bytes 2404
  5.5 12.7 %collective-permute-start.1 = (bf16[256,512]{1,0:T(8,128)(2,1)S(1)}, bf16[256,512]{1,0:T(8,128)(2,1)S(1)}, u32[]{:S(2)}, u32[]{:S(2)}) collective-permute-start(bf16[256,512]{1,0:T(8,128)(2,1)S(1)} %get-tuple-element.22.refs_1_), channel_id=1, source_target_pairs={{0,16},{8,24},{16,0},{24,8},{1,17},{9,25},{17,1},{25,9},{2,18},{10... | collective-permute-start | bytes 786440 | tf_op jit(solution)/shard_map/ppermute | solution.py:298
  9.9 39.8 %collective-permute-start.11 = (f32[1,1024]{1,0:T(1,128)S(1)}, f32[1,1024]{1,0:T(1,128)S(1)}, u32[]{:S(2)}, u32[]{:S(2)}) collective-permute-start(f32[1,1024]{1,0:T(1,128)S(1)} %get-tuple-element.34), channel_id=1, source_target_pairs={{0,16},{8,24},{16,0},{24,8},{1,17},{9,25},{17,1},{25,9},{2,18},{10... | collective-permute-start | bytes 12296 | tf_op jit(solution)/shard_map/ppermute | solution.py:298
  13.0 13.1 %collective-permute-start.4 = (s16[272,512]{1,0:T(8,128)(2,1)S(1)}, s16[272,512]{1,0:T(8,128)(2,1)S(1)}, u32[]{:S(2)}, u32[]{:S(2)}) collective-permute-start(s16[272,512]{1,0:T(8,128)(2,1)S(1)} %shard_map.68.refs_2_), channel_id=1, source_target_pairs={{0,2},{1,3},{2,4},{3,5},{4,6},{5,7},{6,0},{7,1},{8,10},{9,11},{10,... | collective-permute-start | bytes 835592 | tf_op jit(solution)/shard_map/ppermute | solution.py:307
  14.7 9.2 %collective-permute-start.5 = (bf16[256,512]{1,0:T(8,128)(2,1)S(1)}, bf16[256,512]{1,0:T(8,128)(2,1)S(1)}, u32[]{:S(2)}, u32[]{:S(2)}) collective-permute-start(bf16[256,512]{1,0:T(8,128)(2,1)S(1)} %get-tuple-element.27.refs_3_), channel_id=1, source_target_pairs={{0,16},{8,24},{16,0},{24,8},{1,17},{9,25},{17,1},{25,9},{2,18},{10... | collective-permute-start | bytes 786440 | tf_op jit(solution)/shard_map/ppermute | solution.py:298
  18.7 9.9 %collective-permute-start.3 = (s16[272,512]{1,0:T(8,128)(2,1)S(1)}, s16[272,512]{1,0:T(8,128)(2,1)S(1)}, u32[]{:S(2)}, u32[]{:S(2)}) collective-permute-start(s16[272,512]{1,0:T(8,128)(2,1)S(1)} %shard_map.70.refs_2_), channel_id=1, source_target_pairs={{0,2},{1,3},{2,4},{3,5},{4,6},{5,7},{6,0},{7,1},{8,10},{9,11},{10,... | collective-permute-start | bytes 835592 | tf_op jit(solution)/shard_map/ppermute | solution.py:307
  20.4 10.2 %collective-permute-start.2 = (bf16[256,512]{1,0:T(8,128)(2,1)S(1)}, bf16[256,512]{1,0:T(8,128)(2,1)S(1)}, u32[]{:S(2)}, u32[]{:S(2)}) collective-permute-start(bf16[256,512]{1,0:T(8,128)(2,1)S(1)} %get-tuple-element.29.refs_3_), channel_id=1, source_target_pairs={{0,16},{8,24},{16,0},{24,8},{1,17},{9,25},{17,1},{25,9},{2,18},{10... | collective-permute-start | bytes 786440 | tf_op jit(solution)/shard_map/ppermute | solution.py:298
  24.5 13.1 %collective-permute-start.7 = (s16[272,512]{1,0:T(8,128)(2,1)S(1)}, s16[272,512]{1,0:T(8,128)(2,1)S(1)}, u32[]{:S(2)}, u32[]{:S(2)}) collective-permute-start(s16[272,512]{1,0:T(8,128)(2,1)S(1)} %shard_map.72.refs_4_), channel_id=1, source_target_pairs={{0,2},{1,3},{2,4},{3,5},{4,6},{5,7},{6,0},{7,1},{8,10},{9,11},{10,... | collective-permute-start | bytes 835592 | tf_op jit(solution)/shard_map/ppermute | solution.py:307
  26.6 9.1 %collective-permute-start.8 = (s16[272,512]{1,0:T(8,128)(2,1)S(1)}, s16[272,512]{1,0:T(8,128)(2,1)S(1)}, u32[]{:S(2)}, u32[]{:S(2)}) collective-permute-start(s16[272,512]{1,0:T(8,128)(2,1)S(1)} %shard_map.73.refs_4_), channel_id=1, source_target_pairs={{0,1},{1,0},{2,3},{3,2},{4,5},{5,4},{6,7},{7,6},{8,9},{9,8},{10,11... | collective-permute-start | bytes 835592 | tf_op jit(solution)/shard_map/ppermute | solution.py:302
  29.1 14.6 %collective-permute-start.13 = (s16[272,512]{1,0:T(8,128)(2,1)S(1)}, s16[272,512]{1,0:T(8,128)(2,1)S(1)}, u32[]{:S(2)}, u32[]{:S(2)}) collective-permute-start(s16[272,512]{1,0:T(8,128)(2,1)S(1)} %shard_map.74.refs_3_), channel_id=1, source_target_pairs={{0,1},{1,0},{2,3},{3,2},{4,5},{5,4},{6,7},{7,6},{8,9},{9,8},{10,11... | collective-permute-start | bytes 835592 | tf_op jit(solution)/shard_map/ppermute | solution.py:302
  31.1 11.4 %collective-permute-start.6 = (s16[272,512]{1,0:T(8,128)(2,1)S(1)}, s16[272,512]{1,0:T(8,128)(2,1)S(1)}, u32[]{:S(2)}, u32[]{:S(2)}) collective-permute-start(s16[272,512]{1,0:T(8,128)(2,1)S(1)} %shard_map.75.refs_4_), channel_id=1, source_target_pairs={{0,2},{1,3},{2,4},{3,5},{4,6},{5,7},{6,0},{7,1},{8,10},{9,11},{10,... | collective-permute-start | bytes 835592 | tf_op jit(solution)/shard_map/ppermute | solution.py:307
  36.2 13.5 %collective-permute-start.10 = (s16[272,512]{1,0:T(8,128)(2,1)S(1)}, s16[272,512]{1,0:T(8,128)(2,1)S(1)}, u32[]{:S(2)}, u32[]{:S(2)}) collective-permute-start(s16[272,512]{1,0:T(8,128)(2,1)S(1)} %shard_map.76.refs_4_), channel_id=1, source_target_pairs={{0,2},{1,3},{2,4},{3,5},{4,6},{5,7},{6,0},{7,1},{8,10},{9,11},{10,... | collective-permute-start | bytes 835592 | tf_op jit(solution)/shard_map/ppermute | solution.py:307
  38.1 9.3 %collective-permute-start.12 = (s16[272,512]{1,0:T(8,128)(2,1)S(1)}, s16[272,512]{1,0:T(8,128)(2,1)S(1)}, u32[]{:S(2)}, u32[]{:S(2)}) collective-permute-start(s16[272,512]{1,0:T(8,128)(2,1)S(1)} %shard_map.77.refs_4_), channel_id=1, source_target_pairs={{0,1},{1,0},{2,3},{3,2},{4,5},{5,4},{6,7},{7,6},{8,9},{9,8},{10,11... | collective-permute-start | bytes 835592 | tf_op jit(solution)/shard_map/ppermute | solution.py:302
  43.1 8.1 %collective-permute-start.9 = (s16[272,512]{1,0:T(8,128)(2,1)S(1)}, s16[272,512]{1,0:T(8,128)(2,1)S(1)}, u32[]{:S(2)}, u32[]{:S(2)}) collective-permute-start(s16[272,512]{1,0:T(8,128)(2,1)S(1)} %shard_map.78.refs_4_), channel_id=1, source_target_pairs={{0,1},{1,0},{2,3},{3,2},{4,5},{5,4},{6,7},{7,6},{8,9},{9,8},{10,11... | collective-permute-start | bytes 835592 | tf_op jit(solution)/shard_map/ppermute | solution.py:302
  44.2 11.4 %collective-permute-start.16 = (s16[272,512]{1,0:T(8,128)(2,1)S(1)}, s16[272,512]{1,0:T(8,128)(2,1)S(1)}, u32[]{:S(2)}, u32[]{:S(2)}) collective-permute-start(s16[272,512]{1,0:T(8,128)(2,1)S(1)} %shard_map.79.refs_4_), channel_id=1, source_target_pairs={{0,2},{1,3},{2,4},{3,5},{4,6},{5,7},{6,0},{7,1},{8,10},{9,11},{10,... | collective-permute-start | bytes 835592 | tf_op jit(solution)/shard_map/ppermute | solution.py:307
  47.9 12.8 %collective-permute-start.15 = (s16[272,512]{1,0:T(8,128)(2,1)S(1)}, s16[272,512]{1,0:T(8,128)(2,1)S(1)}, u32[]{:S(2)}, u32[]{:S(2)}) collective-permute-start(s16[272,512]{1,0:T(8,128)(2,1)S(1)} %shard_map.80.refs_8_), channel_id=1, source_target_pairs={{0,2},{1,3},{2,4},{3,5},{4,6},{5,7},{6,0},{7,1},{8,10},{9,11},{10,... | collective-permute-start | bytes 835592 | tf_op jit(solution)/shard_map/ppermute | solution.py:307
  50.3 15.6 %collective-permute-start.19 = (bf16[256,512]{1,0:T(8,128)(2,1)S(1)}, bf16[256,512]{1,0:T(8,128)(2,1)S(1)}, u32[]{:S(2)}, u32[]{:S(2)}) collective-permute-start(bf16[256,512]{1,0:T(8,128)(2,1)S(1)} %shard_map.81.refs_4_.refs_1_), channel_id=1, source_target_pairs={{0,16},{8,24},{16,0},{24,8},{1,17},{9,25},{17,1},{25,9},{2,18},{10... | collective-permute-start | bytes 786440 | tf_op jit(solution)/shard_map/ppermute | solution.py:298
  51.7 12.0 %collective-permute-start.14 = (s16[272,512]{1,0:T(8,128)(2,1)S(1)}, s16[272,512]{1,0:T(8,128)(2,1)S(1)}, u32[]{:S(2)}, u32[]{:S(2)}) collective-permute-start(s16[272,512]{1,0:T(8,128)(2,1)S(1)} %shard_map.82.refs_8_), channel_id=1, source_target_pairs={{0,2},{1,3},{2,4},{3,5},{4,6},{5,7},{6,0},{7,1},{8,10},{9,11},{10,... | collective-permute-start | bytes 835592 | tf_op jit(solution)/shard_map/ppermute | solution.py:307
  56.2 9.9 %collective-permute-start.18 = (bf16[256,512]{1,0:T(8,128)(2,1)S(1)}, bf16[256,512]{1,0:T(8,128)(2,1)S(1)}, u32[]{:S(2)}, u32[]{:S(2)}) collective-permute-start(bf16[256,512]{1,0:T(8,128)(2,1)S(1)} %shard_map.83.refs_8_.refs_1_), channel_id=1, source_target_pairs={{0,16},{8,24},{16,0},{24,8},{1,17},{9,25},{17,1},{25,9},{2,18},{10... | collective-permute-start | bytes 786440 | tf_op jit(solution)/shard_map/ppermute | solution.py:298
  61.3 7.5 %collective-permute-start.17 = (bf16[256,512]{1,0:T(8,128)(2,1)S(1)}, bf16[256,512]{1,0:T(8,128)(2,1)S(1)}, u32[]{:S(2)}, u32[]{:S(2)}) collective-permute-start(bf16[256,512]{1,0:T(8,128)(2,1)S(1)} %shard_map.84.refs_8_.refs_1_), channel_id=1, source_target_pairs={{0,16},{8,24},{16,0},{24,8},{1,17},{9,25},{17,1},{25,9},{2,18},{10... | collective-permute-start | bytes 786440 | tf_op jit(solution)/shard_map/ppermute | solution.py:298
  64.3 7.3 %collective-permute-start.20 = (bf16[256,512]{1,0:T(8,128)(2,1)S(1)}, bf16[256,512]{1,0:T(8,128)(2,1)S(1)}, u32[]{:S(2)}, u32[]{:S(2)}) collective-permute-start(bf16[256,512]{1,0:T(8,128)(2,1)S(1)} %shard_map.85.refs_3_.refs_1_), channel_id=1, source_target_pairs={{0,16},{8,24},{16,0},{24,8},{1,17},{9,25},{17,1},{25,9},{2,18},{10... | collective-permute-start | bytes 786440 | tf_op jit(solution)/shard_map/ppermute | solution.py:298

commit v8 on v7

--- a/solution.py
+++ b/solution.py
@@ -139,19 +139,29 @@
 
 
 def code(values, out):
-    rows = values.shape[0]
+    rows, width = values.shape
     top = jnp.max(jnp.abs(values), axis=0, keepdims=True)
     level = jnp.ceil(STEPS * jnp.log2(jnp.maximum(top, TINY) * (1.0001 / TOP)))
-    coded = jnp.round(values * jnp.exp2(level * (-1.0 / STEPS)))
-    out[pl.ds(0, rows), :] = coded.astype(jnp.int32).astype(jnp.int16)
-    spread = jnp.broadcast_to(level.astype(jnp.int32), (SCALE_ROWS, values.shape[1]))
-    out[pl.ds(rows, SCALE_ROWS), :] = spread.astype(jnp.int16)
-
-
-def decode(coded):
-    rows = coded.shape[0] - SCALE_ROWS
-    level = coded[pl.ds(rows, SCALE_ROWS), :].astype(jnp.int32).astype(jnp.float32)[0:1, :]
-    return coded[pl.ds(0, rows), :].astype(jnp.int32).astype(jnp.float32) * jnp.exp2(level * (1.0 / STEPS))
+    coded = jnp.round(values * jnp.exp2(level * (-1.0 / STEPS))).astype(jnp.int32).astype(jnp.int16)
+    level = level.astype(jnp.int32)
+    down = lax.broadcasted_iota(jnp.int32, (SCALE_ROWS, LANES), 0)
+    levels = jnp.zeros((SCALE_ROWS, LANES), jnp.int32)
+    for tile in range(width // LANES):
+        cols = slice(tile * LANES, (tile + 1) * LANES)
+        out[pl.ds(tile * rows, rows), :] = coded[:, cols]
+        levels = jnp.where(down == tile, level[:, cols], levels)
+    out[pl.ds(rows * width // LANES, SCALE_ROWS), :] = levels.astype(jnp.int16)
+
+
+def decode(coded, rows):
+    tiles = (coded.shape[0] - SCALE_ROWS) // rows
+    level = coded[pl.ds(tiles * rows, SCALE_ROWS), :].astype(jnp.int32).astype(jnp.float32)
+    scale = jnp.exp2(level * (1.0 / STEPS))
+    parts = []
+    for tile in range(tiles):
+        part = coded[pl.ds(tile * rows, rows), :].astype(jnp.int32).astype(jnp.float32)
+        parts.append(part * scale[tile : tile + 1, :])
+    return jnp.concatenate(parts, axis=1)
 
 
 def first_kernel(own, other, factor, out):
@@ -159,18 +169,18 @@
 
 
 def second_kernel(own, other, factor, arrived, out):
-    code(product(own, other, factor) + decode(arrived), out)
+    code(product(own, other, factor) + decode(arrived, own.shape[0]), out)
 
 
 def third_kernel(own, other, factor, crossed, out):
     here = jnp.where(lax.axis_index("col") % 2 == 0, 1.0, 0.0)
-    code(product(own, other, factor) + decode(crossed) * here, out)
+    code(product(own, other, factor) + decode(crossed, own.shape[0]) * here, out)
 
 
 def last_kernel(begin, own, other, factor, crossed, arrived, occ_here, occ_there, vir_sum, out):
     chunk, width = out.shape
     here = jnp.where(lax.axis_index("col") % 2 == 1, 1.0, 0.0)
-    total = product(own, other, factor) + decode(arrived) + decode(crossed) * here
+    total = product(own, other, factor) + decode(arrived, own.shape[0]) + decode(crossed, own.shape[0]) * here
     part = pl.ds(begin, chunk)
     occ_rows = jnp.where(upper_side() == 0, occ_here[:, part], occ_there[:, part])
     occ_down = jnp.broadcast_to(occ_rows, (LANES, chunk)).T
@@ -318,7 +328,7 @@
         return jax.ShapeDtypeStruct((chunks[index], width), jnp.bfloat16)
 
     def coded_shape(index):
-        return jax.ShapeDtypeStruct((chunks[index] + SCALE_ROWS, width), jnp.int16)
+        return jax.ShapeDtypeStruct((chunks[index] * (width // LANES) + SCALE_ROWS, LANES), jnp.int16)
 
     half_shape = jax.ShapeDtypeStruct((1, half), jnp.float32)
     energy_shapes = [half_shape, half_shape, jax.ShapeDtypeStruct((1, width), jnp.float32)]

time: 73.7 us -> 72.4 us (0.982)
  waiting for transfers between devices: 21.2 us -> 19.3 us
    ppermute x8, waiting for transfers between devices: 7.8 us -> 5.72 us  [two_along(): lax.ppermute(value, 'col', [(i, (i + 2) % count) for i in range(count)])]
  transfers between devices with their start and end apart: 21 -> 21, of which waited for: 11 -> 10; matrix products, arithmetic and copies ran while one was open for 0% -> 0% of each run, Pallas kernels for 17% -> 18%
where the time goes in v8:
time: 72.4 us; the launch traced here: 72 us
  starting transfers between devices  36.8 us (51%)
  waiting for transfers between devices  19.3 us (27%)
  Pallas kernels  15.5 us (21%)
    ppermute x9, starting transfers between devices, across_rows(): lax.ppermute(value, 'row', [(i, i ^ count // 2) for i in range(count)])  18.9 us
    pallas_call x27, Pallas kernels, call(): pl.pallas_call(kernel, out_shape=out_shape, in_specs=[in_spec or VMEM] *...  15.5 us
    ppermute x8, starting transfers between devices, two_along(): lax.ppermute(value, 'col', [(i, (i + 2) % count) for i in range(count)])  12.6 us
    ppermute x9, waiting for transfers between devices, across_rows(): lax.ppermute(value, 'row', [(i, i ^ count // 2) for i in range(count)])  7.02 us
    ppermute x4, waiting for transfers between devices, across_pair(): lax.ppermute(value, 'col', [(i, i ^ 1) for i in range(lax.axis_size('col'...  6.55 us
    ppermute x8, waiting for transfers between devices, two_along(): lax.ppermute(value, 'col', [(i, (i + 2) % count) for i in range(count)])  5.72 us
    ppermute x4, starting transfers between devices, across_pair(): lax.ppermute(value, 'col', [(i, i ^ 1) for i in range(lax.axis_size('col'...  5.32 us
  transfers between devices with their start and end apart: 21, of which 10 were waited for; matrix products, arithmetic and copies ran while one was open for 0% of the time, Pallas kernels for 18%

profile of v8, /device:TPU:0, one launch (start us, length us, event | category | flops | bytes accessed | tf_op | source)
XLA Modules:
  0.0 72.0 jit_solution(8444965871785161154)
XLA Ops:
  0.0 1.2 %shard_map.64.refs_2_ = bf16[256,512]{1,0:T(8,128)(2,1)S(1)} custom-call(s32[1,2048]{1,0:T(1,128)} %bitcast.6, bf16[2048,512]{1,0:T(8,128)(2,1)} %refs_1_.7), custom_call_target="tpu_custom_call" | custom-call | flops 4000000000 | bytes 1 | tf_op jit(solution)/shard_map/pallas_call | solution.py:45
  1.2 4.2 %collective-permute-start = (bf16[256,512]{1,0:T(8,128)(2,1)S(1)}, bf16[256,512]{1,0:T(8,128)(2,1)S(1)}, u32[]{:S(2)}, u32[]{:S(2)}) collective-permute-start(bf16[256,512]{1,0:T(8,128)(2,1)S(1)} %shard_map.64.refs_2_), channel_id=1, source_target_pairs={{0,16},{8,24},{16,0},{24,8},{1,17},{9,25},{17,1},{25,9},{2,18},{10... | collective-permute-start | bytes 786440 | tf_op jit(solution)/shard_map/ppermute | solution.py:308
  5.5 1.3 %collective-permute-start.1 = (bf16[256,512]{1,0:T(8,128)(2,1)S(1)}, bf16[256,512]{1,0:T(8,128)(2,1)S(1)}, u32[]{:S(2)}, u32[]{:S(2)}) collective-permute-start(bf16[256,512]{1,0:T(8,128)(2,1)S(1)} %get-tuple-element.22.refs_1_), channel_id=1, source_target_pairs={{0,16},{8,24},{16,0},{24,8},{1,17},{9,25},{17,1},{25,9},{2,18},{10... | collective-permute-start | bytes 786440 | tf_op jit(solution)/shard_map/ppermute | solution.py:308
  6.8 1.4 %shard_map.66 = (bf16[1024,512]{1,0:T(8,128)(2,1)S(1)}, bf16[1024,512]{1,0:T(8,128)(2,1)S(1)}, bf16[1024,512]{1,0:T(8,128)(2,1)S(1)}, bf16[1024,512]{1,0:T(8,128)(2,1)S(1)}) custom-call(bf16[512,2048]{1,0:T(8,128)(2,1)S(1)} %copy-done, bf16[256,512]{1,0:T(8,128)(2,1)S(1)} %get-tuple-element.22.refs_1_), custom_call_target="tpu_custom_call" | custom-call | flops 4000000000 | bytes 1 | tf_op jit(solution)/shard_map/pallas_call | solution.py:45
  8.3 1.6 %shard_map.67 = (f32[1,1024]{1,0:T(1,128)S(1)}, f32[1,1024]{1,0:T(1,128)S(1)}, f32[1,512]{1,0:T(1,128)S(1)}) custom-call(s32[1,2048]{1,0:T(1,128)S(1)} %bitcast.4, f32[1,200]{1,0:T(1,128)S(1)} %bitcast.14, f32[1,2000]{1,0:T(1,128)S(1)} %bitcast.5, bf16[1024,512]{1,0:T(8,128)(2,1)S(1)} %get-tuple-element.24.refs_3_.refs_2_), custom_call_target="tpu_custom_call" | custom-call | flops 4000000000 | bytes 1 | tf_op jit(solution)/shard_map/pallas_call | solution.py:45
  9.9 0.8 %collective-permute-start.11 = (f32[1,1024]{1,0:T(1,128)S(1)}, f32[1,1024]{1,0:T(1,128)S(1)}, u32[]{:S(2)}, u32[]{:S(2)}) collective-permute-start(f32[1,1024]{1,0:T(1,128)S(1)} %get-tuple-element.34), channel_id=1, source_target_pairs={{0,16},{8,24},{16,0},{24,8},{1,17},{9,25},{17,1},{25,9},{2,18},{10... | collective-permute-start | bytes 12296 | tf_op jit(solution)/shard_map/ppermute | solution.py:308
  10.7 1.8 %collective-permute-done.refs_1_ = bf16[256,512]{1,0:T(8,128)(2,1)S(1)} collective-permute-done((bf16[256,512]{1,0:T(8,128)(2,1)S(1)}, bf16[256,512]{1,0:T(8,128)(2,1)S(1)}, u32[]{:S(2)}, u32[]{:S(2)}) %collective-permute-start) | collective-permute-done | bytes 262176 | tf_op jit(solution)/shard_map/ppermute | solution.py:308
  13.0 1.6 %collective-permute-start.4 = (s16[1040,128]{1,0:T(8,128)(2,1)S(1)}, s16[1040,128]{1,0:T(8,128)(2,1)S(1)}, u32[]{:S(2)}, u32[]{:S(2)}) collective-permute-start(s16[1040,128]{1,0:T(8,128)(2,1)S(1)} %shard_map.68.refs_2_), channel_id=1, source_target_pairs={{0,2},{1,3},{2,4},{3,5},{4,6},{5,7},{6,0},{7,1},{8,10},{9,11},{10,... | collective-permute-start | bytes 798728 | tf_op jit(solution)/shard_map/ppermute | solution.py:317
  14.7 3.3 %collective-permute-start.5 = (bf16[256,512]{1,0:T(8,128)(2,1)S(1)}, bf16[256,512]{1,0:T(8,128)(2,1)S(1)}, u32[]{:S(2)}, u32[]{:S(2)}) collective-permute-start(bf16[256,512]{1,0:T(8,128)(2,1)S(1)} %get-tuple-element.27.refs_3_), channel_id=1, source_target_pairs={{0,16},{8,24},{16,0},{24,8},{1,17},{9,25},{17,1},{25,9},{2,18},{10... | collective-permute-start | bytes 786440 | tf_op jit(solution)/shard_map/ppermute | solution.py:308
  18.7 1.6 %collective-permute-start.3 = (s16[1040,128]{1,0:T(8,128)(2,1)S(1)}, s16[1040,128]{1,0:T(8,128)(2,1)S(1)}, u32[]{:S(2)}, u32[]{:S(2)}) collective-permute-start(s16[1040,128]{1,0:T(8,128)(2,1)S(1)} %shard_map.70.refs_2_), channel_id=1, source_target_pairs={{0,2},{1,3},{2,4},{3,5},{4,6},{5,7},{6,0},{7,1},{8,10},{9,11},{10,... | collective-permute-start | bytes 798728 | tf_op jit(solution)/shard_map/ppermute | solution.py:317
  20.4 3.6 %collective-permute-start.2 = (bf16[256,512]{1,0:T(8,128)(2,1)S(1)}, bf16[256,512]{1,0:T(8,128)(2,1)S(1)}, u32[]{:S(2)}, u32[]{:S(2)}) collective-permute-start(bf16[256,512]{1,0:T(8,128)(2,1)S(1)} %get-tuple-element.29.refs_3_), channel_id=1, source_target_pairs={{0,16},{8,24},{16,0},{24,8},{1,17},{9,25},{17,1},{25,9},{2,18},{10... | collective-permute-start | bytes 786440 | tf_op jit(solution)/shard_map/ppermute | solution.py:308
  24.5 1.6 %collective-permute-start.7 = (s16[1040,128]{1,0:T(8,128)(2,1)S(1)}, s16[1040,128]{1,0:T(8,128)(2,1)S(1)}, u32[]{:S(2)}, u32[]{:S(2)}) collective-permute-start(s16[1040,128]{1,0:T(8,128)(2,1)S(1)} %shard_map.72.refs_4_), channel_id=1, source_target_pairs={{0,2},{1,3},{2,4},{3,5},{4,6},{5,7},{6,0},{7,1},{8,10},{9,11},{10,... | collective-permute-start | bytes 798728 | tf_op jit(solution)/shard_map/ppermute | solution.py:317
  26.6 1.6 %collective-permute-start.8 = (s16[1040,128]{1,0:T(8,128)(2,1)S(1)}, s16[1040,128]{1,0:T(8,128)(2,1)S(1)}, u32[]{:S(2)}, u32[]{:S(2)}) collective-permute-start(s16[1040,128]{1,0:T(8,128)(2,1)S(1)} %shard_map.73.refs_4_), channel_id=1, source_target_pairs={{0,1},{1,0},{2,3},{3,2},{4,5},{5,4},{6,7},{7,6},{8,9},{9,8},{10,11... | collective-permute-start | bytes 798728 | tf_op jit(solution)/shard_map/ppermute | solution.py:312
  28.7 0.9 %collective-permute-start.13 = (s16[1040,128]{1,0:T(8,128)(2,1)S(1)}, s16[1040,128]{1,0:T(8,128)(2,1)S(1)}, u32[]{:S(2)}, u32[]{:S(2)}) collective-permute-start(s16[1040,128]{1,0:T(8,128)(2,1)S(1)} %shard_map.74.refs_3_), channel_id=1, source_target_pairs={{0,1},{1,0},{2,3},{3,2},{4,5},{5,4},{6,7},{7,6},{8,9},{9,8},{10,11... | collective-permute-start | bytes 798728 | tf_op jit(solution)/shard_map/ppermute | solution.py:312
  30.1 1.6 %collective-permute-start.6 = (s16[1040,128]{1,0:T(8,128)(2,1)S(1)}, s16[1040,128]{1,0:T(8,128)(2,1)S(1)}, u32[]{:S(2)}, u32[]{:S(2)}) collective-permute-start(s16[1040,128]{1,0:T(8,128)(2,1)S(1)} %shard_map.75.refs_4_), channel_id=1, source_target_pairs={{0,2},{1,3},{2,4},{3,5},{4,6},{5,7},{6,0},{7,1},{8,10},{9,11},{10,... | collective-permute-start | bytes 798728 | tf_op jit(solution)/shard_map/ppermute | solution.py:317
  31.7 3.8 %collective-permute-done.8.refs_3_ = s16[1040,128]{1,0:T(8,128)(2,1)S(1)} collective-permute-done((s16[1040,128]{1,0:T(8,128)(2,1)S(1)}, s16[1040,128]{1,0:T(8,128)(2,1)S(1)}, u32[]{:S(2)}, u32[]{:S(2)}) %collective-permute-start.8) | collective-permute-done | bytes 266272 | tf_op jit(solution)/shard_map/ppermute | solution.py:312
  36.1 1.2 %collective-permute-start.10 = (s16[1040,128]{1,0:T(8,128)(2,1)S(1)}, s16[1040,128]{1,0:T(8,128)(2,1)S(1)}, u32[]{:S(2)}, u32[]{:S(2)}) collective-permute-start(s16[1040,128]{1,0:T(8,128)(2,1)S(1)} %shard_map.76.refs_4_), channel_id=1, source_target_pairs={{0,2},{1,3},{2,4},{3,5},{4,6},{5,7},{6,0},{7,1},{8,10},{9,11},{10,... | collective-permute-start | bytes 798728 | tf_op jit(solution)/shard_map/ppermute | solution.py:317
  37.8 1.6 %collective-permute-start.12 = (s16[1040,128]{1,0:T(8,128)(2,1)S(1)}, s16[1040,128]{1,0:T(8,128)(2,1)S(1)}, u32[]{:S(2)}, u32[]{:S(2)}) collective-permute-start(s16[1040,128]{1,0:T(8,128)(2,1)S(1)} %shard_map.77.refs_4_), channel_id=1, source_target_pairs={{0,1},{1,0},{2,3},{3,2},{4,5},{5,4},{6,7},{7,6},{8,9},{9,8},{10,11... | collective-permute-start | bytes 798728 | tf_op jit(solution)/shard_map/ppermute | solution.py:312
  39.4 2.0 %collective-permute-done.6.refs_3_ = s16[1040,128]{1,0:T(8,128)(2,1)S(1)} collective-permute-done((s16[1040,128]{1,0:T(8,128)(2,1)S(1)}, s16[1040,128]{1,0:T(8,128)(2,1)S(1)}, u32[]{:S(2)}, u32[]{:S(2)}) %collective-permute-start.6) | collective-permute-done | bytes 266272 | tf_op jit(solution)/shard_map/ppermute | solution.py:317
  41.8 1.3 %collective-permute-start.9 = (s16[1040,128]{1,0:T(8,128)(2,1)S(1)}, s16[1040,128]{1,0:T(8,128)(2,1)S(1)}, u32[]{:S(2)}, u32[]{:S(2)}) collective-permute-start(s16[1040,128]{1,0:T(8,128)(2,1)S(1)} %shard_map.78.refs_4_), channel_id=1, source_target_pairs={{0,1},{1,0},{2,3},{3,2},{4,5},{5,4},{6,7},{7,6},{8,9},{9,8},{10,11... | collective-permute-start | bytes 798728 | tf_op jit(solution)/shard_map/ppermute | solution.py:312
  43.8 2.7 %collective-permute-done.12.refs_3_ = s16[1040,128]{1,0:T(8,128)(2,1)S(1)} collective-permute-done((s16[1040,128]{1,0:T(8,128)(2,1)S(1)}, s16[1040,128]{1,0:T(8,128)(2,1)S(1)}, u32[]{:S(2)}, u32[]{:S(2)}) %collective-permute-start.12) | collective-permute-done | bytes 266272 | tf_op jit(solution)/shard_map/ppermute | solution.py:312
  47.0 1.8 %collective-permute-start.15 = (s16[1040,128]{1,0:T(8,128)(2,1)S(1)}, s16[1040,128]{1,0:T(8,128)(2,1)S(1)}, u32[]{:S(2)}, u32[]{:S(2)}) collective-permute-start(s16[1040,128]{1,0:T(8,128)(2,1)S(1)} %shard_map.80.refs_8_), channel_id=1, source_target_pairs={{0,2},{1,3},{2,4},{3,5},{4,6},{5,7},{6,0},{7,1},{8,10},{9,11},{10,... | collective-permute-start | bytes 798728 | tf_op jit(solution)/shard_map/ppermute | solution.py:317
  49.4 0.9 %collective-permute-start.19 = (bf16[256,512]{1,0:T(8,128)(2,1)S(1)}, bf16[256,512]{1,0:T(8,128)(2,1)S(1)}, u32[]{:S(2)}, u32[]{:S(2)}) collective-permute-start(bf16[256,512]{1,0:T(8,128)(2,1)S(1)} %shard_map.81.refs_4_.refs_1_), channel_id=1, source_target_pairs={{0,16},{8,24},{16,0},{24,8},{1,17},{9,25},{17,1},{25,9},{2,18},{10... | collective-permute-start | bytes 786440 | tf_op jit(solution)/shard_map/ppermute | solution.py:308
  50.8 3.0 %collective-permute-start.14 = (s16[1040,128]{1,0:T(8,128)(2,1)S(1)}, s16[1040,128]{1,0:T(8,128)(2,1)S(1)}, u32[]{:S(2)}, u32[]{:S(2)}) collective-permute-start(s16[1040,128]{1,0:T(8,128)(2,1)S(1)} %shard_map.82.refs_8_), channel_id=1, source_target_pairs={{0,2},{1,3},{2,4},{3,5},{4,6},{5,7},{6,0},{7,1},{8,10},{9,11},{10,... | collective-permute-start | bytes 798728 | tf_op jit(solution)/shard_map/ppermute | solution.py:317
  53.8 1.0 %collective-permute-done.16.refs_4_ = s16[1040,128]{1,0:T(8,128)(2,1)S(1)} collective-permute-done((s16[1040,128]{1,0:T(8,128)(2,1)S(1)}, s16[1040,128]{1,0:T(8,128)(2,1)S(1)}, u32[]{:S(2)}, u32[]{:S(2)}) %collective-permute-start.16) | collective-permute-done | bytes 266272 | tf_op jit(solution)/shard_map/ppermute | solution.py:317
  55.4 1.2 %collective-permute-start.18 = (bf16[256,512]{1,0:T(8,128)(2,1)S(1)}, bf16[256,512]{1,0:T(8,128)(2,1)S(1)}, u32[]{:S(2)}, u32[]{:S(2)}) collective-permute-start(bf16[256,512]{1,0:T(8,128)(2,1)S(1)} %shard_map.83.refs_8_.refs_1_), channel_id=1, source_target_pairs={{0,16},{8,24},{16,0},{24,8},{1,17},{9,25},{17,1},{25,9},{2,18},{10... | collective-permute-start | bytes 786440 | tf_op jit(solution)/shard_map/ppermute | solution.py:308
  56.6 2.2 %collective-permute-done.15.refs_4_ = s16[1040,128]{1,0:T(8,128)(2,1)S(1)} collective-permute-done((s16[1040,128]{1,0:T(8,128)(2,1)S(1)}, s16[1040,128]{1,0:T(8,128)(2,1)S(1)}, u32[]{:S(2)}, u32[]{:S(2)}) %collective-permute-start.15) | collective-permute-done | bytes 266272 | tf_op jit(solution)/shard_map/ppermute | solution.py:317
  59.3 1.7 %collective-permute-start.17 = (bf16[256,512]{1,0:T(8,128)(2,1)S(1)}, bf16[256,512]{1,0:T(8,128)(2,1)S(1)}, u32[]{:S(2)}, u32[]{:S(2)}) collective-permute-start(bf16[256,512]{1,0:T(8,128)(2,1)S(1)} %shard_map.84.refs_8_.refs_1_), channel_id=1, source_target_pairs={{0,16},{8,24},{16,0},{24,8},{1,17},{9,25},{17,1},{25,9},{2,18},{10... | collective-permute-start | bytes 786440 | tf_op jit(solution)/shard_map/ppermute | solution.py:308
  62.2 1.7 %collective-permute-start.20 = (bf16[256,512]{1,0:T(8,128)(2,1)S(1)}, bf16[256,512]{1,0:T(8,128)(2,1)S(1)}, u32[]{:S(2)}, u32[]{:S(2)}) collective-permute-start(bf16[256,512]{1,0:T(8,128)(2,1)S(1)} %shard_map.85.refs_3_.refs_1_), channel_id=1, source_target_pairs={{0,16},{8,24},{16,0},{24,8},{1,17},{9,25},{17,1},{25,9},{2,18},{10... | collective-permute-start | bytes 786440 | tf_op jit(solution)/shard_map/ppermute | solution.py:308
  64.5 2.9 %collective-permute-done.17.refs_2_ = bf16[256,512]{1,0:T(8,128)(2,1)S(1)} collective-permute-done((bf16[256,512]{1,0:T(8,128)(2,1)S(1)}, bf16[256,512]{1,0:T(8,128)(2,1)S(1)}, u32[]{:S(2)}, u32[]{:S(2)}) %collective-permute-start.17) | collective-permute-done | bytes 262176 | tf_op jit(solution)/shard_map/ppermute | solution.py:308
  68.0 2.3 %collective-permute-done.20.refs_2_ = bf16[256,512]{1,0:T(8,128)(2,1)S(1)} collective-permute-done((bf16[256,512]{1,0:T(8,128)(2,1)S(1)}, bf16[256,512]{1,0:T(8,128)(2,1)S(1)}, u32[]{:S(2)}, u32[]{:S(2)}) %collective-permute-start.20) | collective-permute-done | bytes 262176 | tf_op jit(solution)/shard_map/ppermute | solution.py:308
  70.2 1.6 %shard_map.90 = bf16[2048,512]{1,0:T(8,128)(2,1)} custom-call(bf16[2048,512]{1,0:T(8,128)(2,1)S(1)} %get-tuple-element.35.refs_0_, bf16[2048,256]{1,0:T(8,128)(2,1)S(1)} %get-tuple-element.36.refs_1_, bf16[256,512]{1,0:T(8,128)(2,1)S(1)} %collective-permute-done.20.refs_2_), custom_call_target="tpu_custom_call" | custom-call | flops 4000000000 | bytes 1 | tf_op jit(solution)/shard_map/pallas_call | solution.py:45
  (49 shorter events, 10.4 us)
Async XLA Ops:
  0.0 5.4 %copy-start.1 = (bf16[2048,512]{1,0:T(8,128)(2,1)S(1)}, bf16[2048,512]{1,0:T(8,128)(2,1)}, u32[]{:S(2)}) copy-start(bf16[2048,512]{1,0:T(8,128)(2,1)} %refs_1_.7) | copy-start | bytes 6291460
  0.0 5.4 %copy-start.4 = (s32[2048]{0:T(1024)S(1)}, s32[2048]{0:T(1024)}, u32[]{:S(2)}) copy-start(s32[2048]{0:T(1024)} %param.9) | copy-start | bytes 24580
  1.2 5.6 %copy-start = (bf16[512,2048]{1,0:T(8,128)(2,1)S(1)}, bf16[512,2048]{1,0:T(8,128)(2,1)}, u32[]{:S(2)}) copy-start(bf16[512,2048]{1,0:T(8,128)(2,1)} %refs_0_.1) | copy-start | bytes 6291460
  1.2 11.3 %collective-permute-start = (bf16[256,512]{1,0:T(8,128)(2,1)S(1)}, bf16[256,512]{1,0:T(8,128)(2,1)S(1)}, u32[]{:S(2)}, u32[]{:S(2)}) collective-permute-start(bf16[256,512]{1,0:T(8,128)(2,1)S(1)} %shard_map.64.refs_2_), channel_id=1, source_target_pairs={{0,16},{8,24},{16,0},{24,8},{1,17},{9,25},{17,1},{25,9},{2,18},{10... | collective-permute-start | bytes 786440 | tf_op jit(solution)/shard_map/ppermute | solution.py:308
  5.4 2.8 %copy-start.2 = (s32[2048]{0:T(1024)S(1)}, s32[2048]{0:T(1024)}, u32[]{:S(2)}) copy-start(s32[2048]{0:T(1024)} %param.8) | copy-start | bytes 24580
  5.4 2.8 %copy-start.3 = (f32[2000]{0:T(1024)S(1)}, f32[2000]{0:T(1024)}, u32[]{:S(2)}) copy-start(f32[2000]{0:T(1024)} %param.11) | copy-start | bytes 24004
  5.5 2.8 %copy-start.5 = (f32[200]{0:T(256)S(1)}, f32[200]{0:T(256)}, u32[]{:S(2)}) copy-start(f32[200]{0:T(256)} %param.10) | copy-start | bytes 2404
  5.5 12.7 %collective-permute-start.1 = (bf16[256,512]{1,0:T(8,128)(2,1)S(1)}, bf16[256,512]{1,0:T(8,128)(2,1)S(1)}, u32[]{:S(2)}, u32[]{:S(2)}) collective-permute-start(bf16[256,512]{1,0:T(8,128)(2,1)S(1)} %get-tuple-element.22.refs_1_), channel_id=1, source_target_pairs={{0,16},{8,24},{16,0},{24,8},{1,17},{9,25},{17,1},{25,9},{2,18},{10... | collective-permute-start | bytes 786440 | tf_op jit(solution)/shard_map/ppermute | solution.py:308
  9.9 38.9 %collective-permute-start.11 = (f32[1,1024]{1,0:T(1,128)S(1)}, f32[1,1024]{1,0:T(1,128)S(1)}, u32[]{:S(2)}, u32[]{:S(2)}) collective-permute-start(f32[1,1024]{1,0:T(1,128)S(1)} %get-tuple-element.34), channel_id=1, source_target_pairs={{0,16},{8,24},{16,0},{24,8},{1,17},{9,25},{17,1},{25,9},{2,18},{10... | collective-permute-start | bytes 12296 | tf_op jit(solution)/shard_map/ppermute | solution.py:308
  13.0 13.1 %collective-permute-start.4 = (s16[1040,128]{1,0:T(8,128)(2,1)S(1)}, s16[1040,128]{1,0:T(8,128)(2,1)S(1)}, u32[]{:S(2)}, u32[]{:S(2)}) collective-permute-start(s16[1040,128]{1,0:T(8,128)(2,1)S(1)} %shard_map.68.refs_2_), channel_id=1, source_target_pairs={{0,2},{1,3},{2,4},{3,5},{4,6},{5,7},{6,0},{7,1},{8,10},{9,11},{10,... | collective-permute-start | bytes 798728 | tf_op jit(solution)/shard_map/ppermute | solution.py:317
  14.7 9.2 %collective-permute-start.5 = (bf16[256,512]{1,0:T(8,128)(2,1)S(1)}, bf16[256,512]{1,0:T(8,128)(2,1)S(1)}, u32[]{:S(2)}, u32[]{:S(2)}) collective-permute-start(bf16[256,512]{1,0:T(8,128)(2,1)S(1)} %get-tuple-element.27.refs_3_), channel_id=1, source_target_pairs={{0,16},{8,24},{16,0},{24,8},{1,17},{9,25},{17,1},{25,9},{2,18},{10... | collective-permute-start | bytes 786440 | tf_op jit(solution)/shard_map/ppermute | solution.py:308
  18.7 9.6 %collective-permute-start.3 = (s16[1040,128]{1,0:T(8,128)(2,1)S(1)}, s16[1040,128]{1,0:T(8,128)(2,1)S(1)}, u32[]{:S(2)}, u32[]{:S(2)}) collective-permute-start(s16[1040,128]{1,0:T(8,128)(2,1)S(1)} %shard_map.70.refs_2_), channel_id=1, source_target_pairs={{0,2},{1,3},{2,4},{3,5},{4,6},{5,7},{6,0},{7,1},{8,10},{9,11},{10,... | collective-permute-start | bytes 798728 | tf_op jit(solution)/shard_map/ppermute | solution.py:317
  20.4 9.3 %collective-permute-start.2 = (bf16[256,512]{1,0:T(8,128)(2,1)S(1)}, bf16[256,512]{1,0:T(8,128)(2,1)S(1)}, u32[]{:S(2)}, u32[]{:S(2)}) collective-permute-start(bf16[256,512]{1,0:T(8,128)(2,1)S(1)} %get-tuple-element.29.refs_3_), channel_id=1, source_target_pairs={{0,16},{8,24},{16,0},{24,8},{1,17},{9,25},{17,1},{25,9},{2,18},{10... | collective-permute-start | bytes 786440 | tf_op jit(solution)/shard_map/ppermute | solution.py:308
  24.5 12.8 %collective-permute-start.7 = (s16[1040,128]{1,0:T(8,128)(2,1)S(1)}, s16[1040,128]{1,0:T(8,128)(2,1)S(1)}, u32[]{:S(2)}, u32[]{:S(2)}) collective-permute-start(s16[1040,128]{1,0:T(8,128)(2,1)S(1)} %shard_map.72.refs_4_), channel_id=1, source_target_pairs={{0,2},{1,3},{2,4},{3,5},{4,6},{5,7},{6,0},{7,1},{8,10},{9,11},{10,... | collective-permute-start | bytes 798728 | tf_op jit(solution)/shard_map/ppermute | solution.py:317
  26.6 8.9 %collective-permute-start.8 = (s16[1040,128]{1,0:T(8,128)(2,1)S(1)}, s16[1040,128]{1,0:T(8,128)(2,1)S(1)}, u32[]{:S(2)}, u32[]{:S(2)}) collective-permute-start(s16[1040,128]{1,0:T(8,128)(2,1)S(1)} %shard_map.73.refs_4_), channel_id=1, source_target_pairs={{0,1},{1,0},{2,3},{3,2},{4,5},{5,4},{6,7},{7,6},{8,9},{9,8},{10,11... | collective-permute-start | bytes 798728 | tf_op jit(solution)/shard_map/ppermute | solution.py:312
  28.7 14.4 %collective-permute-start.13 = (s16[1040,128]{1,0:T(8,128)(2,1)S(1)}, s16[1040,128]{1,0:T(8,128)(2,1)S(1)}, u32[]{:S(2)}, u32[]{:S(2)}) collective-permute-start(s16[1040,128]{1,0:T(8,128)(2,1)S(1)} %shard_map.74.refs_3_), channel_id=1, source_target_pairs={{0,1},{1,0},{2,3},{3,2},{4,5},{5,4},{6,7},{7,6},{8,9},{9,8},{10,11... | collective-permute-start | bytes 798728 | tf_op jit(solution)/shard_map/ppermute | solution.py:312
  30.1 11.2 %collective-permute-start.6 = (s16[1040,128]{1,0:T(8,128)(2,1)S(1)}, s16[1040,128]{1,0:T(8,128)(2,1)S(1)}, u32[]{:S(2)}, u32[]{:S(2)}) collective-permute-start(s16[1040,128]{1,0:T(8,128)(2,1)S(1)} %shard_map.75.refs_4_), channel_id=1, source_target_pairs={{0,2},{1,3},{2,4},{3,5},{4,6},{5,7},{6,0},{7,1},{8,10},{9,11},{10,... | collective-permute-start | bytes 798728 | tf_op jit(solution)/shard_map/ppermute | solution.py:317
  36.1 12.8 %collective-permute-start.10 = (s16[1040,128]{1,0:T(8,128)(2,1)S(1)}, s16[1040,128]{1,0:T(8,128)(2,1)S(1)}, u32[]{:S(2)}, u32[]{:S(2)}) collective-permute-start(s16[1040,128]{1,0:T(8,128)(2,1)S(1)} %shard_map.76.refs_4_), channel_id=1, source_target_pairs={{0,2},{1,3},{2,4},{3,5},{4,6},{5,7},{6,0},{7,1},{8,10},{9,11},{10,... | collective-permute-start | bytes 798728 | tf_op jit(solution)/shard_map/ppermute | solution.py:317
  37.8 8.7 %collective-permute-start.12 = (s16[1040,128]{1,0:T(8,128)(2,1)S(1)}, s16[1040,128]{1,0:T(8,128)(2,1)S(1)}, u32[]{:S(2)}, u32[]{:S(2)}) collective-permute-start(s16[1040,128]{1,0:T(8,128)(2,1)S(1)} %shard_map.77.refs_4_), channel_id=1, source_target_pairs={{0,1},{1,0},{2,3},{3,2},{4,5},{5,4},{6,7},{7,6},{8,9},{9,8},{10,11... | collective-permute-start | bytes 798728 | tf_op jit(solution)/shard_map/ppermute | solution.py:312
  41.8 8.5 %collective-permute-start.9 = (s16[1040,128]{1,0:T(8,128)(2,1)S(1)}, s16[1040,128]{1,0:T(8,128)(2,1)S(1)}, u32[]{:S(2)}, u32[]{:S(2)}) collective-permute-start(s16[1040,128]{1,0:T(8,128)(2,1)S(1)} %shard_map.78.refs_4_), channel_id=1, source_target_pairs={{0,1},{1,0},{2,3},{3,2},{4,5},{5,4},{6,7},{7,6},{8,9},{9,8},{10,11... | collective-permute-start | bytes 798728 | tf_op jit(solution)/shard_map/ppermute | solution.py:312
  43.7 11.2 %collective-permute-start.16 = (s16[1040,128]{1,0:T(8,128)(2,1)S(1)}, s16[1040,128]{1,0:T(8,128)(2,1)S(1)}, u32[]{:S(2)}, u32[]{:S(2)}) collective-permute-start(s16[1040,128]{1,0:T(8,128)(2,1)S(1)} %shard_map.79.refs_4_), channel_id=1, source_target_pairs={{0,2},{1,3},{2,4},{3,5},{4,6},{5,7},{6,0},{7,1},{8,10},{9,11},{10,... | collective-permute-start | bytes 798728 | tf_op jit(solution)/shard_map/ppermute | solution.py:317
  47.0 11.8 %collective-permute-start.15 = (s16[1040,128]{1,0:T(8,128)(2,1)S(1)}, s16[1040,128]{1,0:T(8,128)(2,1)S(1)}, u32[]{:S(2)}, u32[]{:S(2)}) collective-permute-start(s16[1040,128]{1,0:T(8,128)(2,1)S(1)} %shard_map.80.refs_8_), channel_id=1, source_target_pairs={{0,2},{1,3},{2,4},{3,5},{4,6},{5,7},{6,0},{7,1},{8,10},{9,11},{10,... | collective-permute-start | bytes 798728 | tf_op jit(solution)/shard_map/ppermute | solution.py:317
  49.4 14.5 %collective-permute-start.19 = (bf16[256,512]{1,0:T(8,128)(2,1)S(1)}, bf16[256,512]{1,0:T(8,128)(2,1)S(1)}, u32[]{:S(2)}, u32[]{:S(2)}) collective-permute-start(bf16[256,512]{1,0:T(8,128)(2,1)S(1)} %shard_map.81.refs_4_.refs_1_), channel_id=1, source_target_pairs={{0,16},{8,24},{16,0},{24,8},{1,17},{9,25},{17,1},{25,9},{2,18},{10... | collective-permute-start | bytes 786440 | tf_op jit(solution)/shard_map/ppermute | solution.py:308
  50.8 10.8 %collective-permute-start.14 = (s16[1040,128]{1,0:T(8,128)(2,1)S(1)}, s16[1040,128]{1,0:T(8,128)(2,1)S(1)}, u32[]{:S(2)}, u32[]{:S(2)}) collective-permute-start(s16[1040,128]{1,0:T(8,128)(2,1)S(1)} %shard_map.82.refs_8_), channel_id=1, source_target_pairs={{0,2},{1,3},{2,4},{3,5},{4,6},{5,7},{6,0},{7,1},{8,10},{9,11},{10,... | collective-permute-start | bytes 798728 | tf_op jit(solution)/shard_map/ppermute | solution.py:317
  55.4 8.8 %collective-permute-start.18 = (bf16[256,512]{1,0:T(8,128)(2,1)S(1)}, bf16[256,512]{1,0:T(8,128)(2,1)S(1)}, u32[]{:S(2)}, u32[]{:S(2)}) collective-permute-start(bf16[256,512]{1,0:T(8,128)(2,1)S(1)} %shard_map.83.refs_8_.refs_1_), channel_id=1, source_target_pairs={{0,16},{8,24},{16,0},{24,8},{1,17},{9,25},{17,1},{25,9},{2,18},{10... | collective-permute-start | bytes 786440 | tf_op jit(solution)/shard_map/ppermute | solution.py:308
  59.3 8.1 %collective-permute-start.17 = (bf16[256,512]{1,0:T(8,128)(2,1)S(1)}, bf16[256,512]{1,0:T(8,128)(2,1)S(1)}, u32[]{:S(2)}, u32[]{:S(2)}) collective-permute-start(bf16[256,512]{1,0:T(8,128)(2,1)S(1)} %shard_map.84.refs_8_.refs_1_), channel_id=1, source_target_pairs={{0,16},{8,24},{16,0},{24,8},{1,17},{9,25},{17,1},{25,9},{2,18},{10... | collective-permute-start | bytes 786440 | tf_op jit(solution)/shard_map/ppermute | solution.py:308
  62.2 8.1 %collective-permute-start.20 = (bf16[256,512]{1,0:T(8,128)(2,1)S(1)}, bf16[256,512]{1,0:T(8,128)(2,1)S(1)}, u32[]{:S(2)}, u32[]{:S(2)}) collective-permute-start(bf16[256,512]{1,0:T(8,128)(2,1)S(1)} %shard_map.85.refs_3_.refs_1_), channel_id=1, source_target_pairs={{0,16},{8,24},{16,0},{24,8},{1,17},{9,25},{17,1},{25,9},{2,18},{10... | collective-permute-start | bytes 786440 | tf_op jit(solution)/shard_map/ppermute | solution.py:308

commit v9 on v8

--- a/solution.py
+++ b/solution.py
@@ -101,20 +101,20 @@
         part = pl.ds(block * chunk, chunk)
         return pltpu.make_async_copy(amplitudes.at[part, :], held.at[part, :], arrivals.at[block])
 
+    slots_copy = pltpu.make_async_copy(partner, slots, arrivals.at[blocks])
+    slots_copy.start()
+    for block in range(blocks):
+        fetch(block).start()
+    slots_copy.wait()
+
     @pl.when(upper == 0)
     def _():
-        part = pl.ds(pl.multiple_of(first, LANES), chunk)
-        straight = pltpu.make_async_copy(amplitudes.at[part, :], out, arrivals.at[0])
-        straight.start()
-        straight.wait()
+        for block in range(blocks):
+            fetch(block).wait()
+        out[...] = held[pl.ds(pl.multiple_of(first, LANES), chunk), :]
 
     @pl.when(upper == 1)
     def _():
-        slots_copy = pltpu.make_async_copy(partner, slots, arrivals.at[blocks])
-        slots_copy.start()
-        for block in range(blocks):
-            fetch(block).start()
-        slots_copy.wait()
         target = partner_base(rows) + first + lax.broadcasted_iota(jnp.int32, (chunk, chunk), 0)
         total = jnp.zeros(out.shape, jnp.float32)
         for block in range(blocks):
@@ -335,16 +335,15 @@
 
     own, other, moved, crossed, arrived, done, placed = {}, {}, {}, {}, {}, {}, ()
     operands = [pltpu.with_memory_space_constraint(value, pltpu.HBM) for value in (partner[None, :], amplitudes)]
-    room = (pltpu.VMEM((rows, width), jnp.bfloat16), pltpu.VMEM((1, rows), jnp.int32))
-    room += (pltpu.SemaphoreType.DMA((rows // chunks[0] + 1,)),)
-    result = call(align_first_kernel, chunk_shape(0), operands, in_spec=HBM, scratch=room)
+    room = (pltpu.VMEM((1, rows), jnp.int32), pltpu.SemaphoreType.DMA((rows // chunks[0] + 1,)))
+    result, held = call(align_first_kernel, [chunk_shape(0), whole_shape], operands, in_spec=HBM, scratch=room)
     other[0] = across_rows(result)
     last = (result,)
     for step, index in ORDER:
         if step == "align":
             wanted = tuple((begins[chunk], send) for chunk, send in ALIGNED[index])
             shapes = [chunk_shape(chunk) for chunk, _ in ALIGNED[index]]
-            result = call(functools.partial(align_kernel, wanted), shapes, (partner[None, :], amplitudes), last)
+            result = call(functools.partial(align_kernel, wanted), shapes, (partner[None, :], held), last)
             for (chunk, send), picked in zip(ALIGNED[index], result):
                 if send:
                     other[chunk] = across_rows(picked)
@@ -392,10 +391,10 @@
     picks_shape = jax.ShapeDtypeStruct((rows, chunks[index]), jnp.bfloat16)
     kernel = functools.partial(place_own_kernel, begins[index])
     most, picks = call(kernel, [whole_shape, picks_shape], (partner[None, :], mine, *placed), last)
-    held = pltpu.VMEM((rows, width), jnp.bfloat16)
+    room = pltpu.VMEM((rows, width), jnp.bfloat16)
     arrivals = pltpu.SemaphoreType.DMA((rows // chunks[index],))
     kernel = functools.partial(place_other_kernel, begins[index])
-    return call(kernel, whole_shape, (most, picks, theirs), out_spec=ANY, scratch=(held, arrivals))
+    return call(kernel, whole_shape, (most, picks, theirs), out_spec=ANY, scratch=(room, arrivals))
 
 
 def solution(mesh):

time: 72.4 us -> 72.3 us (level)
  starting transfers between devices: 36.8 us -> 36 us
    ppermute x9, starting transfers between devices: 18.9 us -> 18.2 us  [across_rows(): lax.ppermute(value, 'row', [(i, i ^ count // 2) for i in range(count)])]
where the time goes in v9:
time: 72.3 us; the launch traced here: 71.9 us
  starting transfers between devices  36 us (50%)
  waiting for transfers between devices  19.3 us (27%)
  Pallas kernels  15.9 us (22%)
    ppermute x9, starting transfers between devices, across_rows(): lax.ppermute(value, 'row', [(i, i ^ count // 2) for i in range(count)])  18.2 us
    pallas_call x27, Pallas kernels, call(): pl.pallas_call(kernel, out_shape=out_shape, in_specs=[in_spec or VMEM] *...  15.9 us
    ppermute x8, starting transfers between devices, two_along(): lax.ppermute(value, 'col', [(i, (i + 2) % count) for i in range(count)])  12.5 us
    ppermute x9, waiting for transfers between devices, across_rows(): lax.ppermute(value, 'row', [(i, i ^ count // 2) for i in range(count)])  7.04 us
    ppermute x4, waiting for transfers between devices, across_pair(): lax.ppermute(value, 'col', [(i, i ^ 1) for i in range(lax.axis_size('col'...  6.53 us
    ppermute x8, waiting for transfers between devices, two_along(): lax.ppermute(value, 'col', [(i, (i + 2) % count) for i in range(count)])  5.75 us
    ppermute x4, starting transfers between devices, across_pair(): lax.ppermute(value, 'col', [(i, i ^ 1) for i in range(lax.axis_size('col'...  5.33 us
  transfers between devices with their start and end apart: 21, of which 10 were waited for; matrix products, arithmetic and copies ran while one was open for 0% of the time, Pallas kernels for 18%

profile of v9, /device:TPU:0, one launch (start us, length us, event | category | flops | bytes accessed | tf_op | source)
XLA Modules:
  0.0 71.9 jit_solution(16443562605219742470)
XLA Ops:
  0.0 1.6 %shard_map.64 = (bf16[256,512]{1,0:T(8,128)(2,1)S(1)}, bf16[2048,512]{1,0:T(8,128)(2,1)S(1)}) custom-call(s32[1,2048]{1,0:T(1,128)} %bitcast.6, bf16[2048,512]{1,0:T(8,128)(2,1)} %refs_1_.1), custom_call_target="tpu_custom_call" | custom-call | flops 4000000000 | bytes 1 | tf_op jit(solution)/shard_map/pallas_call | solution.py:45
  1.6 3.6 %collective-permute-start = (bf16[256,512]{1,0:T(8,128)(2,1)S(1)}, bf16[256,512]{1,0:T(8,128)(2,1)S(1)}, u32[]{:S(2)}, u32[]{:S(2)}) collective-permute-start(bf16[256,512]{1,0:T(8,128)(2,1)S(1)} %get-tuple-element.24.refs_2_), channel_id=1, source_target_pairs={{0,16},{8,24},{16,0},{24,8},{1,17},{9,25},{17,1},{25,9},{2,18},{10... | collective-permute-start | bytes 786440 | tf_op jit(solution)/shard_map/ppermute | solution.py:308
  5.3 1.3 %collective-permute-start.1 = (bf16[256,512]{1,0:T(8,128)(2,1)S(1)}, bf16[256,512]{1,0:T(8,128)(2,1)S(1)}, u32[]{:S(2)}, u32[]{:S(2)}) collective-permute-start(bf16[256,512]{1,0:T(8,128)(2,1)S(1)} %get-tuple-element.26.refs_1_), channel_id=1, source_target_pairs={{0,16},{8,24},{16,0},{24,8},{1,17},{9,25},{17,1},{25,9},{2,18},{10... | collective-permute-start | bytes 786440 | tf_op jit(solution)/shard_map/ppermute | solution.py:308
  6.8 1.5 %shard_map.66 = (bf16[1024,512]{1,0:T(8,128)(2,1)S(1)}, bf16[1024,512]{1,0:T(8,128)(2,1)S(1)}, bf16[1024,512]{1,0:T(8,128)(2,1)S(1)}, bf16[1024,512]{1,0:T(8,128)(2,1)S(1)}) custom-call(bf16[512,2048]{1,0:T(8,128)(2,1)S(1)} %copy-done, bf16[256,512]{1,0:T(8,128)(2,1)S(1)} %get-tuple-element.26.refs_1_), custom_call_target="tpu_custom_call" | custom-call | flops 4000000000 | bytes 1 | tf_op jit(solution)/shard_map/pallas_call | solution.py:45
  8.3 1.6 %shard_map.67 = (f32[1,1024]{1,0:T(1,128)S(1)}, f32[1,1024]{1,0:T(1,128)S(1)}, f32[1,512]{1,0:T(1,128)S(1)}) custom-call(s32[1,2048]{1,0:T(1,128)S(1)} %bitcast.4, f32[1,200]{1,0:T(1,128)S(1)} %bitcast.14, f32[1,2000]{1,0:T(1,128)S(1)} %bitcast.5, bf16[1024,512]{1,0:T(8,128)(2,1)S(1)} %get-tuple-element.28.refs_3_.refs_2_), custom_call_target="tpu_custom_call" | custom-call | flops 4000000000 | bytes 1 | tf_op jit(solution)/shard_map/pallas_call | solution.py:45
  10.0 0.7 collective-permute-start.11
  10.6 1.8 %collective-permute-done.refs_1_ = bf16[256,512]{1,0:T(8,128)(2,1)S(1)} collective-permute-done((bf16[256,512]{1,0:T(8,128)(2,1)S(1)}, bf16[256,512]{1,0:T(8,128)(2,1)S(1)}, u32[]{:S(2)}, u32[]{:S(2)}) %collective-permute-start) | collective-permute-done | bytes 262176 | tf_op jit(solution)/shard_map/ppermute | solution.py:308
  12.9 1.6 %collective-permute-start.4 = (s16[1040,128]{1,0:T(8,128)(2,1)S(1)}, s16[1040,128]{1,0:T(8,128)(2,1)S(1)}, u32[]{:S(2)}, u32[]{:S(2)}) collective-permute-start(s16[1040,128]{1,0:T(8,128)(2,1)S(1)} %shard_map.68.refs_2_), channel_id=1, source_target_pairs={{0,2},{1,3},{2,4},{3,5},{4,6},{5,7},{6,0},{7,1},{8,10},{9,11},{10,... | collective-permute-start | bytes 798728 | tf_op jit(solution)/shard_map/ppermute | solution.py:317
  14.6 3.3 %collective-permute-start.5 = (bf16[256,512]{1,0:T(8,128)(2,1)S(1)}, bf16[256,512]{1,0:T(8,128)(2,1)S(1)}, u32[]{:S(2)}, u32[]{:S(2)}) collective-permute-start(bf16[256,512]{1,0:T(8,128)(2,1)S(1)} %get-tuple-element.31.refs_3_), channel_id=1, source_target_pairs={{0,16},{8,24},{16,0},{24,8},{1,17},{9,25},{17,1},{25,9},{2,18},{10... | collective-permute-start | bytes 786440 | tf_op jit(solution)/shard_map/ppermute | solution.py:308
  18.5 1.6 %collective-permute-start.3 = (s16[1040,128]{1,0:T(8,128)(2,1)S(1)}, s16[1040,128]{1,0:T(8,128)(2,1)S(1)}, u32[]{:S(2)}, u32[]{:S(2)}) collective-permute-start(s16[1040,128]{1,0:T(8,128)(2,1)S(1)} %shard_map.70.refs_2_), channel_id=1, source_target_pairs={{0,2},{1,3},{2,4},{3,5},{4,6},{5,7},{6,0},{7,1},{8,10},{9,11},{10,... | collective-permute-start | bytes 798728 | tf_op jit(solution)/shard_map/ppermute | solution.py:317
  20.2 3.6 %collective-permute-start.2 = (bf16[256,512]{1,0:T(8,128)(2,1)S(1)}, bf16[256,512]{1,0:T(8,128)(2,1)S(1)}, u32[]{:S(2)}, u32[]{:S(2)}) collective-permute-start(bf16[256,512]{1,0:T(8,128)(2,1)S(1)} %get-tuple-element.33.refs_3_), channel_id=1, source_target_pairs={{0,16},{8,24},{16,0},{24,8},{1,17},{9,25},{17,1},{25,9},{2,18},{10... | collective-permute-start | bytes 786440 | tf_op jit(solution)/shard_map/ppermute | solution.py:308
  24.3 1.6 %collective-permute-start.7 = (s16[1040,128]{1,0:T(8,128)(2,1)S(1)}, s16[1040,128]{1,0:T(8,128)(2,1)S(1)}, u32[]{:S(2)}, u32[]{:S(2)}) collective-permute-start(s16[1040,128]{1,0:T(8,128)(2,1)S(1)} %shard_map.72.refs_4_), channel_id=1, source_target_pairs={{0,2},{1,3},{2,4},{3,5},{4,6},{5,7},{6,0},{7,1},{8,10},{9,11},{10,... | collective-permute-start | bytes 798728 | tf_op jit(solution)/shard_map/ppermute | solution.py:317
  26.5 1.6 %collective-permute-start.8 = (s16[1040,128]{1,0:T(8,128)(2,1)S(1)}, s16[1040,128]{1,0:T(8,128)(2,1)S(1)}, u32[]{:S(2)}, u32[]{:S(2)}) collective-permute-start(s16[1040,128]{1,0:T(8,128)(2,1)S(1)} %shard_map.73.refs_4_), channel_id=1, source_target_pairs={{0,1},{1,0},{2,3},{3,2},{4,5},{5,4},{6,7},{7,6},{8,9},{9,8},{10,11... | collective-permute-start | bytes 798728 | tf_op jit(solution)/shard_map/ppermute | solution.py:312
  28.6 0.9 %collective-permute-start.13 = (s16[1040,128]{1,0:T(8,128)(2,1)S(1)}, s16[1040,128]{1,0:T(8,128)(2,1)S(1)}, u32[]{:S(2)}, u32[]{:S(2)}) collective-permute-start(s16[1040,128]{1,0:T(8,128)(2,1)S(1)} %shard_map.74.refs_3_), channel_id=1, source_target_pairs={{0,1},{1,0},{2,3},{3,2},{4,5},{5,4},{6,7},{7,6},{8,9},{9,8},{10,11... | collective-permute-start | bytes 798728 | tf_op jit(solution)/shard_map/ppermute | solution.py:312
  30.0 1.6 %collective-permute-start.6 = (s16[1040,128]{1,0:T(8,128)(2,1)S(1)}, s16[1040,128]{1,0:T(8,128)(2,1)S(1)}, u32[]{:S(2)}, u32[]{:S(2)}) collective-permute-start(s16[1040,128]{1,0:T(8,128)(2,1)S(1)} %shard_map.75.refs_4_), channel_id=1, source_target_pairs={{0,2},{1,3},{2,4},{3,5},{4,6},{5,7},{6,0},{7,1},{8,10},{9,11},{10,... | collective-permute-start | bytes 798728 | tf_op jit(solution)/shard_map/ppermute | solution.py:317
  31.6 3.8 %collective-permute-done.8.refs_3_ = s16[1040,128]{1,0:T(8,128)(2,1)S(1)} collective-permute-done((s16[1040,128]{1,0:T(8,128)(2,1)S(1)}, s16[1040,128]{1,0:T(8,128)(2,1)S(1)}, u32[]{:S(2)}, u32[]{:S(2)}) %collective-permute-start.8) | collective-permute-done | bytes 266272 | tf_op jit(solution)/shard_map/ppermute | solution.py:312
  35.9 1.1 %collective-permute-start.10 = (s16[1040,128]{1,0:T(8,128)(2,1)S(1)}, s16[1040,128]{1,0:T(8,128)(2,1)S(1)}, u32[]{:S(2)}, u32[]{:S(2)}) collective-permute-start(s16[1040,128]{1,0:T(8,128)(2,1)S(1)} %shard_map.76.refs_4_), channel_id=1, source_target_pairs={{0,2},{1,3},{2,4},{3,5},{4,6},{5,7},{6,0},{7,1},{8,10},{9,11},{10,... | collective-permute-start | bytes 798728 | tf_op jit(solution)/shard_map/ppermute | solution.py:317
  37.6 1.6 %collective-permute-start.12 = (s16[1040,128]{1,0:T(8,128)(2,1)S(1)}, s16[1040,128]{1,0:T(8,128)(2,1)S(1)}, u32[]{:S(2)}, u32[]{:S(2)}) collective-permute-start(s16[1040,128]{1,0:T(8,128)(2,1)S(1)} %shard_map.77.refs_4_), channel_id=1, source_target_pairs={{0,1},{1,0},{2,3},{3,2},{4,5},{5,4},{6,7},{7,6},{8,9},{9,8},{10,11... | collective-permute-start | bytes 798728 | tf_op jit(solution)/shard_map/ppermute | solution.py:312
  39.2 2.0 %collective-permute-done.6.refs_3_ = s16[1040,128]{1,0:T(8,128)(2,1)S(1)} collective-permute-done((s16[1040,128]{1,0:T(8,128)(2,1)S(1)}, s16[1040,128]{1,0:T(8,128)(2,1)S(1)}, u32[]{:S(2)}, u32[]{:S(2)}) %collective-permute-start.6) | collective-permute-done | bytes 266272 | tf_op jit(solution)/shard_map/ppermute | solution.py:317
  41.7 1.3 %collective-permute-start.9 = (s16[1040,128]{1,0:T(8,128)(2,1)S(1)}, s16[1040,128]{1,0:T(8,128)(2,1)S(1)}, u32[]{:S(2)}, u32[]{:S(2)}) collective-permute-start(s16[1040,128]{1,0:T(8,128)(2,1)S(1)} %shard_map.78.refs_4_), channel_id=1, source_target_pairs={{0,1},{1,0},{2,3},{3,2},{4,5},{5,4},{6,7},{7,6},{8,9},{9,8},{10,11... | collective-permute-start | bytes 798728 | tf_op jit(solution)/shard_map/ppermute | solution.py:312
  43.6 2.7 %collective-permute-done.12.refs_3_ = s16[1040,128]{1,0:T(8,128)(2,1)S(1)} collective-permute-done((s16[1040,128]{1,0:T(8,128)(2,1)S(1)}, s16[1040,128]{1,0:T(8,128)(2,1)S(1)}, u32[]{:S(2)}, u32[]{:S(2)}) %collective-permute-start.12) | collective-permute-done | bytes 266272 | tf_op jit(solution)/shard_map/ppermute | solution.py:312
  46.9 1.8 %collective-permute-start.15 = (s16[1040,128]{1,0:T(8,128)(2,1)S(1)}, s16[1040,128]{1,0:T(8,128)(2,1)S(1)}, u32[]{:S(2)}, u32[]{:S(2)}) collective-permute-start(s16[1040,128]{1,0:T(8,128)(2,1)S(1)} %shard_map.80.refs_8_), channel_id=1, source_target_pairs={{0,2},{1,3},{2,4},{3,5},{4,6},{5,7},{6,0},{7,1},{8,10},{9,11},{10,... | collective-permute-start | bytes 798728 | tf_op jit(solution)/shard_map/ppermute | solution.py:317
  49.2 0.9 %collective-permute-start.19 = (bf16[256,512]{1,0:T(8,128)(2,1)S(1)}, bf16[256,512]{1,0:T(8,128)(2,1)S(1)}, u32[]{:S(2)}, u32[]{:S(2)}) collective-permute-start(bf16[256,512]{1,0:T(8,128)(2,1)S(1)} %shard_map.81.refs_4_.refs_1_), channel_id=1, source_target_pairs={{0,16},{8,24},{16,0},{24,8},{1,17},{9,25},{17,1},{25,9},{2,18},{10... | collective-permute-start | bytes 786440 | tf_op jit(solution)/shard_map/ppermute | solution.py:308
  50.7 3.0 %collective-permute-start.14 = (s16[1040,128]{1,0:T(8,128)(2,1)S(1)}, s16[1040,128]{1,0:T(8,128)(2,1)S(1)}, u32[]{:S(2)}, u32[]{:S(2)}) collective-permute-start(s16[1040,128]{1,0:T(8,128)(2,1)S(1)} %shard_map.82.refs_8_), channel_id=1, source_target_pairs={{0,2},{1,3},{2,4},{3,5},{4,6},{5,7},{6,0},{7,1},{8,10},{9,11},{10,... | collective-permute-start | bytes 798728 | tf_op jit(solution)/shard_map/ppermute | solution.py:317
  53.7 1.0 %collective-permute-done.16.refs_4_ = s16[1040,128]{1,0:T(8,128)(2,1)S(1)} collective-permute-done((s16[1040,128]{1,0:T(8,128)(2,1)S(1)}, s16[1040,128]{1,0:T(8,128)(2,1)S(1)}, u32[]{:S(2)}, u32[]{:S(2)}) %collective-permute-start.16) | collective-permute-done | bytes 266272 | tf_op jit(solution)/shard_map/ppermute | solution.py:317
  55.3 1.2 %collective-permute-start.18 = (bf16[256,512]{1,0:T(8,128)(2,1)S(1)}, bf16[256,512]{1,0:T(8,128)(2,1)S(1)}, u32[]{:S(2)}, u32[]{:S(2)}) collective-permute-start(bf16[256,512]{1,0:T(8,128)(2,1)S(1)} %shard_map.83.refs_8_.refs_1_), channel_id=1, source_target_pairs={{0,16},{8,24},{16,0},{24,8},{1,17},{9,25},{17,1},{25,9},{2,18},{10... | collective-permute-start | bytes 786440 | tf_op jit(solution)/shard_map/ppermute | solution.py:308
  56.5 2.1 %collective-permute-done.15.refs_4_ = s16[1040,128]{1,0:T(8,128)(2,1)S(1)} collective-permute-done((s16[1040,128]{1,0:T(8,128)(2,1)S(1)}, s16[1040,128]{1,0:T(8,128)(2,1)S(1)}, u32[]{:S(2)}, u32[]{:S(2)}) %collective-permute-start.15) | collective-permute-done | bytes 266272 | tf_op jit(solution)/shard_map/ppermute | solution.py:317
  59.2 1.8 %collective-permute-start.17 = (bf16[256,512]{1,0:T(8,128)(2,1)S(1)}, bf16[256,512]{1,0:T(8,128)(2,1)S(1)}, u32[]{:S(2)}, u32[]{:S(2)}) collective-permute-start(bf16[256,512]{1,0:T(8,128)(2,1)S(1)} %shard_map.84.refs_8_.refs_1_), channel_id=1, source_target_pairs={{0,16},{8,24},{16,0},{24,8},{1,17},{9,25},{17,1},{25,9},{2,18},{10... | collective-permute-start | bytes 786440 | tf_op jit(solution)/shard_map/ppermute | solution.py:308
  62.0 1.8 %collective-permute-start.20 = (bf16[256,512]{1,0:T(8,128)(2,1)S(1)}, bf16[256,512]{1,0:T(8,128)(2,1)S(1)}, u32[]{:S(2)}, u32[]{:S(2)}) collective-permute-start(bf16[256,512]{1,0:T(8,128)(2,1)S(1)} %shard_map.85.refs_3_.refs_1_), channel_id=1, source_target_pairs={{0,16},{8,24},{16,0},{24,8},{1,17},{9,25},{17,1},{25,9},{2,18},{10... | collective-permute-start | bytes 786440 | tf_op jit(solution)/shard_map/ppermute | solution.py:308
  64.4 2.9 %collective-permute-done.17.refs_2_ = bf16[256,512]{1,0:T(8,128)(2,1)S(1)} collective-permute-done((bf16[256,512]{1,0:T(8,128)(2,1)S(1)}, bf16[256,512]{1,0:T(8,128)(2,1)S(1)}, u32[]{:S(2)}, u32[]{:S(2)}) %collective-permute-start.17) | collective-permute-done | bytes 262176 | tf_op jit(solution)/shard_map/ppermute | solution.py:308
  67.9 2.3 %collective-permute-done.20.refs_2_ = bf16[256,512]{1,0:T(8,128)(2,1)S(1)} collective-permute-done((bf16[256,512]{1,0:T(8,128)(2,1)S(1)}, bf16[256,512]{1,0:T(8,128)(2,1)S(1)}, u32[]{:S(2)}, u32[]{:S(2)}) %collective-permute-start.20) | collective-permute-done | bytes 262176 | tf_op jit(solution)/shard_map/ppermute | solution.py:308
  70.1 1.6 %shard_map.90 = bf16[2048,512]{1,0:T(8,128)(2,1)} custom-call(bf16[2048,512]{1,0:T(8,128)(2,1)S(1)} %get-tuple-element.39.refs_0_, bf16[2048,256]{1,0:T(8,128)(2,1)S(1)} %get-tuple-element.40.refs_1_, bf16[256,512]{1,0:T(8,128)(2,1)S(1)} %collective-permute-done.20.refs_2_), custom_call_target="tpu_custom_call" | custom-call | flops 4000000000 | bytes 1 | tf_op jit(solution)/shard_map/pallas_call | solution.py:45
  (47 shorter events, 10.6 us)
Async XLA Ops:
  0.0 5.2 %copy-start.3 = (s32[2048]{0:T(1024)S(1)}, s32[2048]{0:T(1024)}, u32[]{:S(2)}) copy-start(s32[2048]{0:T(1024)} %param.9) | copy-start | bytes 24580
  1.6 10.7 %collective-permute-start = (bf16[256,512]{1,0:T(8,128)(2,1)S(1)}, bf16[256,512]{1,0:T(8,128)(2,1)S(1)}, u32[]{:S(2)}, u32[]{:S(2)}) collective-permute-start(bf16[256,512]{1,0:T(8,128)(2,1)S(1)} %get-tuple-element.24.refs_2_), channel_id=1, source_target_pairs={{0,16},{8,24},{16,0},{24,8},{1,17},{9,25},{17,1},{25,9},{2,18},{10... | collective-permute-start | bytes 786440 | tf_op jit(solution)/shard_map/ppermute | solution.py:308
  5.2 1.6 %copy-start = (bf16[512,2048]{1,0:T(8,128)(2,1)S(1)}, bf16[512,2048]{1,0:T(8,128)(2,1)}, u32[]{:S(2)}) copy-start(bf16[512,2048]{1,0:T(8,128)(2,1)} %refs_0_.1) | copy-start | bytes 6291460
  5.3 3.0 %copy-start.1 = (s32[2048]{0:T(1024)S(1)}, s32[2048]{0:T(1024)}, u32[]{:S(2)}) copy-start(s32[2048]{0:T(1024)} %param.8) | copy-start | bytes 24580
  5.3 3.0 %copy-start.2 = (f32[2000]{0:T(1024)S(1)}, f32[2000]{0:T(1024)}, u32[]{:S(2)}) copy-start(f32[2000]{0:T(1024)} %param.11) | copy-start | bytes 24004
  5.3 3.0 %copy-start.4 = (f32[200]{0:T(256)S(1)}, f32[200]{0:T(256)}, u32[]{:S(2)}) copy-start(f32[200]{0:T(256)} %param.10) | copy-start | bytes 2404
  5.3 12.7 %collective-permute-start.1 = (bf16[256,512]{1,0:T(8,128)(2,1)S(1)}, bf16[256,512]{1,0:T(8,128)(2,1)S(1)}, u32[]{:S(2)}, u32[]{:S(2)}) collective-permute-start(bf16[256,512]{1,0:T(8,128)(2,1)S(1)} %get-tuple-element.26.refs_1_), channel_id=1, source_target_pairs={{0,16},{8,24},{16,0},{24,8},{1,17},{9,25},{17,1},{25,9},{2,18},{10... | collective-permute-start | bytes 786440 | tf_op jit(solution)/shard_map/ppermute | solution.py:308
  10.0 38.7 %collective-permute-start.11 = (f32[1,1024]{1,0:T(1,128)S(1)}, f32[1,1024]{1,0:T(1,128)S(1)}, u32[]{:S(2)}, u32[]{:S(2)}) collective-permute-start(f32[1,1024]{1,0:T(1,128)S(1)} %get-tuple-element.38), channel_id=1, source_target_pairs={{0,16},{8,24},{16,0},{24,8},{1,17},{9,25},{17,1},{25,9},{2,18},{10... | collective-permute-start | bytes 12296 | tf_op jit(solution)/shard_map/ppermute | solution.py:308
  12.9 13.1 %collective-permute-start.4 = (s16[1040,128]{1,0:T(8,128)(2,1)S(1)}, s16[1040,128]{1,0:T(8,128)(2,1)S(1)}, u32[]{:S(2)}, u32[]{:S(2)}) collective-permute-start(s16[1040,128]{1,0:T(8,128)(2,1)S(1)} %shard_map.68.refs_2_), channel_id=1, source_target_pairs={{0,2},{1,3},{2,4},{3,5},{4,6},{5,7},{6,0},{7,1},{8,10},{9,11},{10,... | collective-permute-start | bytes 798728 | tf_op jit(solution)/shard_map/ppermute | solution.py:317
  14.6 9.2 %collective-permute-start.5 = (bf16[256,512]{1,0:T(8,128)(2,1)S(1)}, bf16[256,512]{1,0:T(8,128)(2,1)S(1)}, u32[]{:S(2)}, u32[]{:S(2)}) collective-permute-start(bf16[256,512]{1,0:T(8,128)(2,1)S(1)} %get-tuple-element.31.refs_3_), channel_id=1, source_target_pairs={{0,16},{8,24},{16,0},{24,8},{1,17},{9,25},{17,1},{25,9},{2,18},{10... | collective-permute-start | bytes 786440 | tf_op jit(solution)/shard_map/ppermute | solution.py:308
  18.5 9.6 %collective-permute-start.3 = (s16[1040,128]{1,0:T(8,128)(2,1)S(1)}, s16[1040,128]{1,0:T(8,128)(2,1)S(1)}, u32[]{:S(2)}, u32[]{:S(2)}) collective-permute-start(s16[1040,128]{1,0:T(8,128)(2,1)S(1)} %shard_map.70.refs_2_), channel_id=1, source_target_pairs={{0,2},{1,3},{2,4},{3,5},{4,6},{5,7},{6,0},{7,1},{8,10},{9,11},{10,... | collective-permute-start | bytes 798728 | tf_op jit(solution)/shard_map/ppermute | solution.py:317
  20.2 9.3 %collective-permute-start.2 = (bf16[256,512]{1,0:T(8,128)(2,1)S(1)}, bf16[256,512]{1,0:T(8,128)(2,1)S(1)}, u32[]{:S(2)}, u32[]{:S(2)}) collective-permute-start(bf16[256,512]{1,0:T(8,128)(2,1)S(1)} %get-tuple-element.33.refs_3_), channel_id=1, source_target_pairs={{0,16},{8,24},{16,0},{24,8},{1,17},{9,25},{17,1},{25,9},{2,18},{10... | collective-permute-start | bytes 786440 | tf_op jit(solution)/shard_map/ppermute | solution.py:308
  24.3 12.7 %collective-permute-start.7 = (s16[1040,128]{1,0:T(8,128)(2,1)S(1)}, s16[1040,128]{1,0:T(8,128)(2,1)S(1)}, u32[]{:S(2)}, u32[]{:S(2)}) collective-permute-start(s16[1040,128]{1,0:T(8,128)(2,1)S(1)} %shard_map.72.refs_4_), channel_id=1, source_target_pairs={{0,2},{1,3},{2,4},{3,5},{4,6},{5,7},{6,0},{7,1},{8,10},{9,11},{10,... | collective-permute-start | bytes 798728 | tf_op jit(solution)/shard_map/ppermute | solution.py:317
  26.5 8.9 %collective-permute-start.8 = (s16[1040,128]{1,0:T(8,128)(2,1)S(1)}, s16[1040,128]{1,0:T(8,128)(2,1)S(1)}, u32[]{:S(2)}, u32[]{:S(2)}) collective-permute-start(s16[1040,128]{1,0:T(8,128)(2,1)S(1)} %shard_map.73.refs_4_), channel_id=1, source_target_pairs={{0,1},{1,0},{2,3},{3,2},{4,5},{5,4},{6,7},{7,6},{8,9},{9,8},{10,11... | collective-permute-start | bytes 798728 | tf_op jit(solution)/shard_map/ppermute | solution.py:312
  28.6 14.4 %collective-permute-start.13 = (s16[1040,128]{1,0:T(8,128)(2,1)S(1)}, s16[1040,128]{1,0:T(8,128)(2,1)S(1)}, u32[]{:S(2)}, u32[]{:S(2)}) collective-permute-start(s16[1040,128]{1,0:T(8,128)(2,1)S(1)} %shard_map.74.refs_3_), channel_id=1, source_target_pairs={{0,1},{1,0},{2,3},{3,2},{4,5},{5,4},{6,7},{7,6},{8,9},{9,8},{10,11... | collective-permute-start | bytes 798728 | tf_op jit(solution)/shard_map/ppermute | solution.py:312
  30.0 11.2 %collective-permute-start.6 = (s16[1040,128]{1,0:T(8,128)(2,1)S(1)}, s16[1040,128]{1,0:T(8,128)(2,1)S(1)}, u32[]{:S(2)}, u32[]{:S(2)}) collective-permute-start(s16[1040,128]{1,0:T(8,128)(2,1)S(1)} %shard_map.75.refs_4_), channel_id=1, source_target_pairs={{0,2},{1,3},{2,4},{3,5},{4,6},{5,7},{6,0},{7,1},{8,10},{9,11},{10,... | collective-permute-start | bytes 798728 | tf_op jit(solution)/shard_map/ppermute | solution.py:317
  35.9 12.7 %collective-permute-start.10 = (s16[1040,128]{1,0:T(8,128)(2,1)S(1)}, s16[1040,128]{1,0:T(8,128)(2,1)S(1)}, u32[]{:S(2)}, u32[]{:S(2)}) collective-permute-start(s16[1040,128]{1,0:T(8,128)(2,1)S(1)} %shard_map.76.refs_4_), channel_id=1, source_target_pairs={{0,2},{1,3},{2,4},{3,5},{4,6},{5,7},{6,0},{7,1},{8,10},{9,11},{10,... | collective-permute-start | bytes 798728 | tf_op jit(solution)/shard_map/ppermute | solution.py:317
  37.6 8.7 %collective-permute-start.12 = (s16[1040,128]{1,0:T(8,128)(2,1)S(1)}, s16[1040,128]{1,0:T(8,128)(2,1)S(1)}, u32[]{:S(2)}, u32[]{:S(2)}) collective-permute-start(s16[1040,128]{1,0:T(8,128)(2,1)S(1)} %shard_map.77.refs_4_), channel_id=1, source_target_pairs={{0,1},{1,0},{2,3},{3,2},{4,5},{5,4},{6,7},{7,6},{8,9},{9,8},{10,11... | collective-permute-start | bytes 798728 | tf_op jit(solution)/shard_map/ppermute | solution.py:312
  41.7 8.4 %collective-permute-start.9 = (s16[1040,128]{1,0:T(8,128)(2,1)S(1)}, s16[1040,128]{1,0:T(8,128)(2,1)S(1)}, u32[]{:S(2)}, u32[]{:S(2)}) collective-permute-start(s16[1040,128]{1,0:T(8,128)(2,1)S(1)} %shard_map.78.refs_4_), channel_id=1, source_target_pairs={{0,1},{1,0},{2,3},{3,2},{4,5},{5,4},{6,7},{7,6},{8,9},{9,8},{10,11... | collective-permute-start | bytes 798728 | tf_op jit(solution)/shard_map/ppermute | solution.py:312
  43.5 11.2 %collective-permute-start.16 = (s16[1040,128]{1,0:T(8,128)(2,1)S(1)}, s16[1040,128]{1,0:T(8,128)(2,1)S(1)}, u32[]{:S(2)}, u32[]{:S(2)}) collective-permute-start(s16[1040,128]{1,0:T(8,128)(2,1)S(1)} %shard_map.79.refs_4_), channel_id=1, source_target_pairs={{0,2},{1,3},{2,4},{3,5},{4,6},{5,7},{6,0},{7,1},{8,10},{9,11},{10,... | collective-permute-start | bytes 798728 | tf_op jit(solution)/shard_map/ppermute | solution.py:317
  46.9 11.8 %collective-permute-start.15 = (s16[1040,128]{1,0:T(8,128)(2,1)S(1)}, s16[1040,128]{1,0:T(8,128)(2,1)S(1)}, u32[]{:S(2)}, u32[]{:S(2)}) collective-permute-start(s16[1040,128]{1,0:T(8,128)(2,1)S(1)} %shard_map.80.refs_8_), channel_id=1, source_target_pairs={{0,2},{1,3},{2,4},{3,5},{4,6},{5,7},{6,0},{7,1},{8,10},{9,11},{10,... | collective-permute-start | bytes 798728 | tf_op jit(solution)/shard_map/ppermute | solution.py:317
  49.2 14.6 %collective-permute-start.19 = (bf16[256,512]{1,0:T(8,128)(2,1)S(1)}, bf16[256,512]{1,0:T(8,128)(2,1)S(1)}, u32[]{:S(2)}, u32[]{:S(2)}) collective-permute-start(bf16[256,512]{1,0:T(8,128)(2,1)S(1)} %shard_map.81.refs_4_.refs_1_), channel_id=1, source_target_pairs={{0,16},{8,24},{16,0},{24,8},{1,17},{9,25},{17,1},{25,9},{2,18},{10... | collective-permute-start | bytes 786440 | tf_op jit(solution)/shard_map/ppermute | solution.py:308
  50.7 10.8 %collective-permute-start.14 = (s16[1040,128]{1,0:T(8,128)(2,1)S(1)}, s16[1040,128]{1,0:T(8,128)(2,1)S(1)}, u32[]{:S(2)}, u32[]{:S(2)}) collective-permute-start(s16[1040,128]{1,0:T(8,128)(2,1)S(1)} %shard_map.82.refs_8_), channel_id=1, source_target_pairs={{0,2},{1,3},{2,4},{3,5},{4,6},{5,7},{6,0},{7,1},{8,10},{9,11},{10,... | collective-permute-start | bytes 798728 | tf_op jit(solution)/shard_map/ppermute | solution.py:317
  55.3 8.8 %collective-permute-start.18 = (bf16[256,512]{1,0:T(8,128)(2,1)S(1)}, bf16[256,512]{1,0:T(8,128)(2,1)S(1)}, u32[]{:S(2)}, u32[]{:S(2)}) collective-permute-start(bf16[256,512]{1,0:T(8,128)(2,1)S(1)} %shard_map.83.refs_8_.refs_1_), channel_id=1, source_target_pairs={{0,16},{8,24},{16,0},{24,8},{1,17},{9,25},{17,1},{25,9},{2,18},{10... | collective-permute-start | bytes 786440 | tf_op jit(solution)/shard_map/ppermute | solution.py:308
  59.2 8.2 %collective-permute-start.17 = (bf16[256,512]{1,0:T(8,128)(2,1)S(1)}, bf16[256,512]{1,0:T(8,128)(2,1)S(1)}, u32[]{:S(2)}, u32[]{:S(2)}) collective-permute-start(bf16[256,512]{1,0:T(8,128)(2,1)S(1)} %shard_map.84.refs_8_.refs_1_), channel_id=1, source_target_pairs={{0,16},{8,24},{16,0},{24,8},{1,17},{9,25},{17,1},{25,9},{2,18},{10... | collective-permute-start | bytes 786440 | tf_op jit(solution)/shard_map/ppermute | solution.py:308
  62.0 8.1 %collective-permute-start.20 = (bf16[256,512]{1,0:T(8,128)(2,1)S(1)}, bf16[256,512]{1,0:T(8,128)(2,1)S(1)}, u32[]{:S(2)}, u32[]{:S(2)}) collective-permute-start(bf16[256,512]{1,0:T(8,128)(2,1)S(1)} %shard_map.85.refs_3_.refs_1_), channel_id=1, source_target_pairs={{0,16},{8,24},{16,0},{24,8},{1,17},{9,25},{17,1},{25,9},{2,18},{10... | collective-permute-start | bytes 786440 | tf_op jit(solution)/shard_map/ppermute | solution.py:308

commit v10 on v9

--- a/solution.py
+++ b/solution.py
@@ -249,28 +249,31 @@
     rows, chunk = held.shape[0], other.shape[0]
     upper = upper_side()
     there = (1 - upper) * (rows // 2) + begin
+    size = chunk // 2
+
+    def leave(block):
+        part = pl.ds(block * size, size)
+        return pltpu.make_async_copy(held.at[part, :], out.at[part, :], arrivals.at[block])
+
     opposite = exchanged(other[...].astype(jnp.float32)).astype(jnp.bfloat16)
 
-    def leave(block):
-        part = pl.ds(block * chunk, chunk)
-        return pltpu.make_async_copy(held.at[part, :], out.at[part, :], arrivals.at[block])
-
     @pl.when(upper == 0)
     def _():
-        for block in range(rows // chunk):
-            part = pl.ds(block * chunk, chunk)
-            held[part, :] = jnp.where(there == block * chunk, opposite, earlier[part, :])
+        for block in range(rows // size):
+            part = pl.ds(block * size, size)
+            half = opposite[size * (block % 2) : size * (block % 2 + 1), :]
+            held[part, :] = jnp.where(there == block // 2 * chunk, half, earlier[part, :])
             leave(block).start()
 
     @pl.when(upper == 1)
     def _():
-        for block in range(rows // chunk):
-            part = pl.ds(block * chunk, chunk)
+        for block in range(rows // size):
+            part = pl.ds(block * size, size)
             found = jnp.dot(picks[part, :], opposite, preferred_element_type=jnp.float32)
             held[part, :] = (found + earlier[part, :].astype(jnp.float32)).astype(jnp.bfloat16)
             leave(block).start()
 
-    for block in range(rows // chunk):
+    for block in range(rows // size):
         leave(block).wait()
 
 
@@ -392,7 +395,7 @@
     kernel = functools.partial(place_own_kernel, begins[index])
     most, picks = call(kernel, [whole_shape, picks_shape], (partner[None, :], mine, *placed), last)
     room = pltpu.VMEM((rows, width), jnp.bfloat16)
-    arrivals = pltpu.SemaphoreType.DMA((rows // chunks[index],))
+    arrivals = pltpu.SemaphoreType.DMA((2 * rows // chunks[index],))
     kernel = functools.partial(place_other_kernel, begins[index])
     return call(kernel, whole_shape, (most, picks, theirs), out_spec=ANY, scratch=(room, arrivals))
 

time: 72.3 us -> 72.3 us (level)
  no operation moved by 1% of the time
where the time goes in v10:
time: 72.3 us; the launch traced here: 71.9 us
  starting transfers between devices  36 us (50%)
  waiting for transfers between devices  19.3 us (27%)
  Pallas kernels  16 us (22%)
    ppermute x9, starting transfers between devices, across_rows(): lax.ppermute(value, 'row', [(i, i ^ count // 2) for i in range(count)])  18.2 us
    pallas_call x27, Pallas kernels, call(): pl.pallas_call(kernel, out_shape=out_shape, in_specs=[in_spec or VMEM] *...  16 us
    ppermute x8, starting transfers between devices, two_along(): lax.ppermute(value, 'col', [(i, (i + 2) % count) for i in range(count)])  12.5 us
    ppermute x9, waiting for transfers between devices, across_rows(): lax.ppermute(value, 'row', [(i, i ^ count // 2) for i in range(count)])  7.04 us
    ppermute x4, waiting for transfers between devices, across_pair(): lax.ppermute(value, 'col', [(i, i ^ 1) for i in range(lax.axis_size('col'...  6.53 us
    ppermute x8, waiting for transfers between devices, two_along(): lax.ppermute(value, 'col', [(i, (i + 2) % count) for i in range(count)])  5.75 us
    ppermute x4, starting transfers between devices, across_pair(): lax.ppermute(value, 'col', [(i, i ^ 1) for i in range(lax.axis_size('col'...  5.33 us
  transfers between devices with their start and end apart: 21, of which 10 were waited for; matrix products, arithmetic and copies ran while one was open for 0% of the time, Pallas kernels for 18%

profile of v10, /device:TPU:0, one launch (start us, length us, event | category | flops | bytes accessed | tf_op | source)
XLA Modules:
  0.0 71.9 jit_solution(3866476374979975666)
XLA Ops:
  0.0 1.6 %shard_map.64 = (bf16[256,512]{1,0:T(8,128)(2,1)S(1)}, bf16[2048,512]{1,0:T(8,128)(2,1)S(1)}) custom-call(s32[1,2048]{1,0:T(1,128)} %bitcast.6, bf16[2048,512]{1,0:T(8,128)(2,1)} %refs_1_.1), custom_call_target="tpu_custom_call" | custom-call | flops 4000000000 | bytes 1 | tf_op jit(solution)/shard_map/pallas_call | solution.py:45
  1.6 3.6 %collective-permute-start = (bf16[256,512]{1,0:T(8,128)(2,1)S(1)}, bf16[256,512]{1,0:T(8,128)(2,1)S(1)}, u32[]{:S(2)}, u32[]{:S(2)}) collective-permute-start(bf16[256,512]{1,0:T(8,128)(2,1)S(1)} %get-tuple-element.24.refs_2_), channel_id=1, source_target_pairs={{0,16},{8,24},{16,0},{24,8},{1,17},{9,25},{17,1},{25,9},{2,18},{10... | collective-permute-start | bytes 786440 | tf_op jit(solution)/shard_map/ppermute | solution.py:311
  5.3 1.3 %collective-permute-start.1 = (bf16[256,512]{1,0:T(8,128)(2,1)S(1)}, bf16[256,512]{1,0:T(8,128)(2,1)S(1)}, u32[]{:S(2)}, u32[]{:S(2)}) collective-permute-start(bf16[256,512]{1,0:T(8,128)(2,1)S(1)} %get-tuple-element.26.refs_1_), channel_id=1, source_target_pairs={{0,16},{8,24},{16,0},{24,8},{1,17},{9,25},{17,1},{25,9},{2,18},{10... | collective-permute-start | bytes 786440 | tf_op jit(solution)/shard_map/ppermute | solution.py:311
  6.8 1.5 %shard_map.66 = (bf16[1024,512]{1,0:T(8,128)(2,1)S(1)}, bf16[1024,512]{1,0:T(8,128)(2,1)S(1)}, bf16[1024,512]{1,0:T(8,128)(2,1)S(1)}, bf16[1024,512]{1,0:T(8,128)(2,1)S(1)}) custom-call(bf16[512,2048]{1,0:T(8,128)(2,1)S(1)} %copy-done, bf16[256,512]{1,0:T(8,128)(2,1)S(1)} %get-tuple-element.26.refs_1_), custom_call_target="tpu_custom_call" | custom-call | flops 4000000000 | bytes 1 | tf_op jit(solution)/shard_map/pallas_call | solution.py:45
  8.3 1.6 %shard_map.67 = (f32[1,1024]{1,0:T(1,128)S(1)}, f32[1,1024]{1,0:T(1,128)S(1)}, f32[1,512]{1,0:T(1,128)S(1)}) custom-call(s32[1,2048]{1,0:T(1,128)S(1)} %bitcast.4, f32[1,200]{1,0:T(1,128)S(1)} %bitcast.14, f32[1,2000]{1,0:T(1,128)S(1)} %bitcast.5, bf16[1024,512]{1,0:T(8,128)(2,1)S(1)} %get-tuple-element.28.refs_3_.refs_2_), custom_call_target="tpu_custom_call" | custom-call | flops 4000000000 | bytes 1 | tf_op jit(solution)/shard_map/pallas_call | solution.py:45
  10.0 0.7 collective-permute-start.11
  10.6 1.8 %collective-permute-done.refs_1_ = bf16[256,512]{1,0:T(8,128)(2,1)S(1)} collective-permute-done((bf16[256,512]{1,0:T(8,128)(2,1)S(1)}, bf16[256,512]{1,0:T(8,128)(2,1)S(1)}, u32[]{:S(2)}, u32[]{:S(2)}) %collective-permute-start) | collective-permute-done | bytes 262176 | tf_op jit(solution)/shard_map/ppermute | solution.py:311
  12.9 1.6 %collective-permute-start.4 = (s16[1040,128]{1,0:T(8,128)(2,1)S(1)}, s16[1040,128]{1,0:T(8,128)(2,1)S(1)}, u32[]{:S(2)}, u32[]{:S(2)}) collective-permute-start(s16[1040,128]{1,0:T(8,128)(2,1)S(1)} %shard_map.68.refs_2_), channel_id=1, source_target_pairs={{0,2},{1,3},{2,4},{3,5},{4,6},{5,7},{6,0},{7,1},{8,10},{9,11},{10,... | collective-permute-start | bytes 798728 | tf_op jit(solution)/shard_map/ppermute | solution.py:320
  14.6 3.3 %collective-permute-start.5 = (bf16[256,512]{1,0:T(8,128)(2,1)S(1)}, bf16[256,512]{1,0:T(8,128)(2,1)S(1)}, u32[]{:S(2)}, u32[]{:S(2)}) collective-permute-start(bf16[256,512]{1,0:T(8,128)(2,1)S(1)} %get-tuple-element.31.refs_3_), channel_id=1, source_target_pairs={{0,16},{8,24},{16,0},{24,8},{1,17},{9,25},{17,1},{25,9},{2,18},{10... | collective-permute-start | bytes 786440 | tf_op jit(solution)/shard_map/ppermute | solution.py:311
  18.5 1.6 %collective-permute-start.3 = (s16[1040,128]{1,0:T(8,128)(2,1)S(1)}, s16[1040,128]{1,0:T(8,128)(2,1)S(1)}, u32[]{:S(2)}, u32[]{:S(2)}) collective-permute-start(s16[1040,128]{1,0:T(8,128)(2,1)S(1)} %shard_map.70.refs_2_), channel_id=1, source_target_pairs={{0,2},{1,3},{2,4},{3,5},{4,6},{5,7},{6,0},{7,1},{8,10},{9,11},{10,... | collective-permute-start | bytes 798728 | tf_op jit(solution)/shard_map/ppermute | solution.py:320
  20.2 3.6 %collective-permute-start.2 = (bf16[256,512]{1,0:T(8,128)(2,1)S(1)}, bf16[256,512]{1,0:T(8,128)(2,1)S(1)}, u32[]{:S(2)}, u32[]{:S(2)}) collective-permute-start(bf16[256,512]{1,0:T(8,128)(2,1)S(1)} %get-tuple-element.33.refs_3_), channel_id=1, source_target_pairs={{0,16},{8,24},{16,0},{24,8},{1,17},{9,25},{17,1},{25,9},{2,18},{10... | collective-permute-start | bytes 786440 | tf_op jit(solution)/shard_map/ppermute | solution.py:311
  24.3 1.6 %collective-permute-start.7 = (s16[1040,128]{1,0:T(8,128)(2,1)S(1)}, s16[1040,128]{1,0:T(8,128)(2,1)S(1)}, u32[]{:S(2)}, u32[]{:S(2)}) collective-permute-start(s16[1040,128]{1,0:T(8,128)(2,1)S(1)} %shard_map.72.refs_4_), channel_id=1, source_target_pairs={{0,2},{1,3},{2,4},{3,5},{4,6},{5,7},{6,0},{7,1},{8,10},{9,11},{10,... | collective-permute-start | bytes 798728 | tf_op jit(solution)/shard_map/ppermute | solution.py:320
  26.5 1.6 %collective-permute-start.8 = (s16[1040,128]{1,0:T(8,128)(2,1)S(1)}, s16[1040,128]{1,0:T(8,128)(2,1)S(1)}, u32[]{:S(2)}, u32[]{:S(2)}) collective-permute-start(s16[1040,128]{1,0:T(8,128)(2,1)S(1)} %shard_map.73.refs_4_), channel_id=1, source_target_pairs={{0,1},{1,0},{2,3},{3,2},{4,5},{5,4},{6,7},{7,6},{8,9},{9,8},{10,11... | collective-permute-start | bytes 798728 | tf_op jit(solution)/shard_map/ppermute | solution.py:315
  28.6 0.9 %collective-permute-start.13 = (s16[1040,128]{1,0:T(8,128)(2,1)S(1)}, s16[1040,128]{1,0:T(8,128)(2,1)S(1)}, u32[]{:S(2)}, u32[]{:S(2)}) collective-permute-start(s16[1040,128]{1,0:T(8,128)(2,1)S(1)} %shard_map.74.refs_3_), channel_id=1, source_target_pairs={{0,1},{1,0},{2,3},{3,2},{4,5},{5,4},{6,7},{7,6},{8,9},{9,8},{10,11... | collective-permute-start | bytes 798728 | tf_op jit(solution)/shard_map/ppermute | solution.py:315
  30.0 1.6 %collective-permute-start.6 = (s16[1040,128]{1,0:T(8,128)(2,1)S(1)}, s16[1040,128]{1,0:T(8,128)(2,1)S(1)}, u32[]{:S(2)}, u32[]{:S(2)}) collective-permute-start(s16[1040,128]{1,0:T(8,128)(2,1)S(1)} %shard_map.75.refs_4_), channel_id=1, source_target_pairs={{0,2},{1,3},{2,4},{3,5},{4,6},{5,7},{6,0},{7,1},{8,10},{9,11},{10,... | collective-permute-start | bytes 798728 | tf_op jit(solution)/shard_map/ppermute | solution.py:320
  31.6 3.8 %collective-permute-done.8.refs_3_ = s16[1040,128]{1,0:T(8,128)(2,1)S(1)} collective-permute-done((s16[1040,128]{1,0:T(8,128)(2,1)S(1)}, s16[1040,128]{1,0:T(8,128)(2,1)S(1)}, u32[]{:S(2)}, u32[]{:S(2)}) %collective-permute-start.8) | collective-permute-done | bytes 266272 | tf_op jit(solution)/shard_map/ppermute | solution.py:315
  35.9 1.1 %collective-permute-start.10 = (s16[1040,128]{1,0:T(8,128)(2,1)S(1)}, s16[1040,128]{1,0:T(8,128)(2,1)S(1)}, u32[]{:S(2)}, u32[]{:S(2)}) collective-permute-start(s16[1040,128]{1,0:T(8,128)(2,1)S(1)} %shard_map.76.refs_4_), channel_id=1, source_target_pairs={{0,2},{1,3},{2,4},{3,5},{4,6},{5,7},{6,0},{7,1},{8,10},{9,11},{10,... | collective-permute-start | bytes 798728 | tf_op jit(solution)/shard_map/ppermute | solution.py:320
  37.6 1.6 %collective-permute-start.12 = (s16[1040,128]{1,0:T(8,128)(2,1)S(1)}, s16[1040,128]{1,0:T(8,128)(2,1)S(1)}, u32[]{:S(2)}, u32[]{:S(2)}) collective-permute-start(s16[1040,128]{1,0:T(8,128)(2,1)S(1)} %shard_map.77.refs_4_), channel_id=1, source_target_pairs={{0,1},{1,0},{2,3},{3,2},{4,5},{5,4},{6,7},{7,6},{8,9},{9,8},{10,11... | collective-permute-start | bytes 798728 | tf_op jit(solution)/shard_map/ppermute | solution.py:315
  39.2 2.0 %collective-permute-done.6.refs_3_ = s16[1040,128]{1,0:T(8,128)(2,1)S(1)} collective-permute-done((s16[1040,128]{1,0:T(8,128)(2,1)S(1)}, s16[1040,128]{1,0:T(8,128)(2,1)S(1)}, u32[]{:S(2)}, u32[]{:S(2)}) %collective-permute-start.6) | collective-permute-done | bytes 266272 | tf_op jit(solution)/shard_map/ppermute | solution.py:320
  41.7 1.3 %collective-permute-start.9 = (s16[1040,128]{1,0:T(8,128)(2,1)S(1)}, s16[1040,128]{1,0:T(8,128)(2,1)S(1)}, u32[]{:S(2)}, u32[]{:S(2)}) collective-permute-start(s16[1040,128]{1,0:T(8,128)(2,1)S(1)} %shard_map.78.refs_4_), channel_id=1, source_target_pairs={{0,1},{1,0},{2,3},{3,2},{4,5},{5,4},{6,7},{7,6},{8,9},{9,8},{10,11... | collective-permute-start | bytes 798728 | tf_op jit(solution)/shard_map/ppermute | solution.py:315
  43.6 2.7 %collective-permute-done.12.refs_3_ = s16[1040,128]{1,0:T(8,128)(2,1)S(1)} collective-permute-done((s16[1040,128]{1,0:T(8,128)(2,1)S(1)}, s16[1040,128]{1,0:T(8,128)(2,1)S(1)}, u32[]{:S(2)}, u32[]{:S(2)}) %collective-permute-start.12) | collective-permute-done | bytes 266272 | tf_op jit(solution)/shard_map/ppermute | solution.py:315
  46.9 1.8 %collective-permute-start.15 = (s16[1040,128]{1,0:T(8,128)(2,1)S(1)}, s16[1040,128]{1,0:T(8,128)(2,1)S(1)}, u32[]{:S(2)}, u32[]{:S(2)}) collective-permute-start(s16[1040,128]{1,0:T(8,128)(2,1)S(1)} %shard_map.80.refs_8_), channel_id=1, source_target_pairs={{0,2},{1,3},{2,4},{3,5},{4,6},{5,7},{6,0},{7,1},{8,10},{9,11},{10,... | collective-permute-start | bytes 798728 | tf_op jit(solution)/shard_map/ppermute | solution.py:320
  49.2 0.9 %collective-permute-start.19 = (bf16[256,512]{1,0:T(8,128)(2,1)S(1)}, bf16[256,512]{1,0:T(8,128)(2,1)S(1)}, u32[]{:S(2)}, u32[]{:S(2)}) collective-permute-start(bf16[256,512]{1,0:T(8,128)(2,1)S(1)} %shard_map.81.refs_4_.refs_1_), channel_id=1, source_target_pairs={{0,16},{8,24},{16,0},{24,8},{1,17},{9,25},{17,1},{25,9},{2,18},{10... | collective-permute-start | bytes 786440 | tf_op jit(solution)/shard_map/ppermute | solution.py:311
  50.7 3.0 %collective-permute-start.14 = (s16[1040,128]{1,0:T(8,128)(2,1)S(1)}, s16[1040,128]{1,0:T(8,128)(2,1)S(1)}, u32[]{:S(2)}, u32[]{:S(2)}) collective-permute-start(s16[1040,128]{1,0:T(8,128)(2,1)S(1)} %shard_map.82.refs_8_), channel_id=1, source_target_pairs={{0,2},{1,3},{2,4},{3,5},{4,6},{5,7},{6,0},{7,1},{8,10},{9,11},{10,... | collective-permute-start | bytes 798728 | tf_op jit(solution)/shard_map/ppermute | solution.py:320
  53.7 1.0 %collective-permute-done.16.refs_4_ = s16[1040,128]{1,0:T(8,128)(2,1)S(1)} collective-permute-done((s16[1040,128]{1,0:T(8,128)(2,1)S(1)}, s16[1040,128]{1,0:T(8,128)(2,1)S(1)}, u32[]{:S(2)}, u32[]{:S(2)}) %collective-permute-start.16) | collective-permute-done | bytes 266272 | tf_op jit(solution)/shard_map/ppermute | solution.py:320
  55.3 1.2 %collective-permute-start.18 = (bf16[256,512]{1,0:T(8,128)(2,1)S(1)}, bf16[256,512]{1,0:T(8,128)(2,1)S(1)}, u32[]{:S(2)}, u32[]{:S(2)}) collective-permute-start(bf16[256,512]{1,0:T(8,128)(2,1)S(1)} %shard_map.83.refs_8_.refs_1_), channel_id=1, source_target_pairs={{0,16},{8,24},{16,0},{24,8},{1,17},{9,25},{17,1},{25,9},{2,18},{10... | collective-permute-start | bytes 786440 | tf_op jit(solution)/shard_map/ppermute | solution.py:311
  56.5 2.1 %collective-permute-done.15.refs_4_ = s16[1040,128]{1,0:T(8,128)(2,1)S(1)} collective-permute-done((s16[1040,128]{1,0:T(8,128)(2,1)S(1)}, s16[1040,128]{1,0:T(8,128)(2,1)S(1)}, u32[]{:S(2)}, u32[]{:S(2)}) %collective-permute-start.15) | collective-permute-done | bytes 266272 | tf_op jit(solution)/shard_map/ppermute | solution.py:320
  59.2 1.8 %collective-permute-start.17 = (bf16[256,512]{1,0:T(8,128)(2,1)S(1)}, bf16[256,512]{1,0:T(8,128)(2,1)S(1)}, u32[]{:S(2)}, u32[]{:S(2)}) collective-permute-start(bf16[256,512]{1,0:T(8,128)(2,1)S(1)} %shard_map.84.refs_8_.refs_1_), channel_id=1, source_target_pairs={{0,16},{8,24},{16,0},{24,8},{1,17},{9,25},{17,1},{25,9},{2,18},{10... | collective-permute-start | bytes 786440 | tf_op jit(solution)/shard_map/ppermute | solution.py:311
  62.0 1.8 %collective-permute-start.20 = (bf16[256,512]{1,0:T(8,128)(2,1)S(1)}, bf16[256,512]{1,0:T(8,128)(2,1)S(1)}, u32[]{:S(2)}, u32[]{:S(2)}) collective-permute-start(bf16[256,512]{1,0:T(8,128)(2,1)S(1)} %shard_map.85.refs_3_.refs_1_), channel_id=1, source_target_pairs={{0,16},{8,24},{16,0},{24,8},{1,17},{9,25},{17,1},{25,9},{2,18},{10... | collective-permute-start | bytes 786440 | tf_op jit(solution)/shard_map/ppermute | solution.py:311
  64.4 2.9 %collective-permute-done.17.refs_2_ = bf16[256,512]{1,0:T(8,128)(2,1)S(1)} collective-permute-done((bf16[256,512]{1,0:T(8,128)(2,1)S(1)}, bf16[256,512]{1,0:T(8,128)(2,1)S(1)}, u32[]{:S(2)}, u32[]{:S(2)}) %collective-permute-start.17) | collective-permute-done | bytes 262176 | tf_op jit(solution)/shard_map/ppermute | solution.py:311
  67.9 2.3 %collective-permute-done.20.refs_2_ = bf16[256,512]{1,0:T(8,128)(2,1)S(1)} collective-permute-done((bf16[256,512]{1,0:T(8,128)(2,1)S(1)}, bf16[256,512]{1,0:T(8,128)(2,1)S(1)}, u32[]{:S(2)}, u32[]{:S(2)}) %collective-permute-start.20) | collective-permute-done | bytes 262176 | tf_op jit(solution)/shard_map/ppermute | solution.py:311
  70.1 1.7 %shard_map.90 = bf16[2048,512]{1,0:T(8,128)(2,1)} custom-call(bf16[2048,512]{1,0:T(8,128)(2,1)S(1)} %get-tuple-element.39.refs_0_, bf16[2048,256]{1,0:T(8,128)(2,1)S(1)} %get-tuple-element.40.refs_1_, bf16[256,512]{1,0:T(8,128)(2,1)S(1)} %collective-permute-done.20.refs_2_), custom_call_target="tpu_custom_call" | custom-call | flops 4000000000 | bytes 1 | tf_op jit(solution)/shard_map/pallas_call | solution.py:45
  (47 shorter events, 10.6 us)
Async XLA Ops:
  0.0 5.2 %copy-start.3 = (s32[2048]{0:T(1024)S(1)}, s32[2048]{0:T(1024)}, u32[]{:S(2)}) copy-start(s32[2048]{0:T(1024)} %param.9) | copy-start | bytes 24580
  1.6 10.7 %collective-permute-start = (bf16[256,512]{1,0:T(8,128)(2,1)S(1)}, bf16[256,512]{1,0:T(8,128)(2,1)S(1)}, u32[]{:S(2)}, u32[]{:S(2)}) collective-permute-start(bf16[256,512]{1,0:T(8,128)(2,1)S(1)} %get-tuple-element.24.refs_2_), channel_id=1, source_target_pairs={{0,16},{8,24},{16,0},{24,8},{1,17},{9,25},{17,1},{25,9},{2,18},{10... | collective-permute-start | bytes 786440 | tf_op jit(solution)/shard_map/ppermute | solution.py:311
  5.2 1.6 %copy-start = (bf16[512,2048]{1,0:T(8,128)(2,1)S(1)}, bf16[512,2048]{1,0:T(8,128)(2,1)}, u32[]{:S(2)}) copy-start(bf16[512,2048]{1,0:T(8,128)(2,1)} %refs_0_.1) | copy-start | bytes 6291460
  5.3 3.0 %copy-start.1 = (s32[2048]{0:T(1024)S(1)}, s32[2048]{0:T(1024)}, u32[]{:S(2)}) copy-start(s32[2048]{0:T(1024)} %param.8) | copy-start | bytes 24580
  5.3 3.0 %copy-start.2 = (f32[2000]{0:T(1024)S(1)}, f32[2000]{0:T(1024)}, u32[]{:S(2)}) copy-start(f32[2000]{0:T(1024)} %param.11) | copy-start | bytes 24004
  5.3 3.0 %copy-start.4 = (f32[200]{0:T(256)S(1)}, f32[200]{0:T(256)}, u32[]{:S(2)}) copy-start(f32[200]{0:T(256)} %param.10) | copy-start | bytes 2404
  5.3 12.7 %collective-permute-start.1 = (bf16[256,512]{1,0:T(8,128)(2,1)S(1)}, bf16[256,512]{1,0:T(8,128)(2,1)S(1)}, u32[]{:S(2)}, u32[]{:S(2)}) collective-permute-start(bf16[256,512]{1,0:T(8,128)(2,1)S(1)} %get-tuple-element.26.refs_1_), channel_id=1, source_target_pairs={{0,16},{8,24},{16,0},{24,8},{1,17},{9,25},{17,1},{25,9},{2,18},{10... | collective-permute-start | bytes 786440 | tf_op jit(solution)/shard_map/ppermute | solution.py:311
  10.0 38.7 %collective-permute-start.11 = (f32[1,1024]{1,0:T(1,128)S(1)}, f32[1,1024]{1,0:T(1,128)S(1)}, u32[]{:S(2)}, u32[]{:S(2)}) collective-permute-start(f32[1,1024]{1,0:T(1,128)S(1)} %get-tuple-element.38), channel_id=1, source_target_pairs={{0,16},{8,24},{16,0},{24,8},{1,17},{9,25},{17,1},{25,9},{2,18},{10... | collective-permute-start | bytes 12296 | tf_op jit(solution)/shard_map/ppermute | solution.py:311
  12.9 13.1 %collective-permute-start.4 = (s16[1040,128]{1,0:T(8,128)(2,1)S(1)}, s16[1040,128]{1,0:T(8,128)(2,1)S(1)}, u32[]{:S(2)}, u32[]{:S(2)}) collective-permute-start(s16[1040,128]{1,0:T(8,128)(2,1)S(1)} %shard_map.68.refs_2_), channel_id=1, source_target_pairs={{0,2},{1,3},{2,4},{3,5},{4,6},{5,7},{6,0},{7,1},{8,10},{9,11},{10,... | collective-permute-start | bytes 798728 | tf_op jit(solution)/shard_map/ppermute | solution.py:320
  14.6 9.2 %collective-permute-start.5 = (bf16[256,512]{1,0:T(8,128)(2,1)S(1)}, bf16[256,512]{1,0:T(8,128)(2,1)S(1)}, u32[]{:S(2)}, u32[]{:S(2)}) collective-permute-start(bf16[256,512]{1,0:T(8,128)(2,1)S(1)} %get-tuple-element.31.refs_3_), channel_id=1, source_target_pairs={{0,16},{8,24},{16,0},{24,8},{1,17},{9,25},{17,1},{25,9},{2,18},{10... | collective-permute-start | bytes 786440 | tf_op jit(solution)/shard_map/ppermute | solution.py:311
  18.5 9.6 %collective-permute-start.3 = (s16[1040,128]{1,0:T(8,128)(2,1)S(1)}, s16[1040,128]{1,0:T(8,128)(2,1)S(1)}, u32[]{:S(2)}, u32[]{:S(2)}) collective-permute-start(s16[1040,128]{1,0:T(8,128)(2,1)S(1)} %shard_map.70.refs_2_), channel_id=1, source_target_pairs={{0,2},{1,3},{2,4},{3,5},{4,6},{5,7},{6,0},{7,1},{8,10},{9,11},{10,... | collective-permute-start | bytes 798728 | tf_op jit(solution)/shard_map/ppermute | solution.py:320
  20.2 9.3 %collective-permute-start.2 = (bf16[256,512]{1,0:T(8,128)(2,1)S(1)}, bf16[256,512]{1,0:T(8,128)(2,1)S(1)}, u32[]{:S(2)}, u32[]{:S(2)}) collective-permute-start(bf16[256,512]{1,0:T(8,128)(2,1)S(1)} %get-tuple-element.33.refs_3_), channel_id=1, source_target_pairs={{0,16},{8,24},{16,0},{24,8},{1,17},{9,25},{17,1},{25,9},{2,18},{10... | collective-permute-start | bytes 786440 | tf_op jit(solution)/shard_map/ppermute | solution.py:311
  24.3 12.7 %collective-permute-start.7 = (s16[1040,128]{1,0:T(8,128)(2,1)S(1)}, s16[1040,128]{1,0:T(8,128)(2,1)S(1)}, u32[]{:S(2)}, u32[]{:S(2)}) collective-permute-start(s16[1040,128]{1,0:T(8,128)(2,1)S(1)} %shard_map.72.refs_4_), channel_id=1, source_target_pairs={{0,2},{1,3},{2,4},{3,5},{4,6},{5,7},{6,0},{7,1},{8,10},{9,11},{10,... | collective-permute-start | bytes 798728 | tf_op jit(solution)/shard_map/ppermute | solution.py:320
  26.5 8.9 %collective-permute-start.8 = (s16[1040,128]{1,0:T(8,128)(2,1)S(1)}, s16[1040,128]{1,0:T(8,128)(2,1)S(1)}, u32[]{:S(2)}, u32[]{:S(2)}) collective-permute-start(s16[1040,128]{1,0:T(8,128)(2,1)S(1)} %shard_map.73.refs_4_), channel_id=1, source_target_pairs={{0,1},{1,0},{2,3},{3,2},{4,5},{5,4},{6,7},{7,6},{8,9},{9,8},{10,11... | collective-permute-start | bytes 798728 | tf_op jit(solution)/shard_map/ppermute | solution.py:315
  28.6 14.4 %collective-permute-start.13 = (s16[1040,128]{1,0:T(8,128)(2,1)S(1)}, s16[1040,128]{1,0:T(8,128)(2,1)S(1)}, u32[]{:S(2)}, u32[]{:S(2)}) collective-permute-start(s16[1040,128]{1,0:T(8,128)(2,1)S(1)} %shard_map.74.refs_3_), channel_id=1, source_target_pairs={{0,1},{1,0},{2,3},{3,2},{4,5},{5,4},{6,7},{7,6},{8,9},{9,8},{10,11... | collective-permute-start | bytes 798728 | tf_op jit(solution)/shard_map/ppermute | solution.py:315
  30.0 11.2 %collective-permute-start.6 = (s16[1040,128]{1,0:T(8,128)(2,1)S(1)}, s16[1040,128]{1,0:T(8,128)(2,1)S(1)}, u32[]{:S(2)}, u32[]{:S(2)}) collective-permute-start(s16[1040,128]{1,0:T(8,128)(2,1)S(1)} %shard_map.75.refs_4_), channel_id=1, source_target_pairs={{0,2},{1,3},{2,4},{3,5},{4,6},{5,7},{6,0},{7,1},{8,10},{9,11},{10,... | collective-permute-start | bytes 798728 | tf_op jit(solution)/shard_map/ppermute | solution.py:320
  35.9 12.7 %collective-permute-start.10 = (s16[1040,128]{1,0:T(8,128)(2,1)S(1)}, s16[1040,128]{1,0:T(8,128)(2,1)S(1)}, u32[]{:S(2)}, u32[]{:S(2)}) collective-permute-start(s16[1040,128]{1,0:T(8,128)(2,1)S(1)} %shard_map.76.refs_4_), channel_id=1, source_target_pairs={{0,2},{1,3},{2,4},{3,5},{4,6},{5,7},{6,0},{7,1},{8,10},{9,11},{10,... | collective-permute-start | bytes 798728 | tf_op jit(solution)/shard_map/ppermute | solution.py:320
  37.6 8.7 %collective-permute-start.12 = (s16[1040,128]{1,0:T(8,128)(2,1)S(1)}, s16[1040,128]{1,0:T(8,128)(2,1)S(1)}, u32[]{:S(2)}, u32[]{:S(2)}) collective-permute-start(s16[1040,128]{1,0:T(8,128)(2,1)S(1)} %shard_map.77.refs_4_), channel_id=1, source_target_pairs={{0,1},{1,0},{2,3},{3,2},{4,5},{5,4},{6,7},{7,6},{8,9},{9,8},{10,11... | collective-permute-start | bytes 798728 | tf_op jit(solution)/shard_map/ppermute | solution.py:315
  41.7 8.4 %collective-permute-start.9 = (s16[1040,128]{1,0:T(8,128)(2,1)S(1)}, s16[1040,128]{1,0:T(8,128)(2,1)S(1)}, u32[]{:S(2)}, u32[]{:S(2)}) collective-permute-start(s16[1040,128]{1,0:T(8,128)(2,1)S(1)} %shard_map.78.refs_4_), channel_id=1, source_target_pairs={{0,1},{1,0},{2,3},{3,2},{4,5},{5,4},{6,7},{7,6},{8,9},{9,8},{10,11... | collective-permute-start | bytes 798728 | tf_op jit(solution)/shard_map/ppermute | solution.py:315
  43.5 11.2 %collective-permute-start.16 = (s16[1040,128]{1,0:T(8,128)(2,1)S(1)}, s16[1040,128]{1,0:T(8,128)(2,1)S(1)}, u32[]{:S(2)}, u32[]{:S(2)}) collective-permute-start(s16[1040,128]{1,0:T(8,128)(2,1)S(1)} %shard_map.79.refs_4_), channel_id=1, source_target_pairs={{0,2},{1,3},{2,4},{3,5},{4,6},{5,7},{6,0},{7,1},{8,10},{9,11},{10,... | collective-permute-start | bytes 798728 | tf_op jit(solution)/shard_map/ppermute | solution.py:320
  46.9 11.8 %collective-permute-start.15 = (s16[1040,128]{1,0:T(8,128)(2,1)S(1)}, s16[1040,128]{1,0:T(8,128)(2,1)S(1)}, u32[]{:S(2)}, u32[]{:S(2)}) collective-permute-start(s16[1040,128]{1,0:T(8,128)(2,1)S(1)} %shard_map.80.refs_8_), channel_id=1, source_target_pairs={{0,2},{1,3},{2,4},{3,5},{4,6},{5,7},{6,0},{7,1},{8,10},{9,11},{10,... | collective-permute-start | bytes 798728 | tf_op jit(solution)/shard_map/ppermute | solution.py:320
  49.2 14.6 %collective-permute-start.19 = (bf16[256,512]{1,0:T(8,128)(2,1)S(1)}, bf16[256,512]{1,0:T(8,128)(2,1)S(1)}, u32[]{:S(2)}, u32[]{:S(2)}) collective-permute-start(bf16[256,512]{1,0:T(8,128)(2,1)S(1)} %shard_map.81.refs_4_.refs_1_), channel_id=1, source_target_pairs={{0,16},{8,24},{16,0},{24,8},{1,17},{9,25},{17,1},{25,9},{2,18},{10... | collective-permute-start | bytes 786440 | tf_op jit(solution)/shard_map/ppermute | solution.py:311
  50.7 10.8 %collective-permute-start.14 = (s16[1040,128]{1,0:T(8,128)(2,1)S(1)}, s16[1040,128]{1,0:T(8,128)(2,1)S(1)}, u32[]{:S(2)}, u32[]{:S(2)}) collective-permute-start(s16[1040,128]{1,0:T(8,128)(2,1)S(1)} %shard_map.82.refs_8_), channel_id=1, source_target_pairs={{0,2},{1,3},{2,4},{3,5},{4,6},{5,7},{6,0},{7,1},{8,10},{9,11},{10,... | collective-permute-start | bytes 798728 | tf_op jit(solution)/shard_map/ppermute | solution.py:320
  55.3 8.8 %collective-permute-start.18 = (bf16[256,512]{1,0:T(8,128)(2,1)S(1)}, bf16[256,512]{1,0:T(8,128)(2,1)S(1)}, u32[]{:S(2)}, u32[]{:S(2)}) collective-permute-start(bf16[256,512]{1,0:T(8,128)(2,1)S(1)} %shard_map.83.refs_8_.refs_1_), channel_id=1, source_target_pairs={{0,16},{8,24},{16,0},{24,8},{1,17},{9,25},{17,1},{25,9},{2,18},{10... | collective-permute-start | bytes 786440 | tf_op jit(solution)/shard_map/ppermute | solution.py:311
  59.2 8.2 %collective-permute-start.17 = (bf16[256,512]{1,0:T(8,128)(2,1)S(1)}, bf16[256,512]{1,0:T(8,128)(2,1)S(1)}, u32[]{:S(2)}, u32[]{:S(2)}) collective-permute-start(bf16[256,512]{1,0:T(8,128)(2,1)S(1)} %shard_map.84.refs_8_.refs_1_), channel_id=1, source_target_pairs={{0,16},{8,24},{16,0},{24,8},{1,17},{9,25},{17,1},{25,9},{2,18},{10... | collective-permute-start | bytes 786440 | tf_op jit(solution)/shard_map/ppermute | solution.py:311
  62.0 8.1 %collective-permute-start.20 = (bf16[256,512]{1,0:T(8,128)(2,1)S(1)}, bf16[256,512]{1,0:T(8,128)(2,1)S(1)}, u32[]{:S(2)}, u32[]{:S(2)}) collective-permute-start(bf16[256,512]{1,0:T(8,128)(2,1)S(1)} %shard_map.85.refs_3_.refs_1_), channel_id=1, source_target_pairs={{0,16},{8,24},{16,0},{24,8},{1,17},{9,25},{17,1},{25,9},{2,18},{10... | collective-permute-start | bytes 786440 | tf_op jit(solution)/shard_map/ppermute | solution.py:311

commit v11 on v10

--- a/solution.py
+++ b/solution.py
@@ -22,7 +22,7 @@
     (("align", 1), ("factor", 0), ("energy", 0), ("first", 0), ("align", 2), ("first", 1))
     + (("align", 3), ("first", 2), ("second", 0), ("second", 1), ("first", 3), ("third", 0))
     + (("second", 2), ("second", 3), ("third", 1), ("third", 2), ("last", 0), ("third", 3))
-    + (("last", 1), ("last", 2), ("last", 3), ("place", 0), ("place", 1), ("place", 2))
+    + (("last", 1), ("last", 2), ("place", 0), ("last", 3), ("place", 1), ("place", 2))
 )
 ALIGNED = (
     (),

time: 72.3 us -> 72.3 us (level)
  no operation moved by 1% of the time
where the time goes in v11:
time: 72.3 us; the launch traced here: 71.9 us
  starting transfers between devices  36 us (50%)
  waiting for transfers between devices  19.3 us (27%)
  Pallas kernels  16 us (22%)
    ppermute x9, starting transfers between devices, across_rows(): lax.ppermute(value, 'row', [(i, i ^ count // 2) for i in range(count)])  18.2 us
    pallas_call x27, Pallas kernels, call(): pl.pallas_call(kernel, out_shape=out_shape, in_specs=[in_spec or VMEM] *...  16 us
    ppermute x8, starting transfers between devices, two_along(): lax.ppermute(value, 'col', [(i, (i + 2) % count) for i in range(count)])  12.5 us
    ppermute x9, waiting for transfers between devices, across_rows(): lax.ppermute(value, 'row', [(i, i ^ count // 2) for i in range(count)])  7.29 us
    ppermute x4, waiting for transfers between devices, across_pair(): lax.ppermute(value, 'col', [(i, i ^ 1) for i in range(lax.axis_size('col'...  6.54 us
    ppermute x8, waiting for transfers between devices, two_along(): lax.ppermute(value, 'col', [(i, (i + 2) % count) for i in range(count)])  5.48 us
    ppermute x4, starting transfers between devices, across_pair(): lax.ppermute(value, 'col', [(i, i ^ 1) for i in range(lax.axis_size('col'...  5.33 us
  transfers between devices with their start and end apart: 21, of which 10 were waited for; matrix products, arithmetic and copies ran while one was open for 0% of the time, Pallas kernels for 18%

profile of v11, /device:TPU:0, one launch (start us, length us, event | category | flops | bytes accessed | tf_op | source)
XLA Modules:
  0.0 71.9 jit_solution(1207377070575648798)
XLA Ops:
  0.0 1.6 %shard_map.64 = (bf16[256,512]{1,0:T(8,128)(2,1)S(1)}, bf16[2048,512]{1,0:T(8,128)(2,1)S(1)}) custom-call(s32[1,2048]{1,0:T(1,128)} %bitcast.6, bf16[2048,512]{1,0:T(8,128)(2,1)} %refs_1_.1), custom_call_target="tpu_custom_call" | custom-call | flops 4000000000 | bytes 1 | tf_op jit(solution)/shard_map/pallas_call | solution.py:45
  1.6 3.6 %collective-permute-start = (bf16[256,512]{1,0:T(8,128)(2,1)S(1)}, bf16[256,512]{1,0:T(8,128)(2,1)S(1)}, u32[]{:S(2)}, u32[]{:S(2)}) collective-permute-start(bf16[256,512]{1,0:T(8,128)(2,1)S(1)} %get-tuple-element.24.refs_2_), channel_id=1, source_target_pairs={{0,16},{8,24},{16,0},{24,8},{1,17},{9,25},{17,1},{25,9},{2,18},{10... | collective-permute-start | bytes 786440 | tf_op jit(solution)/shard_map/ppermute | solution.py:311
  5.3 1.3 %collective-permute-start.1 = (bf16[256,512]{1,0:T(8,128)(2,1)S(1)}, bf16[256,512]{1,0:T(8,128)(2,1)S(1)}, u32[]{:S(2)}, u32[]{:S(2)}) collective-permute-start(bf16[256,512]{1,0:T(8,128)(2,1)S(1)} %get-tuple-element.26.refs_1_), channel_id=1, source_target_pairs={{0,16},{8,24},{16,0},{24,8},{1,17},{9,25},{17,1},{25,9},{2,18},{10... | collective-permute-start | bytes 786440 | tf_op jit(solution)/shard_map/ppermute | solution.py:311
  6.8 1.5 %shard_map.66 = (bf16[1024,512]{1,0:T(8,128)(2,1)S(1)}, bf16[1024,512]{1,0:T(8,128)(2,1)S(1)}, bf16[1024,512]{1,0:T(8,128)(2,1)S(1)}, bf16[1024,512]{1,0:T(8,128)(2,1)S(1)}) custom-call(bf16[512,2048]{1,0:T(8,128)(2,1)S(1)} %copy-done, bf16[256,512]{1,0:T(8,128)(2,1)S(1)} %get-tuple-element.26.refs_1_), custom_call_target="tpu_custom_call" | custom-call | flops 4000000000 | bytes 1 | tf_op jit(solution)/shard_map/pallas_call | solution.py:45
  8.3 1.6 %shard_map.67 = (f32[1,1024]{1,0:T(1,128)S(1)}, f32[1,1024]{1,0:T(1,128)S(1)}, f32[1,512]{1,0:T(1,128)S(1)}) custom-call(s32[1,2048]{1,0:T(1,128)S(1)} %bitcast.4, f32[1,200]{1,0:T(1,128)S(1)} %bitcast.14, f32[1,2000]{1,0:T(1,128)S(1)} %bitcast.5, bf16[1024,512]{1,0:T(8,128)(2,1)S(1)} %get-tuple-element.28.refs_3_.refs_2_), custom_call_target="tpu_custom_call" | custom-call | flops 4000000000 | bytes 1 | tf_op jit(solution)/shard_map/pallas_call | solution.py:45
  10.0 0.7 collective-permute-start.11
  10.6 1.8 %collective-permute-done.refs_1_ = bf16[256,512]{1,0:T(8,128)(2,1)S(1)} collective-permute-done((bf16[256,512]{1,0:T(8,128)(2,1)S(1)}, bf16[256,512]{1,0:T(8,128)(2,1)S(1)}, u32[]{:S(2)}, u32[]{:S(2)}) %collective-permute-start) | collective-permute-done | bytes 262176 | tf_op jit(solution)/shard_map/ppermute | solution.py:311
  12.9 1.6 %collective-permute-start.4 = (s16[1040,128]{1,0:T(8,128)(2,1)S(1)}, s16[1040,128]{1,0:T(8,128)(2,1)S(1)}, u32[]{:S(2)}, u32[]{:S(2)}) collective-permute-start(s16[1040,128]{1,0:T(8,128)(2,1)S(1)} %shard_map.68.refs_2_), channel_id=1, source_target_pairs={{0,2},{1,3},{2,4},{3,5},{4,6},{5,7},{6,0},{7,1},{8,10},{9,11},{10,... | collective-permute-start | bytes 798728 | tf_op jit(solution)/shard_map/ppermute | solution.py:320
  14.6 3.3 %collective-permute-start.5 = (bf16[256,512]{1,0:T(8,128)(2,1)S(1)}, bf16[256,512]{1,0:T(8,128)(2,1)S(1)}, u32[]{:S(2)}, u32[]{:S(2)}) collective-permute-start(bf16[256,512]{1,0:T(8,128)(2,1)S(1)} %get-tuple-element.31.refs_3_), channel_id=1, source_target_pairs={{0,16},{8,24},{16,0},{24,8},{1,17},{9,25},{17,1},{25,9},{2,18},{10... | collective-permute-start | bytes 786440 | tf_op jit(solution)/shard_map/ppermute | solution.py:311
  18.5 1.6 %collective-permute-start.3 = (s16[1040,128]{1,0:T(8,128)(2,1)S(1)}, s16[1040,128]{1,0:T(8,128)(2,1)S(1)}, u32[]{:S(2)}, u32[]{:S(2)}) collective-permute-start(s16[1040,128]{1,0:T(8,128)(2,1)S(1)} %shard_map.70.refs_2_), channel_id=1, source_target_pairs={{0,2},{1,3},{2,4},{3,5},{4,6},{5,7},{6,0},{7,1},{8,10},{9,11},{10,... | collective-permute-start | bytes 798728 | tf_op jit(solution)/shard_map/ppermute | solution.py:320
  20.2 3.6 %collective-permute-start.2 = (bf16[256,512]{1,0:T(8,128)(2,1)S(1)}, bf16[256,512]{1,0:T(8,128)(2,1)S(1)}, u32[]{:S(2)}, u32[]{:S(2)}) collective-permute-start(bf16[256,512]{1,0:T(8,128)(2,1)S(1)} %get-tuple-element.33.refs_3_), channel_id=1, source_target_pairs={{0,16},{8,24},{16,0},{24,8},{1,17},{9,25},{17,1},{25,9},{2,18},{10... | collective-permute-start | bytes 786440 | tf_op jit(solution)/shard_map/ppermute | solution.py:311
  24.3 1.6 %collective-permute-start.7 = (s16[1040,128]{1,0:T(8,128)(2,1)S(1)}, s16[1040,128]{1,0:T(8,128)(2,1)S(1)}, u32[]{:S(2)}, u32[]{:S(2)}) collective-permute-start(s16[1040,128]{1,0:T(8,128)(2,1)S(1)} %shard_map.72.refs_4_), channel_id=1, source_target_pairs={{0,2},{1,3},{2,4},{3,5},{4,6},{5,7},{6,0},{7,1},{8,10},{9,11},{10,... | collective-permute-start | bytes 798728 | tf_op jit(solution)/shard_map/ppermute | solution.py:320
  26.5 1.6 %collective-permute-start.8 = (s16[1040,128]{1,0:T(8,128)(2,1)S(1)}, s16[1040,128]{1,0:T(8,128)(2,1)S(1)}, u32[]{:S(2)}, u32[]{:S(2)}) collective-permute-start(s16[1040,128]{1,0:T(8,128)(2,1)S(1)} %shard_map.73.refs_4_), channel_id=1, source_target_pairs={{0,1},{1,0},{2,3},{3,2},{4,5},{5,4},{6,7},{7,6},{8,9},{9,8},{10,11... | collective-permute-start | bytes 798728 | tf_op jit(solution)/shard_map/ppermute | solution.py:315
  28.6 0.9 %collective-permute-start.13 = (s16[1040,128]{1,0:T(8,128)(2,1)S(1)}, s16[1040,128]{1,0:T(8,128)(2,1)S(1)}, u32[]{:S(2)}, u32[]{:S(2)}) collective-permute-start(s16[1040,128]{1,0:T(8,128)(2,1)S(1)} %shard_map.74.refs_3_), channel_id=1, source_target_pairs={{0,1},{1,0},{2,3},{3,2},{4,5},{5,4},{6,7},{7,6},{8,9},{9,8},{10,11... | collective-permute-start | bytes 798728 | tf_op jit(solution)/shard_map/ppermute | solution.py:315
  30.0 1.6 %collective-permute-start.6 = (s16[1040,128]{1,0:T(8,128)(2,1)S(1)}, s16[1040,128]{1,0:T(8,128)(2,1)S(1)}, u32[]{:S(2)}, u32[]{:S(2)}) collective-permute-start(s16[1040,128]{1,0:T(8,128)(2,1)S(1)} %shard_map.75.refs_4_), channel_id=1, source_target_pairs={{0,2},{1,3},{2,4},{3,5},{4,6},{5,7},{6,0},{7,1},{8,10},{9,11},{10,... | collective-permute-start | bytes 798728 | tf_op jit(solution)/shard_map/ppermute | solution.py:320
  31.6 3.8 %collective-permute-done.8.refs_3_ = s16[1040,128]{1,0:T(8,128)(2,1)S(1)} collective-permute-done((s16[1040,128]{1,0:T(8,128)(2,1)S(1)}, s16[1040,128]{1,0:T(8,128)(2,1)S(1)}, u32[]{:S(2)}, u32[]{:S(2)}) %collective-permute-start.8) | collective-permute-done | bytes 266272 | tf_op jit(solution)/shard_map/ppermute | solution.py:315
  35.9 1.1 %collective-permute-start.10 = (s16[1040,128]{1,0:T(8,128)(2,1)S(1)}, s16[1040,128]{1,0:T(8,128)(2,1)S(1)}, u32[]{:S(2)}, u32[]{:S(2)}) collective-permute-start(s16[1040,128]{1,0:T(8,128)(2,1)S(1)} %shard_map.76.refs_4_), channel_id=1, source_target_pairs={{0,2},{1,3},{2,4},{3,5},{4,6},{5,7},{6,0},{7,1},{8,10},{9,11},{10,... | collective-permute-start | bytes 798728 | tf_op jit(solution)/shard_map/ppermute | solution.py:320
  37.6 1.6 %collective-permute-start.12 = (s16[1040,128]{1,0:T(8,128)(2,1)S(1)}, s16[1040,128]{1,0:T(8,128)(2,1)S(1)}, u32[]{:S(2)}, u32[]{:S(2)}) collective-permute-start(s16[1040,128]{1,0:T(8,128)(2,1)S(1)} %shard_map.77.refs_4_), channel_id=1, source_target_pairs={{0,1},{1,0},{2,3},{3,2},{4,5},{5,4},{6,7},{7,6},{8,9},{9,8},{10,11... | collective-permute-start | bytes 798728 | tf_op jit(solution)/shard_map/ppermute | solution.py:315
  39.2 2.0 %collective-permute-done.6.refs_3_ = s16[1040,128]{1,0:T(8,128)(2,1)S(1)} collective-permute-done((s16[1040,128]{1,0:T(8,128)(2,1)S(1)}, s16[1040,128]{1,0:T(8,128)(2,1)S(1)}, u32[]{:S(2)}, u32[]{:S(2)}) %collective-permute-start.6) | collective-permute-done | bytes 266272 | tf_op jit(solution)/shard_map/ppermute | solution.py:320
  41.7 1.3 %collective-permute-start.9 = (s16[1040,128]{1,0:T(8,128)(2,1)S(1)}, s16[1040,128]{1,0:T(8,128)(2,1)S(1)}, u32[]{:S(2)}, u32[]{:S(2)}) collective-permute-start(s16[1040,128]{1,0:T(8,128)(2,1)S(1)} %shard_map.78.refs_4_), channel_id=1, source_target_pairs={{0,1},{1,0},{2,3},{3,2},{4,5},{5,4},{6,7},{7,6},{8,9},{9,8},{10,11... | collective-permute-start | bytes 798728 | tf_op jit(solution)/shard_map/ppermute | solution.py:315
  43.6 2.7 %collective-permute-done.12.refs_3_ = s16[1040,128]{1,0:T(8,128)(2,1)S(1)} collective-permute-done((s16[1040,128]{1,0:T(8,128)(2,1)S(1)}, s16[1040,128]{1,0:T(8,128)(2,1)S(1)}, u32[]{:S(2)}, u32[]{:S(2)}) %collective-permute-start.12) | collective-permute-done | bytes 266272 | tf_op jit(solution)/shard_map/ppermute | solution.py:315
  46.9 1.8 %collective-permute-start.16 = (s16[1040,128]{1,0:T(8,128)(2,1)S(1)}, s16[1040,128]{1,0:T(8,128)(2,1)S(1)}, u32[]{:S(2)}, u32[]{:S(2)}) collective-permute-start(s16[1040,128]{1,0:T(8,128)(2,1)S(1)} %shard_map.80.refs_8_), channel_id=1, source_target_pairs={{0,2},{1,3},{2,4},{3,5},{4,6},{5,7},{6,0},{7,1},{8,10},{9,11},{10,... | collective-permute-start | bytes 798728 | tf_op jit(solution)/shard_map/ppermute | solution.py:320
  49.2 0.9 %collective-permute-start.15 = (bf16[256,512]{1,0:T(8,128)(2,1)S(1)}, bf16[256,512]{1,0:T(8,128)(2,1)S(1)}, u32[]{:S(2)}, u32[]{:S(2)}) collective-permute-start(bf16[256,512]{1,0:T(8,128)(2,1)S(1)} %shard_map.81.refs_4_.refs_1_), channel_id=1, source_target_pairs={{0,16},{8,24},{16,0},{24,8},{1,17},{9,25},{17,1},{25,9},{2,18},{10... | collective-permute-start | bytes 786440 | tf_op jit(solution)/shard_map/ppermute | solution.py:311
  50.7 3.0 %collective-permute-start.14 = (s16[1040,128]{1,0:T(8,128)(2,1)S(1)}, s16[1040,128]{1,0:T(8,128)(2,1)S(1)}, u32[]{:S(2)}, u32[]{:S(2)}) collective-permute-start(s16[1040,128]{1,0:T(8,128)(2,1)S(1)} %shard_map.82.refs_8_), channel_id=1, source_target_pairs={{0,2},{1,3},{2,4},{3,5},{4,6},{5,7},{6,0},{7,1},{8,10},{9,11},{10,... | collective-permute-start | bytes 798728 | tf_op jit(solution)/shard_map/ppermute | solution.py:320
  53.7 1.0 %collective-permute-done.17.refs_4_ = s16[1040,128]{1,0:T(8,128)(2,1)S(1)} collective-permute-done((s16[1040,128]{1,0:T(8,128)(2,1)S(1)}, s16[1040,128]{1,0:T(8,128)(2,1)S(1)}, u32[]{:S(2)}, u32[]{:S(2)}) %collective-permute-start.17) | collective-permute-done | bytes 266272 | tf_op jit(solution)/shard_map/ppermute | solution.py:320
  55.3 1.2 %collective-permute-start.19 = (bf16[256,512]{1,0:T(8,128)(2,1)S(1)}, bf16[256,512]{1,0:T(8,128)(2,1)S(1)}, u32[]{:S(2)}, u32[]{:S(2)}) collective-permute-start(bf16[256,512]{1,0:T(8,128)(2,1)S(1)} %shard_map.83.refs_8_.refs_1_), channel_id=1, source_target_pairs={{0,16},{8,24},{16,0},{24,8},{1,17},{9,25},{17,1},{25,9},{2,18},{10... | collective-permute-start | bytes 786440 | tf_op jit(solution)/shard_map/ppermute | solution.py:311
  56.5 2.1 %collective-permute-done.16.refs_4_ = s16[1040,128]{1,0:T(8,128)(2,1)S(1)} collective-permute-done((s16[1040,128]{1,0:T(8,128)(2,1)S(1)}, s16[1040,128]{1,0:T(8,128)(2,1)S(1)}, u32[]{:S(2)}, u32[]{:S(2)}) %collective-permute-start.16) | collective-permute-done | bytes 266272 | tf_op jit(solution)/shard_map/ppermute | solution.py:320
  59.2 1.8 %collective-permute-start.18 = (bf16[256,512]{1,0:T(8,128)(2,1)S(1)}, bf16[256,512]{1,0:T(8,128)(2,1)S(1)}, u32[]{:S(2)}, u32[]{:S(2)}) collective-permute-start(bf16[256,512]{1,0:T(8,128)(2,1)S(1)} %shard_map.84.refs_3_.refs_1_), channel_id=1, source_target_pairs={{0,16},{8,24},{16,0},{24,8},{1,17},{9,25},{17,1},{25,9},{2,18},{10... | collective-permute-start | bytes 786440 | tf_op jit(solution)/shard_map/ppermute | solution.py:311
  62.0 1.8 %collective-permute-start.20 = (bf16[256,512]{1,0:T(8,128)(2,1)S(1)}, bf16[256,512]{1,0:T(8,128)(2,1)S(1)}, u32[]{:S(2)}, u32[]{:S(2)}) collective-permute-start(bf16[256,512]{1,0:T(8,128)(2,1)S(1)} %shard_map.86.refs_4_.refs_1_), channel_id=1, source_target_pairs={{0,16},{8,24},{16,0},{24,8},{1,17},{9,25},{17,1},{25,9},{2,18},{10... | collective-permute-start | bytes 786440 | tf_op jit(solution)/shard_map/ppermute | solution.py:311
  64.1 3.2 %collective-permute-done.18.refs_2_ = bf16[256,512]{1,0:T(8,128)(2,1)S(1)} collective-permute-done((bf16[256,512]{1,0:T(8,128)(2,1)S(1)}, bf16[256,512]{1,0:T(8,128)(2,1)S(1)}, u32[]{:S(2)}, u32[]{:S(2)}) %collective-permute-start.18) | collective-permute-done | bytes 262176 | tf_op jit(solution)/shard_map/ppermute | solution.py:311
  67.9 2.2 %collective-permute-done.20.refs_2_ = bf16[256,512]{1,0:T(8,128)(2,1)S(1)} collective-permute-done((bf16[256,512]{1,0:T(8,128)(2,1)S(1)}, bf16[256,512]{1,0:T(8,128)(2,1)S(1)}, u32[]{:S(2)}, u32[]{:S(2)}) %collective-permute-start.20) | collective-permute-done | bytes 262176 | tf_op jit(solution)/shard_map/ppermute | solution.py:311
  70.1 1.7 %shard_map.90 = bf16[2048,512]{1,0:T(8,128)(2,1)} custom-call(bf16[2048,512]{1,0:T(8,128)(2,1)S(1)} %get-tuple-element.39.refs_0_, bf16[2048,256]{1,0:T(8,128)(2,1)S(1)} %get-tuple-element.40.refs_1_, bf16[256,512]{1,0:T(8,128)(2,1)S(1)} %collective-permute-done.20.refs_2_), custom_call_target="tpu_custom_call" | custom-call | flops 4000000000 | bytes 1 | tf_op jit(solution)/shard_map/pallas_call | solution.py:45
  (47 shorter events, 10.3 us)
Async XLA Ops:
  0.0 5.2 %copy-start.3 = (s32[2048]{0:T(1024)S(1)}, s32[2048]{0:T(1024)}, u32[]{:S(2)}) copy-start(s32[2048]{0:T(1024)} %param.9) | copy-start | bytes 24580
  1.6 10.7 %collective-permute-start = (bf16[256,512]{1,0:T(8,128)(2,1)S(1)}, bf16[256,512]{1,0:T(8,128)(2,1)S(1)}, u32[]{:S(2)}, u32[]{:S(2)}) collective-permute-start(bf16[256,512]{1,0:T(8,128)(2,1)S(1)} %get-tuple-element.24.refs_2_), channel_id=1, source_target_pairs={{0,16},{8,24},{16,0},{24,8},{1,17},{9,25},{17,1},{25,9},{2,18},{10... | collective-permute-start | bytes 786440 | tf_op jit(solution)/shard_map/ppermute | solution.py:311
  5.2 1.6 %copy-start = (bf16[512,2048]{1,0:T(8,128)(2,1)S(1)}, bf16[512,2048]{1,0:T(8,128)(2,1)}, u32[]{:S(2)}) copy-start(bf16[512,2048]{1,0:T(8,128)(2,1)} %refs_0_.1) | copy-start | bytes 6291460
  5.3 3.0 %copy-start.1 = (s32[2048]{0:T(1024)S(1)}, s32[2048]{0:T(1024)}, u32[]{:S(2)}) copy-start(s32[2048]{0:T(1024)} %param.8) | copy-start | bytes 24580
  5.3 3.0 %copy-start.2 = (f32[2000]{0:T(1024)S(1)}, f32[2000]{0:T(1024)}, u32[]{:S(2)}) copy-start(f32[2000]{0:T(1024)} %param.11) | copy-start | bytes 24004
  5.3 3.0 %copy-start.4 = (f32[200]{0:T(256)S(1)}, f32[200]{0:T(256)}, u32[]{:S(2)}) copy-start(f32[200]{0:T(256)} %param.10) | copy-start | bytes 2404
  5.3 12.7 %collective-permute-start.1 = (bf16[256,512]{1,0:T(8,128)(2,1)S(1)}, bf16[256,512]{1,0:T(8,128)(2,1)S(1)}, u32[]{:S(2)}, u32[]{:S(2)}) collective-permute-start(bf16[256,512]{1,0:T(8,128)(2,1)S(1)} %get-tuple-element.26.refs_1_), channel_id=1, source_target_pairs={{0,16},{8,24},{16,0},{24,8},{1,17},{9,25},{17,1},{25,9},{2,18},{10... | collective-permute-start | bytes 786440 | tf_op jit(solution)/shard_map/ppermute | solution.py:311
  10.0 38.7 %collective-permute-start.11 = (f32[1,1024]{1,0:T(1,128)S(1)}, f32[1,1024]{1,0:T(1,128)S(1)}, u32[]{:S(2)}, u32[]{:S(2)}) collective-permute-start(f32[1,1024]{1,0:T(1,128)S(1)} %get-tuple-element.38), channel_id=1, source_target_pairs={{0,16},{8,24},{16,0},{24,8},{1,17},{9,25},{17,1},{25,9},{2,18},{10... | collective-permute-start | bytes 12296 | tf_op jit(solution)/shard_map/ppermute | solution.py:311
  12.9 13.1 %collective-permute-start.4 = (s16[1040,128]{1,0:T(8,128)(2,1)S(1)}, s16[1040,128]{1,0:T(8,128)(2,1)S(1)}, u32[]{:S(2)}, u32[]{:S(2)}) collective-permute-start(s16[1040,128]{1,0:T(8,128)(2,1)S(1)} %shard_map.68.refs_2_), channel_id=1, source_target_pairs={{0,2},{1,3},{2,4},{3,5},{4,6},{5,7},{6,0},{7,1},{8,10},{9,11},{10,... | collective-permute-start | bytes 798728 | tf_op jit(solution)/shard_map/ppermute | solution.py:320
  14.6 9.2 %collective-permute-start.5 = (bf16[256,512]{1,0:T(8,128)(2,1)S(1)}, bf16[256,512]{1,0:T(8,128)(2,1)S(1)}, u32[]{:S(2)}, u32[]{:S(2)}) collective-permute-start(bf16[256,512]{1,0:T(8,128)(2,1)S(1)} %get-tuple-element.31.refs_3_), channel_id=1, source_target_pairs={{0,16},{8,24},{16,0},{24,8},{1,17},{9,25},{17,1},{25,9},{2,18},{10... | collective-permute-start | bytes 786440 | tf_op jit(solution)/shard_map/ppermute | solution.py:311
  18.5 9.6 %collective-permute-start.3 = (s16[1040,128]{1,0:T(8,128)(2,1)S(1)}, s16[1040,128]{1,0:T(8,128)(2,1)S(1)}, u32[]{:S(2)}, u32[]{:S(2)}) collective-permute-start(s16[1040,128]{1,0:T(8,128)(2,1)S(1)} %shard_map.70.refs_2_), channel_id=1, source_target_pairs={{0,2},{1,3},{2,4},{3,5},{4,6},{5,7},{6,0},{7,1},{8,10},{9,11},{10,... | collective-permute-start | bytes 798728 | tf_op jit(solution)/shard_map/ppermute | solution.py:320
  20.2 9.3 %collective-permute-start.2 = (bf16[256,512]{1,0:T(8,128)(2,1)S(1)}, bf16[256,512]{1,0:T(8,128)(2,1)S(1)}, u32[]{:S(2)}, u32[]{:S(2)}) collective-permute-start(bf16[256,512]{1,0:T(8,128)(2,1)S(1)} %get-tuple-element.33.refs_3_), channel_id=1, source_target_pairs={{0,16},{8,24},{16,0},{24,8},{1,17},{9,25},{17,1},{25,9},{2,18},{10... | collective-permute-start | bytes 786440 | tf_op jit(solution)/shard_map/ppermute | solution.py:311
  24.3 12.7 %collective-permute-start.7 = (s16[1040,128]{1,0:T(8,128)(2,1)S(1)}, s16[1040,128]{1,0:T(8,128)(2,1)S(1)}, u32[]{:S(2)}, u32[]{:S(2)}) collective-permute-start(s16[1040,128]{1,0:T(8,128)(2,1)S(1)} %shard_map.72.refs_4_), channel_id=1, source_target_pairs={{0,2},{1,3},{2,4},{3,5},{4,6},{5,7},{6,0},{7,1},{8,10},{9,11},{10,... | collective-permute-start | bytes 798728 | tf_op jit(solution)/shard_map/ppermute | solution.py:320
  26.5 8.9 %collective-permute-start.8 = (s16[1040,128]{1,0:T(8,128)(2,1)S(1)}, s16[1040,128]{1,0:T(8,128)(2,1)S(1)}, u32[]{:S(2)}, u32[]{:S(2)}) collective-permute-start(s16[1040,128]{1,0:T(8,128)(2,1)S(1)} %shard_map.73.refs_4_), channel_id=1, source_target_pairs={{0,1},{1,0},{2,3},{3,2},{4,5},{5,4},{6,7},{7,6},{8,9},{9,8},{10,11... | collective-permute-start | bytes 798728 | tf_op jit(solution)/shard_map/ppermute | solution.py:315
  28.6 14.4 %collective-permute-start.13 = (s16[1040,128]{1,0:T(8,128)(2,1)S(1)}, s16[1040,128]{1,0:T(8,128)(2,1)S(1)}, u32[]{:S(2)}, u32[]{:S(2)}) collective-permute-start(s16[1040,128]{1,0:T(8,128)(2,1)S(1)} %shard_map.74.refs_3_), channel_id=1, source_target_pairs={{0,1},{1,0},{2,3},{3,2},{4,5},{5,4},{6,7},{7,6},{8,9},{9,8},{10,11... | collective-permute-start | bytes 798728 | tf_op jit(solution)/shard_map/ppermute | solution.py:315
  30.0 11.2 %collective-permute-start.6 = (s16[1040,128]{1,0:T(8,128)(2,1)S(1)}, s16[1040,128]{1,0:T(8,128)(2,1)S(1)}, u32[]{:S(2)}, u32[]{:S(2)}) collective-permute-start(s16[1040,128]{1,0:T(8,128)(2,1)S(1)} %shard_map.75.refs_4_), channel_id=1, source_target_pairs={{0,2},{1,3},{2,4},{3,5},{4,6},{5,7},{6,0},{7,1},{8,10},{9,11},{10,... | collective-permute-start | bytes 798728 | tf_op jit(solution)/shard_map/ppermute | solution.py:320
  35.9 12.7 %collective-permute-start.10 = (s16[1040,128]{1,0:T(8,128)(2,1)S(1)}, s16[1040,128]{1,0:T(8,128)(2,1)S(1)}, u32[]{:S(2)}, u32[]{:S(2)}) collective-permute-start(s16[1040,128]{1,0:T(8,128)(2,1)S(1)} %shard_map.76.refs_4_), channel_id=1, source_target_pairs={{0,2},{1,3},{2,4},{3,5},{4,6},{5,7},{6,0},{7,1},{8,10},{9,11},{10,... | collective-permute-start | bytes 798728 | tf_op jit(solution)/shard_map/ppermute | solution.py:320
  37.6 8.7 %collective-permute-start.12 = (s16[1040,128]{1,0:T(8,128)(2,1)S(1)}, s16[1040,128]{1,0:T(8,128)(2,1)S(1)}, u32[]{:S(2)}, u32[]{:S(2)}) collective-permute-start(s16[1040,128]{1,0:T(8,128)(2,1)S(1)} %shard_map.77.refs_4_), channel_id=1, source_target_pairs={{0,1},{1,0},{2,3},{3,2},{4,5},{5,4},{6,7},{7,6},{8,9},{9,8},{10,11... | collective-permute-start | bytes 798728 | tf_op jit(solution)/shard_map/ppermute | solution.py:315
  41.7 8.5 %collective-permute-start.9 = (s16[1040,128]{1,0:T(8,128)(2,1)S(1)}, s16[1040,128]{1,0:T(8,128)(2,1)S(1)}, u32[]{:S(2)}, u32[]{:S(2)}) collective-permute-start(s16[1040,128]{1,0:T(8,128)(2,1)S(1)} %shard_map.78.refs_4_), channel_id=1, source_target_pairs={{0,1},{1,0},{2,3},{3,2},{4,5},{5,4},{6,7},{7,6},{8,9},{9,8},{10,11... | collective-permute-start | bytes 798728 | tf_op jit(solution)/shard_map/ppermute | solution.py:315
  43.5 11.2 %collective-permute-start.17 = (s16[1040,128]{1,0:T(8,128)(2,1)S(1)}, s16[1040,128]{1,0:T(8,128)(2,1)S(1)}, u32[]{:S(2)}, u32[]{:S(2)}) collective-permute-start(s16[1040,128]{1,0:T(8,128)(2,1)S(1)} %shard_map.79.refs_4_), channel_id=1, source_target_pairs={{0,2},{1,3},{2,4},{3,5},{4,6},{5,7},{6,0},{7,1},{8,10},{9,11},{10,... | collective-permute-start | bytes 798728 | tf_op jit(solution)/shard_map/ppermute | solution.py:320
  46.9 11.8 %collective-permute-start.16 = (s16[1040,128]{1,0:T(8,128)(2,1)S(1)}, s16[1040,128]{1,0:T(8,128)(2,1)S(1)}, u32[]{:S(2)}, u32[]{:S(2)}) collective-permute-start(s16[1040,128]{1,0:T(8,128)(2,1)S(1)} %shard_map.80.refs_8_), channel_id=1, source_target_pairs={{0,2},{1,3},{2,4},{3,5},{4,6},{5,7},{6,0},{7,1},{8,10},{9,11},{10,... | collective-permute-start | bytes 798728 | tf_op jit(solution)/shard_map/ppermute | solution.py:320
  49.2 11.7 %collective-permute-start.15 = (bf16[256,512]{1,0:T(8,128)(2,1)S(1)}, bf16[256,512]{1,0:T(8,128)(2,1)S(1)}, u32[]{:S(2)}, u32[]{:S(2)}) collective-permute-start(bf16[256,512]{1,0:T(8,128)(2,1)S(1)} %shard_map.81.refs_4_.refs_1_), channel_id=1, source_target_pairs={{0,16},{8,24},{16,0},{24,8},{1,17},{9,25},{17,1},{25,9},{2,18},{10... | collective-permute-start | bytes 786440 | tf_op jit(solution)/shard_map/ppermute | solution.py:311
  50.7 10.8 %collective-permute-start.14 = (s16[1040,128]{1,0:T(8,128)(2,1)S(1)}, s16[1040,128]{1,0:T(8,128)(2,1)S(1)}, u32[]{:S(2)}, u32[]{:S(2)}) collective-permute-start(s16[1040,128]{1,0:T(8,128)(2,1)S(1)} %shard_map.82.refs_8_), channel_id=1, source_target_pairs={{0,2},{1,3},{2,4},{3,5},{4,6},{5,7},{6,0},{7,1},{8,10},{9,11},{10,... | collective-permute-start | bytes 798728 | tf_op jit(solution)/shard_map/ppermute | solution.py:320
  55.3 8.5 %collective-permute-start.19 = (bf16[256,512]{1,0:T(8,128)(2,1)S(1)}, bf16[256,512]{1,0:T(8,128)(2,1)S(1)}, u32[]{:S(2)}, u32[]{:S(2)}) collective-permute-start(bf16[256,512]{1,0:T(8,128)(2,1)S(1)} %shard_map.83.refs_8_.refs_1_), channel_id=1, source_target_pairs={{0,16},{8,24},{16,0},{24,8},{1,17},{9,25},{17,1},{25,9},{2,18},{10... | collective-permute-start | bytes 786440 | tf_op jit(solution)/shard_map/ppermute | solution.py:311
  59.2 8.2 %collective-permute-start.18 = (bf16[256,512]{1,0:T(8,128)(2,1)S(1)}, bf16[256,512]{1,0:T(8,128)(2,1)S(1)}, u32[]{:S(2)}, u32[]{:S(2)}) collective-permute-start(bf16[256,512]{1,0:T(8,128)(2,1)S(1)} %shard_map.84.refs_3_.refs_1_), channel_id=1, source_target_pairs={{0,16},{8,24},{16,0},{24,8},{1,17},{9,25},{17,1},{25,9},{2,18},{10... | collective-permute-start | bytes 786440 | tf_op jit(solution)/shard_map/ppermute | solution.py:311
  62.0 8.1 %collective-permute-start.20 = (bf16[256,512]{1,0:T(8,128)(2,1)S(1)}, bf16[256,512]{1,0:T(8,128)(2,1)S(1)}, u32[]{:S(2)}, u32[]{:S(2)}) collective-permute-start(bf16[256,512]{1,0:T(8,128)(2,1)S(1)} %shard_map.86.refs_4_.refs_1_), channel_id=1, source_target_pairs={{0,16},{8,24},{16,0},{24,8},{1,17},{9,25},{17,1},{25,9},{2,18},{10... | collective-permute-start | bytes 786440 | tf_op jit(solution)/shard_map/ppermute | solution.py:311
